TPU v7x, 32 devices: a whole 2x2x4 slice. The times are simulated.
32 devices in a mesh: row: 4 (over y, x), col: 8 (over z, core).
Axes of the slice: x: 2, y: 2, z: 4, core: 2. Of those that a mesh axis runs over, the one named last changes fastest.
Arguments:
- features: bfloat16 [8192, 256], P(('row', 'col')), may hold values from -6 to 6
- weight: bfloat16 [256, 256], replicated, may hold values from -0.375 to 0.375
- cotangent: bfloat16 [8192, 256], P(('row', 'col')), may hold values from -6 to 6
- tiles: int32 [4, 8, 2, 64], P('row', 'col'), may hold values from 0 to 15, as said below
- tile_count: int32 [4, 8], P('row', 'col'), may hold values from 8 to 64, as said below
- patterns: int32 [4, 8, 64, 16, 128], P('row', 'col'), may hold values from 0 to 255
Outputs:
- activated: bfloat16 [8192, 256], P(('row', 'col'))
- grad_features: bfloat16 [8192, 256], P(('row', 'col'))
- grad_weight: float32 [256, 256], replicated
Inputs may be any that keep to these rules, and one draw needn't show every extreme that they name: `tiles`: on each device the slots name distinct pairs (block row a among its 16 block rows, block column b among its 8 block columns); slots at or after tile_count are not part of S. `tile_count`: live slots of one device; some device has exactly 64 in every draw.
All inputs are finite; a program needn't handle non-finite values.
Results may differ from a plain program's by a relative error of at most 0.018.
Values may be sent and summed in bfloat16 or wider, within the bound.
No kernel may reach another device: no remote copies, remote signals or barrier semaphores. Data moves between devices by JAX's collectives and lax.ppermute only.
A program may use at most 64 MiB of HBM per device.

v0:
```python
import jax
import jax.numpy as jnp
from jax import lax
from jax.sharding import PartitionSpec as P

group_size = 32


def unpack_tiles(packed):
    shifts = jnp.arange(8, dtype=jnp.int32)
    bits = jnp.bitwise_and(jnp.right_shift(packed[:, :, None, :], shifts[:, None]), 1)
    return bits.reshape(packed.shape[0], packed.shape[1] * 8, packed.shape[2])


def one_hot_table(index, count, dtype):
    return (index[:, None] == jnp.arange(count, dtype=jnp.int32)[None, :]).astype(dtype)


def pick_blocks(index, blocks_all):
    table = one_hot_table(index, blocks_all.shape[0], jnp.bfloat16)
    return jnp.einsum("gc,ckf->gkf", table, blocks_all, preferred_element_type=jnp.float32).astype(
        jnp.bfloat16
    )


def place_blocks(index, count, values):
    table = one_hot_table(index, count, jnp.float32)
    return jnp.einsum(
        "gr,gif->rif",
        table,
        values,
        precision=lax.Precision.HIGHEST,
        preferred_element_type=jnp.float32,
    )


def tile_loop(turns, packed_all, live_count, apply, initial):

    def step(turn, carry):
        first = turn * group_size
        packed = lax.dynamic_slice_in_dim(packed_all, first, group_size, 0)
        live = (first + jnp.arange(group_size, dtype=jnp.int32) < live_count).astype(jnp.int32)
        pattern = (unpack_tiles(packed) * live[:, None, None]).astype(jnp.bfloat16)
        return apply(carry, pattern, first)

    return lax.fori_loop(0, turns, step, initial)


def per_device(features, weight, cotangent, tiles, tile_count, patterns):
    rows_dev, width = features.shape
    packed_all = patterns[0, 0]
    tile = packed_all.shape[-1]
    slots_dev = packed_all.shape[0]
    blocks = rows_dev // tile
    n_row = lax.axis_size("row")
    n_col = lax.axis_size("col")
    my_col = lax.axis_index("col")
    row_blocks = n_col * blocks
    col_blocks = n_row * blocks
    tile_rows = tiles[0, 0, 0]
    tile_cols = tiles[0, 0, 1]
    live_count = tile_count[0, 0]
    turns = slots_dev // group_size
    column_feats = lax.all_gather(features, "row", axis=0, tiled=True).reshape(
        col_blocks, tile, width
    )

    def forward_add(carry, pattern, first):
        summed, degree = carry
        row_index = lax.dynamic_slice_in_dim(tile_rows, first, group_size, 0)
        col_index = lax.dynamic_slice_in_dim(tile_cols, first, group_size, 0)
        picked = pick_blocks(col_index, column_feats)
        product = jnp.einsum("gki,gkf->gif", pattern, picked, preferred_element_type=jnp.float32)
        counted = jnp.sum(pattern, axis=1, dtype=jnp.float32)
        row_table = one_hot_table(row_index, row_blocks, jnp.float32)
        degree_add = jnp.dot(
            row_table.T,
            counted,
            precision=lax.Precision.HIGHEST,
            preferred_element_type=jnp.float32,
        )
        return (summed + place_blocks(row_index, row_blocks, product), degree + degree_add)

    initial = (
        jnp.zeros((row_blocks, tile, width), jnp.float32),
        jnp.zeros((row_blocks, tile), jnp.float32),
    )
    summed, degree = tile_loop(turns, packed_all, live_count, forward_add, initial)
    summed = summed.reshape(row_blocks * tile, width)
    degree = degree.reshape(row_blocks * tile)
    whole_sum, whole_degree = (
        lax.psum(summed.astype(jnp.bfloat16), "col").astype(jnp.float32),
        lax.psum(degree.astype(jnp.bfloat16), "col").astype(jnp.float32),
    )
    row_feats, row_cot = (
        lax.all_gather(features, "col", axis=0, tiled=True),
        lax.all_gather(cotangent, "col", axis=0, tiled=True),
    )
    scale = lax.rsqrt(whole_degree + 1.0)
    aggregated = (whole_sum * scale[:, None] + row_feats.astype(jnp.float32)).astype(jnp.bfloat16)
    preact = jnp.dot(aggregated, weight, preferred_element_type=jnp.float32)
    gate_value = jax.nn.sigmoid(preact)
    result = (preact * gate_value).astype(jnp.bfloat16)
    grad_preact = (
        row_cot.astype(jnp.float32) * gate_value * (1.0 + preact * (1.0 - gate_value))
    ).astype(jnp.bfloat16)
    weight_part = lax.dot_general(
        aggregated, grad_preact, (((0,), (0,)), ((), ())), preferred_element_type=jnp.float32
    )
    grad_agg = lax.dot_general(
        grad_preact, weight, (((1,), (1,)), ((), ())), preferred_element_type=jnp.float32
    )
    grad_scaled = (grad_agg * scale[:, None]).astype(jnp.bfloat16)
    row_result, weight_part, row_grad, scaled_rows = (result, weight_part, grad_agg, grad_scaled)
    grad_weight = lax.psum(weight_part.astype(jnp.bfloat16), "row").astype(jnp.float32)
    activated = lax.dynamic_slice_in_dim(row_result, my_col * rows_dev, rows_dev, 0)
    self_grad = lax.dynamic_slice_in_dim(row_grad, my_col * rows_dev, rows_dev, 0)
    scaled_blocks = scaled_rows.reshape(row_blocks, tile, width)

    def backward_add(back, pattern, first):
        row_index = lax.dynamic_slice_in_dim(tile_rows, first, group_size, 0)
        col_index = lax.dynamic_slice_in_dim(tile_cols, first, group_size, 0)
        picked = pick_blocks(row_index, scaled_blocks)
        product = jnp.einsum("gki,gif->gkf", pattern, picked, preferred_element_type=jnp.float32)
        return back + place_blocks(col_index, col_blocks, product)

    back = tile_loop(
        turns,
        packed_all,
        live_count,
        backward_add,
        jnp.zeros((col_blocks, tile, width), jnp.float32),
    )
    back = back.reshape(col_blocks * tile, width)
    grad_features = (
        lax.psum_scatter(back.astype(jnp.bfloat16), "row", scatter_dimension=0, tiled=True).astype(
            jnp.float32
        )
        + self_grad
    ).astype(jnp.bfloat16)
    return (activated, grad_features, grad_weight)


def solution(mesh):
    return jax.shard_map(
        per_device,
        mesh=mesh,
        in_specs=(
            P(("row", "col"), None),
            P(),
            P(("row", "col"), None),
            P("row", "col", None, None),
            P("row", "col"),
            P("row", "col", None, None, None),
        ),
        out_specs=(P(("row", "col"), None), P(("row", "col"), None), P()),
        check_vma=False,
    )
```

profile of v0, /device:TPU:0, one launch (start us, length us, event | category | flops | bytes accessed | tf_op | source)
XLA Modules:
  0.0 255.6 jit_solution(15694206981121143930)
XLA Ops:
  8.0 11.8 %all_gather.9 = bf16[1024,256]{1,0:T(8,128)(2,1)S(1)} all-gather(bf16[256,256]{1,0:T(8,128)(2,1)} %param.10), channel_id=1, replica_groups=mesh['row'=4,'col'=8] {'row'}, dimensions={0}, use_global_device_ids=true | all-gather | bytes 655360 | tf_op jit(solution)/shard_map/all_gather | solution.py:64
  20.1 39.2 %while.30 = (s32[]{:T(128)}, f32[16,128,256]{2,0,1:T(8,128)}, f32[16,128]{1,0:T(8,128)S(1)}, s32[64]{0:T(128)S(1)}, s32[64,16,128]{2,1,0:T(8,128)}, /*index=5*/s...) while((s32[]{:T(128)}, f32[16,128,256]{2,0,1:T(8,128)}, ...), condition=%wide.region_2.0_spmd.clone, body=%wide.region_0.0_spmd.clone.sunk | while | flops 494667104 | bytes 28888548 | solution.py:46
  21.2 1.6 broadcast_bitcast_fusion.2
  22.8 2.9 %copy.49 = s32[32,128,128]{1,2,0:T(8,128)} copy(s32[32,128,128]{2,1,0:T(8,128)} %broadcast_bitcast_fusion.2) | data formatting | bytes 4194304 | tf_op jit(solution)/shard_map/while/body/eval_jaxpr/shift_right_arithmetic | solution.py:11
  26.5 5.0 %fusion.69 = f32[32,128,256]{2,1,0:T(8,128)} fusion(bf16[32,128,256]{2,0,1:T(8,128)(2,1)S(1)} %convolution_convert_fusion.5, s32[32,128,128]{1,2,0:T(8,128)} %copy.49, s32[32]{0:T(128)S(1)} %compare_convert_fusion.4, s32[128]{0:T(128)S(1)} %shift_right_arithmetic.143), kind=kOutput, calls=%fused_computation.2.clone.1 | convolution fusion | flops 270532608 | bytes 8389248 | tf_op jit(solution)/shard_map/while/body/eval_jaxpr/gki,gkf->gif/dot_general | solution.py:73
  31.6 7.3 %select_add_fusion.2 = f32[16,128,256]{2,0,1:T(8,128)} fusion(f32[16,128,256]{2,0,1:T(8,128)} %get-tuple-element.485, f32[32,128,256]{2,1,0:T(8,128)} %fusion.69, pred[]{:T(512)S(6)} %compare.6, s32[32]{0:T(128)S(1)} %dynamic_slice.73), kind=kOutput, calls=%fused_computation.4.clone.1 | convolution fusion | flops 202375680 | bytes 8388737 | tf_op jit(solution)/shard_map/while/body/eval_jaxpr/gr,gif->rif/dot_general | solution.py:28
  40.5 1.6 broadcast_bitcast_fusion.2
  42.1 2.9 %copy.49 = s32[32,128,128]{1,2,0:T(8,128)} copy(s32[32,128,128]{2,1,0:T(8,128)} %broadcast_bitcast_fusion.2) | data formatting | bytes 4194304 | tf_op jit(solution)/shard_map/while/body/eval_jaxpr/shift_right_arithmetic | solution.py:11
  45.7 5.0 %fusion.69 = f32[32,128,256]{2,1,0:T(8,128)} fusion(bf16[32,128,256]{2,0,1:T(8,128)(2,1)S(1)} %convolution_convert_fusion.5, s32[32,128,128]{1,2,0:T(8,128)} %copy.49, s32[32]{0:T(128)S(1)} %compare_convert_fusion.4, s32[128]{0:T(128)S(1)} %shift_right_arithmetic.143), kind=kOutput, calls=%fused_computation.2.clone.1 | convolution fusion | flops 270532608 | bytes 8389248 | tf_op jit(solution)/shard_map/while/body/eval_jaxpr/gki,gkf->gif/dot_general | solution.py:73
  50.8 8.0 %select_add_fusion.2 = f32[16,128,256]{2,0,1:T(8,128)} fusion(f32[16,128,256]{2,0,1:T(8,128)} %get-tuple-element.485, f32[32,128,256]{2,1,0:T(8,128)} %fusion.69, pred[]{:T(512)S(6)} %compare.6, s32[32]{0:T(128)S(1)} %dynamic_slice.73), kind=kOutput, calls=%fused_computation.4.clone.1 | convolution fusion | flops 202375680 | bytes 8388737 | tf_op jit(solution)/shard_map/while/body/eval_jaxpr/gr,gif->rif/dot_general | solution.py:28
  59.4 1.7 convert_element_type.130
  61.1 1.4 copy.27
  64.0 15.2 %psum.22 = bf16[2048]{0:T(1024)(128)(2,1)S(1)} all-reduce(bf16[2048]{0:T(1024)(128)(2,1)S(1)} %convert_bitcast_fusion), channel_id=1, replica_groups=mesh['row'=4,'col'=8] {'col'}, use_global_device_ids=true, to_apply=%region_4.0 | all-reduce | flops 2048 | bytes 8192 | tf_op jit(solution)/shard_map/psum | solution.py:93
  79.3 42.6 %all-reduce.3.cloned.1.call-done = bf16[2048,256]{1,0:T(8,128)(2,1)} async-done(((bf16[2048,256]{1,0:T(8,128)(2,1)}), bf16[2048,256]{1,0:T(8,128)(2,1)}) %all-reduce.3.cloned.1.call-update) | async-done | bytes 1048592 | tf_op jit(solution)/shard_map/psum | solution.py:92
  121.9 22.7 %all-gather.5.cloned.1.call-done = bf16[2048,256]{1,0:T(8,128)(2,1)} async-done(((bf16[256,256]{1,0:T(8,128)(2,1)}), bf16[2048,256]{1,0:T(8,128)(2,1)}) %all-gather.5.cloned.1.call-update) | async-done | bytes 1048592 | tf_op jit(solution)/shard_map/all_gather | solution.py:97
  144.6 23.4 %all-gather.3.cloned.1.call-done = bf16[2048,256]{1,0:T(8,128)(2,1)} async-done(((bf16[256,256]{1,0:T(8,128)(2,1)}), bf16[2048,256]{1,0:T(8,128)(2,1)}) %all-gather.3.cloned.1.call-update) | async-done | bytes 1048592 | tf_op jit(solution)/shard_map/all_gather | solution.py:96
  167.9 4.9 %multiply_convert_fusion.4 = (bf16[2048,256]{1,0:T(8,128)(2,1)S(1)}, f32[2048,256]{1,0:T(8,128)}, f32[2048,256]{1,0:T(8,128)}) fusion(bf16[2048,256]{1,0:T(8,128)(2,1)} %all-gather.5.cloned.1.call-done, bf16[256,256]{1,0:T(8,128)(2,1)S(1)} %copy-done, bf16[2048,256]{1,0:T(8,128)(2,1)} %all-gather.3.cloned.1.call-done, ...), kind=kOutput, calls=%fused_computation.48 | convolution fusion | flops 276299776 | bytes 8527872 | tf_op jit(solution)/shard_map/dot_general | solution.py:101
  172.9 1.8 multiply_convert_fusion.3
  176.2 1.6 convolution_convert_fusion.2
  178.0 26.1 %while.31 = (s32[]{:T(128)}, f32[8,128,256]{2,0,1:T(8,128)}, s32[64]{0:T(128)S(1)}, s32[64,16,128]{2,1,0:T(8,128)}, s32[]{:T(128)}, /*index=5*/s32[64]{0:T(128)S...) while((s32[]{:T(128)}, f32[8,128,256]{2,0,1:T(8,128)}, ...), condition=%wide.region_6.0_spmd.clone, body=%wide.region_5.0_spmd.clone.sunk | while | flops 406324064 | bytes 16518337 | solution.py:46
  179.6 1.0 constant_dynamic-slice_fusion.5
  180.6 3.5 %fusion.76 = f32[32,128,256]{2,1,0:T(8,128)} fusion(bf16[32,128,256]{2,0,1:T(8,128)(2,1)S(1)} %convolution_convert_fusion.6, s32[32]{0:T(128)S(1)} %compare_convert_fusion.5, s32[128]{0:T(128)S(1)} %shift_right_arithmetic.148, s32[32,16,128]{2,1,0:T(8,128)S(1)} %constant_dynamic-slice_fusion.5), kind=kOutput, calls=%fused_computation.30.clone.1 | convolution fusion | flops 270532608 | bytes 6554240 | tf_op jit(solution)/shard_map/while/body/eval_jaxpr/gki,gif->gkf/dot_general | solution.py:124
  184.2 6.8 %fusion.77 = f32[8,128,256]{2,0,1:T(8,128)} fusion(f32[32,128,256]{2,1,0:T(8,128)} %fusion.76, f32[8,128,256]{2,0,1:T(8,128)} %get-tuple-element.520, pred[]{:T(512)S(6)} %compare.7, s32[32]{0:T(128)S(1)} %dynamic_slice.76), kind=kOutput, calls=%fused_computation.33.clone.1 | convolution fusion | flops 101187840 | bytes 6291585 | tf_op jit(solution)/shard_map/while/body/eval_jaxpr/gr,gif->rif/dot_general | solution.py:28
  192.5 1.0 constant_dynamic-slice_fusion.5
  193.5 3.5 %fusion.76 = f32[32,128,256]{2,1,0:T(8,128)} fusion(bf16[32,128,256]{2,0,1:T(8,128)(2,1)S(1)} %convolution_convert_fusion.6, s32[32]{0:T(128)S(1)} %compare_convert_fusion.5, s32[128]{0:T(128)S(1)} %shift_right_arithmetic.148, s32[32,16,128]{2,1,0:T(8,128)S(1)} %constant_dynamic-slice_fusion.5), kind=kOutput, calls=%fused_computation.30.clone.1 | convolution fusion | flops 270532608 | bytes 6554240 | tf_op jit(solution)/shard_map/while/body/eval_jaxpr/gki,gif->gkf/dot_general | solution.py:124
  197.0 7.1 %fusion.77 = f32[8,128,256]{2,0,1:T(8,128)} fusion(f32[32,128,256]{2,1,0:T(8,128)} %fusion.76, f32[8,128,256]{2,0,1:T(8,128)} %get-tuple-element.520, pred[]{:T(512)S(6)} %compare.7, s32[32]{0:T(128)S(1)} %dynamic_slice.76), kind=kOutput, calls=%fused_computation.33.clone.1 | convolution fusion | flops 101187840 | bytes 6291585 | tf_op jit(solution)/shard_map/while/body/eval_jaxpr/gr,gif->rif/dot_general | solution.py:28
  204.1 1.3 convert_element_type.142
  206.3 1.7 fusion.39
  208.0 11.6 %all-reduce.5.cloned.1.call-done = bf16[256,256]{1,0:T(8,128)(2,1)} async-done(((bf16[256,256]{1,0:T(8,128)(2,1)}), bf16[256,256]{1,0:T(8,128)(2,1)}) %all-reduce.5.cloned.1.call-update) | async-done | bytes 131088 | tf_op jit(solution)/shard_map/psum | solution.py:115
  219.6 1.6 convert_element_type.147
  221.3 26.1 %reduce-scatter.2.cloned.1.call-done = bf16[256,256]{1,0:T(8,128)(2,1)} async-done(((bf16[1024,256]{1,0:T(8,128)(2,1)}), bf16[256,256]{1,0:T(8,128)(2,1)}) %reduce-scatter.2.cloned.1.call-update) | async-done | bytes 131088 | tf_op jit(solution)/shard_map/reduce_scatter | solution.py:136
  247.4 1.7 add_convert_fusion.1
  (59 shorter events, 13.4 us)
Async XLA Ops:
  7.2 160.8 %copy-start = (bf16[256,256]{1,0:T(8,128)(2,1)S(1)}, bf16[256,256]{1,0:T(8,128)(2,1)}, u32[]{:S(2)}) copy-start(bf16[256,256]{1,0:T(8,128)(2,1)} %param.11) | copy-start | bytes 393220
  7.2 114.7 %all-reduce.3.cloned.1.call-start = ((), (), s32[]{:S(2)}) async-start(), calls=%async_computation.1 | async-start | bytes 2097152 | tf_op jit(solution)/shard_map/psum | solution.py:92
  20.1 1.0 copy-start.1
  39.4 1.1 copy-start.1
  62.5 82.1 %all-gather.5.cloned.1.call-start = ((), (), s32[]{:S(2)}) async-start(), calls=%async_computation.3 | async-start | bytes 1179648 | tf_op jit(solution)/shard_map/all_gather | solution.py:97
  63.2 104.7 %all-gather.3.cloned.1.call-start = ((), (), s32[]{:S(2)}) async-start(), calls=%async_computation.2 | async-start | bytes 1179648 | tf_op jit(solution)/shard_map/all_gather | solution.py:96
  64.0 155.7 %all-reduce.5.cloned.1.call-start = ((), (), s32[]{:S(2)}) async-start(), calls=%async_computation.5 | async-start | bytes 262144 | tf_op jit(solution)/shard_map/psum | solution.py:115
  174.7 1.2 copy-start.2
  174.7 1.5 copy-start.3
  177.8 69.6 %reduce-scatter.2.cloned.1.call-start = ((), (), s32[]{:S(2)}) async-start(), calls=%async_computation.4 | async-start | bytes 655360 | tf_op jit(solution)/shard_map/reduce_scatter | solution.py:136
Sparse Core Ops, SparseCore 0:
  62.6 59.2 all-reduce.2
  123.5 21.0 all-gather.4
  146.2 21.7 all-gather.2
  177.9 41.6 all-reduce.4
  222.5 24.7 reduce-scatter.1
where the time goes:
time: 256 us
  waiting for transfers between devices  128 us (50%)
  matrix products  57.6 us (22%)
  blocking collectives  27 us (11%)
  local copies, waits for them, and re-layouts  17.2 us (7%)
  between operations  13.8 us (5%)
  other arithmetic  11.4 us (4%)
    psum x1, waiting for transfers between devices, per_device(): lax.psum(summed.astype(jnp.bfloat16), 'col').astype(jnp.float32)  42.6 us
    dot_general x4, matrix products, place_blocks(): jnp.einsum('gr,gif->rif', table, values, precision=lax.Precision.HIGHEST,...  29.2 us
    reduce_scatter x1, waiting for transfers between devices, per_device(): lax.psum_scatter(back.astype(jnp.bfloat16), 'row', scatter_dimension=0, t...  26.1 us
    all_gather x1, waiting for transfers between devices, per_device(): lax.all_gather(features, 'col', axis=0, tiled=True)  23.4 us
    all_gather x1, waiting for transfers between devices, per_device(): lax.all_gather(cotangent, 'col', axis=0, tiled=True)  22.7 us
    psum x1, blocking collectives, per_device(): lax.psum(degree.astype(jnp.bfloat16), 'col').astype(jnp.float32)  15.2 us
    all_gather x1, blocking collectives, per_device(): lax.all_gather(features, 'row', axis=0, tiled=True)  11.8 us
    psum x1, waiting for transfers between devices, per_device(): lax.psum(weight_part.astype(jnp.bfloat16), 'row').astype(jnp.float32)  11.6 us
  transfers between devices with their start and end apart: 5, of which 5 were waited for; matrix products, arithmetic and copies ran while one was open for 12% of the time, Pallas kernels for 0%

commit v1 on v0

v1 whole, which is shorter than its diff:
```python
import functools

import jax
import jax.numpy as jnp
from jax import lax
from jax.experimental import pallas as pl
from jax.experimental.pallas import tpu as pltpu
from jax.sharding import PartitionSpec as P

VMEM_LIMIT = 56 * 1024 * 1024
pad_rows = 16


def vmem(count):
    return [pl.BlockSpec(memory_space=pltpu.VMEM)] * count


def smem(count):
    return [pl.BlockSpec(memory_space=pltpu.SMEM)] * count


def params():
    return pltpu.CompilerParams(vmem_limit_bytes=VMEM_LIMIT)


def cost(flops, nbytes):
    return pl.CostEstimate(flops=int(flops), bytes_accessed=int(nbytes), transcendentals=0)


def clear(ref):
    rows, width = ref.shape
    step = 128
    zeros = jnp.zeros((step, width), ref.dtype)

    def body(i, _):
        ref[pl.ds(pl.multiple_of(i * step, step), step), :] = zeros
        return 0

    lax.fori_loop(0, rows // step, body, 0)


def unpack_tile(words):
    groups, tile = words.shape
    wide = jnp.broadcast_to(words[:, None, :], (groups, 8, tile))
    shifts = lax.broadcasted_iota(jnp.int32, (groups, 8, tile), 1)
    bits = jnp.bitwise_and(jnp.right_shift(wide, shifts), 1)
    return bits.reshape(groups * 8, tile).astype(jnp.float32).astype(jnp.bfloat16)


def build_forward(blocks, tiles, count, patterns, tiles2, count2, patterns2, st_ref, degree_ref):
    my_row = lax.axis_index("row")
    my_col = lax.axis_index("col")
    my_z, core = my_col // 2, my_col % 2
    tile = patterns.shape[-1]
    half = st_ref.shape[0] // 2
    clear(st_ref)

    def add(tiles_ref, patterns_ref, first):
        def step(t, _):
            a, b = tiles_ref[0, t], tiles_ref[1, t]
            dest = a // blocks

            @pl.when(dest % 2 == core)
            def _():
                i0 = (((dest // 2) ^ my_z) * blocks + a % blocks) * tile
                k0 = first + (((b // blocks) ^ my_row) * blocks + b % blocks) * tile
                st_ref[pl.ds(pl.multiple_of(k0, tile), tile), pl.ds(pl.multiple_of(i0, tile), tile)] = unpack_tile(
                    patterns_ref[t]
                )

            return 0

        return step

    lax.fori_loop(0, count[0, 0], add(tiles, patterns, 0), 0)
    lax.fori_loop(0, count2[0, 0], add(tiles2, patterns2, half), 0)
    ones = jnp.ones((pad_rows, st_ref.shape[0]), jnp.bfloat16)
    degree = jnp.dot(ones, st_ref[...], preferred_element_type=jnp.float32)
    high = jnp.floor(degree * (1.0 / 64.0)) * 64.0
    line = lax.broadcasted_iota(jnp.int32, degree.shape, 0)
    degree_ref[...] = jnp.where(line == 0, high, jnp.where(line == 1, degree - high, 0.0)).astype(jnp.bfloat16)


def build_backward(blocks, n_z, tiles, count, patterns, st_ref):
    my_row = lax.axis_index("row")
    my_col = lax.axis_index("col")
    my_z, core = my_col // 2, my_col % 2
    tile = patterns.shape[-1]
    clear(st_ref)

    def step(t, _):
        a, b = tiles[0, t], tiles[1, t]
        dest = a // blocks
        i0 = ((((dest % 2) ^ core) * n_z + ((dest // 2) ^ my_z)) * blocks + a % blocks) * tile
        k0 = (((b // blocks) ^ my_row) * blocks + b % blocks) * tile
        st_ref[pl.ds(pl.multiple_of(k0, tile), tile), pl.ds(pl.multiple_of(i0, tile), tile)] = unpack_tile(patterns[t])
        return 0

    lax.fori_loop(0, count[0, 0], step, 0)


def forward_kernel(n_feats, n_z, *refs):
    feats, st_ref, degree_ref, outs, feats_t = (
        refs[:n_feats],
        refs[n_feats],
        refs[n_feats + 1],
        refs[n_feats + 2 : n_feats + 2 + n_z],
        refs[-1],
    )
    rows, width = feats[0].shape
    for i, ref in enumerate(feats):
        feats_t[:, i * rows : (i + 1) * rows] = ref[...].T
    for j, out in enumerate(outs):
        columns = slice(j * rows, (j + 1) * rows)
        out[:width, :] = jnp.dot(
            feats_t[...], st_ref[:, columns], preferred_element_type=jnp.float32
        ).astype(jnp.bfloat16)
        out[width:, :] = degree_ref[:, columns]


def dense_kernel(n_z, *refs):
    parts = refs[:n_z]
    feats, cotangent, weight = refs[n_z : n_z + 3]
    act_ref, scaled_ref, agg_grad_ref, keep_ref, send_ref = refs[n_z + 3 :]
    width = weight.shape[0]
    core = lax.axis_index("col") % 2
    total = parts[0][...].astype(jnp.float32)
    for part in parts[1:]:
        total = total + part[...].astype(jnp.float32)
    degree = total[width : width + 1] + total[width + 1 : width + 2]
    scale = lax.rsqrt(degree + 1.0)
    agg_t = (total[:width] * scale + feats[...].astype(jnp.float32).T).astype(jnp.bfloat16)
    agg = agg_t.T
    w = weight[...]
    preact = jnp.dot(agg, w, preferred_element_type=jnp.float32)
    gate = jax.nn.sigmoid(preact)
    act_ref[...] = (preact * gate).astype(jnp.bfloat16)
    grad_pre = (cotangent[...].astype(jnp.float32) * gate * (1.0 + preact * (1.0 - gate))).astype(jnp.bfloat16)
    grad_agg = lax.dot_general(grad_pre, w, (((1,), (1,)), ((), ())), preferred_element_type=jnp.float32)
    agg_grad_ref[...] = grad_agg
    scale_rows = jnp.broadcast_to(scale, agg_t.shape).T
    scaled_ref[...] = (grad_agg * scale_rows).astype(jnp.bfloat16)
    part = jnp.dot(agg_t, grad_pre, preferred_element_type=jnp.float32).astype(jnp.bfloat16)
    half = width // 2
    low, high = part[:half], part[half:]
    first = core == 0
    keep_ref[...] = jnp.where(first, low, high)
    send_ref[...] = jnp.where(first, high, low)


def backward_kernel(n_grads, n_row, *refs):
    st_ref, grads, outs = refs[0], refs[1 : 1 + n_grads], refs[1 + n_grads : 1 + n_grads + n_row]
    gathered = refs[-1]
    rows, _ = grads[0].shape
    for i, ref in enumerate(grads):
        gathered[i * rows : (i + 1) * rows, :] = ref[...]
    for j, out in enumerate(outs):
        out[...] = jnp.dot(
            st_ref[j * rows : (j + 1) * rows, :], gathered[...], preferred_element_type=jnp.float32
        ).astype(out.dtype)


def weight_kernel(n_z, mine, other, out_ref):
    my_col = lax.axis_index("col")
    my_z, core = my_col // 2, my_col % 2
    piece = mine.shape[0] // n_z
    half = out_ref.shape[0] // 2
    for flip, ref in enumerate((mine, other)):
        for j in range(n_z):
            at = (core ^ flip) * half + (my_z ^ j) * piece
            out_ref[pl.ds(pl.multiple_of(at, piece), piece), :] = ref[j * piece : (j + 1) * piece, :].astype(
                out_ref.dtype
            )


def tree_sum(values):
    while len(values) > 1:
        values = [values[i] + values[i + 1] for i in range(0, len(values), 2)]
    return values[0]


def per_device(features, weight, cotangent, tiles, tile_count, patterns):
    rows, width = features.shape
    slots, words, tile = patterns.shape[2:]
    blocks = rows // tile
    n_row = lax.axis_size("row")
    n_col = lax.axis_size("col")
    n_z = n_col // 2
    my_z = lax.axis_index("col") // 2
    row_len = n_z * rows
    col_len = n_row * rows
    bf16, f32 = jnp.bfloat16, jnp.float32
    shape = jax.ShapeDtypeStruct

    def over_row(x, k):
        return lax.ppermute(x, "row", [(i, i ^ k) for i in range(n_row)])

    def over_z(x, k):
        return lax.ppermute(x, "col", [(i, i ^ (2 * k)) for i in range(n_col)])

    def over_core(x):
        return lax.ppermute(x, "col", [(i, i ^ 1) for i in range(n_col)])

    tiles, patterns = tiles[0, 0], patterns[0, 0]
    patterns2, tiles2, count2 = over_core(patterns), over_core(tiles), over_core(tile_count)

    feats = [features] + [over_row(features, k) for k in range(1, n_row)]
    feats = feats + [over_core(x) for x in feats]

    st_forward, degree = pl.pallas_call(
        functools.partial(build_forward, blocks),
        out_shape=(shape((2 * col_len, row_len), bf16), shape((pad_rows, row_len), bf16)),
        in_specs=smem(2) + vmem(1) + smem(2) + vmem(1),
        out_specs=tuple(vmem(2)),
        compiler_params=params(),
        cost_estimate=cost(2e9, 8e6),
        name="build_forward",
    )(tiles, tile_count, patterns, tiles2, count2, patterns2)

    parts = pl.pallas_call(
        functools.partial(forward_kernel, len(feats), n_z),
        out_shape=[shape((width + pad_rows, rows), bf16)] * n_z,
        in_specs=vmem(len(feats) + 2),
        out_specs=vmem(n_z),
        scratch_shapes=[pltpu.VMEM((width, 2 * col_len), bf16)],
        compiler_params=params(),
        cost_estimate=cost(2 * width * 2 * col_len * row_len, 6e6),
        name="forward",
    )(*feats, st_forward, degree)
    parts = [parts[0]] + [over_z(parts[k], k) for k in range(1, n_z)]

    st_backward = pl.pallas_call(
        functools.partial(build_backward, blocks, n_z),
        out_shape=shape((col_len, 2 * row_len), bf16),
        in_specs=smem(2) + vmem(1),
        out_specs=vmem(1)[0],
        compiler_params=params(),
        cost_estimate=cost(2e9, 8e6),
        name="build_backward",
    )(tiles, tile_count, patterns)

    activated, scaled, grad_agg, keep, send = pl.pallas_call(
        functools.partial(dense_kernel, n_z),
        out_shape=(
            shape((rows, width), bf16),
            shape((rows, width), bf16),
            shape((rows, width), f32),
            shape((width // 2, width), bf16),
            shape((width // 2, width), bf16),
        ),
        in_specs=vmem(n_z + 3),
        out_specs=tuple(vmem(5)),
        compiler_params=params(),
        cost_estimate=cost(6 * rows * width * width, 2e6),
        name="dense",
    )(*parts, features, cotangent, weight)

    grads = [scaled] + [over_z(scaled, k) for k in range(1, n_z)]
    grads = grads + [over_core(x) for x in grads]

    half = keep.astype(f32) + over_core(send).astype(f32)
    piece = width // 2 // n_z
    cut = [lax.dynamic_slice_in_dim(half, (my_z ^ k) * piece, piece, 0).astype(bf16) for k in range(n_z)]
    got = [cut[0]] + [over_z(cut[k], k) for k in range(1, n_z)]
    got = tree_sum([x.astype(f32) for x in got]).astype(bf16)
    got = [got] + [over_row(got, k) for k in range(1, n_row)]
    got = tree_sum([x.astype(f32) for x in got]).astype(bf16)
    mine = jnp.concatenate([got] + [over_z(got, k) for k in range(1, n_z)], axis=0)
    other = over_core(mine)
    grad_weight = pl.pallas_call(
        functools.partial(weight_kernel, n_z),
        out_shape=shape((width, width), f32),
        in_specs=vmem(2),
        out_specs=vmem(1)[0],
        compiler_params=params(),
        cost_estimate=cost(1e6, 4e5),
        name="weight_out",
    )(mine, other)

    backs = pl.pallas_call(
        functools.partial(backward_kernel, len(grads), n_row),
        out_shape=[shape((rows, width), bf16)] * n_row,
        in_specs=vmem(1 + len(grads)),
        out_specs=vmem(n_row),
        scratch_shapes=[pltpu.VMEM((2 * row_len, width), bf16)],
        compiler_params=params(),
        cost_estimate=cost(2 * width * 2 * col_len * row_len, 6e6),
        name="backward",
    )(st_backward, *grads)
    backs = [backs[0]] + [over_row(backs[k], k) for k in range(1, n_row)]
    grad_features = (tree_sum([x.astype(f32) for x in backs]) + grad_agg).astype(bf16)
    return activated, grad_features, grad_weight


def solution(mesh):
    return jax.shard_map(
        per_device,
        mesh=mesh,
        in_specs=(
            P(("row", "col"), None),
            P(),
            P(("row", "col"), None),
            P("row", "col", None, None),
            P("row", "col"),
            P("row", "col", None, None, None),
        ),
        out_specs=(P(("row", "col"), None), P(("row", "col"), None), P()),
        check_vma=False,
    )
```

time: 256 us -> 89.2 us (0.35)
  waiting for transfers between devices: 128 us -> 25.7 us
  matrix products: 57.6 us -> 0 us
  starting transfers between devices: 0.38 us -> 32.4 us
  blocking collectives: 27 us -> 0 us
  Pallas kernels: 0 us -> 22.5 us
  local copies, waits for them, and re-layouts: 17.2 us -> 4.11 us
  between operations: 13.8 us -> 1.57 us
  other arithmetic: 11.4 us -> 2.52 us
    dot_general x17 -> x0, matrix products: 57.6 us -> none  [the longest x4 29.2 us: place_blocks(): jnp.einsum('gr,gif->rif', table, values, precision=lax.Precision.HIGHEST,...]
    psum x2 -> x0, waiting for transfers between devices: 54.2 us -> none  [the longest x1 42.6 us: per_device(): lax.psum(summed.astype(jnp.bfloat16), 'col').astype(jnp.float32)]
    all_gather x2 -> x0, waiting for transfers between devices: 46 us -> none  [the longest x1 23.4 us: per_device(): lax.all_gather(features, 'col', axis=0, tiled=True)]
    ppermute x0 -> x34, starting transfers between devices: none -> 32.4 us  [the longest x12 17.7 us: over_z(): return lax.ppermute(x, 'col', [(i, i ^ 2 * k) for i in range(n_col)])]
    reduce_scatter x1 -> x0, waiting for transfers between devices: 26.1 us -> none  [per_device(): lax.psum_scatter(back.astype(jnp.bfloat16), 'row', scatter_dimension=0, t...]
    ppermute x0 -> x34, waiting for transfers between devices: none -> 25.7 us  [the longest x12 16.6 us: over_z(): return lax.ppermute(x, 'col', [(i, i ^ 2 * k) for i in range(n_col)])]
    pallas_call x0 -> x6, Pallas kernels: none -> 22.5 us  [the longest x1 5.48 us: per_device(): pl.pallas_call(functools.partial(build_forward, blocks), out_shape=(shape...]
    psum x1 -> x0, blocking collectives: 15.2 us -> none  [per_device(): lax.psum(degree.astype(jnp.bfloat16), 'col').astype(jnp.float32)]
  transfers between devices with their start and end apart: 5 -> 34, of which waited for: 5 -> 13; matrix products, arithmetic and copies ran while one was open for 12% -> 0% of each run, Pallas kernels for 0% -> 17%
where the time goes in v1:
time: 89.2 us; the launch traced here: 88.8 us
  starting transfers between devices  32.4 us (36%)
  waiting for transfers between devices  25.7 us (29%)
  Pallas kernels  22.5 us (25%)
  local copies, waits for them, and re-layouts  4.11 us (5%)
  other arithmetic  2.52 us (3%)
  between operations  1.57 us (2%)
    ppermute x12, starting transfers between devices, over_z(): return lax.ppermute(x, 'col', [(i, i ^ 2 * k) for i in range(n_col)])  17.7 us
    ppermute x12, waiting for transfers between devices, over_z(): return lax.ppermute(x, 'col', [(i, i ^ 2 * k) for i in range(n_col)])  16.6 us
    ppermute x9, starting transfers between devices, over_row(): return lax.ppermute(x, 'row', [(i, i ^ k) for i in range(n_row)])  11.9 us
    pallas_call x1, Pallas kernels, per_device(): pl.pallas_call(functools.partial(build_forward, blocks), out_shape=(shape...  5.48 us
    ppermute x9, waiting for transfers between devices, over_row(): return lax.ppermute(x, 'row', [(i, i ^ k) for i in range(n_row)])  4.66 us
    pallas_call x1, Pallas kernels, per_device(): pl.pallas_call(functools.partial(forward_kernel, len(feats), n_z), out_sh...  4.62 us
    pallas_call x1, Pallas kernels, per_device(): pl.pallas_call(functools.partial(backward_kernel, len(grads), n_row), out...  4.5 us
    ppermute x13, waiting for transfers between devices, over_core(): return lax.ppermute(x, 'col', [(i, i ^ 1) for i in range(n_col)])  4.39 us
  transfers between devices with their start and end apart: 34, of which 13 were waited for; matrix products, arithmetic and copies ran while one was open for 0% of the time, Pallas kernels for 17%

profile of v1, /device:TPU:0, one launch (start us, length us, event | category | flops | bytes accessed | tf_op | source)
XLA Modules:
  0.0 88.8 jit_solution(5671535742469838579)
XLA Ops:
  1.1 2.6 %collective-permute-start = (bf16[256,256]{1,0:T(8,128)(2,1)}, bf16[256,256]{1,0:T(8,128)(2,1)S(1)}, u32[]{:S(2)}, u32[]{:S(2)}) collective-permute-start(bf16[256,256]{1,0:T(8,128)(2,1)} %refs_4_.1), channel_id=1, source_target_pairs={{0,8},{8,0},{16,24},{24,16},{1,9},{9,1},{17,25},{25,17},{2,10},{10... | collective-permute-start | bytes 393224 | tf_op jit(solution)/shard_map/ppermute | solution.py:196
  3.7 1.5 %collective-permute-start.1 = (bf16[256,256]{1,0:T(8,128)(2,1)}, bf16[256,256]{1,0:T(8,128)(2,1)S(1)}, u32[]{:S(2)}, u32[]{:S(2)}) collective-permute-start(bf16[256,256]{1,0:T(8,128)(2,1)} %refs_4_.1), channel_id=1, source_target_pairs={{0,16},{8,24},{16,0},{24,8},{1,17},{9,25},{17,1},{25,9},{2,18},{10... | collective-permute-start | bytes 393224 | tf_op jit(solution)/shard_map/ppermute | solution.py:196
  5.3 1.2 %collective-permute-done.8.count2 = s32[1,1]{1,0:T(1,128)} collective-permute-done((s32[1,1]{1,0:T(1,128)}, s32[1,1]{1,0:T(1,128)}, u32[]{:S(2)}, u32[]{:S(2)}) %collective-permute-start.8) | collective-permute-done | bytes 36 | tf_op jit(solution)/shard_map/ppermute | solution.py:202
  8.4 3.9 %collective-permute-done.1.refs_2_ = bf16[256,256]{1,0:T(8,128)(2,1)S(1)} collective-permute-done((bf16[256,256]{1,0:T(8,128)(2,1)}, bf16[256,256]{1,0:T(8,128)(2,1)S(1)}, u32[]{:S(2)}, u32[]{:S(2)}) %collective-permute-start.1) | collective-permute-done | bytes 131104 | tf_op jit(solution)/shard_map/ppermute | solution.py:196
  13.6 5.5 %build_forward.1 = (bf16[2048,1024]{1,0:T(8,128)(2,1)}, bf16[16,1024]{1,0:T(8,128)(2,1)}) custom-call(s32[2,64]{1,0:T(2,128)} %bitcast.6, s32[1,1]{1,0:T(1,128)S(6)} %copy.9.count, s32[64,16,128]{2,1,0:T(8,128)} %bitcast.3, s32[2,64]{1,0:T(2,128)} %copy-done.22, s32[1,1]{1,0:T(1,128)} %collective-permute-done.8.count2, s32[64,16,128]{2,1,0:T(8,128)} %copy-done.21), custom_call_target="tpu_custom_call" | custom-call | flops 2000000000 | bytes 8000000 | tf_op jit(solution)/shard_map/build_forward/pallas_call | solution.py:210
  19.9 4.6 %forward.1 = (bf16[272,256]{1,0:T(8,128)(2,1)}, bf16[272,256]{1,0:T(8,128)(2,1)}, bf16[272,256]{1,0:T(8,128)(2,1)}, bf16[272,256]{1,0:T(8,128)(2,1)}) custom-call(bf16[256,256]{1,0:T(8,128)(2,1)} %refs_4_.1, bf16[256,256]{1,0:T(8,128)(2,1)} %copy-done.9, bf16[256,256]{1,0:T(8,128)(2,1)} %copy-done.10, bf16[256,256]{1,0:T(8,128)(2,1)} %copy-done.11, ...), custom_call_target="tpu_custom_call" | custom-call | flops 1073741824 | bytes 6000000 | tf_op jit(solution)/shard_map/forward/pallas_call | solution.py:220
  24.5 1.8 %collective-permute-start.10 = (bf16[272,256]{1,0:T(8,128)(2,1)}, bf16[272,256]{1,0:T(8,128)(2,1)S(1)}, u32[]{:S(2)}, u32[]{:S(2)}) collective-permute-start(bf16[272,256]{1,0:T(8,128)(2,1)} %get-tuple-element.21), channel_id=1, source_target_pairs={{0,2},{1,3},{2,0},{3,1},{4,6},{5,7},{6,4},{7,5},{8,10},{9,11},{10,... | collective-permute-start | bytes 417800 | tf_op jit(solution)/shard_map/ppermute | solution.py:199
  26.3 2.3 %collective-permute-start.11 = (bf16[272,256]{1,0:T(8,128)(2,1)}, bf16[272,256]{1,0:T(8,128)(2,1)S(1)}, u32[]{:S(2)}, u32[]{:S(2)}) collective-permute-start(bf16[272,256]{1,0:T(8,128)(2,1)} %get-tuple-element.22), channel_id=1, source_target_pairs={{0,4},{1,5},{2,6},{3,7},{4,0},{5,1},{6,2},{7,3},{8,12},{9,13},{10,... | collective-permute-start | bytes 417800 | tf_op jit(solution)/shard_map/ppermute | solution.py:199
  28.9 3.4 %collective-permute-done.10.refs_1_ = bf16[272,256]{1,0:T(8,128)(2,1)S(1)} collective-permute-done((bf16[272,256]{1,0:T(8,128)(2,1)}, bf16[272,256]{1,0:T(8,128)(2,1)S(1)}, u32[]{:S(2)}, u32[]{:S(2)}) %collective-permute-start.10) | collective-permute-done | bytes 139296 | tf_op jit(solution)/shard_map/ppermute | solution.py:199
  32.3 7.7 %collective-permute-done.11.refs_2_ = bf16[272,256]{1,0:T(8,128)(2,1)S(1)} collective-permute-done((bf16[272,256]{1,0:T(8,128)(2,1)}, bf16[272,256]{1,0:T(8,128)(2,1)S(1)}, u32[]{:S(2)}, u32[]{:S(2)}) %collective-permute-start.11) | collective-permute-done | bytes 139296 | tf_op jit(solution)/shard_map/ppermute | solution.py:199
  40.7 2.5 %dense.1 = (bf16[256,256]{1,0:T(8,128)(2,1)}, bf16[256,256]{1,0:T(8,128)(2,1)}, f32[256,256]{1,0:T(8,128)}, bf16[128,256]{1,0:T(8,128)(2,1)}, bf16[128,256]{1,0:T(8,128)(2,1)}) custom-call(bf16[272,256]{1,0:T(8,128)(2,1)} %get-tuple-element.20.refs_0_, bf16[272,256]{1,0:T(8,128)(2,1)} %copy-done.2, bf16[272,256]{1,0:T(8,128)(2,1)} %copy-done.3, ...), custom_call_target="tpu_custom_call" | custom-call | flops 100663296 | bytes 2000000 | tf_op jit(solution)/shard_map/dense/pallas_call | solution.py:242
  43.3 1.4 %collective-permute-done.23 = bf16[128,256]{1,0:T(8,128)(2,1)S(1)} collective-permute-done((bf16[128,256]{1,0:T(8,128)(2,1)}, bf16[128,256]{1,0:T(8,128)(2,1)S(1)}, u32[]{:S(2)}, u32[]{:S(2)}) %collective-permute-start.23) | collective-permute-done | bytes 65568 | tf_op jit(solution)/shard_map/ppermute | solution.py:202
  44.7 0.9 convert_add_fusion
  45.6 2.3 %collective-permute-start.26 = (bf16[32,256]{1,0:T(8,128)(2,1)S(1)}, bf16[32,256]{1,0:T(8,128)(2,1)S(1)}, u32[]{:S(2)}, u32[]{:S(2)}) collective-permute-start(bf16[32,256]{1,0:T(8,128)(2,1)S(1)} %get-tuple-element.34), channel_id=1, source_target_pairs={{0,6},{1,7},{2,4},{3,5},{4,2},{5,3},{6,0},{7,1},{8,14},{9,15},{10,... | collective-permute-start | bytes 49160 | tf_op jit(solution)/shard_map/ppermute | solution.py:199
  47.9 1.3 %collective-permute-start.25 = (bf16[32,256]{1,0:T(8,128)(2,1)S(1)}, bf16[32,256]{1,0:T(8,128)(2,1)S(1)}, u32[]{:S(2)}, u32[]{:S(2)}) collective-permute-start(bf16[32,256]{1,0:T(8,128)(2,1)S(1)} %get-tuple-element.35), channel_id=1, source_target_pairs={{0,4},{1,5},{2,6},{3,7},{4,0},{5,1},{6,2},{7,3},{8,12},{9,13},{10,... | collective-permute-start | bytes 49160 | tf_op jit(solution)/shard_map/ppermute | solution.py:199
  49.2 0.8 collective-permute-start.24
  50.0 1.1 %collective-permute-done.26 = bf16[32,256]{1,0:T(8,128)(2,1)S(1)} collective-permute-done((bf16[32,256]{1,0:T(8,128)(2,1)S(1)}, bf16[32,256]{1,0:T(8,128)(2,1)S(1)}, u32[]{:S(2)}, u32[]{:S(2)}) %collective-permute-start.26) | collective-permute-done | bytes 16416 | tf_op jit(solution)/shard_map/ppermute | solution.py:199
  51.2 1.4 %collective-permute-done.25 = bf16[32,256]{1,0:T(8,128)(2,1)S(1)} collective-permute-done((bf16[32,256]{1,0:T(8,128)(2,1)S(1)}, bf16[32,256]{1,0:T(8,128)(2,1)S(1)}, u32[]{:S(2)}, u32[]{:S(2)}) %collective-permute-start.25) | collective-permute-done | bytes 16416 | tf_op jit(solution)/shard_map/ppermute | solution.py:199
  53.0 3.7 %collective-permute-start.29 = (bf16[32,256]{1,0:T(8,128)(2,1)S(1)}, bf16[32,256]{1,0:T(8,128)(2,1)S(1)}, u32[]{:S(2)}, u32[]{:S(2)}) collective-permute-start(bf16[32,256]{1,0:T(8,128)(2,1)S(1)} %add_convert_fusion.2), channel_id=1, source_target_pairs={{0,24},{8,16},{16,8},{24,0},{1,25},{9,17},{17,9},{25,1},{2,26},{10... | collective-permute-start | bytes 49160 | tf_op jit(solution)/shard_map/ppermute | solution.py:196
  56.8 1.4 %collective-permute-start.14 = (bf16[256,256]{1,0:T(8,128)(2,1)}, bf16[256,256]{1,0:T(8,128)(2,1)S(1)}, u32[]{:S(2)}, u32[]{:S(2)}) collective-permute-start(bf16[256,256]{1,0:T(8,128)(2,1)} %get-tuple-element.25.refs_1_), channel_id=1, source_target_pairs={{0,4},{1,5},{2,6},{3,7},{4,0},{5,1},{6,2},{7,3},{8,12},{9,13},{10,... | collective-permute-start | bytes 393224 | tf_op jit(solution)/shard_map/ppermute | solution.py:199
  58.2 2.8 %collective-permute-start.15 = (bf16[256,256]{1,0:T(8,128)(2,1)}, bf16[256,256]{1,0:T(8,128)(2,1)S(1)}, u32[]{:S(2)}, u32[]{:S(2)}) collective-permute-start(bf16[256,256]{1,0:T(8,128)(2,1)} %get-tuple-element.25.refs_1_), channel_id=1, source_target_pairs={{0,6},{1,7},{2,4},{3,5},{4,2},{5,3},{6,0},{7,1},{8,14},{9,15},{10,... | collective-permute-start | bytes 393224 | tf_op jit(solution)/shard_map/ppermute | solution.py:199
  61.7 3.8 %build_backward.1.refs_0_ = bf16[1024,2048]{1,0:T(8,128)(2,1)} custom-call(s32[2,64]{1,0:T(2,128)} %bitcast.7, s32[1,1]{1,0:T(1,128)S(6)} %copy.9.count, s32[64,16,128]{2,1,0:T(8,128)} %bitcast.4), custom_call_target="tpu_custom_call" | custom-call | flops 2000000000 | bytes 8000000 | tf_op jit(solution)/shard_map/build_backward/pallas_call | solution.py:232
  66.0 2.6 %collective-permute-done.14.refs_3_ = bf16[256,256]{1,0:T(8,128)(2,1)S(1)} collective-permute-done((bf16[256,256]{1,0:T(8,128)(2,1)}, bf16[256,256]{1,0:T(8,128)(2,1)S(1)}, u32[]{:S(2)}, u32[]{:S(2)}) %collective-permute-start.14) | collective-permute-done | bytes 131104 | tf_op jit(solution)/shard_map/ppermute | solution.py:199
  69.2 2.1 %collective-permute-start.32 = (bf16[32,256]{1,0:T(8,128)(2,1)S(1)}, bf16[32,256]{1,0:T(8,128)(2,1)S(1)}, u32[]{:S(2)}, u32[]{:S(2)}) collective-permute-start(bf16[32,256]{1,0:T(8,128)(2,1)S(1)} %add_convert_fusion.1), channel_id=1, source_target_pairs={{0,6},{1,7},{2,4},{3,5},{4,2},{5,3},{6,0},{7,1},{8,14},{9,15},{10,... | collective-permute-start | bytes 49160 | tf_op jit(solution)/shard_map/ppermute | solution.py:199
  71.3 1.1 %collective-permute-start.31 = (bf16[32,256]{1,0:T(8,128)(2,1)S(1)}, bf16[32,256]{1,0:T(8,128)(2,1)S(1)}, u32[]{:S(2)}, u32[]{:S(2)}) collective-permute-start(bf16[32,256]{1,0:T(8,128)(2,1)S(1)} %add_convert_fusion.1), channel_id=1, source_target_pairs={{0,4},{1,5},{2,6},{3,7},{4,0},{5,1},{6,2},{7,3},{8,12},{9,13},{10,... | collective-permute-start | bytes 49160 | tf_op jit(solution)/shard_map/ppermute | solution.py:199
  72.4 1.2 %collective-permute-start.30 = (bf16[32,256]{1,0:T(8,128)(2,1)S(1)}, bf16[32,256]{1,0:T(8,128)(2,1)S(1)}, u32[]{:S(2)}, u32[]{:S(2)}) collective-permute-start(bf16[32,256]{1,0:T(8,128)(2,1)S(1)} %add_convert_fusion.1), channel_id=1, source_target_pairs={{0,2},{1,3},{2,0},{3,1},{4,6},{5,7},{6,4},{7,5},{8,10},{9,11},{10,... | collective-permute-start | bytes 49160 | tf_op jit(solution)/shard_map/ppermute | solution.py:199
  74.9 4.5 %backward.1 = (bf16[256,256]{1,0:T(8,128)(2,1)}, bf16[256,256]{1,0:T(8,128)(2,1)}, bf16[256,256]{1,0:T(8,128)(2,1)}, bf16[256,256]{1,0:T(8,128)(2,1)}) custom-call(bf16[1024,2048]{1,0:T(8,128)(2,1)} %build_backward.1.refs_0_, bf16[256,256]{1,0:T(8,128)(2,1)} %get-tuple-element.25.refs_1_, bf16[256,256]{1,0:T(8,128)(2,1)} %copy-done.6, ...), custom_call_target="tpu_custom_call" | custom-call | flops 1073741824 | bytes 6000000 | tf_op jit(solution)/shard_map/backward/pallas_call | solution.py:280
  79.8 0.8 collective-permute-start.21
  80.6 2.3 %collective-permute-start.20 = (bf16[256,256]{1,0:T(8,128)(2,1)}, bf16[256,256]{1,0:T(8,128)(2,1)S(1)}, u32[]{:S(2)}, u32[]{:S(2)}) collective-permute-start(bf16[256,256]{1,0:T(8,128)(2,1)} %get-tuple-element.27), channel_id=1, source_target_pairs={{0,8},{8,0},{16,24},{24,16},{1,9},{9,1},{17,25},{25,17},{2,10},{10... | collective-permute-start | bytes 393224 | tf_op jit(solution)/shard_map/ppermute | solution.py:196
  83.0 1.2 %collective-permute-done.33.other = bf16[128,256]{1,0:T(8,128)(2,1)S(1)} collective-permute-done((bf16[128,256]{1,0:T(8,128)(2,1)S(1)}, bf16[128,256]{1,0:T(8,128)(2,1)S(1)}, u32[]{:S(2)}, u32[]{:S(2)}) %collective-permute-start.33) | collective-permute-done | bytes 65568 | tf_op jit(solution)/shard_map/ppermute | solution.py:202
  84.9 1.6 %weight_out.1 = f32[256,256]{1,0:T(8,128)} custom-call(bf16[128,256]{1,0:T(8,128)(2,1)} %copy-done.1, bf16[128,256]{1,0:T(8,128)(2,1)} %copy-done.20), custom_call_target="tpu_custom_call" | custom-call | flops 1000000 | bytes 400000 | tf_op jit(solution)/shard_map/weight_out/pallas_call | solution.py:270
  87.2 1.6 %add_convert_fusion = bf16[256,256]{1,0:T(8,128)(2,1)} fusion(f32[256,256]{1,0:T(8,128)S(1)} %copy-done, bf16[256,256]{1,0:T(8,128)(2,1)S(1)} %collective-permute-done.22, bf16[256,256]{1,0:T(8,128)(2,1)S(1)} %collective-permute-done.21, bf16[256,256]{1,0:T(8,128)(2,1)S(1)} %collective-permute-done.20, bf16[256,256]{1,0:T(8,128)(2,1)} %get-tuple-element.26), kind=kLoop, calls=%fused_computation | loop fusion | flops 589824 | bytes 917504 | tf_op jit(solution)/shard_map/convert_element_type | solution.py:291
  (94 shorter events, 10.1 us)
Async XLA Ops:
  0.6 12.2 %collective-permute-start.9 = (s32[64,16,128]{2,1,0:T(8,128)}, s32[64,16,128]{2,1,0:T(8,128)S(1)}, u32[]{:S(2)}, u32[]{:S(2)}) collective-permute-start(s32[64,16,128]{2,1,0:T(8,128)} %bitcast.2), channel_id=1, source_target_pairs={{0,1},{1,0},{2,3},{3,2},{4,5},{5,4},{6,7},{7,6},{8,9},{9,8},{10,11... | collective-permute-start | bytes 1572872 | tf_op jit(solution)/shard_map/ppermute | solution.py:202
  1.1 6.9 %collective-permute-start = (bf16[256,256]{1,0:T(8,128)(2,1)}, bf16[256,256]{1,0:T(8,128)(2,1)S(1)}, u32[]{:S(2)}, u32[]{:S(2)}) collective-permute-start(bf16[256,256]{1,0:T(8,128)(2,1)} %refs_4_.1), channel_id=1, source_target_pairs={{0,8},{8,0},{16,24},{24,16},{1,9},{9,1},{17,25},{25,17},{2,10},{10... | collective-permute-start | bytes 393224 | tf_op jit(solution)/shard_map/ppermute | solution.py:196
  3.7 8.6 %collective-permute-start.1 = (bf16[256,256]{1,0:T(8,128)(2,1)}, bf16[256,256]{1,0:T(8,128)(2,1)S(1)}, u32[]{:S(2)}, u32[]{:S(2)}) collective-permute-start(bf16[256,256]{1,0:T(8,128)(2,1)} %refs_4_.1), channel_id=1, source_target_pairs={{0,16},{8,24},{16,0},{24,8},{1,17},{9,25},{17,1},{25,9},{2,18},{10... | collective-permute-start | bytes 393224 | tf_op jit(solution)/shard_map/ppermute | solution.py:196
  5.2 7.1 %collective-permute-start.2 = (bf16[256,256]{1,0:T(8,128)(2,1)}, bf16[256,256]{1,0:T(8,128)(2,1)S(1)}, u32[]{:S(2)}, u32[]{:S(2)}) collective-permute-start(bf16[256,256]{1,0:T(8,128)(2,1)} %refs_4_.1), channel_id=1, source_target_pairs={{0,24},{8,16},{16,8},{24,0},{1,25},{9,17},{17,9},{25,1},{2,26},{10... | collective-permute-start | bytes 393224 | tf_op jit(solution)/shard_map/ppermute | solution.py:196
  6.5 1.4 %collective-permute-start.7 = (s32[2,64]{1,0:T(2,128)}, s32[2,64]{1,0:T(2,128)S(1)}, u32[]{:S(2)}, u32[]{:S(2)}) collective-permute-start(s32[2,64]{1,0:T(2,128)} %bitcast.5), channel_id=1, source_target_pairs={{0,1},{1,0},{2,3},{3,2},{4,5},{5,4},{6,7},{7,6},{8,9},{9,8},{10,11... | collective-permute-start | bytes 1544 | tf_op jit(solution)/shard_map/ppermute | solution.py:202
  7.8 11.3 %collective-permute-start.3 = (bf16[256,256]{1,0:T(8,128)(2,1)}, bf16[256,256]{1,0:T(8,128)(2,1)S(1)}, u32[]{:S(2)}, u32[]{:S(2)}) collective-permute-start(bf16[256,256]{1,0:T(8,128)(2,1)} %refs_4_.1), channel_id=1, source_target_pairs={{0,1},{1,0},{2,3},{3,2},{4,5},{5,4},{6,7},{7,6},{8,9},{9,8},{10,11... | collective-permute-start | bytes 393224 | tf_op jit(solution)/shard_map/ppermute | solution.py:202
  8.1 11.0 %collective-permute-start.4 = (bf16[256,256]{1,0:T(8,128)(2,1)S(1)}, bf16[256,256]{1,0:T(8,128)(2,1)S(1)}, u32[]{:S(2)}, u32[]{:S(2)}) collective-permute-start(bf16[256,256]{1,0:T(8,128)(2,1)S(1)} %collective-permute-done.refs_1_), channel_id=1, source_target_pairs={{0,1},{1,0},{2,3},{3,2},{4,5},{5,4},{6,7},{7,6},{8,9},{9,8},{10,11... | collective-permute-start | bytes 393224 | tf_op jit(solution)/shard_map/ppermute | solution.py:202
  12.3 6.8 %collective-permute-start.5 = (bf16[256,256]{1,0:T(8,128)(2,1)S(1)}, bf16[256,256]{1,0:T(8,128)(2,1)S(1)}, u32[]{:S(2)}, u32[]{:S(2)}) collective-permute-start(bf16[256,256]{1,0:T(8,128)(2,1)S(1)} %collective-permute-done.1.refs_2_), channel_id=1, source_target_pairs={{0,1},{1,0},{2,3},{3,2},{4,5},{5,4},{6,7},{7,6},{8,9},{9,8},{10,11... | collective-permute-start | bytes 393224 | tf_op jit(solution)/shard_map/ppermute | solution.py:202
  12.3 6.8 %collective-permute-start.6 = (bf16[256,256]{1,0:T(8,128)(2,1)S(1)}, bf16[256,256]{1,0:T(8,128)(2,1)S(1)}, u32[]{:S(2)}, u32[]{:S(2)}) collective-permute-start(bf16[256,256]{1,0:T(8,128)(2,1)S(1)} %collective-permute-done.2.refs_3_), channel_id=1, source_target_pairs={{0,1},{1,0},{2,3},{3,2},{4,5},{5,4},{6,7},{7,6},{8,9},{9,8},{10,11... | collective-permute-start | bytes 393224 | tf_op jit(solution)/shard_map/ppermute | solution.py:202
  24.5 7.8 %collective-permute-start.10 = (bf16[272,256]{1,0:T(8,128)(2,1)}, bf16[272,256]{1,0:T(8,128)(2,1)S(1)}, u32[]{:S(2)}, u32[]{:S(2)}) collective-permute-start(bf16[272,256]{1,0:T(8,128)(2,1)} %get-tuple-element.21), channel_id=1, source_target_pairs={{0,2},{1,3},{2,0},{3,1},{4,6},{5,7},{6,4},{7,5},{8,10},{9,11},{10,... | collective-permute-start | bytes 417800 | tf_op jit(solution)/shard_map/ppermute | solution.py:199
  26.3 13.7 %collective-permute-start.11 = (bf16[272,256]{1,0:T(8,128)(2,1)}, bf16[272,256]{1,0:T(8,128)(2,1)S(1)}, u32[]{:S(2)}, u32[]{:S(2)}) collective-permute-start(bf16[272,256]{1,0:T(8,128)(2,1)} %get-tuple-element.22), channel_id=1, source_target_pairs={{0,4},{1,5},{2,6},{3,7},{4,0},{5,1},{6,2},{7,3},{8,12},{9,13},{10,... | collective-permute-start | bytes 417800 | tf_op jit(solution)/shard_map/ppermute | solution.py:199
  28.6 11.4 %collective-permute-start.12 = (bf16[272,256]{1,0:T(8,128)(2,1)}, bf16[272,256]{1,0:T(8,128)(2,1)S(1)}, u32[]{:S(2)}, u32[]{:S(2)}) collective-permute-start(bf16[272,256]{1,0:T(8,128)(2,1)} %get-tuple-element.23), channel_id=1, source_target_pairs={{0,6},{1,7},{2,4},{3,5},{4,2},{5,3},{6,0},{7,1},{8,14},{9,15},{10,... | collective-permute-start | bytes 417800 | tf_op jit(solution)/shard_map/ppermute | solution.py:199
  43.2 1.5 %collective-permute-start.23 = (bf16[128,256]{1,0:T(8,128)(2,1)}, bf16[128,256]{1,0:T(8,128)(2,1)S(1)}, u32[]{:S(2)}, u32[]{:S(2)}) collective-permute-start(bf16[128,256]{1,0:T(8,128)(2,1)} %get-tuple-element.32), channel_id=1, source_target_pairs={{0,1},{1,0},{2,3},{3,2},{4,5},{5,4},{6,7},{7,6},{8,9},{9,8},{10,11... | collective-permute-start | bytes 196616 | tf_op jit(solution)/shard_map/ppermute | solution.py:202
  45.6 5.6 %collective-permute-start.26 = (bf16[32,256]{1,0:T(8,128)(2,1)S(1)}, bf16[32,256]{1,0:T(8,128)(2,1)S(1)}, u32[]{:S(2)}, u32[]{:S(2)}) collective-permute-start(bf16[32,256]{1,0:T(8,128)(2,1)S(1)} %get-tuple-element.34), channel_id=1, source_target_pairs={{0,6},{1,7},{2,4},{3,5},{4,2},{5,3},{6,0},{7,1},{8,14},{9,15},{10,... | collective-permute-start | bytes 49160 | tf_op jit(solution)/shard_map/ppermute | solution.py:199
  47.9 4.7 %collective-permute-start.25 = (bf16[32,256]{1,0:T(8,128)(2,1)S(1)}, bf16[32,256]{1,0:T(8,128)(2,1)S(1)}, u32[]{:S(2)}, u32[]{:S(2)}) collective-permute-start(bf16[32,256]{1,0:T(8,128)(2,1)S(1)} %get-tuple-element.35), channel_id=1, source_target_pairs={{0,4},{1,5},{2,6},{3,7},{4,0},{5,1},{6,2},{7,3},{8,12},{9,13},{10,... | collective-permute-start | bytes 49160 | tf_op jit(solution)/shard_map/ppermute | solution.py:199
  49.2 3.7 %collective-permute-start.24 = (bf16[32,256]{1,0:T(8,128)(2,1)S(1)}, bf16[32,256]{1,0:T(8,128)(2,1)S(1)}, u32[]{:S(2)}, u32[]{:S(2)}) collective-permute-start(bf16[32,256]{1,0:T(8,128)(2,1)S(1)} %get-tuple-element.33), channel_id=1, source_target_pairs={{0,2},{1,3},{2,0},{3,1},{4,6},{5,7},{6,4},{7,5},{8,10},{9,11},{10,... | collective-permute-start | bytes 49160 | tf_op jit(solution)/shard_map/ppermute | solution.py:199
  53.0 8.1 %collective-permute-start.29 = (bf16[32,256]{1,0:T(8,128)(2,1)S(1)}, bf16[32,256]{1,0:T(8,128)(2,1)S(1)}, u32[]{:S(2)}, u32[]{:S(2)}) collective-permute-start(bf16[32,256]{1,0:T(8,128)(2,1)S(1)} %add_convert_fusion.2), channel_id=1, source_target_pairs={{0,24},{8,16},{16,8},{24,0},{1,25},{9,17},{17,9},{25,1},{2,26},{10... | collective-permute-start | bytes 49160 | tf_op jit(solution)/shard_map/ppermute | solution.py:196
  56.6 8.9 %collective-permute-start.13 = (bf16[256,256]{1,0:T(8,128)(2,1)}, bf16[256,256]{1,0:T(8,128)(2,1)S(1)}, u32[]{:S(2)}, u32[]{:S(2)}) collective-permute-start(bf16[256,256]{1,0:T(8,128)(2,1)} %get-tuple-element.25.refs_1_), channel_id=1, source_target_pairs={{0,2},{1,3},{2,0},{3,1},{4,6},{5,7},{6,4},{7,5},{8,10},{9,11},{10,... | collective-permute-start | bytes 393224 | tf_op jit(solution)/shard_map/ppermute | solution.py:199
  56.8 11.8 %collective-permute-start.14 = (bf16[256,256]{1,0:T(8,128)(2,1)}, bf16[256,256]{1,0:T(8,128)(2,1)S(1)}, u32[]{:S(2)}, u32[]{:S(2)}) collective-permute-start(bf16[256,256]{1,0:T(8,128)(2,1)} %get-tuple-element.25.refs_1_), channel_id=1, source_target_pairs={{0,4},{1,5},{2,6},{3,7},{4,0},{5,1},{6,2},{7,3},{8,12},{9,13},{10,... | collective-permute-start | bytes 393224 | tf_op jit(solution)/shard_map/ppermute | solution.py:199
  58.2 10.5 %collective-permute-start.15 = (bf16[256,256]{1,0:T(8,128)(2,1)}, bf16[256,256]{1,0:T(8,128)(2,1)S(1)}, u32[]{:S(2)}, u32[]{:S(2)}) collective-permute-start(bf16[256,256]{1,0:T(8,128)(2,1)} %get-tuple-element.25.refs_1_), channel_id=1, source_target_pairs={{0,6},{1,7},{2,4},{3,5},{4,2},{5,3},{6,0},{7,1},{8,14},{9,15},{10,... | collective-permute-start | bytes 393224 | tf_op jit(solution)/shard_map/ppermute | solution.py:199
  61.0 4.4 %collective-permute-start.28 = (bf16[32,256]{1,0:T(8,128)(2,1)S(1)}, bf16[32,256]{1,0:T(8,128)(2,1)S(1)}, u32[]{:S(2)}, u32[]{:S(2)}) collective-permute-start(bf16[32,256]{1,0:T(8,128)(2,1)S(1)} %add_convert_fusion.2), channel_id=1, source_target_pairs={{0,16},{8,24},{16,0},{24,8},{1,17},{9,25},{17,1},{25,9},{2,18},{10... | collective-permute-start | bytes 49160 | tf_op jit(solution)/shard_map/ppermute | solution.py:196
  61.0 8.1 %collective-permute-start.27 = (bf16[32,256]{1,0:T(8,128)(2,1)S(1)}, bf16[32,256]{1,0:T(8,128)(2,1)S(1)}, u32[]{:S(2)}, u32[]{:S(2)}) collective-permute-start(bf16[32,256]{1,0:T(8,128)(2,1)S(1)} %add_convert_fusion.2), channel_id=1, source_target_pairs={{0,8},{8,0},{16,24},{24,16},{1,9},{9,1},{17,25},{25,17},{2,10},{10... | collective-permute-start | bytes 49160 | tf_op jit(solution)/shard_map/ppermute | solution.py:196
  65.5 5.8 %collective-permute-start.16 = (bf16[256,256]{1,0:T(8,128)(2,1)S(1)}, bf16[256,256]{1,0:T(8,128)(2,1)S(1)}, u32[]{:S(2)}, u32[]{:S(2)}) collective-permute-start(bf16[256,256]{1,0:T(8,128)(2,1)S(1)} %copy-done.5), channel_id=1, source_target_pairs={{0,1},{1,0},{2,3},{3,2},{4,5},{5,4},{6,7},{7,6},{8,9},{9,8},{10,11... | collective-permute-start | bytes 393224 | tf_op jit(solution)/shard_map/ppermute | solution.py:202
  65.6 6.8 %collective-permute-start.17 = (bf16[256,256]{1,0:T(8,128)(2,1)S(1)}, bf16[256,256]{1,0:T(8,128)(2,1)S(1)}, u32[]{:S(2)}, u32[]{:S(2)}) collective-permute-start(bf16[256,256]{1,0:T(8,128)(2,1)S(1)} %collective-permute-done.13.refs_2_), channel_id=1, source_target_pairs={{0,1},{1,0},{2,3},{3,2},{4,5},{5,4},{6,7},{7,6},{8,9},{9,8},{10,11... | collective-permute-start | bytes 393224 | tf_op jit(solution)/shard_map/ppermute | solution.py:202
  68.6 5.0 %collective-permute-start.18 = (bf16[256,256]{1,0:T(8,128)(2,1)S(1)}, bf16[256,256]{1,0:T(8,128)(2,1)S(1)}, u32[]{:S(2)}, u32[]{:S(2)}) collective-permute-start(bf16[256,256]{1,0:T(8,128)(2,1)S(1)} %collective-permute-done.14.refs_3_), channel_id=1, source_target_pairs={{0,1},{1,0},{2,3},{3,2},{4,5},{5,4},{6,7},{7,6},{8,9},{9,8},{10,11... | collective-permute-start | bytes 393224 | tf_op jit(solution)/shard_map/ppermute | solution.py:202
  68.6 5.0 %collective-permute-start.19 = (bf16[256,256]{1,0:T(8,128)(2,1)S(1)}, bf16[256,256]{1,0:T(8,128)(2,1)S(1)}, u32[]{:S(2)}, u32[]{:S(2)}) collective-permute-start(bf16[256,256]{1,0:T(8,128)(2,1)S(1)} %collective-permute-done.15.refs_4_), channel_id=1, source_target_pairs={{0,1},{1,0},{2,3},{3,2},{4,5},{5,4},{6,7},{7,6},{8,9},{9,8},{10,11... | collective-permute-start | bytes 393224 | tf_op jit(solution)/shard_map/ppermute | solution.py:202
  69.2 11.5 %collective-permute-start.32 = (bf16[32,256]{1,0:T(8,128)(2,1)S(1)}, bf16[32,256]{1,0:T(8,128)(2,1)S(1)}, u32[]{:S(2)}, u32[]{:S(2)}) collective-permute-start(bf16[32,256]{1,0:T(8,128)(2,1)S(1)} %add_convert_fusion.1), channel_id=1, source_target_pairs={{0,6},{1,7},{2,4},{3,5},{4,2},{5,3},{6,0},{7,1},{8,14},{9,15},{10,... | collective-permute-start | bytes 49160 | tf_op jit(solution)/shard_map/ppermute | solution.py:199
  71.3 11.7 %collective-permute-start.31 = (bf16[32,256]{1,0:T(8,128)(2,1)S(1)}, bf16[32,256]{1,0:T(8,128)(2,1)S(1)}, u32[]{:S(2)}, u32[]{:S(2)}) collective-permute-start(bf16[32,256]{1,0:T(8,128)(2,1)S(1)} %add_convert_fusion.1), channel_id=1, source_target_pairs={{0,4},{1,5},{2,6},{3,7},{4,0},{5,1},{6,2},{7,3},{8,12},{9,13},{10,... | collective-permute-start | bytes 49160 | tf_op jit(solution)/shard_map/ppermute | solution.py:199
  72.4 10.5 %collective-permute-start.30 = (bf16[32,256]{1,0:T(8,128)(2,1)S(1)}, bf16[32,256]{1,0:T(8,128)(2,1)S(1)}, u32[]{:S(2)}, u32[]{:S(2)}) collective-permute-start(bf16[32,256]{1,0:T(8,128)(2,1)S(1)} %add_convert_fusion.1), channel_id=1, source_target_pairs={{0,2},{1,3},{2,0},{3,1},{4,6},{5,7},{6,4},{7,5},{8,10},{9,11},{10,... | collective-permute-start | bytes 49160 | tf_op jit(solution)/shard_map/ppermute | solution.py:199
  79.4 7.2 %collective-permute-start.22 = (bf16[256,256]{1,0:T(8,128)(2,1)}, bf16[256,256]{1,0:T(8,128)(2,1)S(1)}, u32[]{:S(2)}, u32[]{:S(2)}) collective-permute-start(bf16[256,256]{1,0:T(8,128)(2,1)} %get-tuple-element.29), channel_id=1, source_target_pairs={{0,24},{8,16},{16,8},{24,0},{1,25},{9,17},{17,9},{25,1},{2,26},{10... | collective-permute-start | bytes 393224 | tf_op jit(solution)/shard_map/ppermute | solution.py:196
  79.8 7.4 %collective-permute-start.21 = (bf16[256,256]{1,0:T(8,128)(2,1)}, bf16[256,256]{1,0:T(8,128)(2,1)S(1)}, u32[]{:S(2)}, u32[]{:S(2)}) collective-permute-start(bf16[256,256]{1,0:T(8,128)(2,1)} %get-tuple-element.28), channel_id=1, source_target_pairs={{0,16},{8,24},{16,0},{24,8},{1,17},{9,25},{17,1},{25,9},{2,18},{10... | collective-permute-start | bytes 393224 | tf_op jit(solution)/shard_map/ppermute | solution.py:196
  80.6 6.6 %collective-permute-start.20 = (bf16[256,256]{1,0:T(8,128)(2,1)}, bf16[256,256]{1,0:T(8,128)(2,1)S(1)}, u32[]{:S(2)}, u32[]{:S(2)}) collective-permute-start(bf16[256,256]{1,0:T(8,128)(2,1)} %get-tuple-element.27), channel_id=1, source_target_pairs={{0,8},{8,0},{16,24},{24,16},{1,9},{9,1},{17,25},{25,17},{2,10},{10... | collective-permute-start | bytes 393224 | tf_op jit(solution)/shard_map/ppermute | solution.py:196
  (25 other events, 114.1 us)

commit v2 on v1

v2 whole, which is shorter than its diff:
```python
import functools
import math

import jax
import jax.numpy as jnp
from jax import lax
from jax.experimental import pallas as pl
from jax.experimental.pallas import tpu as pltpu
from jax.sharding import PartitionSpec as P

pad_rows = 16
resident_bytes = 9 << 20
bf16, f32 = jnp.bfloat16, jnp.float32


def fits(shape, dtype):
    return math.prod(shape) * jnp.dtype(dtype).itemsize <= resident_bytes


def smem(count):
    return [pl.BlockSpec(memory_space=pltpu.SMEM)] * count


def call(body, name, outs, args, n_smem=0, scratch=(), limit=24, flops=1e6, final=()):
    kept = [
        x if i < n_smem or not fits(x.shape, x.dtype) else pltpu.with_memory_space_constraint(x, pltpu.VMEM)
        for i, x in enumerate(args)
    ]
    shapes = [
        pltpu.VMEM(shape, dtype) if i not in final and fits(shape, dtype) else jax.ShapeDtypeStruct(shape, dtype)
        for i, (shape, dtype) in enumerate(outs)
    ]
    vmem = pl.BlockSpec(memory_space=pltpu.VMEM)
    large = any(not fits(x.shape, x.dtype) for x in args) or any(not fits(*out) for out in outs)
    return pl.pallas_call(
        body,
        out_shape=shapes,
        in_specs=smem(n_smem) + [vmem] * (len(args) - n_smem),
        out_specs=[vmem] * len(outs),
        scratch_shapes=scratch,
        compiler_params=pltpu.CompilerParams(vmem_limit_bytes=(48 if large else limit) << 20),
        cost_estimate=pl.CostEstimate(flops=int(flops), bytes_accessed=1 << 20, transcendentals=0),
        name=name,
    )(*kept)


def clear(ref):
    rows, width = ref.shape
    step = 128
    zeros = jnp.zeros((step, width), ref.dtype)

    def body(i, _):
        ref[pl.ds(pl.multiple_of(i * step, step), step), :] = zeros
        return 0

    lax.fori_loop(0, rows // step, body, 0)


def unpack_tile(words):
    groups, tile = words.shape
    wide = jnp.broadcast_to(words[:, None, :], (groups, 8, tile))
    shifts = lax.broadcasted_iota(jnp.int32, (groups, 8, tile), 1)
    bits = jnp.bitwise_and(jnp.right_shift(wide, shifts), 1)
    return bits.reshape(groups * 8, tile).astype(jnp.float32).astype(jnp.bfloat16)


def build_forward(blocks, meta, meta2, patterns, patterns2, st_ref):
    my_row = lax.axis_index("row")
    my_col = lax.axis_index("col")
    my_z, core = my_col // 2, my_col % 2
    tile = patterns.shape[-1]
    half = st_ref.shape[0] // 2
    clear(st_ref)

    def add(meta_ref, patterns_ref, first):
        def step(t, _):
            a, b = meta_ref[0, t], meta_ref[1, t]
            dest = a // blocks

            @pl.when(dest % 2 == core)
            def _():
                i0 = (((dest // 2) ^ my_z) * blocks + a % blocks) * tile
                k0 = first + (((b // blocks) ^ my_row) * blocks + b % blocks) * tile
                st_ref[pl.ds(pl.multiple_of(k0, tile), tile), pl.ds(pl.multiple_of(i0, tile), tile)] = unpack_tile(
                    patterns_ref[t]
                )

            return 0

        return step

    lax.fori_loop(0, meta[2, 0], add(meta, patterns, 0), 0)
    lax.fori_loop(0, meta2[2, 0], add(meta2, patterns2, half), 0)


def build_backward(blocks, n_z, meta, patterns, st_ref):
    my_row = lax.axis_index("row")
    my_col = lax.axis_index("col")
    my_z, core = my_col // 2, my_col % 2
    tile = patterns.shape[-1]
    clear(st_ref)

    def step(t, _):
        a, b = meta[0, t], meta[1, t]
        dest = a // blocks
        i0 = ((((dest % 2) ^ core) * n_z + ((dest // 2) ^ my_z)) * blocks + a % blocks) * tile
        k0 = (((b // blocks) ^ my_row) * blocks + b % blocks) * tile
        st_ref[pl.ds(pl.multiple_of(k0, tile), tile), pl.ds(pl.multiple_of(i0, tile), tile)] = unpack_tile(patterns[t])
        return 0

    lax.fori_loop(0, meta[2, 0], step, 0)


def forward_kernel(n_feats, n_z, *refs):
    st_ref, feats, outs, feats_t = refs[0], refs[1 : 1 + n_feats], refs[1 + n_feats : 1 + n_feats + n_z], refs[-1]
    rows, width = feats[0].shape
    for i, ref in enumerate(feats):
        feats_t[:width, i * rows : (i + 1) * rows] = ref[...].T
    feats_t[width:, :] = jnp.ones((pad_rows, feats_t.shape[1]), bf16)
    line = lax.broadcasted_iota(jnp.int32, (pad_rows, rows), 0)
    for j, out in enumerate(outs):
        product = jnp.dot(feats_t[...], st_ref[:, j * rows : (j + 1) * rows], preferred_element_type=f32)
        out[:width, :] = product[:width].astype(bf16)
        degree = product[width:]
        high = jnp.floor(degree * (1.0 / 64.0)) * 64.0
        out[width:, :] = jnp.where(line == 0, high, jnp.where(line == 1, degree - high, 0.0)).astype(bf16)


def dense_kernel(n_z, *refs):
    parts = refs[:n_z]
    feats, cotangent, weight = refs[n_z : n_z + 3]
    act_ref, scaled_ref, agg_grad_ref, agg_ref, grad_ref = refs[n_z + 3 :]
    width = weight.shape[0]
    total = parts[0][...].astype(f32)
    for part in parts[1:]:
        total = total + part[...].astype(f32)
    degree = total[width : width + 1] + total[width + 1 : width + 2]
    scale = lax.rsqrt(degree + 1.0)
    agg_t = (total[:width] * scale + feats[...].astype(f32).T).astype(bf16)
    agg_ref[...] = agg_t
    w = weight[...]
    preact = jnp.dot(agg_t.T, w, preferred_element_type=f32)
    gate = jax.nn.sigmoid(preact)
    act_ref[...] = (preact * gate).astype(bf16)
    grad_pre = (cotangent[...].astype(f32) * gate * (1.0 + preact * (1.0 - gate))).astype(bf16)
    grad_ref[...] = grad_pre
    grad_agg = lax.dot_general(grad_pre, w, (((1,), (1,)), ((), ())), preferred_element_type=f32)
    agg_grad_ref[...] = grad_agg
    scale_rows = jnp.broadcast_to(scale, agg_t.shape).T
    scaled_ref[...] = (grad_agg * scale_rows).astype(bf16)


def weight_kernel(agg_t, grad_pre, keep_ref, send_ref):
    first = lax.axis_index("col") % 2 == 0
    half = agg_t.shape[0] // 2
    part = jnp.dot(agg_t[...], grad_pre[...], preferred_element_type=f32).astype(bf16)
    keep_ref[...] = jnp.where(first, part[:half], part[half:])
    send_ref[...] = jnp.where(first, part[half:], part[:half])


def backward_kernel(n_grads, n_row, *refs):
    st_ref, grads, outs = refs[0], refs[1 : 1 + n_grads], refs[1 + n_grads : 1 + n_grads + n_row]
    gathered = refs[-1]
    rows, _ = grads[0].shape
    for i, ref in enumerate(grads):
        gathered[i * rows : (i + 1) * rows, :] = ref[...]
    for j, out in enumerate(outs):
        out[...] = jnp.dot(st_ref[j * rows : (j + 1) * rows, :], gathered[...], preferred_element_type=f32).astype(
            out.dtype
        )


def tree_sum(values):
    values = [x.astype(f32) for x in values]
    while len(values) > 1:
        values = [values[i] + values[i + 1] for i in range(0, len(values), 2)]
    return values[0]


def per_device(features, weight, cotangent, tiles, tile_count, patterns):
    rows, width = features.shape
    slots, words, tile = patterns.shape[2:]
    blocks = rows // tile
    n_row = lax.axis_size("row")
    n_col = lax.axis_size("col")
    n_z = n_col // 2
    core = lax.axis_index("col") % 2
    row_len = n_z * rows
    col_len = n_row * rows
    flops = 4 * width * col_len * row_len

    def over_row(x, k):
        return lax.ppermute(x, "row", [(i, i ^ k) for i in range(n_row)])

    def over_z(x, k):
        return lax.ppermute(x, "col", [(i, i ^ (2 * k)) for i in range(n_col)])

    def over_core(x):
        return lax.ppermute(x, "col", [(i, i ^ 1) for i in range(n_col)])

    patterns = patterns[0, 0]
    meta = jnp.concatenate([tiles[0, 0], jnp.broadcast_to(tile_count, (1, slots))], axis=0)
    patterns2, meta2 = over_core(patterns), over_core(meta)
    feats = [features] + [over_row(features, k) for k in range(1, n_row)]

    (st_forward,) = call(
        functools.partial(build_forward, blocks),
        "build_forward",
        [((2 * col_len, row_len), bf16)],
        [meta, meta2, patterns, patterns2],
        n_smem=2,
        flops=2e9,
    )
    feats, st_forward = lax.optimization_barrier((feats, st_forward))
    feats = feats + [over_core(x) for x in feats]

    parts = call(
        functools.partial(forward_kernel, len(feats), n_z),
        "forward",
        [((width + pad_rows, rows), bf16)] * n_z,
        [st_forward] + feats,
        scratch=[pltpu.VMEM((width + pad_rows, 2 * col_len), bf16)],
        flops=flops,
    )
    travelling = [over_z(parts[k], k) for k in range(1, n_z)]
    (st_backward,) = call(
        functools.partial(build_backward, blocks, n_z),
        "build_backward",
        [((col_len, 2 * row_len), bf16)],
        [meta, patterns],
        n_smem=1,
        flops=2e9,
    )
    own, travelling, st_backward = lax.optimization_barrier((parts[0], travelling, st_backward))

    activated, scaled, grad_agg, agg_t, grad_pre = call(
        functools.partial(dense_kernel, n_z),
        "dense",
        [((rows, width), bf16), ((rows, width), bf16), ((rows, width), f32), ((width, rows), bf16), ((rows, width), bf16)],
        [own] + travelling + [features, cotangent, weight],
        flops=4 * rows * width * width,
        final=(0,),
    )
    grads = [scaled] + [over_z(scaled, k) for k in range(1, n_z)]
    grads = grads + [over_core(x) for x in grads]

    keep, send = call(
        weight_kernel,
        "weight_part",
        [((width // 2, width), bf16)] * 2,
        [agg_t, grad_pre],
        flops=2e9,
    )
    half = (keep.astype(f32) + over_core(send).astype(f32)).astype(bf16)
    half = tree_sum([half] + [over_row(half, k) for k in range(1, n_row)]).astype(bf16)
    half = tree_sum([half] + [over_z(half, k) for k in range(1, n_z)])
    other = over_core(half)
    grad_weight = jnp.concatenate([jnp.where(core == 0, half, other), jnp.where(core == 0, other, half)], axis=0)

    backs = call(
        functools.partial(backward_kernel, len(grads), n_row),
        "backward",
        [((rows, width), bf16)] * n_row,
        [st_backward] + grads,
        scratch=[pltpu.VMEM((2 * row_len, width), bf16)],
        flops=flops,
    )
    backs = [backs[0]] + [over_row(backs[k], k) for k in range(1, n_row)]
    grad_features = (tree_sum(backs) + grad_agg).astype(bf16)
    return activated, grad_features, grad_weight


def solution(mesh):
    return jax.shard_map(
        per_device,
        mesh=mesh,
        in_specs=(
            P(("row", "col"), None),
            P(),
            P(("row", "col"), None),
            P("row", "col", None, None),
            P("row", "col"),
            P("row", "col", None, None, None),
        ),
        out_specs=(P(("row", "col"), None), P(("row", "col"), None), P()),
        check_vma=False,
    )
```

time: 89.2 us -> 74 us (0.83)
  Pallas kernels: 22.5 us -> 8.27 us
  waiting for transfers between devices: 25.7 us -> 22.1 us
  starting transfers between devices: 32.4 us -> 34.6 us
  local copies, waits for them, and re-layouts: 4.11 us -> 5.9 us
  other arithmetic: 2.52 us -> 1.56 us
    pallas_call x6, Pallas kernels: 22.5 us -> 8.27 us  [call(): pl.pallas_call(body, out_shape=shapes, in_specs=smem(n_smem) + [vmem] * (...]
    ppermute x12 -> x9, waiting for transfers between devices: 16.6 us -> 11.2 us  [over_z(): return lax.ppermute(x, 'col', [(i, i ^ 2 * k) for i in range(n_col)])]
    ppermute x9, waiting for transfers between devices: 4.66 us -> 7.91 us  [over_row(): return lax.ppermute(x, 'row', [(i, i ^ k) for i in range(n_row)])]
    ppermute x12 -> x9, starting transfers between devices: 17.7 us -> 20.2 us  [over_z(): return lax.ppermute(x, 'col', [(i, i ^ 2 * k) for i in range(n_col)])]
    ppermute x13 -> x12, waiting for transfers between devices: 4.39 us -> 3 us  [over_core(): return lax.ppermute(x, 'col', [(i, i ^ 1) for i in range(n_col)])]
    unnamed x46 -> x14, local copies, waits for them, and re-layouts: 4.1 us -> 5.22 us
    ppermute x13 -> x12, starting transfers between devices: 2.87 us -> 2.82 us  [over_core(): return lax.ppermute(x, 'col', [(i, i ^ 1) for i in range(n_col)])]
  transfers between devices with their start and end apart: 34 -> 30, of which waited for: 13 -> 14; matrix products, arithmetic and copies ran while one was open for 0% -> 2% of each run, Pallas kernels for 17% -> 8%
where the time goes in v2:
time: 74 us; the launch traced here: 73.8 us
  starting transfers between devices  34.6 us (47%)
  waiting for transfers between devices  22.1 us (30%)
  Pallas kernels  8.27 us (11%)
  local copies, waits for them, and re-layouts  5.9 us (8%)
  other arithmetic  1.56 us (2%)
  between operations  1.44 us (2%)
    ppermute x9, starting transfers between devices, over_z(): return lax.ppermute(x, 'col', [(i, i ^ 2 * k) for i in range(n_col)])  20.2 us
    ppermute x9, starting transfers between devices, over_row(): return lax.ppermute(x, 'row', [(i, i ^ k) for i in range(n_row)])  11.6 us
    ppermute x9, waiting for transfers between devices, over_z(): return lax.ppermute(x, 'col', [(i, i ^ 2 * k) for i in range(n_col)])  11.2 us
    pallas_call x6, Pallas kernels, call(): pl.pallas_call(body, out_shape=shapes, in_specs=smem(n_smem) + [vmem] * (...  8.27 us
    ppermute x9, waiting for transfers between devices, over_row(): return lax.ppermute(x, 'row', [(i, i ^ k) for i in range(n_row)])  7.91 us
    unnamed x14, local copies, waits for them, and re-layouts  5.22 us
    ppermute x12, waiting for transfers between devices, over_core(): return lax.ppermute(x, 'col', [(i, i ^ 1) for i in range(n_col)])  3 us
    ppermute x12, starting transfers between devices, over_core(): return lax.ppermute(x, 'col', [(i, i ^ 1) for i in range(n_col)])  2.82 us
  transfers between devices with their start and end apart: 30, of which 14 were waited for; matrix products, arithmetic and copies ran while one was open for 2% of the time, Pallas kernels for 8%

profile of v2, /device:TPU:0, one launch (start us, length us, event | category | flops | bytes accessed | tf_op | source)
XLA Modules:
  0.0 73.8 jit_solution(16956796393525169456)
XLA Ops:
  1.8 0.7 concatenate.6.meta
  2.6 3.9 %collective-permute-start.2 = (bf16[256,256]{1,0:T(8,128)(2,1)}, bf16[256,256]{1,0:T(8,128)(2,1)S(1)}, u32[]{:S(2)}, u32[]{:S(2)}) collective-permute-start(bf16[256,256]{1,0:T(8,128)(2,1)} %refs_4_.1), channel_id=1, source_target_pairs={{0,24},{8,16},{16,8},{24,0},{1,25},{9,17},{17,9},{25,1},{2,26},{10... | collective-permute-start | bytes 393224 | tf_op jit(solution)/shard_map/ppermute | solution.py:193
  7.0 1.0 %copy-done.5 = s32[1,1,64,16,128]{4,3,2,1,0:T(8,128)S(1)} copy-done((s32[1,1,64,16,128]{4,3,2,1,0:T(8,128)S(1)}, s32[1,1,64,16,128]{4,3,2,1,0:T(8,128)}, u32[]{:S(2)}) %copy-start.5) | copy-done | bytes 524312
  8.1 2.8 %build_forward.1.refs_0_ = bf16[2048,1024]{1,0:T(8,128)(2,1)S(1)} custom-call(s32[3,64]{1,0:T(4,128)S(1)} %concatenate.6.meta, s32[3,64]{1,0:T(4,128)S(1)} %collective-permute-done.3.meta2, s32[64,16,128]{2,1,0:T(8,128)S(1)} %bitcast.5, s32[64,16,128]{2,1,0:T(8,128)S(1)} %collective-permute-done.4.patterns2), custom_call_target="tpu_custom_call" | custom-call | flops 2000000000 | bytes 1048576 | tf_op jit(solution)/shard_map/build_forward/pallas_call | solution.py:35
  10.9 2.3 %collective-permute-done.1.refs_3_ = bf16[256,256]{1,0:T(8,128)(2,1)S(1)} collective-permute-done((bf16[256,256]{1,0:T(8,128)(2,1)}, bf16[256,256]{1,0:T(8,128)(2,1)S(1)}, u32[]{:S(2)}, u32[]{:S(2)}) %collective-permute-start.1) | collective-permute-done | bytes 131104 | tf_op jit(solution)/shard_map/ppermute | solution.py:193
  15.5 1.3 %forward.1 = (bf16[272,256]{1,0:T(8,128)(2,1)S(1)}, bf16[272,256]{1,0:T(8,128)(2,1)S(1)}, bf16[272,256]{1,0:T(8,128)(2,1)S(1)}, bf16[272,256]{1,0:T(8,128)(2,1)S(1)}) custom-call(bf16[2048,1024]{1,0:T(8,128)(2,1)S(1)} %build_forward.1.refs_0_, bf16[256,256]{1,0:T(8,128)(2,1)S(1)} %copy-done.2, bf16[256,256]{1,0:T(8,128)(2,1)S(1)} %collective-permute-done.refs_2_, ...), custom_call_target="tpu_custom_call" | custom-call | flops 1073741824 | bytes 1048576 | tf_op jit(solution)/shard_map/forward/pallas_call | solution.py:35
  16.8 1.6 %collective-permute-start.9 = (bf16[272,256]{1,0:T(8,128)(2,1)S(1)}, bf16[272,256]{1,0:T(8,128)(2,1)S(1)}, u32[]{:S(2)}, u32[]{:S(2)}) collective-permute-start(bf16[272,256]{1,0:T(8,128)(2,1)S(1)} %get-tuple-element.34), channel_id=1, source_target_pairs={{0,2},{1,3},{2,0},{3,1},{4,6},{5,7},{6,4},{7,5},{8,10},{9,11},{10,... | collective-permute-start | bytes 417800 | tf_op jit(solution)/shard_map/ppermute | solution.py:196
  18.5 2.6 %collective-permute-start.10 = (bf16[272,256]{1,0:T(8,128)(2,1)S(1)}, bf16[272,256]{1,0:T(8,128)(2,1)S(1)}, u32[]{:S(2)}, u32[]{:S(2)}) collective-permute-start(bf16[272,256]{1,0:T(8,128)(2,1)S(1)} %get-tuple-element.35), channel_id=1, source_target_pairs={{0,4},{1,5},{2,6},{3,7},{4,0},{5,1},{6,2},{7,3},{8,12},{9,13},{10,... | collective-permute-start | bytes 417800 | tf_op jit(solution)/shard_map/ppermute | solution.py:196
  21.3 1.7 %build_backward.1.refs_0_ = bf16[1024,2048]{1,0:T(8,128)(2,1)S(1)} custom-call(s32[3,64]{1,0:T(4,128)S(1)} %concatenate.6.meta, s32[64,16,128]{2,1,0:T(8,128)S(1)} %bitcast.6), custom_call_target="tpu_custom_call" | custom-call | flops 2000000000 | bytes 1048576 | tf_op jit(solution)/shard_map/build_backward/pallas_call | solution.py:35
  23.0 2.0 %copy-done = bf16[1024,2048]{1,0:T(8,128)(2,1)} copy-done((bf16[1024,2048]{1,0:T(8,128)(2,1)}, bf16[1024,2048]{1,0:T(8,128)(2,1)S(1)}, u32[]{:S(2)}) %copy-start) | copy-done | bytes 4194328
  25.1 6.8 %collective-permute-done.10.refs_2_ = bf16[272,256]{1,0:T(8,128)(2,1)S(1)} collective-permute-done((bf16[272,256]{1,0:T(8,128)(2,1)S(1)}, bf16[272,256]{1,0:T(8,128)(2,1)S(1)}, u32[]{:S(2)}, u32[]{:S(2)}) %collective-permute-start.10) | collective-permute-done | bytes 139296 | tf_op jit(solution)/shard_map/ppermute | solution.py:196
  31.9 1.0 %dense.1 = (bf16[256,256]{1,0:T(8,128)(2,1)}, bf16[256,256]{1,0:T(8,128)(2,1)S(1)}, f32[256,256]{1,0:T(8,128)S(1)}, bf16[256,256]{1,0:T(8,128)(2,1)S(1)}, bf16[256,256]{1,0:T(8,128)(2,1)S(1)}) custom-call(bf16[272,256]{1,0:T(8,128)(2,1)S(1)} %get-tuple-element.37.refs_0_, bf16[272,256]{1,0:T(8,128)(2,1)S(1)} %collective-permute-done.9.refs_1_, ...), custom_call_target="tpu_custom_call" | custom-call | flops 67108864 | bytes 1048576 | tf_op jit(solution)/shard_map/dense/pallas_call | solution.py:35
  33.2 1.2 %collective-permute-done.22 = bf16[128,256]{1,0:T(8,128)(2,1)S(1)} collective-permute-done((bf16[128,256]{1,0:T(8,128)(2,1)S(1)}, bf16[128,256]{1,0:T(8,128)(2,1)S(1)}, u32[]{:S(2)}, u32[]{:S(2)}) %collective-permute-start.22) | collective-permute-done | bytes 65568 | tf_op jit(solution)/shard_map/ppermute | solution.py:199
  34.5 1.7 %collective-permute-start.25 = (bf16[128,256]{1,0:T(8,128)(2,1)S(1)}, bf16[128,256]{1,0:T(8,128)(2,1)S(1)}, u32[]{:S(2)}, u32[]{:S(2)}) collective-permute-start(bf16[128,256]{1,0:T(8,128)(2,1)S(1)} %add_convert_fusion.2), channel_id=1, source_target_pairs={{0,24},{8,16},{16,8},{24,0},{1,25},{9,17},{17,9},{25,1},{2,26},{10... | collective-permute-start | bytes 196616 | tf_op jit(solution)/shard_map/ppermute | solution.py:193
  36.2 1.3 %collective-permute-start.24 = (bf16[128,256]{1,0:T(8,128)(2,1)S(1)}, bf16[128,256]{1,0:T(8,128)(2,1)S(1)}, u32[]{:S(2)}, u32[]{:S(2)}) collective-permute-start(bf16[128,256]{1,0:T(8,128)(2,1)S(1)} %add_convert_fusion.2), channel_id=1, source_target_pairs={{0,16},{8,24},{16,0},{24,8},{1,17},{9,25},{17,1},{25,9},{2,18},{10... | collective-permute-start | bytes 196616 | tf_op jit(solution)/shard_map/ppermute | solution.py:193
  38.0 2.5 %collective-permute-start.14 = (bf16[256,256]{1,0:T(8,128)(2,1)S(1)}, bf16[256,256]{1,0:T(8,128)(2,1)S(1)}, u32[]{:S(2)}, u32[]{:S(2)}) collective-permute-start(bf16[256,256]{1,0:T(8,128)(2,1)S(1)} %get-tuple-element.43.refs_1_), channel_id=1, source_target_pairs={{0,6},{1,7},{2,4},{3,5},{4,2},{5,3},{6,0},{7,1},{8,14},{9,15},{10,... | collective-permute-start | bytes 393224 | tf_op jit(solution)/shard_map/ppermute | solution.py:196
  40.5 1.6 %collective-permute-start.13 = (bf16[256,256]{1,0:T(8,128)(2,1)S(1)}, bf16[256,256]{1,0:T(8,128)(2,1)S(1)}, u32[]{:S(2)}, u32[]{:S(2)}) collective-permute-start(bf16[256,256]{1,0:T(8,128)(2,1)S(1)} %get-tuple-element.43.refs_1_), channel_id=1, source_target_pairs={{0,4},{1,5},{2,6},{3,7},{4,0},{5,1},{6,2},{7,3},{8,12},{9,13},{10,... | collective-permute-start | bytes 393224 | tf_op jit(solution)/shard_map/ppermute | solution.py:196
  42.5 2.5 %collective-permute-start.28 = (bf16[128,256]{1,0:T(8,128)(2,1)S(1)}, bf16[128,256]{1,0:T(8,128)(2,1)S(1)}, u32[]{:S(2)}, u32[]{:S(2)}) collective-permute-start(bf16[128,256]{1,0:T(8,128)(2,1)S(1)} %add_convert_fusion.1), channel_id=1, source_target_pairs={{0,6},{1,7},{2,4},{3,5},{4,2},{5,3},{6,0},{7,1},{8,14},{9,15},{10,... | collective-permute-start | bytes 196616 | tf_op jit(solution)/shard_map/ppermute | solution.py:196
  45.0 1.0 %collective-permute-start.27 = (bf16[128,256]{1,0:T(8,128)(2,1)S(1)}, bf16[128,256]{1,0:T(8,128)(2,1)S(1)}, u32[]{:S(2)}, u32[]{:S(2)}) collective-permute-start(bf16[128,256]{1,0:T(8,128)(2,1)S(1)} %add_convert_fusion.1), channel_id=1, source_target_pairs={{0,4},{1,5},{2,6},{3,7},{4,0},{5,1},{6,2},{7,3},{8,12},{9,13},{10,... | collective-permute-start | bytes 196616 | tf_op jit(solution)/shard_map/ppermute | solution.py:196
  46.0 7.8 %collective-permute-start.26 = (bf16[128,256]{1,0:T(8,128)(2,1)S(1)}, bf16[128,256]{1,0:T(8,128)(2,1)S(1)}, u32[]{:S(2)}, u32[]{:S(2)}) collective-permute-start(bf16[128,256]{1,0:T(8,128)(2,1)S(1)} %add_convert_fusion.1), channel_id=1, source_target_pairs={{0,2},{1,3},{2,0},{3,1},{4,6},{5,7},{6,4},{7,5},{8,10},{9,11},{10,... | collective-permute-start | bytes 196616 | tf_op jit(solution)/shard_map/ppermute | solution.py:196
  53.8 2.2 %collective-permute-done.13.refs_3_ = bf16[256,256]{1,0:T(8,128)(2,1)S(1)} collective-permute-done((bf16[256,256]{1,0:T(8,128)(2,1)S(1)}, bf16[256,256]{1,0:T(8,128)(2,1)S(1)}, u32[]{:S(2)}, u32[]{:S(2)}) %collective-permute-start.13) | collective-permute-done | bytes 131104 | tf_op jit(solution)/shard_map/ppermute | solution.py:196
  56.7 2.0 %collective-permute-done.27 = bf16[128,256]{1,0:T(8,128)(2,1)S(1)} collective-permute-done((bf16[128,256]{1,0:T(8,128)(2,1)S(1)}, bf16[128,256]{1,0:T(8,128)(2,1)S(1)}, u32[]{:S(2)}, u32[]{:S(2)}) %collective-permute-start.27) | collective-permute-done | bytes 65568 | tf_op jit(solution)/shard_map/ppermute | solution.py:196
  59.2 0.7 collective-permute-done.16.refs_6_
  60.0 2.2 %copy-done.1 = bf16[1024,2048]{1,0:T(8,128)(2,1)S(1)} copy-done((bf16[1024,2048]{1,0:T(8,128)(2,1)S(1)}, bf16[1024,2048]{1,0:T(8,128)(2,1)}, u32[]{:S(2)}) %copy-start.1) | copy-done | bytes 4194328
  62.1 1.2 %backward.1 = (bf16[256,256]{1,0:T(8,128)(2,1)S(1)}, bf16[256,256]{1,0:T(8,128)(2,1)S(1)}, bf16[256,256]{1,0:T(8,128)(2,1)S(1)}, bf16[256,256]{1,0:T(8,128)(2,1)S(1)}) custom-call(bf16[1024,2048]{1,0:T(8,128)(2,1)S(1)} %copy-done.1, bf16[256,256]{1,0:T(8,128)(2,1)S(1)} %get-tuple-element.43.refs_1_, bf16[256,256]{1,0:T(8,128)(2,1)S(1)} %collective-permute-done.12.refs_2_, ...), custom_call_target="tpu_custom_call" | custom-call | flops 1073741824 | bytes 1048576 | tf_op jit(solution)/shard_map/backward/pallas_call | solution.py:35
  63.4 1.6 %collective-permute-start.19 = (bf16[256,256]{1,0:T(8,128)(2,1)S(1)}, bf16[256,256]{1,0:T(8,128)(2,1)S(1)}, u32[]{:S(2)}, u32[]{:S(2)}) collective-permute-start(bf16[256,256]{1,0:T(8,128)(2,1)S(1)} %get-tuple-element.45), channel_id=1, source_target_pairs={{0,8},{8,0},{16,24},{24,16},{1,9},{9,1},{17,25},{25,17},{2,10},{10... | collective-permute-start | bytes 393224 | tf_op jit(solution)/shard_map/ppermute | solution.py:193
  65.0 0.7 collective-permute-start.20
  65.7 1.2 %collective-permute-start.21 = (bf16[256,256]{1,0:T(8,128)(2,1)S(1)}, bf16[256,256]{1,0:T(8,128)(2,1)S(1)}, u32[]{:S(2)}, u32[]{:S(2)}) collective-permute-start(bf16[256,256]{1,0:T(8,128)(2,1)S(1)} %get-tuple-element.47), channel_id=1, source_target_pairs={{0,24},{8,16},{16,8},{24,0},{1,25},{9,17},{17,9},{25,1},{2,26},{10... | collective-permute-start | bytes 393224 | tf_op jit(solution)/shard_map/ppermute | solution.py:193
  67.0 0.7 pad_maximum_fusion
  67.7 1.6 %collective-permute-done.19 = bf16[256,256]{1,0:T(8,128)(2,1)S(1)} collective-permute-done((bf16[256,256]{1,0:T(8,128)(2,1)S(1)}, bf16[256,256]{1,0:T(8,128)(2,1)S(1)}, u32[]{:S(2)}, u32[]{:S(2)}) %collective-permute-start.19) | collective-permute-done | bytes 131104 | tf_op jit(solution)/shard_map/ppermute | solution.py:193
  69.3 3.7 %collective-permute-done.20 = bf16[256,256]{1,0:T(8,128)(2,1)S(1)} collective-permute-done((bf16[256,256]{1,0:T(8,128)(2,1)S(1)}, bf16[256,256]{1,0:T(8,128)(2,1)S(1)}, u32[]{:S(2)}, u32[]{:S(2)}) %collective-permute-start.20) | collective-permute-done | bytes 131104 | tf_op jit(solution)/shard_map/ppermute | solution.py:193
  73.1 0.7 add_convert_fusion
  (55 shorter events, 6.3 us)
Async XLA Ops:
  0.6 6.4 %collective-permute-start.4 = (s32[64,16,128]{2,1,0:T(8,128)}, s32[64,16,128]{2,1,0:T(8,128)S(1)}, u32[]{:S(2)}, u32[]{:S(2)}) collective-permute-start(s32[64,16,128]{2,1,0:T(8,128)} %bitcast.4), channel_id=1, source_target_pairs={{0,1},{1,0},{2,3},{3,2},{4,5},{5,4},{6,7},{7,6},{8,9},{9,8},{10,11... | collective-permute-start | bytes 1572872 | tf_op jit(solution)/shard_map/ppermute | solution.py:199
  2.5 4.5 %collective-permute-start.3 = (s32[3,64]{1,0:T(4,128)S(1)}, s32[3,64]{1,0:T(4,128)S(1)}, u32[]{:S(2)}, u32[]{:S(2)}) collective-permute-start(s32[3,64]{1,0:T(4,128)S(1)} %concatenate.6.meta), channel_id=1, source_target_pairs={{0,1},{1,0},{2,3},{3,2},{4,5},{5,4},{6,7},{7,6},{8,9},{9,8},{10,11... | collective-permute-start | bytes 2312 | tf_op jit(solution)/shard_map/ppermute | solution.py:199
  2.6 8.3 %collective-permute-start.2 = (bf16[256,256]{1,0:T(8,128)(2,1)}, bf16[256,256]{1,0:T(8,128)(2,1)S(1)}, u32[]{:S(2)}, u32[]{:S(2)}) collective-permute-start(bf16[256,256]{1,0:T(8,128)(2,1)} %refs_4_.1), channel_id=1, source_target_pairs={{0,24},{8,16},{16,8},{24,0},{1,25},{9,17},{17,9},{25,1},{2,26},{10... | collective-permute-start | bytes 393224 | tf_op jit(solution)/shard_map/ppermute | solution.py:193
  6.5 6.7 %collective-permute-start.1 = (bf16[256,256]{1,0:T(8,128)(2,1)}, bf16[256,256]{1,0:T(8,128)(2,1)S(1)}, u32[]{:S(2)}, u32[]{:S(2)}) collective-permute-start(bf16[256,256]{1,0:T(8,128)(2,1)} %refs_4_.1), channel_id=1, source_target_pairs={{0,16},{8,24},{16,0},{24,8},{1,17},{9,25},{17,1},{25,9},{2,18},{10... | collective-permute-start | bytes 393224 | tf_op jit(solution)/shard_map/ppermute | solution.py:193
  7.0 6.4 %collective-permute-start = (bf16[256,256]{1,0:T(8,128)(2,1)}, bf16[256,256]{1,0:T(8,128)(2,1)S(1)}, u32[]{:S(2)}, u32[]{:S(2)}) collective-permute-start(bf16[256,256]{1,0:T(8,128)(2,1)} %refs_4_.1), channel_id=1, source_target_pairs={{0,8},{8,0},{16,24},{24,16},{1,9},{9,1},{17,25},{25,17},{2,10},{10... | collective-permute-start | bytes 393224 | tf_op jit(solution)/shard_map/ppermute | solution.py:193
  13.4 1.3 %collective-permute-start.5 = (bf16[256,256]{1,0:T(8,128)(2,1)S(1)}, bf16[256,256]{1,0:T(8,128)(2,1)S(1)}, u32[]{:S(2)}, u32[]{:S(2)}) collective-permute-start(bf16[256,256]{1,0:T(8,128)(2,1)S(1)} %copy-done.2), channel_id=1, source_target_pairs={{0,1},{1,0},{2,3},{3,2},{4,5},{5,4},{6,7},{7,6},{8,9},{9,8},{10,11... | collective-permute-start | bytes 393224 | tf_op jit(solution)/shard_map/ppermute | solution.py:199
  13.4 1.5 %collective-permute-start.6 = (bf16[256,256]{1,0:T(8,128)(2,1)S(1)}, bf16[256,256]{1,0:T(8,128)(2,1)S(1)}, u32[]{:S(2)}, u32[]{:S(2)}) collective-permute-start(bf16[256,256]{1,0:T(8,128)(2,1)S(1)} %collective-permute-done.refs_2_), channel_id=1, source_target_pairs={{0,1},{1,0},{2,3},{3,2},{4,5},{5,4},{6,7},{7,6},{8,9},{9,8},{10,11... | collective-permute-start | bytes 393224 | tf_op jit(solution)/shard_map/ppermute | solution.py:199
  13.9 1.3 %collective-permute-start.7 = (bf16[256,256]{1,0:T(8,128)(2,1)S(1)}, bf16[256,256]{1,0:T(8,128)(2,1)S(1)}, u32[]{:S(2)}, u32[]{:S(2)}) collective-permute-start(bf16[256,256]{1,0:T(8,128)(2,1)S(1)} %collective-permute-done.1.refs_3_), channel_id=1, source_target_pairs={{0,1},{1,0},{2,3},{3,2},{4,5},{5,4},{6,7},{7,6},{8,9},{9,8},{10,11... | collective-permute-start | bytes 393224 | tf_op jit(solution)/shard_map/ppermute | solution.py:199
  13.9 1.5 %collective-permute-start.8 = (bf16[256,256]{1,0:T(8,128)(2,1)S(1)}, bf16[256,256]{1,0:T(8,128)(2,1)S(1)}, u32[]{:S(2)}, u32[]{:S(2)}) collective-permute-start(bf16[256,256]{1,0:T(8,128)(2,1)S(1)} %collective-permute-done.2.refs_4_), channel_id=1, source_target_pairs={{0,1},{1,0},{2,3},{3,2},{4,5},{5,4},{6,7},{7,6},{8,9},{9,8},{10,11... | collective-permute-start | bytes 393224 | tf_op jit(solution)/shard_map/ppermute | solution.py:199
  16.8 15.1 %copy-start.3 = (bf16[256,256]{1,0:T(8,128)(2,1)S(1)}, bf16[256,256]{1,0:T(8,128)(2,1)}, u32[]{:S(2)}) copy-start(bf16[256,256]{1,0:T(8,128)(2,1)} %refs_5_.1) | copy-start | bytes 393220
  16.8 15.1 %copy-start.4 = (bf16[256,256]{1,0:T(8,128)(2,1)S(1)}, bf16[256,256]{1,0:T(8,128)(2,1)}, u32[]{:S(2)}) copy-start(bf16[256,256]{1,0:T(8,128)(2,1)} %refs_6_.1) | copy-start | bytes 393220
  16.8 8.3 %collective-permute-start.9 = (bf16[272,256]{1,0:T(8,128)(2,1)S(1)}, bf16[272,256]{1,0:T(8,128)(2,1)S(1)}, u32[]{:S(2)}, u32[]{:S(2)}) collective-permute-start(bf16[272,256]{1,0:T(8,128)(2,1)S(1)} %get-tuple-element.34), channel_id=1, source_target_pairs={{0,2},{1,3},{2,0},{3,1},{4,6},{5,7},{6,4},{7,5},{8,10},{9,11},{10,... | collective-permute-start | bytes 417800 | tf_op jit(solution)/shard_map/ppermute | solution.py:196
  18.5 13.4 %collective-permute-start.10 = (bf16[272,256]{1,0:T(8,128)(2,1)S(1)}, bf16[272,256]{1,0:T(8,128)(2,1)S(1)}, u32[]{:S(2)}, u32[]{:S(2)}) collective-permute-start(bf16[272,256]{1,0:T(8,128)(2,1)S(1)} %get-tuple-element.35), channel_id=1, source_target_pairs={{0,4},{1,5},{2,6},{3,7},{4,0},{5,1},{6,2},{7,3},{8,12},{9,13},{10,... | collective-permute-start | bytes 417800 | tf_op jit(solution)/shard_map/ppermute | solution.py:196
  21.1 10.9 %collective-permute-start.11 = (bf16[272,256]{1,0:T(8,128)(2,1)S(1)}, bf16[272,256]{1,0:T(8,128)(2,1)S(1)}, u32[]{:S(2)}, u32[]{:S(2)}) collective-permute-start(bf16[272,256]{1,0:T(8,128)(2,1)S(1)} %get-tuple-element.36), channel_id=1, source_target_pairs={{0,6},{1,7},{2,4},{3,5},{4,2},{5,3},{6,0},{7,1},{8,14},{9,15},{10,... | collective-permute-start | bytes 417800 | tf_op jit(solution)/shard_map/ppermute | solution.py:196
  33.1 1.3 %collective-permute-start.22 = (bf16[128,256]{1,0:T(8,128)(2,1)S(1)}, bf16[128,256]{1,0:T(8,128)(2,1)S(1)}, u32[]{:S(2)}, u32[]{:S(2)}) collective-permute-start(bf16[128,256]{1,0:T(8,128)(2,1)S(1)} %get-tuple-element.52), channel_id=1, source_target_pairs={{0,1},{1,0},{2,3},{3,2},{4,5},{5,4},{6,7},{7,6},{8,9},{9,8},{10,11... | collective-permute-start | bytes 196616 | tf_op jit(solution)/shard_map/ppermute | solution.py:199
  34.5 7.6 %collective-permute-start.25 = (bf16[128,256]{1,0:T(8,128)(2,1)S(1)}, bf16[128,256]{1,0:T(8,128)(2,1)S(1)}, u32[]{:S(2)}, u32[]{:S(2)}) collective-permute-start(bf16[128,256]{1,0:T(8,128)(2,1)S(1)} %add_convert_fusion.2), channel_id=1, source_target_pairs={{0,24},{8,16},{16,8},{24,0},{1,25},{9,17},{17,9},{25,1},{2,26},{10... | collective-permute-start | bytes 196616 | tf_op jit(solution)/shard_map/ppermute | solution.py:193
  36.2 6.2 %collective-permute-start.24 = (bf16[128,256]{1,0:T(8,128)(2,1)S(1)}, bf16[128,256]{1,0:T(8,128)(2,1)S(1)}, u32[]{:S(2)}, u32[]{:S(2)}) collective-permute-start(bf16[128,256]{1,0:T(8,128)(2,1)S(1)} %add_convert_fusion.2), channel_id=1, source_target_pairs={{0,16},{8,24},{16,0},{24,8},{1,17},{9,25},{17,1},{25,9},{2,18},{10... | collective-permute-start | bytes 196616 | tf_op jit(solution)/shard_map/ppermute | solution.py:193
  37.5 4.9 %collective-permute-start.23 = (bf16[128,256]{1,0:T(8,128)(2,1)S(1)}, bf16[128,256]{1,0:T(8,128)(2,1)S(1)}, u32[]{:S(2)}, u32[]{:S(2)}) collective-permute-start(bf16[128,256]{1,0:T(8,128)(2,1)S(1)} %add_convert_fusion.2), channel_id=1, source_target_pairs={{0,8},{8,0},{16,24},{24,16},{1,9},{9,1},{17,25},{25,17},{2,10},{10... | collective-permute-start | bytes 196616 | tf_op jit(solution)/shard_map/ppermute | solution.py:193
  38.0 8.0 %collective-permute-start.14 = (bf16[256,256]{1,0:T(8,128)(2,1)S(1)}, bf16[256,256]{1,0:T(8,128)(2,1)S(1)}, u32[]{:S(2)}, u32[]{:S(2)}) collective-permute-start(bf16[256,256]{1,0:T(8,128)(2,1)S(1)} %get-tuple-element.43.refs_1_), channel_id=1, source_target_pairs={{0,6},{1,7},{2,4},{3,5},{4,2},{5,3},{6,0},{7,1},{8,14},{9,15},{10,... | collective-permute-start | bytes 393224 | tf_op jit(solution)/shard_map/ppermute | solution.py:196
  40.5 15.6 %collective-permute-start.13 = (bf16[256,256]{1,0:T(8,128)(2,1)S(1)}, bf16[256,256]{1,0:T(8,128)(2,1)S(1)}, u32[]{:S(2)}, u32[]{:S(2)}) collective-permute-start(bf16[256,256]{1,0:T(8,128)(2,1)S(1)} %get-tuple-element.43.refs_1_), channel_id=1, source_target_pairs={{0,4},{1,5},{2,6},{3,7},{4,0},{5,1},{6,2},{7,3},{8,12},{9,13},{10,... | collective-permute-start | bytes 393224 | tf_op jit(solution)/shard_map/ppermute | solution.py:196
  42.1 13.9 %collective-permute-start.12 = (bf16[256,256]{1,0:T(8,128)(2,1)S(1)}, bf16[256,256]{1,0:T(8,128)(2,1)S(1)}, u32[]{:S(2)}, u32[]{:S(2)}) collective-permute-start(bf16[256,256]{1,0:T(8,128)(2,1)S(1)} %get-tuple-element.43.refs_1_), channel_id=1, source_target_pairs={{0,2},{1,3},{2,0},{3,1},{4,6},{5,7},{6,4},{7,5},{8,10},{9,11},{10,... | collective-permute-start | bytes 393224 | tf_op jit(solution)/shard_map/ppermute | solution.py:196
  42.5 14.1 %collective-permute-start.28 = (bf16[128,256]{1,0:T(8,128)(2,1)S(1)}, bf16[128,256]{1,0:T(8,128)(2,1)S(1)}, u32[]{:S(2)}, u32[]{:S(2)}) collective-permute-start(bf16[128,256]{1,0:T(8,128)(2,1)S(1)} %add_convert_fusion.1), channel_id=1, source_target_pairs={{0,6},{1,7},{2,4},{3,5},{4,2},{5,3},{6,0},{7,1},{8,14},{9,15},{10,... | collective-permute-start | bytes 196616 | tf_op jit(solution)/shard_map/ppermute | solution.py:196
  45.0 13.6 %collective-permute-start.27 = (bf16[128,256]{1,0:T(8,128)(2,1)S(1)}, bf16[128,256]{1,0:T(8,128)(2,1)S(1)}, u32[]{:S(2)}, u32[]{:S(2)}) collective-permute-start(bf16[128,256]{1,0:T(8,128)(2,1)S(1)} %add_convert_fusion.1), channel_id=1, source_target_pairs={{0,4},{1,5},{2,6},{3,7},{4,0},{5,1},{6,2},{7,3},{8,12},{9,13},{10,... | collective-permute-start | bytes 196616 | tf_op jit(solution)/shard_map/ppermute | solution.py:196
  46.0 12.6 %collective-permute-start.26 = (bf16[128,256]{1,0:T(8,128)(2,1)S(1)}, bf16[128,256]{1,0:T(8,128)(2,1)S(1)}, u32[]{:S(2)}, u32[]{:S(2)}) collective-permute-start(bf16[128,256]{1,0:T(8,128)(2,1)S(1)} %add_convert_fusion.1), channel_id=1, source_target_pairs={{0,2},{1,3},{2,0},{3,1},{4,6},{5,7},{6,4},{7,5},{8,10},{9,11},{10,... | collective-permute-start | bytes 196616 | tf_op jit(solution)/shard_map/ppermute | solution.py:196
  56.1 3.2 %collective-permute-start.15 = (bf16[256,256]{1,0:T(8,128)(2,1)S(1)}, bf16[256,256]{1,0:T(8,128)(2,1)S(1)}, u32[]{:S(2)}, u32[]{:S(2)}) collective-permute-start(bf16[256,256]{1,0:T(8,128)(2,1)S(1)} %get-tuple-element.43.refs_1_), channel_id=1, source_target_pairs={{0,1},{1,0},{2,3},{3,2},{4,5},{5,4},{6,7},{7,6},{8,9},{9,8},{10,11... | collective-permute-start | bytes 393224 | tf_op jit(solution)/shard_map/ppermute | solution.py:199
  56.1 3.2 %collective-permute-start.18 = (bf16[256,256]{1,0:T(8,128)(2,1)S(1)}, bf16[256,256]{1,0:T(8,128)(2,1)S(1)}, u32[]{:S(2)}, u32[]{:S(2)}) collective-permute-start(bf16[256,256]{1,0:T(8,128)(2,1)S(1)} %collective-permute-done.14.refs_4_), channel_id=1, source_target_pairs={{0,1},{1,0},{2,3},{3,2},{4,5},{5,4},{6,7},{7,6},{8,9},{9,8},{10,11... | collective-permute-start | bytes 393224 | tf_op jit(solution)/shard_map/ppermute | solution.py:199
  56.6 2.6 %collective-permute-start.17 = (bf16[256,256]{1,0:T(8,128)(2,1)S(1)}, bf16[256,256]{1,0:T(8,128)(2,1)S(1)}, u32[]{:S(2)}, u32[]{:S(2)}) collective-permute-start(bf16[256,256]{1,0:T(8,128)(2,1)S(1)} %collective-permute-done.13.refs_3_), channel_id=1, source_target_pairs={{0,1},{1,0},{2,3},{3,2},{4,5},{5,4},{6,7},{7,6},{8,9},{9,8},{10,11... | collective-permute-start | bytes 393224 | tf_op jit(solution)/shard_map/ppermute | solution.py:199
  58.6 1.3 %collective-permute-start.16 = (bf16[256,256]{1,0:T(8,128)(2,1)S(1)}, bf16[256,256]{1,0:T(8,128)(2,1)S(1)}, u32[]{:S(2)}, u32[]{:S(2)}) collective-permute-start(bf16[256,256]{1,0:T(8,128)(2,1)S(1)} %collective-permute-done.12.refs_2_), channel_id=1, source_target_pairs={{0,1},{1,0},{2,3},{3,2},{4,5},{5,4},{6,7},{7,6},{8,9},{9,8},{10,11... | collective-permute-start | bytes 393224 | tf_op jit(solution)/shard_map/ppermute | solution.py:199
  58.7 8.3 %collective-permute-start.29 = (f32[128,256]{1,0:T(8,128)S(1)}, f32[128,256]{1,0:T(8,128)S(1)}, u32[]{:S(2)}, u32[]{:S(2)}) collective-permute-start(f32[128,256]{1,0:T(8,128)S(1)} %add_add_fusion), channel_id=1, source_target_pairs={{0,1},{1,0},{2,3},{3,2},{4,5},{5,4},{6,7},{7,6},{8,9},{9,8},{10,11... | collective-permute-start | bytes 393224 | tf_op jit(solution)/shard_map/ppermute | solution.py:199
  63.4 5.9 %collective-permute-start.19 = (bf16[256,256]{1,0:T(8,128)(2,1)S(1)}, bf16[256,256]{1,0:T(8,128)(2,1)S(1)}, u32[]{:S(2)}, u32[]{:S(2)}) collective-permute-start(bf16[256,256]{1,0:T(8,128)(2,1)S(1)} %get-tuple-element.45), channel_id=1, source_target_pairs={{0,8},{8,0},{16,24},{24,16},{1,9},{9,1},{17,25},{25,17},{2,10},{10... | collective-permute-start | bytes 393224 | tf_op jit(solution)/shard_map/ppermute | solution.py:193
  65.0 8.1 %collective-permute-start.20 = (bf16[256,256]{1,0:T(8,128)(2,1)S(1)}, bf16[256,256]{1,0:T(8,128)(2,1)S(1)}, u32[]{:S(2)}, u32[]{:S(2)}) collective-permute-start(bf16[256,256]{1,0:T(8,128)(2,1)S(1)} %get-tuple-element.46), channel_id=1, source_target_pairs={{0,16},{8,24},{16,0},{24,8},{1,17},{9,25},{17,1},{25,9},{2,18},{10... | collective-permute-start | bytes 393224 | tf_op jit(solution)/shard_map/ppermute | solution.py:193
  65.7 7.4 %collective-permute-start.21 = (bf16[256,256]{1,0:T(8,128)(2,1)S(1)}, bf16[256,256]{1,0:T(8,128)(2,1)S(1)}, u32[]{:S(2)}, u32[]{:S(2)}) collective-permute-start(bf16[256,256]{1,0:T(8,128)(2,1)S(1)} %get-tuple-element.47), channel_id=1, source_target_pairs={{0,24},{8,16},{16,8},{24,0},{1,25},{9,17},{17,9},{25,1},{2,26},{10... | collective-permute-start | bytes 393224 | tf_op jit(solution)/shard_map/ppermute | solution.py:193
  (5 other events, 28.4 us)

commit v3 on v2

--- a/solution.py
+++ b/solution.py
@@ -21,9 +21,9 @@
     return [pl.BlockSpec(memory_space=pltpu.SMEM)] * count
 
 
-def call(body, name, outs, args, n_smem=0, scratch=(), limit=24, flops=1e6, final=()):
+def call(body, name, outs, args, n_smem=0, anywhere=(), scratch=(), limit=8, flops=1e6, final=()):
     kept = [
-        x if i < n_smem or not fits(x.shape, x.dtype) else pltpu.with_memory_space_constraint(x, pltpu.VMEM)
+        x if i < n_smem or i in anywhere or not fits(x.shape, x.dtype) else pltpu.with_memory_space_constraint(x, pltpu.VMEM)
         for i, x in enumerate(args)
     ]
     shapes = [
@@ -35,7 +35,8 @@
     return pl.pallas_call(
         body,
         out_shape=shapes,
-        in_specs=smem(n_smem) + [vmem] * (len(args) - n_smem),
+        in_specs=smem(n_smem)
+        + [pl.BlockSpec(memory_space=pl.ANY) if i in anywhere else vmem for i in range(n_smem, len(args))],
         out_specs=[vmem] * len(outs),
         scratch_shapes=scratch,
         compiler_params=pltpu.CompilerParams(vmem_limit_bytes=(48 if large else limit) << 20),
@@ -64,66 +65,58 @@
     return bits.reshape(groups * 8, tile).astype(jnp.float32).astype(jnp.bfloat16)
 
 
-def build_forward(blocks, meta, meta2, patterns, patterns2, st_ref):
+def build_kernel(blocks, n_z, tiles, count, patterns, st_ref, held, sem):
     my_row = lax.axis_index("row")
     my_col = lax.axis_index("col")
     my_z, core = my_col // 2, my_col % 2
     tile = patterns.shape[-1]
-    half = st_ref.shape[0] // 2
+    copy = pltpu.make_async_copy(patterns, held, sem)
+    copy.start()
     clear(st_ref)
-
-    def add(meta_ref, patterns_ref, first):
-        def step(t, _):
-            a, b = meta_ref[0, t], meta_ref[1, t]
-            dest = a // blocks
-
-            @pl.when(dest % 2 == core)
-            def _():
-                i0 = (((dest // 2) ^ my_z) * blocks + a % blocks) * tile
-                k0 = first + (((b // blocks) ^ my_row) * blocks + b % blocks) * tile
-                st_ref[pl.ds(pl.multiple_of(k0, tile), tile), pl.ds(pl.multiple_of(i0, tile), tile)] = unpack_tile(
-                    patterns_ref[t]
-                )
-
-            return 0
-
-        return step
-
-    lax.fori_loop(0, meta[2, 0], add(meta, patterns, 0), 0)
-    lax.fori_loop(0, meta2[2, 0], add(meta2, patterns2, half), 0)
-
-
-def build_backward(blocks, n_z, meta, patterns, st_ref):
-    my_row = lax.axis_index("row")
-    my_col = lax.axis_index("col")
-    my_z, core = my_col // 2, my_col % 2
-    tile = patterns.shape[-1]
-    clear(st_ref)
+    copy.wait()
 
     def step(t, _):
-        a, b = meta[0, t], meta[1, t]
+        a, b = tiles[0, t], tiles[1, t]
         dest = a // blocks
         i0 = ((((dest % 2) ^ core) * n_z + ((dest // 2) ^ my_z)) * blocks + a % blocks) * tile
         k0 = (((b // blocks) ^ my_row) * blocks + b % blocks) * tile
-        st_ref[pl.ds(pl.multiple_of(k0, tile), tile), pl.ds(pl.multiple_of(i0, tile), tile)] = unpack_tile(patterns[t])
+        st_ref[pl.ds(pl.multiple_of(k0, tile), tile), pl.ds(pl.multiple_of(i0, tile), tile)] = unpack_tile(held[t])
         return 0
 
-    lax.fori_loop(0, meta[2, 0], step, 0)
-
-
-def forward_kernel(n_feats, n_z, *refs):
-    st_ref, feats, outs, feats_t = refs[0], refs[1 : 1 + n_feats], refs[1 + n_feats : 1 + n_feats + n_z], refs[-1]
+    lax.fori_loop(0, count[0, 0], step, 0)
+
+
+def forward_block(feats_t, st_ref, first, rows, width):
+    line = lax.broadcasted_iota(jnp.int32, (pad_rows, rows), 0)
+    product = jnp.dot(feats_t[...], st_ref[:, first : first + rows], preferred_element_type=f32)
+    degree = product[width:]
+    high = jnp.floor(degree * (1.0 / 64.0)) * 64.0
+    return product[:width].astype(bf16), jnp.where(line == 0, high, jnp.where(line == 1, degree - high, 0.0)).astype(bf16)
+
+
+def forward_other(n_row, n_z, *refs):
+    st_ref, feats, out, feats_t = refs[0], refs[1 : 1 + n_row], refs[-2], refs[-1]
     rows, width = feats[0].shape
     for i, ref in enumerate(feats):
         feats_t[:width, i * rows : (i + 1) * rows] = ref[...].T
     feats_t[width:, :] = jnp.ones((pad_rows, feats_t.shape[1]), bf16)
-    line = lax.broadcasted_iota(jnp.int32, (pad_rows, rows), 0)
+    for j in range(n_z):
+        sums, degree = forward_block(feats_t, st_ref, (n_z + j) * rows, rows, width)
+        out[j, :width, :] = sums
+        out[j, width:, :] = degree
+
+
+def forward_own(n_z, st_ref, feats_t, out):
+    width, rows = out.shape[1] - pad_rows, out.shape[2]
+    for j in range(n_z):
+        sums, degree = forward_block(feats_t, st_ref, j * rows, rows, width)
+        out[j, :width, :] = sums
+        out[j, width:, :] = degree
+
+
+def pair_kernel(own, other, *outs):
     for j, out in enumerate(outs):
-        product = jnp.dot(feats_t[...], st_ref[:, j * rows : (j + 1) * rows], preferred_element_type=f32)
-        out[:width, :] = product[:width].astype(bf16)
-        degree = product[width:]
-        high = jnp.floor(degree * (1.0 / 64.0)) * 64.0
-        out[width:, :] = jnp.where(line == 0, high, jnp.where(line == 1, degree - high, 0.0)).astype(bf16)
+        out[...] = (own[j].astype(f32) + other[j].astype(f32)).astype(bf16)
 
 
 def dense_kernel(n_z, *refs):
@@ -188,6 +181,7 @@
     row_len = n_z * rows
     col_len = n_row * rows
     flops = 4 * width * col_len * row_len
+    high = width + pad_rows
 
     def over_row(x, k):
         return lax.ppermute(x, "row", [(i, i ^ k) for i in range(n_row)])
@@ -198,51 +192,40 @@
     def over_core(x):
         return lax.ppermute(x, "col", [(i, i ^ 1) for i in range(n_col)])
 
-    patterns = patterns[0, 0]
-    meta = jnp.concatenate([tiles[0, 0], jnp.broadcast_to(tile_count, (1, slots))], axis=0)
-    patterns2, meta2 = over_core(patterns), over_core(meta)
     feats = [features] + [over_row(features, k) for k in range(1, n_row)]
-
-    (st_forward,) = call(
-        functools.partial(build_forward, blocks),
-        "build_forward",
-        [((2 * col_len, row_len), bf16)],
-        [meta, meta2, patterns, patterns2],
+    (st,) = call(
+        functools.partial(build_kernel, blocks, n_z),
+        "build",
+        [((col_len, 2 * row_len), bf16)],
+        [tiles[0, 0], tile_count, patterns[0, 0]],
         n_smem=2,
-        flops=2e9,
-    )
-    feats, st_forward = lax.optimization_barrier((feats, st_forward))
-    feats = feats + [over_core(x) for x in feats]
-
-    parts = call(
-        functools.partial(forward_kernel, len(feats), n_z),
-        "forward",
-        [((width + pad_rows, rows), bf16)] * n_z,
-        [st_forward] + feats,
-        scratch=[pltpu.VMEM((width + pad_rows, 2 * col_len), bf16)],
-        flops=flops,
-    )
-    travelling = [over_z(parts[k], k) for k in range(1, n_z)]
-    (st_backward,) = call(
-        functools.partial(build_backward, blocks, n_z),
-        "build_backward",
-        [((col_len, 2 * row_len), bf16)],
-        [meta, patterns],
-        n_smem=1,
-        flops=2e9,
-    )
-    own, travelling, st_backward = lax.optimization_barrier((parts[0], travelling, st_backward))
+        anywhere=(2,),
+        scratch=[pltpu.VMEM((slots, words, tile), jnp.int32), pltpu.SemaphoreType.DMA],
+        flops=4e9,
+    )
+
+    sent, feats_t = call(
+        functools.partial(forward_other, n_row, n_z),
+        "forward_other",
+        [((n_z, high, rows), bf16), ((high, col_len), bf16)],
+        [st] + feats,
+        flops=flops // 2,
+    )
+    (own,) = call(
+        functools.partial(forward_own, n_z), "forward_own", [((n_z, high, rows), bf16)], [st, feats_t], flops=flops // 2
+    )
+    parts = call(pair_kernel, "pair_sum", [((high, rows), bf16)] * n_z, [own, over_core(sent)])
+    parts = [parts[0]] + [over_z(parts[k], k) for k in range(1, n_z)]
 
     activated, scaled, grad_agg, agg_t, grad_pre = call(
         functools.partial(dense_kernel, n_z),
         "dense",
         [((rows, width), bf16), ((rows, width), bf16), ((rows, width), f32), ((width, rows), bf16), ((rows, width), bf16)],
-        [own] + travelling + [features, cotangent, weight],
+        parts + [features, cotangent, weight],
         flops=4 * rows * width * width,
         final=(0,),
     )
-    grads = [scaled] + [over_z(scaled, k) for k in range(1, n_z)]
-    grads = grads + [over_core(x) for x in grads]
+    far = {k: over_z(scaled, k) for k in range(2, n_z)}
 
     keep, send = call(
         weight_kernel,
@@ -252,19 +235,24 @@
         flops=2e9,
     )
     half = (keep.astype(f32) + over_core(send).astype(f32)).astype(bf16)
+    near, half = lax.optimization_barrier((scaled, half))
+    grads = [scaled, over_z(near, 1)] + [far[k] for k in range(2, n_z)]
+    grads = grads + [over_core(x) for x in grads]
     half = tree_sum([half] + [over_row(half, k) for k in range(1, n_row)]).astype(bf16)
-    half = tree_sum([half] + [over_z(half, k) for k in range(1, n_z)])
-    other = over_core(half)
-    grad_weight = jnp.concatenate([jnp.where(core == 0, half, other), jnp.where(core == 0, other, half)], axis=0)
 
     backs = call(
         functools.partial(backward_kernel, len(grads), n_row),
         "backward",
         [((rows, width), bf16)] * n_row,
-        [st_backward] + grads,
+        [st] + grads,
         scratch=[pltpu.VMEM((2 * row_len, width), bf16)],
         flops=flops,
     )
+    backs, half = lax.optimization_barrier((backs, half))
+    half = tree_sum([half] + [over_z(half, k) for k in range(1, n_z)])
+    other = over_core(half)
+    grad_weight = jnp.concatenate([jnp.where(core == 0, half, other), jnp.where(core == 0, other, half)], axis=0)
+
     backs = [backs[0]] + [over_row(backs[k], k) for k in range(1, n_row)]
     grad_features = (tree_sum(backs) + grad_agg).astype(bf16)
     return activated, grad_features, grad_weight

time: 74 us -> 65.1 us (0.88)
  starting transfers between devices: 34.6 us -> 26.7 us
  waiting for transfers between devices: 22.1 us -> 27.9 us
  local copies, waits for them, and re-layouts: 5.9 us -> 1.73 us
  Pallas kernels: 8.27 us -> 5.51 us
    ppermute x9, waiting for transfers between devices: 11.2 us -> 17.8 us  [over_z(): return lax.ppermute(x, 'col', [(i, i ^ 2 * k) for i in range(n_col)])]
    ppermute x9, starting transfers between devices: 20.2 us -> 13.9 us  [over_z(): return lax.ppermute(x, 'col', [(i, i ^ 2 * k) for i in range(n_col)])]
    unnamed x14 -> x10, local copies, waits for them, and re-layouts: 5.22 us -> 1.73 us
    pallas_call x6 -> x7, Pallas kernels: 8.27 us -> 5.51 us  [call(): pl.pallas_call(body, out_shape=shapes, in_specs=smem(n_smem) + [pl.BlockS...]
    ppermute x12 -> x7, waiting for transfers between devices: 3 us -> 1.21 us  [over_core(): return lax.ppermute(x, 'col', [(i, i ^ 1) for i in range(n_col)])]
    ppermute x12 -> x7, starting transfers between devices: 2.82 us -> 1.23 us  [over_core(): return lax.ppermute(x, 'col', [(i, i ^ 1) for i in range(n_col)])]
    ppermute x9, waiting for transfers between devices: 7.91 us -> 8.92 us  [over_row(): return lax.ppermute(x, 'row', [(i, i ^ k) for i in range(n_row)])]
  transfers between devices with their start and end apart: 30 -> 25, of which waited for: 14 -> 10; matrix products, arithmetic and copies ran while one was open for 2% -> 1% of each run, Pallas kernels for 8% -> 3%
where the time goes in v3:
time: 65.1 us; the launch traced here: 64.9 us
  waiting for transfers between devices  27.9 us (43%)
  starting transfers between devices  26.7 us (41%)
  Pallas kernels  5.51 us (8%)
  local copies, waits for them, and re-layouts  1.73 us (3%)
  other arithmetic  1.57 us (2%)
  between operations  1.47 us (2%)
    ppermute x9, waiting for transfers between devices, over_z(): return lax.ppermute(x, 'col', [(i, i ^ 2 * k) for i in range(n_col)])  17.8 us
    ppermute x9, starting transfers between devices, over_z(): return lax.ppermute(x, 'col', [(i, i ^ 2 * k) for i in range(n_col)])  13.9 us
    ppermute x9, starting transfers between devices, over_row(): return lax.ppermute(x, 'row', [(i, i ^ k) for i in range(n_row)])  11.6 us
    ppermute x9, waiting for transfers between devices, over_row(): return lax.ppermute(x, 'row', [(i, i ^ k) for i in range(n_row)])  8.92 us
    pallas_call x7, Pallas kernels, call(): pl.pallas_call(body, out_shape=shapes, in_specs=smem(n_smem) + [pl.BlockS...  5.51 us
    unnamed x10, local copies, waits for them, and re-layouts  1.73 us
  transfers between devices with their start and end apart: 25, of which 10 were waited for; matrix products, arithmetic and copies ran while one was open for 1% of the time, Pallas kernels for 3%

profile of v3, /device:TPU:0, one launch (start us, length us, event | category | flops | bytes accessed | tf_op | source)
XLA Modules:
  0.0 64.9 jit_solution(7229532241747936282)
XLA Ops:
  0.6 3.0 %collective-permute-start = (bf16[256,256]{1,0:T(8,128)(2,1)}, bf16[256,256]{1,0:T(8,128)(2,1)S(1)}, u32[]{:S(2)}, u32[]{:S(2)}) collective-permute-start(bf16[256,256]{1,0:T(8,128)(2,1)} %refs_4_.1), channel_id=1, source_target_pairs={{0,8},{8,0},{16,24},{24,16},{1,9},{9,1},{17,25},{25,17},{2,10},{10... | collective-permute-start | bytes 393224 | tf_op jit(solution)/shard_map/ppermute | solution.py:187
  3.6 1.5 %collective-permute-start.1 = (bf16[256,256]{1,0:T(8,128)(2,1)}, bf16[256,256]{1,0:T(8,128)(2,1)S(1)}, u32[]{:S(2)}, u32[]{:S(2)}) collective-permute-start(bf16[256,256]{1,0:T(8,128)(2,1)} %refs_4_.1), channel_id=1, source_target_pairs={{0,16},{8,24},{16,0},{24,8},{1,17},{9,25},{17,1},{25,9},{2,18},{10... | collective-permute-start | bytes 393224 | tf_op jit(solution)/shard_map/ppermute | solution.py:187
  5.8 1.0 %copy-done.3 = s32[1,1,64,16,128]{4,3,2,1,0:T(8,128)S(1)} copy-done((s32[1,1,64,16,128]{4,3,2,1,0:T(8,128)S(1)}, s32[1,1,64,16,128]{4,3,2,1,0:T(8,128)}, u32[]{:S(2)}) %copy-start.3) | copy-done | bytes 524312
  6.9 0.7 %copy-done.4 = s32[1,1,2,64]{3,2,1,0:T(2,128)S(1)} copy-done((s32[1,1,2,64]{3,2,1,0:T(2,128)S(1)}, s32[1,1,2,64]{3,2,1,0:T(2,128)}, u32[]{:S(2)}) %copy-start.4) | copy-done | bytes 536
  7.6 1.4 %build.1.refs_0_.st_ref = bf16[1024,2048]{1,0:T(8,128)(2,1)S(1)} custom-call(s32[2,64]{1,0:T(2,128)S(1)} %bitcast.3, s32[1,1]{1,0:T(1,128)S(6)} %copy.9.count, s32[64,16,128]{2,1,0:T(8,128)S(1)} %bitcast.2), custom_call_target="tpu_custom_call" | custom-call | flops 4000000000 | bytes 1048576 | tf_op jit(solution)/shard_map/build/pallas_call | solution.py:35
  9.0 2.6 %collective-permute-done.1.refs_3_ = bf16[256,256]{1,0:T(8,128)(2,1)S(1)} collective-permute-done((bf16[256,256]{1,0:T(8,128)(2,1)}, bf16[256,256]{1,0:T(8,128)(2,1)S(1)}, u32[]{:S(2)}, u32[]{:S(2)}) %collective-permute-start.1) | collective-permute-done | bytes 131104 | tf_op jit(solution)/shard_map/ppermute | solution.py:187
  11.6 0.8 %forward_other.1 = (bf16[4,272,256]{2,1,0:T(8,128)(2,1)S(1)}, bf16[272,1024]{1,0:T(8,128)(2,1)S(1)}) custom-call(bf16[1024,2048]{1,0:T(8,128)(2,1)S(1)} %build.1.refs_0_.st_ref, bf16[256,256]{1,0:T(8,128)(2,1)S(1)} %copy-done, bf16[256,256]{1,0:T(8,128)(2,1)S(1)} %collective-permute-done.refs_2_, bf16[256,256]{1,0:T(8,128)(2,1)S(1)} %collective-permute-done.1.refs_3_, ...), custom_call_target="tpu_custom_call" | custom-call | flops 536870912 | bytes 1048576 | tf_op jit(solution)/shard_map/forward_other/pallas_call | solution.py:35
  12.5 0.7 %forward_own.1.own = bf16[4,272,256]{2,1,0:T(8,128)(2,1)S(1)} custom-call(bf16[1024,2048]{1,0:T(8,128)(2,1)S(1)} %build.1.refs_0_.st_ref, bf16[272,1024]{1,0:T(8,128)(2,1)S(1)} %get-tuple-element.27.feats_t), custom_call_target="tpu_custom_call" | custom-call | flops 536870912 | bytes 1048576 | tf_op jit(solution)/shard_map/forward_own/pallas_call | solution.py:35
  13.3 1.2 %collective-permute-done.3.other = bf16[4,272,256]{2,1,0:T(8,128)(2,1)S(1)} collective-permute-done((bf16[4,272,256]{2,1,0:T(8,128)(2,1)S(1)}, bf16[4,272,256]{2,1,0:T(8,128)(2,1)S(1)}, u32[]{:S(2)}, u32[]{:S(2)}) %collective-permute-start.3) | collective-permute-done | bytes 557088 | tf_op jit(solution)/shard_map/ppermute | solution.py:193
  14.6 1.6 %collective-permute-start.4 = (bf16[272,256]{1,0:T(8,128)(2,1)S(1)}, bf16[272,256]{1,0:T(8,128)(2,1)S(1)}, u32[]{:S(2)}, u32[]{:S(2)}) collective-permute-start(bf16[272,256]{1,0:T(8,128)(2,1)S(1)} %get-tuple-element.30), channel_id=1, source_target_pairs={{0,2},{1,3},{2,0},{3,1},{4,6},{5,7},{6,4},{7,5},{8,10},{9,11},{10,... | collective-permute-start | bytes 417800 | tf_op jit(solution)/shard_map/ppermute | solution.py:190
  16.2 2.6 %collective-permute-start.5 = (bf16[272,256]{1,0:T(8,128)(2,1)S(1)}, bf16[272,256]{1,0:T(8,128)(2,1)S(1)}, u32[]{:S(2)}, u32[]{:S(2)}) collective-permute-start(bf16[272,256]{1,0:T(8,128)(2,1)S(1)} %get-tuple-element.31), channel_id=1, source_target_pairs={{0,4},{1,5},{2,6},{3,7},{4,0},{5,1},{6,2},{7,3},{8,12},{9,13},{10,... | collective-permute-start | bytes 417800 | tf_op jit(solution)/shard_map/ppermute | solution.py:190
  19.0 3.5 %collective-permute-done.4.refs_1_ = bf16[272,256]{1,0:T(8,128)(2,1)S(1)} collective-permute-done((bf16[272,256]{1,0:T(8,128)(2,1)S(1)}, bf16[272,256]{1,0:T(8,128)(2,1)S(1)}, u32[]{:S(2)}, u32[]{:S(2)}) %collective-permute-start.4) | collective-permute-done | bytes 139296 | tf_op jit(solution)/shard_map/ppermute | solution.py:190
  22.5 7.1 %collective-permute-done.5.refs_2_ = bf16[272,256]{1,0:T(8,128)(2,1)S(1)} collective-permute-done((bf16[272,256]{1,0:T(8,128)(2,1)S(1)}, bf16[272,256]{1,0:T(8,128)(2,1)S(1)}, u32[]{:S(2)}, u32[]{:S(2)}) %collective-permute-start.5) | collective-permute-done | bytes 139296 | tf_op jit(solution)/shard_map/ppermute | solution.py:190
  29.7 1.0 %dense.1 = (bf16[256,256]{1,0:T(8,128)(2,1)}, bf16[256,256]{1,0:T(8,128)(2,1)S(1)}, f32[256,256]{1,0:T(8,128)S(1)}, bf16[256,256]{1,0:T(8,128)(2,1)S(1)}, bf16[256,256]{1,0:T(8,128)(2,1)S(1)}) custom-call(bf16[272,256]{1,0:T(8,128)(2,1)S(1)} %get-tuple-element.29.refs_0_, bf16[272,256]{1,0:T(8,128)(2,1)S(1)} %collective-permute-done.4.refs_1_, ...), custom_call_target="tpu_custom_call" | custom-call | flops 67108864 | bytes 1048576 | tf_op jit(solution)/shard_map/dense/pallas_call | solution.py:35
  31.0 3.5 %collective-permute-start.9 = (bf16[256,256]{1,0:T(8,128)(2,1)S(1)}, bf16[256,256]{1,0:T(8,128)(2,1)S(1)}, u32[]{:S(2)}, u32[]{:S(2)}) collective-permute-start(bf16[256,256]{1,0:T(8,128)(2,1)S(1)} %get-tuple-element.39.refs_1_), channel_id=1, source_target_pairs={{0,4},{1,5},{2,6},{3,7},{4,0},{5,1},{6,2},{7,3},{8,12},{9,13},{10,... | collective-permute-start | bytes 393224 | tf_op jit(solution)/shard_map/ppermute | solution.py:190
  34.5 1.3 %collective-permute-start.10 = (bf16[256,256]{1,0:T(8,128)(2,1)S(1)}, bf16[256,256]{1,0:T(8,128)(2,1)S(1)}, u32[]{:S(2)}, u32[]{:S(2)}) collective-permute-start(bf16[256,256]{1,0:T(8,128)(2,1)S(1)} %get-tuple-element.39.refs_1_), channel_id=1, source_target_pairs={{0,6},{1,7},{2,4},{3,5},{4,2},{5,3},{6,0},{7,1},{8,14},{9,15},{10,... | collective-permute-start | bytes 393224 | tf_op jit(solution)/shard_map/ppermute | solution.py:190
  36.0 1.3 %collective-permute-start.15 = (bf16[128,256]{1,0:T(8,128)(2,1)S(1)}, bf16[128,256]{1,0:T(8,128)(2,1)S(1)}, u32[]{:S(2)}, u32[]{:S(2)}) collective-permute-start(bf16[128,256]{1,0:T(8,128)(2,1)S(1)} %add_convert_fusion.2), channel_id=1, source_target_pairs={{0,8},{8,0},{16,24},{24,16},{1,9},{9,1},{17,25},{25,17},{2,10},{10... | collective-permute-start | bytes 196616 | tf_op jit(solution)/shard_map/ppermute | solution.py:187
  37.2 0.8 %collective-permute-start.16 = (bf16[128,256]{1,0:T(8,128)(2,1)S(1)}, bf16[128,256]{1,0:T(8,128)(2,1)S(1)}, u32[]{:S(2)}, u32[]{:S(2)}) collective-permute-start(bf16[128,256]{1,0:T(8,128)(2,1)S(1)} %add_convert_fusion.2), channel_id=1, source_target_pairs={{0,16},{8,24},{16,0},{24,8},{1,17},{9,25},{17,1},{25,9},{2,18},{10... | collective-permute-start | bytes 196616 | tf_op jit(solution)/shard_map/ppermute | solution.py:187
  38.1 6.4 %collective-permute-done.9.refs_3_ = bf16[256,256]{1,0:T(8,128)(2,1)S(1)} collective-permute-done((bf16[256,256]{1,0:T(8,128)(2,1)S(1)}, bf16[256,256]{1,0:T(8,128)(2,1)S(1)}, u32[]{:S(2)}, u32[]{:S(2)}) %collective-permute-start.9) | collective-permute-done | bytes 131104 | tf_op jit(solution)/shard_map/ppermute | solution.py:190
  44.5 1.5 %collective-permute-start.17 = (bf16[128,256]{1,0:T(8,128)(2,1)S(1)}, bf16[128,256]{1,0:T(8,128)(2,1)S(1)}, u32[]{:S(2)}, u32[]{:S(2)}) collective-permute-start(bf16[128,256]{1,0:T(8,128)(2,1)S(1)} %add_convert_fusion.2), channel_id=1, source_target_pairs={{0,24},{8,16},{16,8},{24,0},{1,25},{9,17},{17,9},{25,1},{2,26},{10... | collective-permute-start | bytes 196616 | tf_op jit(solution)/shard_map/ppermute | solution.py:187
  47.0 2.6 %collective-permute-done.17 = bf16[128,256]{1,0:T(8,128)(2,1)S(1)} collective-permute-done((bf16[128,256]{1,0:T(8,128)(2,1)S(1)}, bf16[128,256]{1,0:T(8,128)(2,1)S(1)}, u32[]{:S(2)}, u32[]{:S(2)}) %collective-permute-start.17) | collective-permute-done | bytes 65568 | tf_op jit(solution)/shard_map/ppermute | solution.py:187
  49.8 1.3 %backward.1 = (bf16[256,256]{1,0:T(8,128)(2,1)S(1)}, bf16[256,256]{1,0:T(8,128)(2,1)S(1)}, bf16[256,256]{1,0:T(8,128)(2,1)S(1)}, bf16[256,256]{1,0:T(8,128)(2,1)S(1)}) custom-call(bf16[1024,2048]{1,0:T(8,128)(2,1)S(1)} %build.1.refs_0_.st_ref, bf16[256,256]{1,0:T(8,128)(2,1)S(1)} %get-tuple-element.39.refs_1_, ...), custom_call_target="tpu_custom_call" | custom-call | flops 1073741824 | bytes 1048576 | tf_op jit(solution)/shard_map/backward/pallas_call | solution.py:35
  51.1 2.4 %collective-permute-start.22 = (bf16[128,256]{1,0:T(8,128)(2,1)S(1)}, bf16[128,256]{1,0:T(8,128)(2,1)S(1)}, u32[]{:S(2)}, u32[]{:S(2)}) collective-permute-start(bf16[128,256]{1,0:T(8,128)(2,1)S(1)} %add_convert_fusion.1), channel_id=1, source_target_pairs={{0,4},{1,5},{2,6},{3,7},{4,0},{5,1},{6,2},{7,3},{8,12},{9,13},{10,... | collective-permute-start | bytes 196616 | tf_op jit(solution)/shard_map/ppermute | solution.py:190
  53.5 2.0 %collective-permute-start.23 = (bf16[128,256]{1,0:T(8,128)(2,1)S(1)}, bf16[128,256]{1,0:T(8,128)(2,1)S(1)}, u32[]{:S(2)}, u32[]{:S(2)}) collective-permute-start(bf16[128,256]{1,0:T(8,128)(2,1)S(1)} %add_convert_fusion.1), channel_id=1, source_target_pairs={{0,6},{1,7},{2,4},{3,5},{4,2},{5,3},{6,0},{7,1},{8,14},{9,15},{10,... | collective-permute-start | bytes 196616 | tf_op jit(solution)/shard_map/ppermute | solution.py:190
  55.5 1.2 %collective-permute-start.18 = (bf16[256,256]{1,0:T(8,128)(2,1)S(1)}, bf16[256,256]{1,0:T(8,128)(2,1)S(1)}, u32[]{:S(2)}, u32[]{:S(2)}) collective-permute-start(bf16[256,256]{1,0:T(8,128)(2,1)S(1)} %get-tuple-element.46), channel_id=1, source_target_pairs={{0,8},{8,0},{16,24},{24,16},{1,9},{9,1},{17,25},{25,17},{2,10},{10... | collective-permute-start | bytes 393224 | tf_op jit(solution)/shard_map/ppermute | solution.py:187
  56.7 0.8 %collective-permute-start.19 = (bf16[256,256]{1,0:T(8,128)(2,1)S(1)}, bf16[256,256]{1,0:T(8,128)(2,1)S(1)}, u32[]{:S(2)}, u32[]{:S(2)}) collective-permute-start(bf16[256,256]{1,0:T(8,128)(2,1)S(1)} %get-tuple-element.47), channel_id=1, source_target_pairs={{0,16},{8,24},{16,0},{24,8},{1,17},{9,25},{17,1},{25,9},{2,18},{10... | collective-permute-start | bytes 393224 | tf_op jit(solution)/shard_map/ppermute | solution.py:187
  57.5 1.4 %collective-permute-start.20 = (bf16[256,256]{1,0:T(8,128)(2,1)S(1)}, bf16[256,256]{1,0:T(8,128)(2,1)S(1)}, u32[]{:S(2)}, u32[]{:S(2)}) collective-permute-start(bf16[256,256]{1,0:T(8,128)(2,1)S(1)} %get-tuple-element.48), channel_id=1, source_target_pairs={{0,24},{8,16},{16,8},{24,0},{1,25},{9,17},{17,9},{25,1},{2,26},{10... | collective-permute-start | bytes 393224 | tf_op jit(solution)/shard_map/ppermute | solution.py:187
  59.0 0.7 %collective-permute-done.23 = bf16[128,256]{1,0:T(8,128)(2,1)S(1)} collective-permute-done((bf16[128,256]{1,0:T(8,128)(2,1)S(1)}, bf16[128,256]{1,0:T(8,128)(2,1)S(1)}, u32[]{:S(2)}, u32[]{:S(2)}) %collective-permute-start.23) | collective-permute-done | bytes 65568 | tf_op jit(solution)/shard_map/ppermute | solution.py:190
  59.8 1.3 %collective-permute-done.18 = bf16[256,256]{1,0:T(8,128)(2,1)S(1)} collective-permute-done((bf16[256,256]{1,0:T(8,128)(2,1)S(1)}, bf16[256,256]{1,0:T(8,128)(2,1)S(1)}, u32[]{:S(2)}, u32[]{:S(2)}) %collective-permute-start.18) | collective-permute-done | bytes 131104 | tf_op jit(solution)/shard_map/ppermute | solution.py:187
  61.7 1.7 %collective-permute-done.20 = bf16[256,256]{1,0:T(8,128)(2,1)S(1)} collective-permute-done((bf16[256,256]{1,0:T(8,128)(2,1)S(1)}, bf16[256,256]{1,0:T(8,128)(2,1)S(1)}, u32[]{:S(2)}, u32[]{:S(2)}) %collective-permute-start.20) | collective-permute-done | bytes 131104 | tf_op jit(solution)/shard_map/ppermute | solution.py:187
  63.4 0.7 %add_convert_fusion = bf16[256,256]{1,0:T(8,128)(2,1)} fusion(f32[256,256]{1,0:T(8,128)S(1)} %get-tuple-element.49, bf16[256,256]{1,0:T(8,128)(2,1)S(1)} %collective-permute-done.20, bf16[256,256]{1,0:T(8,128)(2,1)S(1)} %collective-permute-done.19, bf16[256,256]{1,0:T(8,128)(2,1)S(1)} %collective-permute-done.18, bf16[256,256]{1,0:T(8,128)(2,1)S(1)} %get-tuple-element.45), kind=kLoop, calls=%fused_computation.1 | loop fusion | flops 589824 | bytes 917504 | tf_op jit(solution)/shard_map/convert_element_type | solution.py:257
  64.2 0.7 %pad_maximum_fusion = f32[256,256]{1,0:T(8,128)} fusion(f32[128,256]{1,0:T(8,128)S(1)} %get-tuple-element.52, f32[128,256]{1,0:T(8,128)S(1)} %get-tuple-element.51), kind=kLoop, calls=%fused_computation | loop fusion | flops 65536 | bytes 524288 | tf_op jit(solution)/shard_map/concatenate | solution.py:254
  (41 shorter events, 2.7 us)
Async XLA Ops:
  0.6 8.3 %collective-permute-start = (bf16[256,256]{1,0:T(8,128)(2,1)}, bf16[256,256]{1,0:T(8,128)(2,1)S(1)}, u32[]{:S(2)}, u32[]{:S(2)}) collective-permute-start(bf16[256,256]{1,0:T(8,128)(2,1)} %refs_4_.1), channel_id=1, source_target_pairs={{0,8},{8,0},{16,24},{24,16},{1,9},{9,1},{17,25},{25,17},{2,10},{10... | collective-permute-start | bytes 393224 | tf_op jit(solution)/shard_map/ppermute | solution.py:187
  3.6 8.0 %collective-permute-start.1 = (bf16[256,256]{1,0:T(8,128)(2,1)}, bf16[256,256]{1,0:T(8,128)(2,1)S(1)}, u32[]{:S(2)}, u32[]{:S(2)}) collective-permute-start(bf16[256,256]{1,0:T(8,128)(2,1)} %refs_4_.1), channel_id=1, source_target_pairs={{0,16},{8,24},{16,0},{24,8},{1,17},{9,25},{17,1},{25,9},{2,18},{10... | collective-permute-start | bytes 393224 | tf_op jit(solution)/shard_map/ppermute | solution.py:187
  5.2 6.5 %collective-permute-start.2 = (bf16[256,256]{1,0:T(8,128)(2,1)}, bf16[256,256]{1,0:T(8,128)(2,1)S(1)}, u32[]{:S(2)}, u32[]{:S(2)}) collective-permute-start(bf16[256,256]{1,0:T(8,128)(2,1)} %refs_4_.1), channel_id=1, source_target_pairs={{0,24},{8,16},{16,8},{24,0},{1,25},{9,17},{17,9},{25,1},{2,26},{10... | collective-permute-start | bytes 393224 | tf_op jit(solution)/shard_map/ppermute | solution.py:187
  5.8 1.0 %copy-start.3 = (s32[1,1,64,16,128]{4,3,2,1,0:T(8,128)S(1)}, s32[1,1,64,16,128]{4,3,2,1,0:T(8,128)}, u32[]{:S(2)}) copy-start(s32[1,1,64,16,128]{4,3,2,1,0:T(8,128)} %param.11) | copy-start | bytes 1572868
  6.9 0.7 %copy-start.4 = (s32[1,1,2,64]{3,2,1,0:T(2,128)S(1)}, s32[1,1,2,64]{3,2,1,0:T(2,128)}, u32[]{:S(2)}) copy-start(s32[1,1,2,64]{3,2,1,0:T(2,128)} %param.9) | copy-start | bytes 1540
  7.5 4.1 %copy-start = (bf16[256,256]{1,0:T(8,128)(2,1)S(1)}, bf16[256,256]{1,0:T(8,128)(2,1)}, u32[]{:S(2)}) copy-start(bf16[256,256]{1,0:T(8,128)(2,1)} %refs_4_.1) | copy-start | bytes 393220
  12.4 17.3 %copy-start.1 = (bf16[256,256]{1,0:T(8,128)(2,1)S(1)}, bf16[256,256]{1,0:T(8,128)(2,1)}, u32[]{:S(2)}) copy-start(bf16[256,256]{1,0:T(8,128)(2,1)} %refs_5_.1) | copy-start | bytes 393220
  12.4 17.2 %copy-start.2 = (bf16[256,256]{1,0:T(8,128)(2,1)S(1)}, bf16[256,256]{1,0:T(8,128)(2,1)}, u32[]{:S(2)}) copy-start(bf16[256,256]{1,0:T(8,128)(2,1)} %refs_6_.1) | copy-start | bytes 393220
  12.4 2.0 %collective-permute-start.3 = (bf16[4,272,256]{2,1,0:T(8,128)(2,1)S(1)}, bf16[4,272,256]{2,1,0:T(8,128)(2,1)S(1)}, u32[]{:S(2)}, u32[]{:S(2)}) collective-permute-start(bf16[4,272,256]{2,1,0:T(8,128)(2,1)S(1)} %get-tuple-element.28), channel_id=1, source_target_pairs={{0,1},{1,0},{2,3},{3,2},{4,5},{5,4},{6,7},{7,6},{8,9},{9,8},{10,11... | collective-permute-start | bytes 1671176 | tf_op jit(solution)/shard_map/ppermute | solution.py:193
  14.6 8.0 %collective-permute-start.4 = (bf16[272,256]{1,0:T(8,128)(2,1)S(1)}, bf16[272,256]{1,0:T(8,128)(2,1)S(1)}, u32[]{:S(2)}, u32[]{:S(2)}) collective-permute-start(bf16[272,256]{1,0:T(8,128)(2,1)S(1)} %get-tuple-element.30), channel_id=1, source_target_pairs={{0,2},{1,3},{2,0},{3,1},{4,6},{5,7},{6,4},{7,5},{8,10},{9,11},{10,... | collective-permute-start | bytes 417800 | tf_op jit(solution)/shard_map/ppermute | solution.py:190
  16.2 13.4 %collective-permute-start.5 = (bf16[272,256]{1,0:T(8,128)(2,1)S(1)}, bf16[272,256]{1,0:T(8,128)(2,1)S(1)}, u32[]{:S(2)}, u32[]{:S(2)}) collective-permute-start(bf16[272,256]{1,0:T(8,128)(2,1)S(1)} %get-tuple-element.31), channel_id=1, source_target_pairs={{0,4},{1,5},{2,6},{3,7},{4,0},{5,1},{6,2},{7,3},{8,12},{9,13},{10,... | collective-permute-start | bytes 417800 | tf_op jit(solution)/shard_map/ppermute | solution.py:190
  18.8 10.8 %collective-permute-start.6 = (bf16[272,256]{1,0:T(8,128)(2,1)S(1)}, bf16[272,256]{1,0:T(8,128)(2,1)S(1)}, u32[]{:S(2)}, u32[]{:S(2)}) collective-permute-start(bf16[272,256]{1,0:T(8,128)(2,1)S(1)} %get-tuple-element.32), channel_id=1, source_target_pairs={{0,6},{1,7},{2,4},{3,5},{4,2},{5,3},{6,0},{7,1},{8,14},{9,15},{10,... | collective-permute-start | bytes 417800 | tf_op jit(solution)/shard_map/ppermute | solution.py:190
  30.9 5.0 %collective-permute-start.7 = (bf16[128,256]{1,0:T(8,128)(2,1)S(1)}, bf16[128,256]{1,0:T(8,128)(2,1)S(1)}, u32[]{:S(2)}, u32[]{:S(2)}) collective-permute-start(bf16[128,256]{1,0:T(8,128)(2,1)S(1)} %get-tuple-element.38), channel_id=1, source_target_pairs={{0,1},{1,0},{2,3},{3,2},{4,5},{5,4},{6,7},{7,6},{8,9},{9,8},{10,11... | collective-permute-start | bytes 196616 | tf_op jit(solution)/shard_map/ppermute | solution.py:193
  31.0 13.5 %collective-permute-start.9 = (bf16[256,256]{1,0:T(8,128)(2,1)S(1)}, bf16[256,256]{1,0:T(8,128)(2,1)S(1)}, u32[]{:S(2)}, u32[]{:S(2)}) collective-permute-start(bf16[256,256]{1,0:T(8,128)(2,1)S(1)} %get-tuple-element.39.refs_1_), channel_id=1, source_target_pairs={{0,4},{1,5},{2,6},{3,7},{4,0},{5,1},{6,2},{7,3},{8,12},{9,13},{10,... | collective-permute-start | bytes 393224 | tf_op jit(solution)/shard_map/ppermute | solution.py:190
  34.5 11.5 %collective-permute-start.10 = (bf16[256,256]{1,0:T(8,128)(2,1)S(1)}, bf16[256,256]{1,0:T(8,128)(2,1)S(1)}, u32[]{:S(2)}, u32[]{:S(2)}) collective-permute-start(bf16[256,256]{1,0:T(8,128)(2,1)S(1)} %get-tuple-element.39.refs_1_), channel_id=1, source_target_pairs={{0,6},{1,7},{2,4},{3,5},{4,2},{5,3},{6,0},{7,1},{8,14},{9,15},{10,... | collective-permute-start | bytes 393224 | tf_op jit(solution)/shard_map/ppermute | solution.py:190
  35.9 10.7 %collective-permute-start.8 = (bf16[256,256]{1,0:T(8,128)(2,1)S(1)}, bf16[256,256]{1,0:T(8,128)(2,1)S(1)}, u32[]{:S(2)}, u32[]{:S(2)}) collective-permute-start(bf16[256,256]{1,0:T(8,128)(2,1)S(1)} %get-tuple-element.39.refs_1_), channel_id=1, source_target_pairs={{0,2},{1,3},{2,0},{3,1},{4,6},{5,7},{6,4},{7,5},{8,10},{9,11},{10,... | collective-permute-start | bytes 393224 | tf_op jit(solution)/shard_map/ppermute | solution.py:190
  36.0 10.1 %collective-permute-start.15 = (bf16[128,256]{1,0:T(8,128)(2,1)S(1)}, bf16[128,256]{1,0:T(8,128)(2,1)S(1)}, u32[]{:S(2)}, u32[]{:S(2)}) collective-permute-start(bf16[128,256]{1,0:T(8,128)(2,1)S(1)} %add_convert_fusion.2), channel_id=1, source_target_pairs={{0,8},{8,0},{16,24},{24,16},{1,9},{9,1},{17,25},{25,17},{2,10},{10... | collective-permute-start | bytes 196616 | tf_op jit(solution)/shard_map/ppermute | solution.py:187
  37.2 9.3 %collective-permute-start.16 = (bf16[128,256]{1,0:T(8,128)(2,1)S(1)}, bf16[128,256]{1,0:T(8,128)(2,1)S(1)}, u32[]{:S(2)}, u32[]{:S(2)}) collective-permute-start(bf16[128,256]{1,0:T(8,128)(2,1)S(1)} %add_convert_fusion.2), channel_id=1, source_target_pairs={{0,16},{8,24},{16,0},{24,8},{1,17},{9,25},{17,1},{25,9},{2,18},{10... | collective-permute-start | bytes 196616 | tf_op jit(solution)/shard_map/ppermute | solution.py:187
  44.5 5.2 %collective-permute-start.17 = (bf16[128,256]{1,0:T(8,128)(2,1)S(1)}, bf16[128,256]{1,0:T(8,128)(2,1)S(1)}, u32[]{:S(2)}, u32[]{:S(2)}) collective-permute-start(bf16[128,256]{1,0:T(8,128)(2,1)S(1)} %add_convert_fusion.2), channel_id=1, source_target_pairs={{0,24},{8,16},{16,8},{24,0},{1,25},{9,17},{17,9},{25,1},{2,26},{10... | collective-permute-start | bytes 196616 | tf_op jit(solution)/shard_map/ppermute | solution.py:187
  46.0 3.7 %collective-permute-start.11 = (bf16[256,256]{1,0:T(8,128)(2,1)S(1)}, bf16[256,256]{1,0:T(8,128)(2,1)S(1)}, u32[]{:S(2)}, u32[]{:S(2)}) collective-permute-start(bf16[256,256]{1,0:T(8,128)(2,1)S(1)} %get-tuple-element.39.refs_1_), channel_id=1, source_target_pairs={{0,1},{1,0},{2,3},{3,2},{4,5},{5,4},{6,7},{7,6},{8,9},{9,8},{10,11... | collective-permute-start | bytes 393224 | tf_op jit(solution)/shard_map/ppermute | solution.py:193
  46.0 3.7 %collective-permute-start.13 = (bf16[256,256]{1,0:T(8,128)(2,1)S(1)}, bf16[256,256]{1,0:T(8,128)(2,1)S(1)}, u32[]{:S(2)}, u32[]{:S(2)}) collective-permute-start(bf16[256,256]{1,0:T(8,128)(2,1)S(1)} %collective-permute-done.9.refs_3_), channel_id=1, source_target_pairs={{0,1},{1,0},{2,3},{3,2},{4,5},{5,4},{6,7},{7,6},{8,9},{9,8},{10,11... | collective-permute-start | bytes 393224 | tf_op jit(solution)/shard_map/ppermute | solution.py:193
  46.5 3.2 %collective-permute-start.14 = (bf16[256,256]{1,0:T(8,128)(2,1)S(1)}, bf16[256,256]{1,0:T(8,128)(2,1)S(1)}, u32[]{:S(2)}, u32[]{:S(2)}) collective-permute-start(bf16[256,256]{1,0:T(8,128)(2,1)S(1)} %collective-permute-done.10.refs_4_), channel_id=1, source_target_pairs={{0,1},{1,0},{2,3},{3,2},{4,5},{5,4},{6,7},{7,6},{8,9},{9,8},{10,11... | collective-permute-start | bytes 393224 | tf_op jit(solution)/shard_map/ppermute | solution.py:193
  46.6 3.2 %collective-permute-start.12 = (bf16[256,256]{1,0:T(8,128)(2,1)S(1)}, bf16[256,256]{1,0:T(8,128)(2,1)S(1)}, u32[]{:S(2)}, u32[]{:S(2)}) collective-permute-start(bf16[256,256]{1,0:T(8,128)(2,1)S(1)} %collective-permute-done.8.refs_2_), channel_id=1, source_target_pairs={{0,1},{1,0},{2,3},{3,2},{4,5},{5,4},{6,7},{7,6},{8,9},{9,8},{10,11... | collective-permute-start | bytes 393224 | tf_op jit(solution)/shard_map/ppermute | solution.py:193
  51.0 6.5 %collective-permute-start.21 = (bf16[128,256]{1,0:T(8,128)(2,1)S(1)}, bf16[128,256]{1,0:T(8,128)(2,1)S(1)}, u32[]{:S(2)}, u32[]{:S(2)}) collective-permute-start(bf16[128,256]{1,0:T(8,128)(2,1)S(1)} %add_convert_fusion.1), channel_id=1, source_target_pairs={{0,2},{1,3},{2,0},{3,1},{4,6},{5,7},{6,4},{7,5},{8,10},{9,11},{10,... | collective-permute-start | bytes 196616 | tf_op jit(solution)/shard_map/ppermute | solution.py:190
  51.1 7.9 %collective-permute-start.22 = (bf16[128,256]{1,0:T(8,128)(2,1)S(1)}, bf16[128,256]{1,0:T(8,128)(2,1)S(1)}, u32[]{:S(2)}, u32[]{:S(2)}) collective-permute-start(bf16[128,256]{1,0:T(8,128)(2,1)S(1)} %add_convert_fusion.1), channel_id=1, source_target_pairs={{0,4},{1,5},{2,6},{3,7},{4,0},{5,1},{6,2},{7,3},{8,12},{9,13},{10,... | collective-permute-start | bytes 196616 | tf_op jit(solution)/shard_map/ppermute | solution.py:190
  53.5 6.2 %collective-permute-start.23 = (bf16[128,256]{1,0:T(8,128)(2,1)S(1)}, bf16[128,256]{1,0:T(8,128)(2,1)S(1)}, u32[]{:S(2)}, u32[]{:S(2)}) collective-permute-start(bf16[128,256]{1,0:T(8,128)(2,1)S(1)} %add_convert_fusion.1), channel_id=1, source_target_pairs={{0,6},{1,7},{2,4},{3,5},{4,2},{5,3},{6,0},{7,1},{8,14},{9,15},{10,... | collective-permute-start | bytes 196616 | tf_op jit(solution)/shard_map/ppermute | solution.py:190
  55.5 5.6 %collective-permute-start.18 = (bf16[256,256]{1,0:T(8,128)(2,1)S(1)}, bf16[256,256]{1,0:T(8,128)(2,1)S(1)}, u32[]{:S(2)}, u32[]{:S(2)}) collective-permute-start(bf16[256,256]{1,0:T(8,128)(2,1)S(1)} %get-tuple-element.46), channel_id=1, source_target_pairs={{0,8},{8,0},{16,24},{24,16},{1,9},{9,1},{17,25},{25,17},{2,10},{10... | collective-permute-start | bytes 393224 | tf_op jit(solution)/shard_map/ppermute | solution.py:187
  56.7 5.0 %collective-permute-start.19 = (bf16[256,256]{1,0:T(8,128)(2,1)S(1)}, bf16[256,256]{1,0:T(8,128)(2,1)S(1)}, u32[]{:S(2)}, u32[]{:S(2)}) collective-permute-start(bf16[256,256]{1,0:T(8,128)(2,1)S(1)} %get-tuple-element.47), channel_id=1, source_target_pairs={{0,16},{8,24},{16,0},{24,8},{1,17},{9,25},{17,1},{25,9},{2,18},{10... | collective-permute-start | bytes 393224 | tf_op jit(solution)/shard_map/ppermute | solution.py:187
  57.5 5.9 %collective-permute-start.20 = (bf16[256,256]{1,0:T(8,128)(2,1)S(1)}, bf16[256,256]{1,0:T(8,128)(2,1)S(1)}, u32[]{:S(2)}, u32[]{:S(2)}) collective-permute-start(bf16[256,256]{1,0:T(8,128)(2,1)S(1)} %get-tuple-element.48), channel_id=1, source_target_pairs={{0,24},{8,16},{16,8},{24,0},{1,25},{9,17},{17,9},{25,1},{2,26},{10... | collective-permute-start | bytes 393224 | tf_op jit(solution)/shard_map/ppermute | solution.py:187
  59.7 4.4 %collective-permute-start.24 = (f32[128,256]{1,0:T(8,128)S(1)}, f32[128,256]{1,0:T(8,128)S(1)}, u32[]{:S(2)}, u32[]{:S(2)}) collective-permute-start(f32[128,256]{1,0:T(8,128)S(1)} %add_add_fusion), channel_id=1, source_target_pairs={{0,1},{1,0},{2,3},{3,2},{4,5},{5,4},{6,7},{7,6},{8,9},{9,8},{10,11... | collective-permute-start | bytes 393224 | tf_op jit(solution)/shard_map/ppermute | solution.py:193

commit v4 on v3

--- a/solution.py
+++ b/solution.py
@@ -94,22 +94,19 @@
     return product[:width].astype(bf16), jnp.where(line == 0, high, jnp.where(line == 1, degree - high, 0.0)).astype(bf16)
 
 
-def forward_other(n_row, n_z, *refs):
+def forward_first(n_row, start, *refs):
     st_ref, feats, out, feats_t = refs[0], refs[1 : 1 + n_row], refs[-2], refs[-1]
     rows, width = feats[0].shape
     for i, ref in enumerate(feats):
         feats_t[:width, i * rows : (i + 1) * rows] = ref[...].T
     feats_t[width:, :] = jnp.ones((pad_rows, feats_t.shape[1]), bf16)
-    for j in range(n_z):
-        sums, degree = forward_block(feats_t, st_ref, (n_z + j) * rows, rows, width)
-        out[j, :width, :] = sums
-        out[j, width:, :] = degree
-
-
-def forward_own(n_z, st_ref, feats_t, out):
+    forward_more(start, st_ref, feats_t, out)
+
+
+def forward_more(start, st_ref, feats_t, out):
     width, rows = out.shape[1] - pad_rows, out.shape[2]
-    for j in range(n_z):
-        sums, degree = forward_block(feats_t, st_ref, j * rows, rows, width)
+    for j in range(out.shape[0]):
+        sums, degree = forward_block(feats_t, st_ref, (start + j) * rows, rows, width)
         out[j, :width, :] = sums
         out[j, width:, :] = degree
 
@@ -143,24 +140,32 @@
     scaled_ref[...] = (grad_agg * scale_rows).astype(bf16)
 
 
-def weight_kernel(agg_t, grad_pre, keep_ref, send_ref):
-    first = lax.axis_index("col") % 2 == 0
-    half = agg_t.shape[0] // 2
-    part = jnp.dot(agg_t[...], grad_pre[...], preferred_element_type=f32).astype(bf16)
-    keep_ref[...] = jnp.where(first, part[:half], part[half:])
-    send_ref[...] = jnp.where(first, part[half:], part[:half])
-
-
-def backward_kernel(n_grads, n_row, *refs):
-    st_ref, grads, outs = refs[0], refs[1 : 1 + n_grads], refs[1 + n_grads : 1 + n_grads + n_row]
+def weight_kernel(agg_t, grad_pre, out_ref):
+    out_ref[...] = jnp.dot(agg_t[...], grad_pre[...], preferred_element_type=f32).astype(bf16)
+
+
+def backward_near(spots, *refs):
+    st_ref, grads, out = refs[0], refs[1 : 1 + len(spots)], refs[1 + len(spots)]
+    gathered = refs[-1]
+    rows, _ = grads[0].shape
+    for i, ref in enumerate(grads):
+        gathered[i * rows : (i + 1) * rows, :] = ref[...]
+    for j in range(out.shape[0] // rows):
+        lines = slice(j * rows, (j + 1) * rows)
+        columns = jnp.concatenate([st_ref[lines, k * rows : (k + 1) * rows] for k in spots], axis=1)
+        out[lines, :] = jnp.dot(columns, gathered[...], preferred_element_type=f32)
+
+
+def backward_far(spots, n_row, *refs):
+    st_ref, near, grads, outs = refs[0], refs[1], refs[2 : 2 + len(spots)], refs[2 + len(spots) : 2 + len(spots) + n_row]
     gathered = refs[-1]
     rows, _ = grads[0].shape
     for i, ref in enumerate(grads):
         gathered[i * rows : (i + 1) * rows, :] = ref[...]
     for j, out in enumerate(outs):
-        out[...] = jnp.dot(st_ref[j * rows : (j + 1) * rows, :], gathered[...], preferred_element_type=f32).astype(
-            out.dtype
-        )
+        lines = slice(j * rows, (j + 1) * rows)
+        columns = jnp.concatenate([st_ref[lines, k * rows : (k + 1) * rows] for k in spots], axis=1)
+        out[...] = (near[lines, :] + jnp.dot(columns, gathered[...], preferred_element_type=f32)).astype(out.dtype)
 
 
 def tree_sum(values):
@@ -177,7 +182,6 @@
     n_row = lax.axis_size("row")
     n_col = lax.axis_size("col")
     n_z = n_col // 2
-    core = lax.axis_index("col") % 2
     row_len = n_z * rows
     col_len = n_row * rows
     flops = 4 * width * col_len * row_len
@@ -204,18 +208,28 @@
         flops=4e9,
     )
 
+    n_far = n_z - 2
     sent, feats_t = call(
-        functools.partial(forward_other, n_row, n_z),
-        "forward_other",
-        [((n_z, high, rows), bf16), ((high, col_len), bf16)],
+        functools.partial(forward_first, n_row, n_z + 2),
+        "forward_far_other",
+        [((n_far, high, rows), bf16), ((high, col_len), bf16)],
         [st] + feats,
-        flops=flops // 2,
-    )
-    (own,) = call(
-        functools.partial(forward_own, n_z), "forward_own", [((n_z, high, rows), bf16)], [st, feats_t], flops=flops // 2
-    )
-    parts = call(pair_kernel, "pair_sum", [((high, rows), bf16)] * n_z, [own, over_core(sent)])
-    parts = [parts[0]] + [over_z(parts[k], k) for k in range(1, n_z)]
+        flops=flops // 4,
+    )
+
+    def forward(name, start, count):
+        return call(
+            functools.partial(forward_more, start), name, [((count, high, rows), bf16)], [st, feats_t], flops=flops // 4
+        )[0]
+
+    def pair_sum(name, own, other, count):
+        return call(pair_kernel, name, [((high, rows), bf16)] * count, [own, other])
+
+    far = pair_sum("pair_far", forward("forward_far_own", 2, n_far), over_core(sent), n_far)
+    far = [over_z(x, k) for k, x in enumerate(far, 2)]
+    sent = forward("forward_near_other", n_z, 2)
+    near = pair_sum("pair_near", forward("forward_near_own", 0, 2), over_core(sent), 2)
+    parts = [near[0], over_z(near[1], 1)] + far
 
     activated, scaled, grad_agg, agg_t, grad_pre = call(
         functools.partial(dense_kernel, n_z),
@@ -225,33 +239,38 @@
         flops=4 * rows * width * width,
         final=(0,),
     )
-    far = {k: over_z(scaled, k) for k in range(2, n_z)}
-
-    keep, send = call(
-        weight_kernel,
-        "weight_part",
-        [((width // 2, width), bf16)] * 2,
-        [agg_t, grad_pre],
-        flops=2e9,
-    )
-    half = (keep.astype(f32) + over_core(send).astype(f32)).astype(bf16)
-    near, half = lax.optimization_barrier((scaled, half))
-    grads = [scaled, over_z(near, 1)] + [far[k] for k in range(2, n_z)]
+    far = [over_z(scaled, k) for k in range(2, n_z)]
+
+    (part,) = call(weight_kernel, "weight_part", [((width, width), bf16)], [agg_t, grad_pre], flops=2e9)
+    part = tree_sum([part, over_z(part, 1)]).astype(bf16)
+    part = tree_sum([part] + [over_row(part, k) for k in range(1, n_row)]).astype(bf16)
+    part = tree_sum([part, over_core(part)]).astype(bf16)
+
+    grads = [scaled, over_z(scaled, 1)]
     grads = grads + [over_core(x) for x in grads]
-    half = tree_sum([half] + [over_row(half, k) for k in range(1, n_row)]).astype(bf16)
-
+    (product,) = call(
+        functools.partial(backward_near, (0, 1, n_z, n_z + 1)),
+        "backward_near",
+        [((col_len, width), f32)],
+        [st] + grads,
+        scratch=[pltpu.VMEM((4 * rows, width), bf16)],
+        flops=flops // 2,
+    )
+    grads = far + [over_core(x) for x in far]
+    spots = tuple(range(2, n_z)) + tuple(range(n_z + 2, 2 * n_z))
     backs = call(
-        functools.partial(backward_kernel, len(grads), n_row),
-        "backward",
+        functools.partial(backward_far, spots, n_row),
+        "backward_far",
         [((rows, width), bf16)] * n_row,
-        [st] + grads,
-        scratch=[pltpu.VMEM((2 * row_len, width), bf16)],
-        flops=flops,
-    )
-    backs, half = lax.optimization_barrier((backs, half))
-    half = tree_sum([half] + [over_z(half, k) for k in range(1, n_z)])
-    other = over_core(half)
-    grad_weight = jnp.concatenate([jnp.where(core == 0, half, other), jnp.where(core == 0, other, half)], axis=0)
+        [st, product] + grads,
+        scratch=[pltpu.VMEM((len(spots) * rows, width), bf16)],
+        flops=flops // 2,
+    )
+    backs, part = lax.optimization_barrier((backs, part))
+    for step in range(1, (n_z - 1).bit_length()):
+        part = part.astype(bf16)
+        part = tree_sum([part, over_z(part, 1 << step)])
+    grad_weight = part
 
     backs = [backs[0]] + [over_row(backs[k], k) for k in range(1, n_row)]
     grad_features = (tree_sum(backs) + grad_agg).astype(bf16)

time: 65.1 us -> 63.3 us (0.972)
  waiting for transfers between devices: 27.9 us -> 22.9 us
  starting transfers between devices: 26.7 us -> 29 us
  Pallas kernels: 5.51 us -> 6.32 us
    ppermute x9, waiting for transfers between devices: 8.92 us -> 4.87 us  [over_row(): return lax.ppermute(x, 'row', [(i, i ^ k) for i in range(n_row)])]
    ppermute x7, waiting for transfers between devices: 1.21 us -> 0.12 us  [over_core(): return lax.ppermute(x, 'col', [(i, i ^ 1) for i in range(n_col)])]
    ppermute x9, starting transfers between devices: 11.6 us -> 12.7 us  [over_row(): return lax.ppermute(x, 'row', [(i, i ^ k) for i in range(n_row)])]
    ppermute x9 -> x8, starting transfers between devices: 13.9 us -> 14.7 us  [over_z(): return lax.ppermute(x, 'col', [(i, i ^ 2 * k) for i in range(n_col)])]
    pallas_call x7 -> x11, Pallas kernels: 5.51 us -> 6.32 us  [call(): pl.pallas_call(body, out_shape=shapes, in_specs=smem(n_smem) + [pl.BlockS...]
    concatenate x1 -> x0, other arithmetic: 0.72 us -> none  [per_device(): jnp.concatenate([jnp.where(core == 0, half, other), jnp.where(core == 0,...]
    add x1, other arithmetic: 0.03 us -> 0.74 us  [tree_sum(): values = [values[i] + values[i + 1] for i in range(0, len(values), 2)]]
    ppermute x9 -> x8, waiting for transfers between devices: 17.8 us -> 17.9 us  [over_z(): return lax.ppermute(x, 'col', [(i, i ^ 2 * k) for i in range(n_col)])]
  transfers between devices with their start and end apart: 25 -> 24, of which waited for: 10 -> 10; matrix products, arithmetic and copies ran while one was open for 1% -> 1% of each run, Pallas kernels for 3% -> 7%
where the time goes in v4:
time: 63.3 us; the launch traced here: 63.1 us
  starting transfers between devices  29 us (46%)
  waiting for transfers between devices  22.9 us (36%)
  Pallas kernels  6.32 us (10%)
  local copies, waits for them, and re-layouts  1.73 us (3%)
  other arithmetic  1.62 us (3%)
  between operations  1.47 us (2%)
    ppermute x8, waiting for transfers between devices, over_z(): return lax.ppermute(x, 'col', [(i, i ^ 2 * k) for i in range(n_col)])  17.9 us
    ppermute x8, starting transfers between devices, over_z(): return lax.ppermute(x, 'col', [(i, i ^ 2 * k) for i in range(n_col)])  14.7 us
    ppermute x9, starting transfers between devices, over_row(): return lax.ppermute(x, 'row', [(i, i ^ k) for i in range(n_row)])  12.7 us
    pallas_call x11, Pallas kernels, call(): pl.pallas_call(body, out_shape=shapes, in_specs=smem(n_smem) + [pl.BlockS...  6.32 us
    ppermute x9, waiting for transfers between devices, over_row(): return lax.ppermute(x, 'row', [(i, i ^ k) for i in range(n_row)])  4.87 us
    unnamed x10, local copies, waits for them, and re-layouts  1.73 us
    ppermute x7, starting transfers between devices, over_core(): return lax.ppermute(x, 'col', [(i, i ^ 1) for i in range(n_col)])  1.66 us
  transfers between devices with their start and end apart: 24, of which 10 were waited for; matrix products, arithmetic and copies ran while one was open for 1% of the time, Pallas kernels for 7%

profile of v4, /device:TPU:0, one launch (start us, length us, event | category | flops | bytes accessed | tf_op | source)
XLA Modules:
  0.0 63.1 jit_solution(10775448433315943196)
XLA Ops:
  0.6 4.0 %collective-permute-start.2 = (bf16[256,256]{1,0:T(8,128)(2,1)}, bf16[256,256]{1,0:T(8,128)(2,1)S(1)}, u32[]{:S(2)}, u32[]{:S(2)}) collective-permute-start(bf16[256,256]{1,0:T(8,128)(2,1)} %refs_4_.1), channel_id=1, source_target_pairs={{0,24},{8,16},{16,8},{24,0},{1,25},{9,17},{17,9},{25,1},{2,26},{10... | collective-permute-start | bytes 393224 | tf_op jit(solution)/shard_map/ppermute | solution.py:191
  4.6 0.5 collective-permute-start.1
  5.9 1.0 %copy-done.3 = s32[1,1,64,16,128]{4,3,2,1,0:T(8,128)S(1)} copy-done((s32[1,1,64,16,128]{4,3,2,1,0:T(8,128)S(1)}, s32[1,1,64,16,128]{4,3,2,1,0:T(8,128)}, u32[]{:S(2)}) %copy-start.3) | copy-done | bytes 524312
  6.9 0.7 %copy-done.4 = s32[1,1,2,64]{3,2,1,0:T(2,128)S(1)} copy-done((s32[1,1,2,64]{3,2,1,0:T(2,128)S(1)}, s32[1,1,2,64]{3,2,1,0:T(2,128)}, u32[]{:S(2)}) %copy-start.4) | copy-done | bytes 536
  7.6 1.7 %build.1.refs_0_.st_ref = bf16[1024,2048]{1,0:T(8,128)(2,1)S(1)} custom-call(s32[2,64]{1,0:T(2,128)S(1)} %bitcast.3, s32[1,1]{1,0:T(1,128)S(6)} %copy.9.count, s32[64,16,128]{2,1,0:T(8,128)S(1)} %bitcast.2), custom_call_target="tpu_custom_call" | custom-call | flops 4000000000 | bytes 1048576 | tf_op jit(solution)/shard_map/build/pallas_call | solution.py:35
  9.4 1.8 %collective-permute-done.1.refs_3_ = bf16[256,256]{1,0:T(8,128)(2,1)S(1)} collective-permute-done((bf16[256,256]{1,0:T(8,128)(2,1)}, bf16[256,256]{1,0:T(8,128)(2,1)S(1)}, u32[]{:S(2)}, u32[]{:S(2)}) %collective-permute-start.1) | collective-permute-done | bytes 131104 | tf_op jit(solution)/shard_map/ppermute | solution.py:191
  12.4 0.5 collective-permute-start.5
  14.0 1.6 %collective-permute-start.4 = (bf16[272,256]{1,0:T(8,128)(2,1)S(1)}, bf16[272,256]{1,0:T(8,128)(2,1)S(1)}, u32[]{:S(2)}, u32[]{:S(2)}) collective-permute-start(bf16[272,256]{1,0:T(8,128)(2,1)S(1)} %get-tuple-element.25), channel_id=1, source_target_pairs={{0,2},{1,3},{2,0},{3,1},{4,6},{5,7},{6,4},{7,5},{8,10},{9,11},{10,... | collective-permute-start | bytes 417800 | tf_op jit(solution)/shard_map/ppermute | solution.py:194
  15.7 2.7 %collective-permute-start.6 = (bf16[272,256]{1,0:T(8,128)(2,1)S(1)}, bf16[272,256]{1,0:T(8,128)(2,1)S(1)}, u32[]{:S(2)}, u32[]{:S(2)}) collective-permute-start(bf16[272,256]{1,0:T(8,128)(2,1)S(1)} %get-tuple-element.27), channel_id=1, source_target_pairs={{0,4},{1,5},{2,6},{3,7},{4,0},{5,1},{6,2},{7,3},{8,12},{9,13},{10,... | collective-permute-start | bytes 417800 | tf_op jit(solution)/shard_map/ppermute | solution.py:194
  18.6 3.3 %collective-permute-done.4.refs_1_ = bf16[272,256]{1,0:T(8,128)(2,1)S(1)} collective-permute-done((bf16[272,256]{1,0:T(8,128)(2,1)S(1)}, bf16[272,256]{1,0:T(8,128)(2,1)S(1)}, u32[]{:S(2)}, u32[]{:S(2)}) %collective-permute-start.4) | collective-permute-done | bytes 139296 | tf_op jit(solution)/shard_map/ppermute | solution.py:194
  21.9 7.3 %collective-permute-done.6.refs_2_ = bf16[272,256]{1,0:T(8,128)(2,1)S(1)} collective-permute-done((bf16[272,256]{1,0:T(8,128)(2,1)S(1)}, bf16[272,256]{1,0:T(8,128)(2,1)S(1)}, u32[]{:S(2)}, u32[]{:S(2)}) %collective-permute-start.6) | collective-permute-done | bytes 139296 | tf_op jit(solution)/shard_map/ppermute | solution.py:194
  29.2 1.0 %dense.1 = (bf16[256,256]{1,0:T(8,128)(2,1)}, bf16[256,256]{1,0:T(8,128)(2,1)S(1)}, f32[256,256]{1,0:T(8,128)S(1)}, bf16[256,256]{1,0:T(8,128)(2,1)S(1)}, bf16[256,256]{1,0:T(8,128)(2,1)S(1)}) custom-call(bf16[272,256]{1,0:T(8,128)(2,1)S(1)} %get-tuple-element.24.refs_0_, bf16[272,256]{1,0:T(8,128)(2,1)S(1)} %collective-permute-done.4.refs_1_, ...), custom_call_target="tpu_custom_call" | custom-call | flops 67108864 | bytes 1048576 | tf_op jit(solution)/shard_map/dense/pallas_call | solution.py:35
  30.4 2.5 %collective-permute-start.15 = (bf16[256,256]{1,0:T(8,128)(2,1)S(1)}, bf16[256,256]{1,0:T(8,128)(2,1)S(1)}, u32[]{:S(2)}, u32[]{:S(2)}) collective-permute-start(bf16[256,256]{1,0:T(8,128)(2,1)S(1)} %weight_part.1), channel_id=1, source_target_pairs={{0,2},{1,3},{2,0},{3,1},{4,6},{5,7},{6,4},{7,5},{8,10},{9,11},{10,... | collective-permute-start | bytes 393224 | tf_op jit(solution)/shard_map/ppermute | solution.py:194
  33.0 2.6 %collective-permute-start.12 = (bf16[256,256]{1,0:T(8,128)(2,1)S(1)}, bf16[256,256]{1,0:T(8,128)(2,1)S(1)}, u32[]{:S(2)}, u32[]{:S(2)}) collective-permute-start(bf16[256,256]{1,0:T(8,128)(2,1)S(1)} %get-tuple-element.30.refs_1_), channel_id=1, source_target_pairs={{0,6},{1,7},{2,4},{3,5},{4,2},{5,3},{6,0},{7,1},{8,14},{9,15},{10,... | collective-permute-start | bytes 393224 | tf_op jit(solution)/shard_map/ppermute | solution.py:194
  35.5 1.8 %collective-permute-start.8 = (bf16[256,256]{1,0:T(8,128)(2,1)S(1)}, bf16[256,256]{1,0:T(8,128)(2,1)S(1)}, u32[]{:S(2)}, u32[]{:S(2)}) collective-permute-start(bf16[256,256]{1,0:T(8,128)(2,1)S(1)} %get-tuple-element.30.refs_1_), channel_id=1, source_target_pairs={{0,2},{1,3},{2,0},{3,1},{4,6},{5,7},{6,4},{7,5},{8,10},{9,11},{10,... | collective-permute-start | bytes 393224 | tf_op jit(solution)/shard_map/ppermute | solution.py:194
  37.4 1.8 %collective-permute-start.18 = (bf16[256,256]{1,0:T(8,128)(2,1)S(1)}, bf16[256,256]{1,0:T(8,128)(2,1)S(1)}, u32[]{:S(2)}, u32[]{:S(2)}) collective-permute-start(bf16[256,256]{1,0:T(8,128)(2,1)S(1)} %add_convert_fusion.3), channel_id=1, source_target_pairs={{0,24},{8,16},{16,8},{24,0},{1,25},{9,17},{17,9},{25,1},{2,26},{10... | collective-permute-start | bytes 393224 | tf_op jit(solution)/shard_map/ppermute | solution.py:191
  39.2 1.3 %collective-permute-start.17 = (bf16[256,256]{1,0:T(8,128)(2,1)S(1)}, bf16[256,256]{1,0:T(8,128)(2,1)S(1)}, u32[]{:S(2)}, u32[]{:S(2)}) collective-permute-start(bf16[256,256]{1,0:T(8,128)(2,1)S(1)} %add_convert_fusion.3), channel_id=1, source_target_pairs={{0,16},{8,24},{16,0},{24,8},{1,17},{9,25},{17,1},{25,9},{2,18},{10... | collective-permute-start | bytes 393224 | tf_op jit(solution)/shard_map/ppermute | solution.py:191
  40.5 2.3 %collective-permute-done.12.refs_3_ = bf16[256,256]{1,0:T(8,128)(2,1)S(1)} collective-permute-done((bf16[256,256]{1,0:T(8,128)(2,1)S(1)}, bf16[256,256]{1,0:T(8,128)(2,1)S(1)}, u32[]{:S(2)}, u32[]{:S(2)}) %collective-permute-start.12) | collective-permute-done | bytes 131104 | tf_op jit(solution)/shard_map/ppermute | solution.py:194
  42.8 1.5 %collective-permute-start.16 = (bf16[256,256]{1,0:T(8,128)(2,1)S(1)}, bf16[256,256]{1,0:T(8,128)(2,1)S(1)}, u32[]{:S(2)}, u32[]{:S(2)}) collective-permute-start(bf16[256,256]{1,0:T(8,128)(2,1)S(1)} %add_convert_fusion.3), channel_id=1, source_target_pairs={{0,8},{8,0},{16,24},{24,16},{1,9},{9,1},{17,25},{25,17},{2,10},{10... | collective-permute-start | bytes 393224 | tf_op jit(solution)/shard_map/ppermute | solution.py:191
  44.3 1.5 %collective-permute-done.11.refs_2_ = bf16[256,256]{1,0:T(8,128)(2,1)S(1)} collective-permute-done((bf16[256,256]{1,0:T(8,128)(2,1)S(1)}, bf16[256,256]{1,0:T(8,128)(2,1)S(1)}, u32[]{:S(2)}, u32[]{:S(2)}) %collective-permute-start.11) | collective-permute-done | bytes 131104 | tf_op jit(solution)/shard_map/ppermute | solution.py:194
  45.9 0.5 collective-permute-start.14
  46.9 0.9 %collective-permute-done.16 = bf16[256,256]{1,0:T(8,128)(2,1)S(1)} collective-permute-done((bf16[256,256]{1,0:T(8,128)(2,1)S(1)}, bf16[256,256]{1,0:T(8,128)(2,1)S(1)}, u32[]{:S(2)}, u32[]{:S(2)}) %collective-permute-start.16) | collective-permute-done | bytes 131104 | tf_op jit(solution)/shard_map/ppermute | solution.py:191
  47.9 0.7 %backward_near.1.refs_1_ = f32[1024,256]{1,0:T(8,128)S(1)} custom-call(bf16[1024,2048]{1,0:T(8,128)(2,1)S(1)} %build.1.refs_0_.st_ref, bf16[256,256]{1,0:T(8,128)(2,1)S(1)} %get-tuple-element.30.refs_1_, bf16[256,256]{1,0:T(8,128)(2,1)S(1)} %collective-permute-done.8.refs_2_, bf16[256,256]{1,0:T(8,128)(2,1)S(1)} %collective-permute-done.9.refs_3_, ...), custom_call_target="tpu_custom_call" | custom-call | flops 536870912 | bytes 1048576 | tf_op jit(solution)/shard_map/backward_near/pallas_call | solution.py:35
  48.7 0.7 %backward_far.1 = (bf16[256,256]{1,0:T(8,128)(2,1)S(1)}, bf16[256,256]{1,0:T(8,128)(2,1)S(1)}, bf16[256,256]{1,0:T(8,128)(2,1)S(1)}, bf16[256,256]{1,0:T(8,128)(2,1)S(1)}) custom-call(bf16[1024,2048]{1,0:T(8,128)(2,1)S(1)} %build.1.refs_0_.st_ref, f32[1024,256]{1,0:T(8,128)S(1)} %backward_near.1.refs_1_, ...), custom_call_target="tpu_custom_call" | custom-call | flops 536870912 | bytes 1048576 | tf_op jit(solution)/shard_map/backward_far/pallas_call | solution.py:35
  49.4 3.2 %collective-permute-start.23 = (bf16[256,256]{1,0:T(8,128)(2,1)S(1)}, bf16[256,256]{1,0:T(8,128)(2,1)S(1)}, u32[]{:S(2)}, u32[]{:S(2)}) collective-permute-start(bf16[256,256]{1,0:T(8,128)(2,1)S(1)} %add_convert_fusion.1), channel_id=1, source_target_pairs={{0,4},{1,5},{2,6},{3,7},{4,0},{5,1},{6,2},{7,3},{8,12},{9,13},{10,... | collective-permute-start | bytes 393224 | tf_op jit(solution)/shard_map/ppermute | solution.py:194
  52.7 1.5 %collective-permute-start.20 = (bf16[256,256]{1,0:T(8,128)(2,1)S(1)}, bf16[256,256]{1,0:T(8,128)(2,1)S(1)}, u32[]{:S(2)}, u32[]{:S(2)}) collective-permute-start(bf16[256,256]{1,0:T(8,128)(2,1)S(1)} %get-tuple-element.38), channel_id=1, source_target_pairs={{0,8},{8,0},{16,24},{24,16},{1,9},{9,1},{17,25},{25,17},{2,10},{10... | collective-permute-start | bytes 393224 | tf_op jit(solution)/shard_map/ppermute | solution.py:191
  54.2 0.7 %collective-permute-start.21 = (bf16[256,256]{1,0:T(8,128)(2,1)S(1)}, bf16[256,256]{1,0:T(8,128)(2,1)S(1)}, u32[]{:S(2)}, u32[]{:S(2)}) collective-permute-start(bf16[256,256]{1,0:T(8,128)(2,1)S(1)} %get-tuple-element.39), channel_id=1, source_target_pairs={{0,16},{8,24},{16,0},{24,8},{1,17},{9,25},{17,1},{25,9},{2,18},{10... | collective-permute-start | bytes 393224 | tf_op jit(solution)/shard_map/ppermute | solution.py:191
  54.9 1.2 %collective-permute-start.22 = (bf16[256,256]{1,0:T(8,128)(2,1)S(1)}, bf16[256,256]{1,0:T(8,128)(2,1)S(1)}, u32[]{:S(2)}, u32[]{:S(2)}) collective-permute-start(bf16[256,256]{1,0:T(8,128)(2,1)S(1)} %get-tuple-element.40), channel_id=1, source_target_pairs={{0,24},{8,16},{16,8},{24,0},{1,25},{9,17},{17,9},{25,1},{2,26},{10... | collective-permute-start | bytes 393224 | tf_op jit(solution)/shard_map/ppermute | solution.py:191
  56.2 3.4 %collective-permute-done.23 = bf16[256,256]{1,0:T(8,128)(2,1)S(1)} collective-permute-done((bf16[256,256]{1,0:T(8,128)(2,1)S(1)}, bf16[256,256]{1,0:T(8,128)(2,1)S(1)}, u32[]{:S(2)}, u32[]{:S(2)}) %collective-permute-start.23) | collective-permute-done | bytes 131104 | tf_op jit(solution)/shard_map/ppermute | solution.py:194
  59.6 0.7 %convert_add_fusion = f32[256,256]{1,0:T(8,128)} fusion(bf16[256,256]{1,0:T(8,128)(2,1)S(1)} %collective-permute-done.23, bf16[256,256]{1,0:T(8,128)(2,1)S(1)} %add_convert_fusion.1), kind=kLoop, calls=%fused_computation | loop fusion | flops 196608 | bytes 524288 | tf_op jit(solution)/shard_map/add | solution.py:174
  60.3 2.0 %collective-permute-done.21 = bf16[256,256]{1,0:T(8,128)(2,1)S(1)} collective-permute-done((bf16[256,256]{1,0:T(8,128)(2,1)S(1)}, bf16[256,256]{1,0:T(8,128)(2,1)S(1)}, u32[]{:S(2)}, u32[]{:S(2)}) %collective-permute-start.21) | collective-permute-done | bytes 131104 | tf_op jit(solution)/shard_map/ppermute | solution.py:191
  62.3 0.7 %add_convert_fusion = bf16[256,256]{1,0:T(8,128)(2,1)} fusion(f32[256,256]{1,0:T(8,128)S(1)} %get-tuple-element.41, bf16[256,256]{1,0:T(8,128)(2,1)S(1)} %collective-permute-done.22, bf16[256,256]{1,0:T(8,128)(2,1)S(1)} %collective-permute-done.21, bf16[256,256]{1,0:T(8,128)(2,1)S(1)} %collective-permute-done.20, bf16[256,256]{1,0:T(8,128)(2,1)S(1)} %get-tuple-element.37), kind=kLoop, calls=%fused_computation.1 | loop fusion | flops 589824 | bytes 917504 | tf_op jit(solution)/shard_map/convert_element_type | solution.py:276
  (42 shorter events, 3.7 us)
Async XLA Ops:
  0.6 8.7 %collective-permute-start.2 = (bf16[256,256]{1,0:T(8,128)(2,1)}, bf16[256,256]{1,0:T(8,128)(2,1)S(1)}, u32[]{:S(2)}, u32[]{:S(2)}) collective-permute-start(bf16[256,256]{1,0:T(8,128)(2,1)} %refs_4_.1), channel_id=1, source_target_pairs={{0,24},{8,16},{16,8},{24,0},{1,25},{9,17},{17,9},{25,1},{2,26},{10... | collective-permute-start | bytes 393224 | tf_op jit(solution)/shard_map/ppermute | solution.py:191
  4.6 6.5 %collective-permute-start.1 = (bf16[256,256]{1,0:T(8,128)(2,1)}, bf16[256,256]{1,0:T(8,128)(2,1)S(1)}, u32[]{:S(2)}, u32[]{:S(2)}) collective-permute-start(bf16[256,256]{1,0:T(8,128)(2,1)} %refs_4_.1), channel_id=1, source_target_pairs={{0,16},{8,24},{16,0},{24,8},{1,17},{9,25},{17,1},{25,9},{2,18},{10... | collective-permute-start | bytes 393224 | tf_op jit(solution)/shard_map/ppermute | solution.py:191
  5.1 6.3 %collective-permute-start = (bf16[256,256]{1,0:T(8,128)(2,1)}, bf16[256,256]{1,0:T(8,128)(2,1)S(1)}, u32[]{:S(2)}, u32[]{:S(2)}) collective-permute-start(bf16[256,256]{1,0:T(8,128)(2,1)} %refs_4_.1), channel_id=1, source_target_pairs={{0,8},{8,0},{16,24},{24,16},{1,9},{9,1},{17,25},{25,17},{2,10},{10... | collective-permute-start | bytes 393224 | tf_op jit(solution)/shard_map/ppermute | solution.py:191
  5.9 1.0 %copy-start.3 = (s32[1,1,64,16,128]{4,3,2,1,0:T(8,128)S(1)}, s32[1,1,64,16,128]{4,3,2,1,0:T(8,128)}, u32[]{:S(2)}) copy-start(s32[1,1,64,16,128]{4,3,2,1,0:T(8,128)} %param.11) | copy-start | bytes 1572868
  6.9 0.7 %copy-start.4 = (s32[1,1,2,64]{3,2,1,0:T(2,128)S(1)}, s32[1,1,2,64]{3,2,1,0:T(2,128)}, u32[]{:S(2)}) copy-start(s32[1,1,2,64]{3,2,1,0:T(2,128)} %param.9) | copy-start | bytes 1540
  7.6 3.8 %copy-start = (bf16[256,256]{1,0:T(8,128)(2,1)S(1)}, bf16[256,256]{1,0:T(8,128)(2,1)}, u32[]{:S(2)}) copy-start(bf16[256,256]{1,0:T(8,128)(2,1)} %refs_4_.1) | copy-start | bytes 393220
  12.3 1.6 %collective-permute-start.3 = (bf16[2,272,256]{2,1,0:T(8,128)(2,1)S(1)}, bf16[2,272,256]{2,1,0:T(8,128)(2,1)S(1)}, u32[]{:S(2)}, u32[]{:S(2)}) collective-permute-start(bf16[2,272,256]{2,1,0:T(8,128)(2,1)S(1)} %forward_near_other.1), channel_id=1, source_target_pairs={{0,1},{1,0},{2,3},{3,2},{4,5},{5,4},{6,7},{7,6},{8,9},{9,8},{10,11... | collective-permute-start | bytes 835592 | tf_op jit(solution)/shard_map/ppermute | solution.py:197
  12.4 3.3 %collective-permute-start.5 = (bf16[2,272,256]{2,1,0:T(8,128)(2,1)S(1)}, bf16[2,272,256]{2,1,0:T(8,128)(2,1)S(1)}, u32[]{:S(2)}, u32[]{:S(2)}) collective-permute-start(bf16[2,272,256]{2,1,0:T(8,128)(2,1)S(1)} %get-tuple-element.26), channel_id=1, source_target_pairs={{0,1},{1,0},{2,3},{3,2},{4,5},{5,4},{6,7},{7,6},{8,9},{9,8},{10,11... | collective-permute-start | bytes 835592 | tf_op jit(solution)/shard_map/ppermute | solution.py:197
  13.4 15.9 %copy-start.1 = (bf16[256,256]{1,0:T(8,128)(2,1)S(1)}, bf16[256,256]{1,0:T(8,128)(2,1)}, u32[]{:S(2)}) copy-start(bf16[256,256]{1,0:T(8,128)(2,1)} %refs_5_.1) | copy-start | bytes 393220
  13.4 15.9 %copy-start.2 = (bf16[256,256]{1,0:T(8,128)(2,1)S(1)}, bf16[256,256]{1,0:T(8,128)(2,1)}, u32[]{:S(2)}) copy-start(bf16[256,256]{1,0:T(8,128)(2,1)} %refs_6_.1) | copy-start | bytes 393220
  14.0 7.9 %collective-permute-start.4 = (bf16[272,256]{1,0:T(8,128)(2,1)S(1)}, bf16[272,256]{1,0:T(8,128)(2,1)S(1)}, u32[]{:S(2)}, u32[]{:S(2)}) collective-permute-start(bf16[272,256]{1,0:T(8,128)(2,1)S(1)} %get-tuple-element.25), channel_id=1, source_target_pairs={{0,2},{1,3},{2,0},{3,1},{4,6},{5,7},{6,4},{7,5},{8,10},{9,11},{10,... | collective-permute-start | bytes 417800 | tf_op jit(solution)/shard_map/ppermute | solution.py:194
  15.7 13.5 %collective-permute-start.6 = (bf16[272,256]{1,0:T(8,128)(2,1)S(1)}, bf16[272,256]{1,0:T(8,128)(2,1)S(1)}, u32[]{:S(2)}, u32[]{:S(2)}) collective-permute-start(bf16[272,256]{1,0:T(8,128)(2,1)S(1)} %get-tuple-element.27), channel_id=1, source_target_pairs={{0,4},{1,5},{2,6},{3,7},{4,0},{5,1},{6,2},{7,3},{8,12},{9,13},{10,... | collective-permute-start | bytes 417800 | tf_op jit(solution)/shard_map/ppermute | solution.py:194
  18.4 10.8 %collective-permute-start.7 = (bf16[272,256]{1,0:T(8,128)(2,1)S(1)}, bf16[272,256]{1,0:T(8,128)(2,1)S(1)}, u32[]{:S(2)}, u32[]{:S(2)}) collective-permute-start(bf16[272,256]{1,0:T(8,128)(2,1)S(1)} %get-tuple-element.28), channel_id=1, source_target_pairs={{0,6},{1,7},{2,4},{3,5},{4,2},{5,3},{6,0},{7,1},{8,14},{9,15},{10,... | collective-permute-start | bytes 417800 | tf_op jit(solution)/shard_map/ppermute | solution.py:194
  30.4 6.9 %collective-permute-start.15 = (bf16[256,256]{1,0:T(8,128)(2,1)S(1)}, bf16[256,256]{1,0:T(8,128)(2,1)S(1)}, u32[]{:S(2)}, u32[]{:S(2)}) collective-permute-start(bf16[256,256]{1,0:T(8,128)(2,1)S(1)} %weight_part.1), channel_id=1, source_target_pairs={{0,2},{1,3},{2,0},{3,1},{4,6},{5,7},{6,4},{7,5},{8,10},{9,11},{10,... | collective-permute-start | bytes 393224 | tf_op jit(solution)/shard_map/ppermute | solution.py:194
  33.0 9.8 %collective-permute-start.12 = (bf16[256,256]{1,0:T(8,128)(2,1)S(1)}, bf16[256,256]{1,0:T(8,128)(2,1)S(1)}, u32[]{:S(2)}, u32[]{:S(2)}) collective-permute-start(bf16[256,256]{1,0:T(8,128)(2,1)S(1)} %get-tuple-element.30.refs_1_), channel_id=1, source_target_pairs={{0,6},{1,7},{2,4},{3,5},{4,2},{5,3},{6,0},{7,1},{8,14},{9,15},{10,... | collective-permute-start | bytes 393224 | tf_op jit(solution)/shard_map/ppermute | solution.py:194
  35.5 10.4 %collective-permute-start.11 = (bf16[256,256]{1,0:T(8,128)(2,1)S(1)}, bf16[256,256]{1,0:T(8,128)(2,1)S(1)}, u32[]{:S(2)}, u32[]{:S(2)}) collective-permute-start(bf16[256,256]{1,0:T(8,128)(2,1)S(1)} %get-tuple-element.30.refs_1_), channel_id=1, source_target_pairs={{0,4},{1,5},{2,6},{3,7},{4,0},{5,1},{6,2},{7,3},{8,12},{9,13},{10,... | collective-permute-start | bytes 393224 | tf_op jit(solution)/shard_map/ppermute | solution.py:194
  35.5 10.4 %collective-permute-start.8 = (bf16[256,256]{1,0:T(8,128)(2,1)S(1)}, bf16[256,256]{1,0:T(8,128)(2,1)S(1)}, u32[]{:S(2)}, u32[]{:S(2)}) collective-permute-start(bf16[256,256]{1,0:T(8,128)(2,1)S(1)} %get-tuple-element.30.refs_1_), channel_id=1, source_target_pairs={{0,2},{1,3},{2,0},{3,1},{4,6},{5,7},{6,4},{7,5},{8,10},{9,11},{10,... | collective-permute-start | bytes 393224 | tf_op jit(solution)/shard_map/ppermute | solution.py:194
  37.4 9.0 %collective-permute-start.18 = (bf16[256,256]{1,0:T(8,128)(2,1)S(1)}, bf16[256,256]{1,0:T(8,128)(2,1)S(1)}, u32[]{:S(2)}, u32[]{:S(2)}) collective-permute-start(bf16[256,256]{1,0:T(8,128)(2,1)S(1)} %add_convert_fusion.3), channel_id=1, source_target_pairs={{0,24},{8,16},{16,8},{24,0},{1,25},{9,17},{17,9},{25,1},{2,26},{10... | collective-permute-start | bytes 393224 | tf_op jit(solution)/shard_map/ppermute | solution.py:191
  39.2 7.3 %collective-permute-start.17 = (bf16[256,256]{1,0:T(8,128)(2,1)S(1)}, bf16[256,256]{1,0:T(8,128)(2,1)S(1)}, u32[]{:S(2)}, u32[]{:S(2)}) collective-permute-start(bf16[256,256]{1,0:T(8,128)(2,1)S(1)} %add_convert_fusion.3), channel_id=1, source_target_pairs={{0,16},{8,24},{16,0},{24,8},{1,17},{9,25},{17,1},{25,9},{2,18},{10... | collective-permute-start | bytes 393224 | tf_op jit(solution)/shard_map/ppermute | solution.py:191
  42.8 5.0 %collective-permute-start.16 = (bf16[256,256]{1,0:T(8,128)(2,1)S(1)}, bf16[256,256]{1,0:T(8,128)(2,1)S(1)}, u32[]{:S(2)}, u32[]{:S(2)}) collective-permute-start(bf16[256,256]{1,0:T(8,128)(2,1)S(1)} %add_convert_fusion.3), channel_id=1, source_target_pairs={{0,8},{8,0},{16,24},{24,16},{1,9},{9,1},{17,25},{25,17},{2,10},{10... | collective-permute-start | bytes 393224 | tf_op jit(solution)/shard_map/ppermute | solution.py:191
  45.9 2.0 %collective-permute-start.9 = (bf16[256,256]{1,0:T(8,128)(2,1)S(1)}, bf16[256,256]{1,0:T(8,128)(2,1)S(1)}, u32[]{:S(2)}, u32[]{:S(2)}) collective-permute-start(bf16[256,256]{1,0:T(8,128)(2,1)S(1)} %get-tuple-element.30.refs_1_), channel_id=1, source_target_pairs={{0,1},{1,0},{2,3},{3,2},{4,5},{5,4},{6,7},{7,6},{8,9},{9,8},{10,11... | collective-permute-start | bytes 393224 | tf_op jit(solution)/shard_map/ppermute | solution.py:197
  45.9 2.8 %collective-permute-start.14 = (bf16[256,256]{1,0:T(8,128)(2,1)S(1)}, bf16[256,256]{1,0:T(8,128)(2,1)S(1)}, u32[]{:S(2)}, u32[]{:S(2)}) collective-permute-start(bf16[256,256]{1,0:T(8,128)(2,1)S(1)} %collective-permute-done.12.refs_3_), channel_id=1, source_target_pairs={{0,1},{1,0},{2,3},{3,2},{4,5},{5,4},{6,7},{7,6},{8,9},{9,8},{10,11... | collective-permute-start | bytes 393224 | tf_op jit(solution)/shard_map/ppermute | solution.py:197
  46.4 2.3 %collective-permute-start.13 = (bf16[256,256]{1,0:T(8,128)(2,1)S(1)}, bf16[256,256]{1,0:T(8,128)(2,1)S(1)}, u32[]{:S(2)}, u32[]{:S(2)}) collective-permute-start(bf16[256,256]{1,0:T(8,128)(2,1)S(1)} %collective-permute-done.11.refs_2_), channel_id=1, source_target_pairs={{0,1},{1,0},{2,3},{3,2},{4,5},{5,4},{6,7},{7,6},{8,9},{9,8},{10,11... | collective-permute-start | bytes 393224 | tf_op jit(solution)/shard_map/ppermute | solution.py:197
  46.5 1.5 %collective-permute-start.10 = (bf16[256,256]{1,0:T(8,128)(2,1)S(1)}, bf16[256,256]{1,0:T(8,128)(2,1)S(1)}, u32[]{:S(2)}, u32[]{:S(2)}) collective-permute-start(bf16[256,256]{1,0:T(8,128)(2,1)S(1)} %collective-permute-done.8.refs_2_), channel_id=1, source_target_pairs={{0,1},{1,0},{2,3},{3,2},{4,5},{5,4},{6,7},{7,6},{8,9},{9,8},{10,11... | collective-permute-start | bytes 393224 | tf_op jit(solution)/shard_map/ppermute | solution.py:197
  47.8 1.6 %collective-permute-start.19 = (bf16[256,256]{1,0:T(8,128)(2,1)S(1)}, bf16[256,256]{1,0:T(8,128)(2,1)S(1)}, u32[]{:S(2)}, u32[]{:S(2)}) collective-permute-start(bf16[256,256]{1,0:T(8,128)(2,1)S(1)} %add_convert_fusion.2), channel_id=1, source_target_pairs={{0,1},{1,0},{2,3},{3,2},{4,5},{5,4},{6,7},{7,6},{8,9},{9,8},{10,11... | collective-permute-start | bytes 393224 | tf_op jit(solution)/shard_map/ppermute | solution.py:197
  49.4 10.2 %collective-permute-start.23 = (bf16[256,256]{1,0:T(8,128)(2,1)S(1)}, bf16[256,256]{1,0:T(8,128)(2,1)S(1)}, u32[]{:S(2)}, u32[]{:S(2)}) collective-permute-start(bf16[256,256]{1,0:T(8,128)(2,1)S(1)} %add_convert_fusion.1), channel_id=1, source_target_pairs={{0,4},{1,5},{2,6},{3,7},{4,0},{5,1},{6,2},{7,3},{8,12},{9,13},{10,... | collective-permute-start | bytes 393224 | tf_op jit(solution)/shard_map/ppermute | solution.py:194
  52.7 7.7 %collective-permute-start.20 = (bf16[256,256]{1,0:T(8,128)(2,1)S(1)}, bf16[256,256]{1,0:T(8,128)(2,1)S(1)}, u32[]{:S(2)}, u32[]{:S(2)}) collective-permute-start(bf16[256,256]{1,0:T(8,128)(2,1)S(1)} %get-tuple-element.38), channel_id=1, source_target_pairs={{0,8},{8,0},{16,24},{24,16},{1,9},{9,1},{17,25},{25,17},{2,10},{10... | collective-permute-start | bytes 393224 | tf_op jit(solution)/shard_map/ppermute | solution.py:191
  54.2 8.1 %collective-permute-start.21 = (bf16[256,256]{1,0:T(8,128)(2,1)S(1)}, bf16[256,256]{1,0:T(8,128)(2,1)S(1)}, u32[]{:S(2)}, u32[]{:S(2)}) collective-permute-start(bf16[256,256]{1,0:T(8,128)(2,1)S(1)} %get-tuple-element.39), channel_id=1, source_target_pairs={{0,16},{8,24},{16,0},{24,8},{1,17},{9,25},{17,1},{25,9},{2,18},{10... | collective-permute-start | bytes 393224 | tf_op jit(solution)/shard_map/ppermute | solution.py:191
  54.9 7.4 %collective-permute-start.22 = (bf16[256,256]{1,0:T(8,128)(2,1)S(1)}, bf16[256,256]{1,0:T(8,128)(2,1)S(1)}, u32[]{:S(2)}, u32[]{:S(2)}) collective-permute-start(bf16[256,256]{1,0:T(8,128)(2,1)S(1)} %get-tuple-element.40), channel_id=1, source_target_pairs={{0,24},{8,16},{16,8},{24,0},{1,25},{9,17},{17,9},{25,1},{2,26},{10... | collective-permute-start | bytes 393224 | tf_op jit(solution)/shard_map/ppermute | solution.py:191

commit v5 on v4

--- a/solution.py
+++ b/solution.py
@@ -175,6 +175,12 @@
     return values[0]
 
 
+def last_kernel(grad_agg, own, other, *refs):
+    total = tree_sum([ref[...] for ref in refs[:-2]])
+    refs[-2][...] = (total + grad_agg[...]).astype(bf16)
+    refs[-1][...] = own[...].astype(f32) + other[...].astype(f32)
+
+
 def per_device(features, weight, cotangent, tiles, tile_count, patterns):
     rows, width = features.shape
     slots, words, tile = patterns.shape[2:]
@@ -237,14 +243,14 @@
         [((rows, width), bf16), ((rows, width), bf16), ((rows, width), f32), ((width, rows), bf16), ((rows, width), bf16)],
         parts + [features, cotangent, weight],
         flops=4 * rows * width * width,
-        final=(0,),
     )
     far = [over_z(scaled, k) for k in range(2, n_z)]
 
     (part,) = call(weight_kernel, "weight_part", [((width, width), bf16)], [agg_t, grad_pre], flops=2e9)
     part = tree_sum([part, over_z(part, 1)]).astype(bf16)
     part = tree_sum([part] + [over_row(part, k) for k in range(1, n_row)]).astype(bf16)
-    part = tree_sum([part, over_core(part)]).astype(bf16)
+    for step in range(1, (n_z - 1).bit_length()):
+        part = tree_sum([part, over_z(part, 1 << step)]).astype(bf16)
 
     grads = [scaled, over_z(scaled, 1)]
     grads = grads + [over_core(x) for x in grads]
@@ -266,14 +272,15 @@
         scratch=[pltpu.VMEM((len(spots) * rows, width), bf16)],
         flops=flops // 2,
     )
-    backs, part = lax.optimization_barrier((backs, part))
-    for step in range(1, (n_z - 1).bit_length()):
-        part = part.astype(bf16)
-        part = tree_sum([part, over_z(part, 1 << step)])
-    grad_weight = part
 
     backs = [backs[0]] + [over_row(backs[k], k) for k in range(1, n_row)]
-    grad_features = (tree_sum(backs) + grad_agg).astype(bf16)
+    grad_features, grad_weight = call(
+        last_kernel,
+        "last",
+        [((rows, width), bf16), ((width, width), f32)],
+        [grad_agg, part, over_core(part)] + backs,
+        final=(0, 1),
+    )
     return activated, grad_features, grad_weight
 
 

time: 63.3 us -> 61.2 us (0.967)
  waiting for transfers between devices: 22.9 us -> 21.2 us
  other arithmetic: 1.62 us -> 0.14 us
  local copies, waits for them, and re-layouts: 1.73 us -> 2.39 us
    ppermute x8, waiting for transfers between devices: 17.9 us -> 14.6 us  [over_z(): return lax.ppermute(x, 'col', [(i, i ^ 2 * k) for i in range(n_col)])]
    ppermute x9, waiting for transfers between devices: 4.87 us -> 6.53 us  [over_row(): return lax.ppermute(x, 'row', [(i, i ^ k) for i in range(n_row)])]
    convert_element_type x2 -> x1, other arithmetic: 0.77 us -> 0.03 us  [per_device(): part = tree_sum([part, over_z(part, 1 << step)]).astype(bf16)]
    add x1 -> x0, other arithmetic: 0.74 us -> none  [tree_sum(): values = [values[i] + values[i + 1] for i in range(0, len(values), 2)]]
    unnamed x10 -> x11, local copies, waits for them, and re-layouts: 1.73 us -> 2.39 us
    pallas_call x11 -> x12, Pallas kernels: 6.32 us -> 6.73 us  [call(): pl.pallas_call(body, out_shape=shapes, in_specs=smem(n_smem) + [pl.BlockS...]
  transfers between devices with their start and end apart: 24 -> 24, of which waited for: 10 -> 12; matrix products, arithmetic and copies ran while one was open for 1% -> 1% of each run, Pallas kernels for 7% -> 7%
where the time goes in v5:
time: 61.2 us; the launch traced here: 61 us
  starting transfers between devices  29.1 us (48%)
  waiting for transfers between devices  21.2 us (35%)
  Pallas kernels  6.73 us (11%)
  local copies, waits for them, and re-layouts  2.39 us (4%)
  between operations  1.46 us (2%)
    ppermute x8, starting transfers between devices, over_z(): return lax.ppermute(x, 'col', [(i, i ^ 2 * k) for i in range(n_col)])  14.7 us
    ppermute x8, waiting for transfers between devices, over_z(): return lax.ppermute(x, 'col', [(i, i ^ 2 * k) for i in range(n_col)])  14.6 us
    ppermute x9, starting transfers between devices, over_row(): return lax.ppermute(x, 'row', [(i, i ^ k) for i in range(n_row)])  12.8 us
    pallas_call x12, Pallas kernels, call(): pl.pallas_call(body, out_shape=shapes, in_specs=smem(n_smem) + [pl.BlockS...  6.73 us
    ppermute x9, waiting for transfers between devices, over_row(): return lax.ppermute(x, 'row', [(i, i ^ k) for i in range(n_row)])  6.53 us
    unnamed x11, local copies, waits for them, and re-layouts  2.39 us
    ppermute x7, starting transfers between devices, over_core(): return lax.ppermute(x, 'col', [(i, i ^ 1) for i in range(n_col)])  1.66 us
  transfers between devices with their start and end apart: 24, of which 12 were waited for; matrix products, arithmetic and copies ran while one was open for 1% of the time, Pallas kernels for 7%

profile of v5, /device:TPU:0, one launch (start us, length us, event | category | flops | bytes accessed | tf_op | source)
XLA Modules:
  0.0 61.0 jit_solution(14317977712386149755)
XLA Ops:
  0.6 4.0 %collective-permute-start.2 = (bf16[256,256]{1,0:T(8,128)(2,1)}, bf16[256,256]{1,0:T(8,128)(2,1)S(1)}, u32[]{:S(2)}, u32[]{:S(2)}) collective-permute-start(bf16[256,256]{1,0:T(8,128)(2,1)} %refs_4_.1), channel_id=1, source_target_pairs={{0,24},{8,16},{16,8},{24,0},{1,25},{9,17},{17,9},{25,1},{2,26},{10... | collective-permute-start | bytes 393224 | tf_op jit(solution)/shard_map/ppermute | solution.py:197
  4.6 0.5 collective-permute-start.1
  5.9 1.0 %copy-done.3 = s32[1,1,64,16,128]{4,3,2,1,0:T(8,128)S(1)} copy-done((s32[1,1,64,16,128]{4,3,2,1,0:T(8,128)S(1)}, s32[1,1,64,16,128]{4,3,2,1,0:T(8,128)}, u32[]{:S(2)}) %copy-start.3) | copy-done | bytes 524312
  6.9 0.7 %copy-done.4 = s32[1,1,2,64]{3,2,1,0:T(2,128)S(1)} copy-done((s32[1,1,2,64]{3,2,1,0:T(2,128)S(1)}, s32[1,1,2,64]{3,2,1,0:T(2,128)}, u32[]{:S(2)}) %copy-start.4) | copy-done | bytes 536
  7.6 1.8 %build.1.refs_0_.st_ref = bf16[1024,2048]{1,0:T(8,128)(2,1)S(1)} custom-call(s32[2,64]{1,0:T(2,128)S(1)} %bitcast.3, s32[1,1]{1,0:T(1,128)S(6)} %copy.10.count, s32[64,16,128]{2,1,0:T(8,128)S(1)} %bitcast.2), custom_call_target="tpu_custom_call" | custom-call | flops 4000000000 | bytes 1048576 | tf_op jit(solution)/shard_map/build/pallas_call | solution.py:35
  9.5 1.6 %collective-permute-done.1.refs_3_ = bf16[256,256]{1,0:T(8,128)(2,1)S(1)} collective-permute-done((bf16[256,256]{1,0:T(8,128)(2,1)}, bf16[256,256]{1,0:T(8,128)(2,1)S(1)}, u32[]{:S(2)}, u32[]{:S(2)}) %collective-permute-start.1) | collective-permute-done | bytes 131104 | tf_op jit(solution)/shard_map/ppermute | solution.py:197
  12.4 0.5 collective-permute-start.5
  14.0 1.6 %collective-permute-start.4 = (bf16[272,256]{1,0:T(8,128)(2,1)S(1)}, bf16[272,256]{1,0:T(8,128)(2,1)S(1)}, u32[]{:S(2)}, u32[]{:S(2)}) collective-permute-start(bf16[272,256]{1,0:T(8,128)(2,1)S(1)} %get-tuple-element.22), channel_id=1, source_target_pairs={{0,2},{1,3},{2,0},{3,1},{4,6},{5,7},{6,4},{7,5},{8,10},{9,11},{10,... | collective-permute-start | bytes 417800 | tf_op jit(solution)/shard_map/ppermute | solution.py:200
  15.7 2.7 %collective-permute-start.6 = (bf16[272,256]{1,0:T(8,128)(2,1)S(1)}, bf16[272,256]{1,0:T(8,128)(2,1)S(1)}, u32[]{:S(2)}, u32[]{:S(2)}) collective-permute-start(bf16[272,256]{1,0:T(8,128)(2,1)S(1)} %get-tuple-element.24), channel_id=1, source_target_pairs={{0,4},{1,5},{2,6},{3,7},{4,0},{5,1},{6,2},{7,3},{8,12},{9,13},{10,... | collective-permute-start | bytes 417800 | tf_op jit(solution)/shard_map/ppermute | solution.py:200
  18.6 3.3 %collective-permute-done.4.refs_1_ = bf16[272,256]{1,0:T(8,128)(2,1)S(1)} collective-permute-done((bf16[272,256]{1,0:T(8,128)(2,1)S(1)}, bf16[272,256]{1,0:T(8,128)(2,1)S(1)}, u32[]{:S(2)}, u32[]{:S(2)}) %collective-permute-start.4) | collective-permute-done | bytes 139296 | tf_op jit(solution)/shard_map/ppermute | solution.py:200
  21.9 7.3 %collective-permute-done.6.refs_2_ = bf16[272,256]{1,0:T(8,128)(2,1)S(1)} collective-permute-done((bf16[272,256]{1,0:T(8,128)(2,1)S(1)}, bf16[272,256]{1,0:T(8,128)(2,1)S(1)}, u32[]{:S(2)}, u32[]{:S(2)}) %collective-permute-start.6) | collective-permute-done | bytes 139296 | tf_op jit(solution)/shard_map/ppermute | solution.py:200
  29.9 2.5 %collective-permute-start.8 = (bf16[256,256]{1,0:T(8,128)(2,1)S(1)}, bf16[256,256]{1,0:T(8,128)(2,1)S(1)}, u32[]{:S(2)}, u32[]{:S(2)}) collective-permute-start(bf16[256,256]{1,0:T(8,128)(2,1)S(1)} %weight_part.1), channel_id=1, source_target_pairs={{0,2},{1,3},{2,0},{3,1},{4,6},{5,7},{6,4},{7,5},{8,10},{9,11},{10,... | collective-permute-start | bytes 393224 | tf_op jit(solution)/shard_map/ppermute | solution.py:200
  32.4 2.6 %collective-permute-start.18 = (bf16[256,256]{1,0:T(8,128)(2,1)S(1)}, bf16[256,256]{1,0:T(8,128)(2,1)S(1)}, u32[]{:S(2)}, u32[]{:S(2)}) collective-permute-start(bf16[256,256]{1,0:T(8,128)(2,1)S(1)} %get-tuple-element.30.refs_1_), channel_id=1, source_target_pairs={{0,6},{1,7},{2,4},{3,5},{4,2},{5,3},{6,0},{7,1},{8,14},{9,15},{10,... | collective-permute-start | bytes 393224 | tf_op jit(solution)/shard_map/ppermute | solution.py:200
  35.0 1.8 %collective-permute-start.14 = (bf16[256,256]{1,0:T(8,128)(2,1)S(1)}, bf16[256,256]{1,0:T(8,128)(2,1)S(1)}, u32[]{:S(2)}, u32[]{:S(2)}) collective-permute-start(bf16[256,256]{1,0:T(8,128)(2,1)S(1)} %get-tuple-element.30.refs_1_), channel_id=1, source_target_pairs={{0,2},{1,3},{2,0},{3,1},{4,6},{5,7},{6,4},{7,5},{8,10},{9,11},{10,... | collective-permute-start | bytes 393224 | tf_op jit(solution)/shard_map/ppermute | solution.py:200
  36.9 1.8 %collective-permute-start.11 = (bf16[256,256]{1,0:T(8,128)(2,1)S(1)}, bf16[256,256]{1,0:T(8,128)(2,1)S(1)}, u32[]{:S(2)}, u32[]{:S(2)}) collective-permute-start(bf16[256,256]{1,0:T(8,128)(2,1)S(1)} %add_convert_fusion.2), channel_id=1, source_target_pairs={{0,24},{8,16},{16,8},{24,0},{1,25},{9,17},{17,9},{25,1},{2,26},{10... | collective-permute-start | bytes 393224 | tf_op jit(solution)/shard_map/ppermute | solution.py:197
  38.6 1.3 %collective-permute-start.10 = (bf16[256,256]{1,0:T(8,128)(2,1)S(1)}, bf16[256,256]{1,0:T(8,128)(2,1)S(1)}, u32[]{:S(2)}, u32[]{:S(2)}) collective-permute-start(bf16[256,256]{1,0:T(8,128)(2,1)S(1)} %add_convert_fusion.2), channel_id=1, source_target_pairs={{0,16},{8,24},{16,0},{24,8},{1,17},{9,25},{17,1},{25,9},{2,18},{10... | collective-permute-start | bytes 393224 | tf_op jit(solution)/shard_map/ppermute | solution.py:197
  39.9 2.3 %collective-permute-done.18.refs_3_ = bf16[256,256]{1,0:T(8,128)(2,1)S(1)} collective-permute-done((bf16[256,256]{1,0:T(8,128)(2,1)S(1)}, bf16[256,256]{1,0:T(8,128)(2,1)S(1)}, u32[]{:S(2)}, u32[]{:S(2)}) %collective-permute-start.18) | collective-permute-done | bytes 131104 | tf_op jit(solution)/shard_map/ppermute | solution.py:200
  42.3 1.5 %collective-permute-start.9 = (bf16[256,256]{1,0:T(8,128)(2,1)S(1)}, bf16[256,256]{1,0:T(8,128)(2,1)S(1)}, u32[]{:S(2)}, u32[]{:S(2)}) collective-permute-start(bf16[256,256]{1,0:T(8,128)(2,1)S(1)} %add_convert_fusion.2), channel_id=1, source_target_pairs={{0,8},{8,0},{16,24},{24,16},{1,9},{9,1},{17,25},{25,17},{2,10},{10... | collective-permute-start | bytes 393224 | tf_op jit(solution)/shard_map/ppermute | solution.py:197
  43.8 1.5 %collective-permute-done.17.refs_2_ = bf16[256,256]{1,0:T(8,128)(2,1)S(1)} collective-permute-done((bf16[256,256]{1,0:T(8,128)(2,1)S(1)}, bf16[256,256]{1,0:T(8,128)(2,1)S(1)}, u32[]{:S(2)}, u32[]{:S(2)}) %collective-permute-start.17) | collective-permute-done | bytes 131104 | tf_op jit(solution)/shard_map/ppermute | solution.py:200
  45.4 0.5 collective-permute-start.20
  46.4 0.8 %collective-permute-done.9 = bf16[256,256]{1,0:T(8,128)(2,1)S(1)} collective-permute-done((bf16[256,256]{1,0:T(8,128)(2,1)S(1)}, bf16[256,256]{1,0:T(8,128)(2,1)S(1)}, u32[]{:S(2)}, u32[]{:S(2)}) %collective-permute-start.9) | collective-permute-done | bytes 131104 | tf_op jit(solution)/shard_map/ppermute | solution.py:197
  47.3 3.2 %collective-permute-start.12 = (bf16[256,256]{1,0:T(8,128)(2,1)S(1)}, bf16[256,256]{1,0:T(8,128)(2,1)S(1)}, u32[]{:S(2)}, u32[]{:S(2)}) collective-permute-start(bf16[256,256]{1,0:T(8,128)(2,1)S(1)} %add_convert_fusion.1), channel_id=1, source_target_pairs={{0,4},{1,5},{2,6},{3,7},{4,0},{5,1},{6,2},{7,3},{8,12},{9,13},{10,... | collective-permute-start | bytes 393224 | tf_op jit(solution)/shard_map/ppermute | solution.py:200
  50.5 0.7 %backward_near.1.refs_1_ = f32[1024,256]{1,0:T(8,128)S(1)} custom-call(bf16[1024,2048]{1,0:T(8,128)(2,1)S(1)} %build.1.refs_0_.st_ref, bf16[256,256]{1,0:T(8,128)(2,1)S(1)} %get-tuple-element.30.refs_1_, bf16[256,256]{1,0:T(8,128)(2,1)S(1)} %collective-permute-done.14.refs_2_, bf16[256,256]{1,0:T(8,128)(2,1)S(1)} %collective-permute-done.15.refs_3_, ...), custom_call_target="tpu_custom_call" | custom-call | flops 536870912 | bytes 1048576 | tf_op jit(solution)/shard_map/backward_near/pallas_call | solution.py:35
  51.3 0.7 %backward_far.1 = (bf16[256,256]{1,0:T(8,128)(2,1)S(1)}, bf16[256,256]{1,0:T(8,128)(2,1)S(1)}, bf16[256,256]{1,0:T(8,128)(2,1)S(1)}, bf16[256,256]{1,0:T(8,128)(2,1)S(1)}) custom-call(bf16[1024,2048]{1,0:T(8,128)(2,1)S(1)} %build.1.refs_0_.st_ref, f32[1024,256]{1,0:T(8,128)S(1)} %backward_near.1.refs_1_, ...), custom_call_target="tpu_custom_call" | custom-call | flops 536870912 | bytes 1048576 | tf_op jit(solution)/shard_map/backward_far/pallas_call | solution.py:35
  52.0 1.6 %collective-permute-start.21 = (bf16[256,256]{1,0:T(8,128)(2,1)S(1)}, bf16[256,256]{1,0:T(8,128)(2,1)S(1)}, u32[]{:S(2)}, u32[]{:S(2)}) collective-permute-start(bf16[256,256]{1,0:T(8,128)(2,1)S(1)} %get-tuple-element.32), channel_id=1, source_target_pairs={{0,8},{8,0},{16,24},{24,16},{1,9},{9,1},{17,25},{25,17},{2,10},{10... | collective-permute-start | bytes 393224 | tf_op jit(solution)/shard_map/ppermute | solution.py:197
  53.6 0.7 %collective-permute-start.22 = (bf16[256,256]{1,0:T(8,128)(2,1)S(1)}, bf16[256,256]{1,0:T(8,128)(2,1)S(1)}, u32[]{:S(2)}, u32[]{:S(2)}) collective-permute-start(bf16[256,256]{1,0:T(8,128)(2,1)S(1)} %get-tuple-element.33), channel_id=1, source_target_pairs={{0,16},{8,24},{16,0},{24,8},{1,17},{9,25},{17,1},{25,9},{2,18},{10... | collective-permute-start | bytes 393224 | tf_op jit(solution)/shard_map/ppermute | solution.py:197
  54.3 1.2 %collective-permute-start.23 = (bf16[256,256]{1,0:T(8,128)(2,1)S(1)}, bf16[256,256]{1,0:T(8,128)(2,1)S(1)}, u32[]{:S(2)}, u32[]{:S(2)}) collective-permute-start(bf16[256,256]{1,0:T(8,128)(2,1)S(1)} %get-tuple-element.34), channel_id=1, source_target_pairs={{0,24},{8,16},{16,8},{24,0},{1,25},{9,17},{17,9},{25,1},{2,26},{10... | collective-permute-start | bytes 393224 | tf_op jit(solution)/shard_map/ppermute | solution.py:197
  55.7 0.7 %copy.9 = bf16[256,256]{1,0:T(8,128)(2,1)} copy(bf16[256,256]{1,0:T(8,128)(2,1)S(1)} %get-tuple-element.37) | data formatting | bytes 262144
  56.4 0.7 %collective-permute-done.21.refs_1_ = bf16[256,256]{1,0:T(8,128)(2,1)S(1)} collective-permute-done((bf16[256,256]{1,0:T(8,128)(2,1)S(1)}, bf16[256,256]{1,0:T(8,128)(2,1)S(1)}, u32[]{:S(2)}, u32[]{:S(2)}) %collective-permute-start.21) | collective-permute-done | bytes 131104 | tf_op jit(solution)/shard_map/ppermute | solution.py:197
  57.1 1.5 %collective-permute-done.22.refs_2_ = bf16[256,256]{1,0:T(8,128)(2,1)S(1)} collective-permute-done((bf16[256,256]{1,0:T(8,128)(2,1)S(1)}, bf16[256,256]{1,0:T(8,128)(2,1)S(1)}, u32[]{:S(2)}, u32[]{:S(2)}) %collective-permute-start.22) | collective-permute-done | bytes 131104 | tf_op jit(solution)/shard_map/ppermute | solution.py:197
  58.6 1.6 %collective-permute-done.23.refs_3_ = bf16[256,256]{1,0:T(8,128)(2,1)S(1)} collective-permute-done((bf16[256,256]{1,0:T(8,128)(2,1)S(1)}, bf16[256,256]{1,0:T(8,128)(2,1)S(1)}, u32[]{:S(2)}, u32[]{:S(2)}) %collective-permute-start.23) | collective-permute-done | bytes 131104 | tf_op jit(solution)/shard_map/ppermute | solution.py:197
  60.2 0.8 %last.1 = (bf16[256,256]{1,0:T(8,128)(2,1)}, f32[256,256]{1,0:T(8,128)}) custom-call(f32[256,256]{1,0:T(8,128)S(1)} %get-tuple-element.27.grad_agg, bf16[256,256]{1,0:T(8,128)(2,1)S(1)} %add_convert_fusion.own, bf16[256,256]{1,0:T(8,128)(2,1)S(1)} %collective-permute-done.13.other, bf16[256,256]{1,0:T(8,128)(2,1)S(1)} %get-tuple-element.31.refs_0_, ...), custom_call_target="tpu_custom_call" | custom-call | flops 1000000 | bytes 1048576 | tf_op jit(solution)/shard_map/last/pallas_call | solution.py:35
  (42 shorter events, 4.3 us)
Async XLA Ops:
  0.6 8.8 %collective-permute-start.2 = (bf16[256,256]{1,0:T(8,128)(2,1)}, bf16[256,256]{1,0:T(8,128)(2,1)S(1)}, u32[]{:S(2)}, u32[]{:S(2)}) collective-permute-start(bf16[256,256]{1,0:T(8,128)(2,1)} %refs_4_.1), channel_id=1, source_target_pairs={{0,24},{8,16},{16,8},{24,0},{1,25},{9,17},{17,9},{25,1},{2,26},{10... | collective-permute-start | bytes 393224 | tf_op jit(solution)/shard_map/ppermute | solution.py:197
  4.6 6.5 %collective-permute-start.1 = (bf16[256,256]{1,0:T(8,128)(2,1)}, bf16[256,256]{1,0:T(8,128)(2,1)S(1)}, u32[]{:S(2)}, u32[]{:S(2)}) collective-permute-start(bf16[256,256]{1,0:T(8,128)(2,1)} %refs_4_.1), channel_id=1, source_target_pairs={{0,16},{8,24},{16,0},{24,8},{1,17},{9,25},{17,1},{25,9},{2,18},{10... | collective-permute-start | bytes 393224 | tf_op jit(solution)/shard_map/ppermute | solution.py:197
  5.1 6.3 %collective-permute-start = (bf16[256,256]{1,0:T(8,128)(2,1)}, bf16[256,256]{1,0:T(8,128)(2,1)S(1)}, u32[]{:S(2)}, u32[]{:S(2)}) collective-permute-start(bf16[256,256]{1,0:T(8,128)(2,1)} %refs_4_.1), channel_id=1, source_target_pairs={{0,8},{8,0},{16,24},{24,16},{1,9},{9,1},{17,25},{25,17},{2,10},{10... | collective-permute-start | bytes 393224 | tf_op jit(solution)/shard_map/ppermute | solution.py:197
  5.9 1.0 %copy-start.3 = (s32[1,1,64,16,128]{4,3,2,1,0:T(8,128)S(1)}, s32[1,1,64,16,128]{4,3,2,1,0:T(8,128)}, u32[]{:S(2)}) copy-start(s32[1,1,64,16,128]{4,3,2,1,0:T(8,128)} %param.11) | copy-start | bytes 1572868
  6.9 0.7 %copy-start.4 = (s32[1,1,2,64]{3,2,1,0:T(2,128)S(1)}, s32[1,1,2,64]{3,2,1,0:T(2,128)}, u32[]{:S(2)}) copy-start(s32[1,1,2,64]{3,2,1,0:T(2,128)} %param.9) | copy-start | bytes 1540
  7.6 3.8 %copy-start = (bf16[256,256]{1,0:T(8,128)(2,1)S(1)}, bf16[256,256]{1,0:T(8,128)(2,1)}, u32[]{:S(2)}) copy-start(bf16[256,256]{1,0:T(8,128)(2,1)} %refs_4_.1) | copy-start | bytes 393220
  12.3 1.6 %collective-permute-start.3 = (bf16[2,272,256]{2,1,0:T(8,128)(2,1)S(1)}, bf16[2,272,256]{2,1,0:T(8,128)(2,1)S(1)}, u32[]{:S(2)}, u32[]{:S(2)}) collective-permute-start(bf16[2,272,256]{2,1,0:T(8,128)(2,1)S(1)} %forward_near_other.1), channel_id=1, source_target_pairs={{0,1},{1,0},{2,3},{3,2},{4,5},{5,4},{6,7},{7,6},{8,9},{9,8},{10,11... | collective-permute-start | bytes 835592 | tf_op jit(solution)/shard_map/ppermute | solution.py:203
  12.4 3.3 %collective-permute-start.5 = (bf16[2,272,256]{2,1,0:T(8,128)(2,1)S(1)}, bf16[2,272,256]{2,1,0:T(8,128)(2,1)S(1)}, u32[]{:S(2)}, u32[]{:S(2)}) collective-permute-start(bf16[2,272,256]{2,1,0:T(8,128)(2,1)S(1)} %get-tuple-element.23), channel_id=1, source_target_pairs={{0,1},{1,0},{2,3},{3,2},{4,5},{5,4},{6,7},{7,6},{8,9},{9,8},{10,11... | collective-permute-start | bytes 835592 | tf_op jit(solution)/shard_map/ppermute | solution.py:203
  13.4 15.9 %copy-start.1 = (bf16[256,256]{1,0:T(8,128)(2,1)S(1)}, bf16[256,256]{1,0:T(8,128)(2,1)}, u32[]{:S(2)}) copy-start(bf16[256,256]{1,0:T(8,128)(2,1)} %refs_5_.1) | copy-start | bytes 393220
  13.4 15.9 %copy-start.2 = (bf16[256,256]{1,0:T(8,128)(2,1)S(1)}, bf16[256,256]{1,0:T(8,128)(2,1)}, u32[]{:S(2)}) copy-start(bf16[256,256]{1,0:T(8,128)(2,1)} %refs_6_.1) | copy-start | bytes 393220
  14.0 7.9 %collective-permute-start.4 = (bf16[272,256]{1,0:T(8,128)(2,1)S(1)}, bf16[272,256]{1,0:T(8,128)(2,1)S(1)}, u32[]{:S(2)}, u32[]{:S(2)}) collective-permute-start(bf16[272,256]{1,0:T(8,128)(2,1)S(1)} %get-tuple-element.22), channel_id=1, source_target_pairs={{0,2},{1,3},{2,0},{3,1},{4,6},{5,7},{6,4},{7,5},{8,10},{9,11},{10,... | collective-permute-start | bytes 417800 | tf_op jit(solution)/shard_map/ppermute | solution.py:200
  15.7 13.5 %collective-permute-start.6 = (bf16[272,256]{1,0:T(8,128)(2,1)S(1)}, bf16[272,256]{1,0:T(8,128)(2,1)S(1)}, u32[]{:S(2)}, u32[]{:S(2)}) collective-permute-start(bf16[272,256]{1,0:T(8,128)(2,1)S(1)} %get-tuple-element.24), channel_id=1, source_target_pairs={{0,4},{1,5},{2,6},{3,7},{4,0},{5,1},{6,2},{7,3},{8,12},{9,13},{10,... | collective-permute-start | bytes 417800 | tf_op jit(solution)/shard_map/ppermute | solution.py:200
  18.4 10.8 %collective-permute-start.7 = (bf16[272,256]{1,0:T(8,128)(2,1)S(1)}, bf16[272,256]{1,0:T(8,128)(2,1)S(1)}, u32[]{:S(2)}, u32[]{:S(2)}) collective-permute-start(bf16[272,256]{1,0:T(8,128)(2,1)S(1)} %get-tuple-element.25), channel_id=1, source_target_pairs={{0,6},{1,7},{2,4},{3,5},{4,2},{5,3},{6,0},{7,1},{8,14},{9,15},{10,... | collective-permute-start | bytes 417800 | tf_op jit(solution)/shard_map/ppermute | solution.py:200
  29.9 6.9 %collective-permute-start.8 = (bf16[256,256]{1,0:T(8,128)(2,1)S(1)}, bf16[256,256]{1,0:T(8,128)(2,1)S(1)}, u32[]{:S(2)}, u32[]{:S(2)}) collective-permute-start(bf16[256,256]{1,0:T(8,128)(2,1)S(1)} %weight_part.1), channel_id=1, source_target_pairs={{0,2},{1,3},{2,0},{3,1},{4,6},{5,7},{6,4},{7,5},{8,10},{9,11},{10,... | collective-permute-start | bytes 393224 | tf_op jit(solution)/shard_map/ppermute | solution.py:200
  32.4 9.8 %collective-permute-start.18 = (bf16[256,256]{1,0:T(8,128)(2,1)S(1)}, bf16[256,256]{1,0:T(8,128)(2,1)S(1)}, u32[]{:S(2)}, u32[]{:S(2)}) collective-permute-start(bf16[256,256]{1,0:T(8,128)(2,1)S(1)} %get-tuple-element.30.refs_1_), channel_id=1, source_target_pairs={{0,6},{1,7},{2,4},{3,5},{4,2},{5,3},{6,0},{7,1},{8,14},{9,15},{10,... | collective-permute-start | bytes 393224 | tf_op jit(solution)/shard_map/ppermute | solution.py:200
  35.0 10.4 %collective-permute-start.17 = (bf16[256,256]{1,0:T(8,128)(2,1)S(1)}, bf16[256,256]{1,0:T(8,128)(2,1)S(1)}, u32[]{:S(2)}, u32[]{:S(2)}) collective-permute-start(bf16[256,256]{1,0:T(8,128)(2,1)S(1)} %get-tuple-element.30.refs_1_), channel_id=1, source_target_pairs={{0,4},{1,5},{2,6},{3,7},{4,0},{5,1},{6,2},{7,3},{8,12},{9,13},{10,... | collective-permute-start | bytes 393224 | tf_op jit(solution)/shard_map/ppermute | solution.py:200
  35.0 10.4 %collective-permute-start.14 = (bf16[256,256]{1,0:T(8,128)(2,1)S(1)}, bf16[256,256]{1,0:T(8,128)(2,1)S(1)}, u32[]{:S(2)}, u32[]{:S(2)}) collective-permute-start(bf16[256,256]{1,0:T(8,128)(2,1)S(1)} %get-tuple-element.30.refs_1_), channel_id=1, source_target_pairs={{0,2},{1,3},{2,0},{3,1},{4,6},{5,7},{6,4},{7,5},{8,10},{9,11},{10,... | collective-permute-start | bytes 393224 | tf_op jit(solution)/shard_map/ppermute | solution.py:200
  36.9 9.0 %collective-permute-start.11 = (bf16[256,256]{1,0:T(8,128)(2,1)S(1)}, bf16[256,256]{1,0:T(8,128)(2,1)S(1)}, u32[]{:S(2)}, u32[]{:S(2)}) collective-permute-start(bf16[256,256]{1,0:T(8,128)(2,1)S(1)} %add_convert_fusion.2), channel_id=1, source_target_pairs={{0,24},{8,16},{16,8},{24,0},{1,25},{9,17},{17,9},{25,1},{2,26},{10... | collective-permute-start | bytes 393224 | tf_op jit(solution)/shard_map/ppermute | solution.py:197
  38.6 7.3 %collective-permute-start.10 = (bf16[256,256]{1,0:T(8,128)(2,1)S(1)}, bf16[256,256]{1,0:T(8,128)(2,1)S(1)}, u32[]{:S(2)}, u32[]{:S(2)}) collective-permute-start(bf16[256,256]{1,0:T(8,128)(2,1)S(1)} %add_convert_fusion.2), channel_id=1, source_target_pairs={{0,16},{8,24},{16,0},{24,8},{1,17},{9,25},{17,1},{25,9},{2,18},{10... | collective-permute-start | bytes 393224 | tf_op jit(solution)/shard_map/ppermute | solution.py:197
  42.3 5.0 %collective-permute-start.9 = (bf16[256,256]{1,0:T(8,128)(2,1)S(1)}, bf16[256,256]{1,0:T(8,128)(2,1)S(1)}, u32[]{:S(2)}, u32[]{:S(2)}) collective-permute-start(bf16[256,256]{1,0:T(8,128)(2,1)S(1)} %add_convert_fusion.2), channel_id=1, source_target_pairs={{0,8},{8,0},{16,24},{24,16},{1,9},{9,1},{17,25},{25,17},{2,10},{10... | collective-permute-start | bytes 393224 | tf_op jit(solution)/shard_map/ppermute | solution.py:197
  45.3 5.2 %collective-permute-start.15 = (bf16[256,256]{1,0:T(8,128)(2,1)S(1)}, bf16[256,256]{1,0:T(8,128)(2,1)S(1)}, u32[]{:S(2)}, u32[]{:S(2)}) collective-permute-start(bf16[256,256]{1,0:T(8,128)(2,1)S(1)} %get-tuple-element.30.refs_1_), channel_id=1, source_target_pairs={{0,1},{1,0},{2,3},{3,2},{4,5},{5,4},{6,7},{7,6},{8,9},{9,8},{10,11... | collective-permute-start | bytes 393224 | tf_op jit(solution)/shard_map/ppermute | solution.py:203
  45.4 5.9 %collective-permute-start.20 = (bf16[256,256]{1,0:T(8,128)(2,1)S(1)}, bf16[256,256]{1,0:T(8,128)(2,1)S(1)}, u32[]{:S(2)}, u32[]{:S(2)}) collective-permute-start(bf16[256,256]{1,0:T(8,128)(2,1)S(1)} %collective-permute-done.18.refs_3_), channel_id=1, source_target_pairs={{0,1},{1,0},{2,3},{3,2},{4,5},{5,4},{6,7},{7,6},{8,9},{9,8},{10,11... | collective-permute-start | bytes 393224 | tf_op jit(solution)/shard_map/ppermute | solution.py:203
  45.9 5.4 %collective-permute-start.19 = (bf16[256,256]{1,0:T(8,128)(2,1)S(1)}, bf16[256,256]{1,0:T(8,128)(2,1)S(1)}, u32[]{:S(2)}, u32[]{:S(2)}) collective-permute-start(bf16[256,256]{1,0:T(8,128)(2,1)S(1)} %collective-permute-done.17.refs_2_), channel_id=1, source_target_pairs={{0,1},{1,0},{2,3},{3,2},{4,5},{5,4},{6,7},{7,6},{8,9},{9,8},{10,11... | collective-permute-start | bytes 393224 | tf_op jit(solution)/shard_map/ppermute | solution.py:203
  45.9 4.6 %collective-permute-start.16 = (bf16[256,256]{1,0:T(8,128)(2,1)S(1)}, bf16[256,256]{1,0:T(8,128)(2,1)S(1)}, u32[]{:S(2)}, u32[]{:S(2)}) collective-permute-start(bf16[256,256]{1,0:T(8,128)(2,1)S(1)} %collective-permute-done.14.refs_2_), channel_id=1, source_target_pairs={{0,1},{1,0},{2,3},{3,2},{4,5},{5,4},{6,7},{7,6},{8,9},{9,8},{10,11... | collective-permute-start | bytes 393224 | tf_op jit(solution)/shard_map/ppermute | solution.py:203
  47.3 8.3 %collective-permute-start.12 = (bf16[256,256]{1,0:T(8,128)(2,1)S(1)}, bf16[256,256]{1,0:T(8,128)(2,1)S(1)}, u32[]{:S(2)}, u32[]{:S(2)}) collective-permute-start(bf16[256,256]{1,0:T(8,128)(2,1)S(1)} %add_convert_fusion.1), channel_id=1, source_target_pairs={{0,4},{1,5},{2,6},{3,7},{4,0},{5,1},{6,2},{7,3},{8,12},{9,13},{10,... | collective-permute-start | bytes 393224 | tf_op jit(solution)/shard_map/ppermute | solution.py:200
  52.0 5.1 %collective-permute-start.21 = (bf16[256,256]{1,0:T(8,128)(2,1)S(1)}, bf16[256,256]{1,0:T(8,128)(2,1)S(1)}, u32[]{:S(2)}, u32[]{:S(2)}) collective-permute-start(bf16[256,256]{1,0:T(8,128)(2,1)S(1)} %get-tuple-element.32), channel_id=1, source_target_pairs={{0,8},{8,0},{16,24},{24,16},{1,9},{9,1},{17,25},{25,17},{2,10},{10... | collective-permute-start | bytes 393224 | tf_op jit(solution)/shard_map/ppermute | solution.py:197
  53.6 5.0 %collective-permute-start.22 = (bf16[256,256]{1,0:T(8,128)(2,1)S(1)}, bf16[256,256]{1,0:T(8,128)(2,1)S(1)}, u32[]{:S(2)}, u32[]{:S(2)}) collective-permute-start(bf16[256,256]{1,0:T(8,128)(2,1)S(1)} %get-tuple-element.33), channel_id=1, source_target_pairs={{0,16},{8,24},{16,0},{24,8},{1,17},{9,25},{17,1},{25,9},{2,18},{10... | collective-permute-start | bytes 393224 | tf_op jit(solution)/shard_map/ppermute | solution.py:197
  54.3 5.9 %collective-permute-start.23 = (bf16[256,256]{1,0:T(8,128)(2,1)S(1)}, bf16[256,256]{1,0:T(8,128)(2,1)S(1)}, u32[]{:S(2)}, u32[]{:S(2)}) collective-permute-start(bf16[256,256]{1,0:T(8,128)(2,1)S(1)} %get-tuple-element.34), channel_id=1, source_target_pairs={{0,24},{8,16},{16,8},{24,0},{1,25},{9,17},{17,9},{25,1},{2,26},{10... | collective-permute-start | bytes 393224 | tf_op jit(solution)/shard_map/ppermute | solution.py:197
  55.6 4.5 %collective-permute-start.13 = (bf16[256,256]{1,0:T(8,128)(2,1)S(1)}, bf16[256,256]{1,0:T(8,128)(2,1)S(1)}, u32[]{:S(2)}, u32[]{:S(2)}) collective-permute-start(bf16[256,256]{1,0:T(8,128)(2,1)S(1)} %add_convert_fusion.own), channel_id=1, source_target_pairs={{0,1},{1,0},{2,3},{3,2},{4,5},{5,4},{6,7},{7,6},{8,9},{9,8},{10,11... | collective-permute-start | bytes 393224 | tf_op jit(solution)/shard_map/ppermute | solution.py:203

commit v6 on v5

--- a/solution.py
+++ b/solution.py
@@ -140,32 +140,53 @@
     scaled_ref[...] = (grad_agg * scale_rows).astype(bf16)
 
 
-def weight_kernel(agg_t, grad_pre, out_ref):
-    out_ref[...] = jnp.dot(agg_t[...], grad_pre[...], preferred_element_type=f32).astype(bf16)
-
-
-def backward_near(spots, *refs):
-    st_ref, grads, out = refs[0], refs[1 : 1 + len(spots)], refs[1 + len(spots)]
-    gathered = refs[-1]
-    rows, _ = grads[0].shape
-    for i, ref in enumerate(grads):
+def weight_kernel(agg_t, grad_pre, keep_ref, send_ref):
+    my_col = lax.axis_index("col")
+    core, parity = my_col % 2, (my_col // 2) % 2
+    quarter = agg_t.shape[0] // 4
+    part = jnp.dot(agg_t[...], grad_pre[...], preferred_element_type=f32).astype(bf16)
+    cut = [part[i * quarter : (i + 1) * quarter] for i in range(4)]
+    for flip, ref in enumerate((keep_ref, send_ref)):
+        here = (core ^ flip) == 0
+        first, second = jnp.where(here, cut[0], cut[2]), jnp.where(here, cut[1], cut[3])
+        ref[:quarter, :] = jnp.where(parity == 0, first, second)
+        ref[quarter:, :] = jnp.where(parity == 0, second, first)
+
+
+def last_kernel(n_row, grad_agg, *refs):
+    backs, quarters, (feat_ref, weight_ref) = refs[:n_row], refs[n_row:-2], refs[-2:]
+    feat_ref[...] = (tree_sum([ref[...] for ref in backs]) + grad_agg[...]).astype(bf16)
+    my_col = lax.axis_index("col")
+    core, parity = my_col % 2, (my_col // 2) % 2
+    quarter = quarters[0].shape[0]
+    for i, ref in enumerate(quarters):
+        at = ((core ^ (i % 2)) * 2 + (parity ^ (i // 2))) * quarter
+        weight_ref[pl.ds(pl.multiple_of(at, quarter), quarter), :] = ref[...].astype(f32)
+
+
+def gather_rows(refs, gathered):
+    rows, _ = refs[0].shape
+    for i, ref in enumerate(refs):
         gathered[i * rows : (i + 1) * rows, :] = ref[...]
+
+
+def backward_first(n_z, *refs):
+    st_ref, grads, out, gathered = refs[0], refs[1 : 1 + n_z], refs[-2], refs[-1]
+    gather_rows(grads, gathered)
+    rows = grads[0].shape[0]
     for j in range(out.shape[0] // rows):
         lines = slice(j * rows, (j + 1) * rows)
-        columns = jnp.concatenate([st_ref[lines, k * rows : (k + 1) * rows] for k in spots], axis=1)
-        out[lines, :] = jnp.dot(columns, gathered[...], preferred_element_type=f32)
-
-
-def backward_far(spots, n_row, *refs):
-    st_ref, near, grads, outs = refs[0], refs[1], refs[2 : 2 + len(spots)], refs[2 + len(spots) : 2 + len(spots) + n_row]
-    gathered = refs[-1]
-    rows, _ = grads[0].shape
-    for i, ref in enumerate(grads):
-        gathered[i * rows : (i + 1) * rows, :] = ref[...]
+        out[lines, :] = jnp.dot(st_ref[lines, : n_z * rows], gathered[...], preferred_element_type=f32)
+
+
+def backward_rest(n_z, n_row, *refs):
+    st_ref, product, grads, outs, gathered = refs[0], refs[1], refs[2 : 2 + n_z], refs[2 + n_z : -1], refs[-1]
+    gather_rows(grads, gathered)
+    rows = grads[0].shape[0]
     for j, out in enumerate(outs):
         lines = slice(j * rows, (j + 1) * rows)
-        columns = jnp.concatenate([st_ref[lines, k * rows : (k + 1) * rows] for k in spots], axis=1)
-        out[...] = (near[lines, :] + jnp.dot(columns, gathered[...], preferred_element_type=f32)).astype(out.dtype)
+        other = jnp.dot(st_ref[lines, n_z * rows :], gathered[...], preferred_element_type=f32)
+        out[...] = (product[lines, :] + other).astype(out.dtype)
 
 
 def tree_sum(values):
@@ -173,12 +194,6 @@
     while len(values) > 1:
         values = [values[i] + values[i + 1] for i in range(0, len(values), 2)]
     return values[0]
-
-
-def last_kernel(grad_agg, own, other, *refs):
-    total = tree_sum([ref[...] for ref in refs[:-2]])
-    refs[-2][...] = (total + grad_agg[...]).astype(bf16)
-    refs[-1][...] = own[...].astype(f32) + other[...].astype(f32)
 
 
 def per_device(features, weight, cotangent, tiles, tile_count, patterns):
@@ -246,39 +261,38 @@
     )
     far = [over_z(scaled, k) for k in range(2, n_z)]
 
-    (part,) = call(weight_kernel, "weight_part", [((width, width), bf16)], [agg_t, grad_pre], flops=2e9)
-    part = tree_sum([part, over_z(part, 1)]).astype(bf16)
+    keep, send = call(weight_kernel, "weight_part", [((width // 2, width), bf16)] * 2, [agg_t, grad_pre], flops=2e9)
+    half = tree_sum([keep, over_core(send)]).astype(bf16)
+    quarter = width // 4
+    part = tree_sum([half[:quarter], over_z(half[quarter:], 1)]).astype(bf16)
     part = tree_sum([part] + [over_row(part, k) for k in range(1, n_row)]).astype(bf16)
     for step in range(1, (n_z - 1).bit_length()):
         part = tree_sum([part, over_z(part, 1 << step)]).astype(bf16)
 
-    grads = [scaled, over_z(scaled, 1)]
-    grads = grads + [over_core(x) for x in grads]
+    grads = [scaled, over_z(scaled, 1)] + far
     (product,) = call(
-        functools.partial(backward_near, (0, 1, n_z, n_z + 1)),
-        "backward_near",
+        functools.partial(backward_first, n_z),
+        "backward_own",
         [((col_len, width), f32)],
         [st] + grads,
-        scratch=[pltpu.VMEM((4 * rows, width), bf16)],
+        scratch=[pltpu.VMEM((row_len, width), bf16)],
         flops=flops // 2,
     )
-    grads = far + [over_core(x) for x in far]
-    spots = tuple(range(2, n_z)) + tuple(range(n_z + 2, 2 * n_z))
     backs = call(
-        functools.partial(backward_far, spots, n_row),
-        "backward_far",
+        functools.partial(backward_rest, n_z, n_row),
+        "backward_other",
         [((rows, width), bf16)] * n_row,
-        [st, product] + grads,
-        scratch=[pltpu.VMEM((len(spots) * rows, width), bf16)],
+        [st, product] + [over_core(x) for x in grads],
+        scratch=[pltpu.VMEM((row_len, width), bf16)],
         flops=flops // 2,
     )
-
     backs = [backs[0]] + [over_row(backs[k], k) for k in range(1, n_row)]
+    straight = lax.ppermute(part, "col", [(i, i ^ 3) for i in range(n_col)])
     grad_features, grad_weight = call(
-        last_kernel,
+        functools.partial(last_kernel, n_row),
         "last",
         [((rows, width), bf16), ((width, width), f32)],
-        [grad_agg, part, over_core(part)] + backs,
+        [grad_agg] + backs + [part, over_core(part), over_z(part, 1), straight],
         final=(0, 1),
     )
     return activated, grad_features, grad_weight

time: 61.2 us -> 60.4 us (0.987)
  waiting for transfers between devices: 21.2 us -> 19.4 us
  starting transfers between devices: 29.1 us -> 30.7 us
    ppermute x9, waiting for transfers between devices: 6.53 us -> 4.65 us  [over_row(): return lax.ppermute(x, 'row', [(i, i ^ k) for i in range(n_row)])]
    ppermute x8 -> x9, waiting for transfers between devices: 14.6 us -> 12.8 us  [over_z(): return lax.ppermute(x, 'col', [(i, i ^ 2 * k) for i in range(n_col)])]
    ppermute x7 -> x8, starting transfers between devices: 1.66 us -> 3.17 us  [over_core(): return lax.ppermute(x, 'col', [(i, i ^ 1) for i in range(n_col)])]
    ppermute x7 -> x8, waiting for transfers between devices: 0.11 us -> 1.55 us  [over_core(): return lax.ppermute(x, 'col', [(i, i ^ 1) for i in range(n_col)])]
    ppermute x0 -> x1, starting transfers between devices: none -> 1.4 us  [per_device(): straight = lax.ppermute(part, 'col', [(i, i ^ 3) for i in range(n_col)])]
    ppermute x8 -> x9, starting transfers between devices: 14.7 us -> 13.4 us  [over_z(): return lax.ppermute(x, 'col', [(i, i ^ 2 * k) for i in range(n_col)])]
  transfers between devices with their start and end apart: 24 -> 27, of which waited for: 12 -> 11; matrix products, arithmetic and copies ran while one was open for 1% -> 1% of each run, Pallas kernels for 7% -> 6%
where the time goes in v6:
time: 60.4 us; the launch traced here: 60.2 us
  starting transfers between devices  30.7 us (51%)
  waiting for transfers between devices  19.4 us (32%)
  Pallas kernels  6.21 us (10%)
  local copies, waits for them, and re-layouts  2.39 us (4%)
  between operations  1.49 us (2%)
    ppermute x9, starting transfers between devices, over_z(): return lax.ppermute(x, 'col', [(i, i ^ 2 * k) for i in range(n_col)])  13.4 us
    ppermute x9, waiting for transfers between devices, over_z(): return lax.ppermute(x, 'col', [(i, i ^ 2 * k) for i in range(n_col)])  12.8 us
    ppermute x9, starting transfers between devices, over_row(): return lax.ppermute(x, 'row', [(i, i ^ k) for i in range(n_row)])  12.8 us
    pallas_call x12, Pallas kernels, call(): pl.pallas_call(body, out_shape=shapes, in_specs=smem(n_smem) + [pl.BlockS...  6.21 us
    ppermute x9, waiting for transfers between devices, over_row(): return lax.ppermute(x, 'row', [(i, i ^ k) for i in range(n_row)])  4.65 us
    ppermute x8, starting transfers between devices, over_core(): return lax.ppermute(x, 'col', [(i, i ^ 1) for i in range(n_col)])  3.17 us
    unnamed x11, local copies, waits for them, and re-layouts  2.38 us
    ppermute x8, waiting for transfers between devices, over_core(): return lax.ppermute(x, 'col', [(i, i ^ 1) for i in range(n_col)])  1.55 us
  transfers between devices with their start and end apart: 27, of which 11 were waited for; matrix products, arithmetic and copies ran while one was open for 1% of the time, Pallas kernels for 6%

profile of v6, /device:TPU:0, one launch (start us, length us, event | category | flops | bytes accessed | tf_op | source)
XLA Modules:
  0.0 60.2 jit_solution(5185545837050777101)
XLA Ops:
  0.6 4.0 %collective-permute-start.2 = (bf16[256,256]{1,0:T(8,128)(2,1)}, bf16[256,256]{1,0:T(8,128)(2,1)S(1)}, u32[]{:S(2)}, u32[]{:S(2)}) collective-permute-start(bf16[256,256]{1,0:T(8,128)(2,1)} %refs_4_.1), channel_id=1, source_target_pairs={{0,24},{8,16},{16,8},{24,0},{1,25},{9,17},{17,9},{25,1},{2,26},{10... | collective-permute-start | bytes 393224 | tf_op jit(solution)/shard_map/ppermute | solution.py:212
  4.6 0.5 collective-permute-start.1
  5.9 1.0 %copy-done.3 = s32[1,1,64,16,128]{4,3,2,1,0:T(8,128)S(1)} copy-done((s32[1,1,64,16,128]{4,3,2,1,0:T(8,128)S(1)}, s32[1,1,64,16,128]{4,3,2,1,0:T(8,128)}, u32[]{:S(2)}) %copy-start.3) | copy-done | bytes 524312
  6.9 0.7 %copy-done.4 = s32[1,1,2,64]{3,2,1,0:T(2,128)S(1)} copy-done((s32[1,1,2,64]{3,2,1,0:T(2,128)S(1)}, s32[1,1,2,64]{3,2,1,0:T(2,128)}, u32[]{:S(2)}) %copy-start.4) | copy-done | bytes 536
  7.6 1.3 %build.1.refs_0_.st_ref = bf16[1024,2048]{1,0:T(8,128)(2,1)S(1)} custom-call(s32[2,64]{1,0:T(2,128)S(1)} %bitcast.3, s32[1,1]{1,0:T(1,128)S(6)} %copy.10.count, s32[64,16,128]{2,1,0:T(8,128)S(1)} %bitcast.2), custom_call_target="tpu_custom_call" | custom-call | flops 4000000000 | bytes 1048576 | tf_op jit(solution)/shard_map/build/pallas_call | solution.py:35
  8.9 2.2 %collective-permute-done.1.refs_3_ = bf16[256,256]{1,0:T(8,128)(2,1)S(1)} collective-permute-done((bf16[256,256]{1,0:T(8,128)(2,1)}, bf16[256,256]{1,0:T(8,128)(2,1)S(1)}, u32[]{:S(2)}, u32[]{:S(2)}) %collective-permute-start.1) | collective-permute-done | bytes 131104 | tf_op jit(solution)/shard_map/ppermute | solution.py:212
  12.4 0.5 collective-permute-start.5
  14.0 1.6 %collective-permute-start.4 = (bf16[272,256]{1,0:T(8,128)(2,1)S(1)}, bf16[272,256]{1,0:T(8,128)(2,1)S(1)}, u32[]{:S(2)}, u32[]{:S(2)}) collective-permute-start(bf16[272,256]{1,0:T(8,128)(2,1)S(1)} %get-tuple-element.24), channel_id=1, source_target_pairs={{0,2},{1,3},{2,0},{3,1},{4,6},{5,7},{6,4},{7,5},{8,10},{9,11},{10,... | collective-permute-start | bytes 417800 | tf_op jit(solution)/shard_map/ppermute | solution.py:215
  15.7 2.7 %collective-permute-start.6 = (bf16[272,256]{1,0:T(8,128)(2,1)S(1)}, bf16[272,256]{1,0:T(8,128)(2,1)S(1)}, u32[]{:S(2)}, u32[]{:S(2)}) collective-permute-start(bf16[272,256]{1,0:T(8,128)(2,1)S(1)} %get-tuple-element.26), channel_id=1, source_target_pairs={{0,4},{1,5},{2,6},{3,7},{4,0},{5,1},{6,2},{7,3},{8,12},{9,13},{10,... | collective-permute-start | bytes 417800 | tf_op jit(solution)/shard_map/ppermute | solution.py:215
  18.6 3.3 %collective-permute-done.4.refs_1_ = bf16[272,256]{1,0:T(8,128)(2,1)S(1)} collective-permute-done((bf16[272,256]{1,0:T(8,128)(2,1)S(1)}, bf16[272,256]{1,0:T(8,128)(2,1)S(1)}, u32[]{:S(2)}, u32[]{:S(2)}) %collective-permute-start.4) | collective-permute-done | bytes 139296 | tf_op jit(solution)/shard_map/ppermute | solution.py:215
  21.9 7.3 %collective-permute-done.6.refs_2_ = bf16[272,256]{1,0:T(8,128)(2,1)S(1)} collective-permute-done((bf16[272,256]{1,0:T(8,128)(2,1)S(1)}, bf16[272,256]{1,0:T(8,128)(2,1)S(1)}, u32[]{:S(2)}, u32[]{:S(2)}) %collective-permute-start.6) | collective-permute-done | bytes 139296 | tf_op jit(solution)/shard_map/ppermute | solution.py:215
  30.0 1.2 %collective-permute-done.18 = bf16[128,256]{1,0:T(8,128)(2,1)S(1)} collective-permute-done((bf16[128,256]{1,0:T(8,128)(2,1)S(1)}, bf16[128,256]{1,0:T(8,128)(2,1)S(1)}, u32[]{:S(2)}, u32[]{:S(2)}) %collective-permute-start.18) | collective-permute-done | bytes 65568 | tf_op jit(solution)/shard_map/ppermute | solution.py:218
  31.3 2.5 %collective-permute-start.19 = (bf16[64,256]{1,0:T(8,128)(2,1)S(1)}, bf16[64,256]{1,0:T(8,128)(2,1)S(1)}, u32[]{:S(2)}, u32[]{:S(2)}) collective-permute-start(bf16[64,256]{1,0:T(8,128)(2,1)S(1)} %slice.9), channel_id=1, source_target_pairs={{0,2},{1,3},{2,0},{3,1},{4,6},{5,7},{6,4},{7,5},{8,10},{9,11},{10,... | collective-permute-start | bytes 98312 | tf_op jit(solution)/shard_map/ppermute | solution.py:215
  33.8 2.6 %collective-permute-start.10 = (bf16[256,256]{1,0:T(8,128)(2,1)S(1)}, bf16[256,256]{1,0:T(8,128)(2,1)S(1)}, u32[]{:S(2)}, u32[]{:S(2)}) collective-permute-start(bf16[256,256]{1,0:T(8,128)(2,1)S(1)} %get-tuple-element.30.refs_1_), channel_id=1, source_target_pairs={{0,6},{1,7},{2,4},{3,5},{4,2},{5,3},{6,0},{7,1},{8,14},{9,15},{10,... | collective-permute-start | bytes 393224 | tf_op jit(solution)/shard_map/ppermute | solution.py:215
  36.3 1.8 %collective-permute-start.8 = (bf16[256,256]{1,0:T(8,128)(2,1)S(1)}, bf16[256,256]{1,0:T(8,128)(2,1)S(1)}, u32[]{:S(2)}, u32[]{:S(2)}) collective-permute-start(bf16[256,256]{1,0:T(8,128)(2,1)S(1)} %get-tuple-element.30.refs_1_), channel_id=1, source_target_pairs={{0,2},{1,3},{2,0},{3,1},{4,6},{5,7},{6,4},{7,5},{8,10},{9,11},{10,... | collective-permute-start | bytes 393224 | tf_op jit(solution)/shard_map/ppermute | solution.py:215
  38.2 1.8 %collective-permute-start.22 = (bf16[64,256]{1,0:T(8,128)(2,1)S(1)}, bf16[64,256]{1,0:T(8,128)(2,1)S(1)}, u32[]{:S(2)}, u32[]{:S(2)}) collective-permute-start(bf16[64,256]{1,0:T(8,128)(2,1)S(1)} %add_convert_fusion.3), channel_id=1, source_target_pairs={{0,24},{8,16},{16,8},{24,0},{1,25},{9,17},{17,9},{25,1},{2,26},{10... | collective-permute-start | bytes 98312 | tf_op jit(solution)/shard_map/ppermute | solution.py:212
  40.0 1.3 %collective-permute-start.21 = (bf16[64,256]{1,0:T(8,128)(2,1)S(1)}, bf16[64,256]{1,0:T(8,128)(2,1)S(1)}, u32[]{:S(2)}, u32[]{:S(2)}) collective-permute-start(bf16[64,256]{1,0:T(8,128)(2,1)S(1)} %add_convert_fusion.3), channel_id=1, source_target_pairs={{0,16},{8,24},{16,0},{24,8},{1,17},{9,25},{17,1},{25,9},{2,18},{10... | collective-permute-start | bytes 98312 | tf_op jit(solution)/shard_map/ppermute | solution.py:212
  41.3 1.8 %collective-permute-done.22 = bf16[64,256]{1,0:T(8,128)(2,1)S(1)} collective-permute-done((bf16[64,256]{1,0:T(8,128)(2,1)S(1)}, bf16[64,256]{1,0:T(8,128)(2,1)S(1)}, u32[]{:S(2)}, u32[]{:S(2)}) %collective-permute-start.22) | collective-permute-done | bytes 32800 | tf_op jit(solution)/shard_map/ppermute | solution.py:212
  43.1 1.5 %collective-permute-start.20 = (bf16[64,256]{1,0:T(8,128)(2,1)S(1)}, bf16[64,256]{1,0:T(8,128)(2,1)S(1)}, u32[]{:S(2)}, u32[]{:S(2)}) collective-permute-start(bf16[64,256]{1,0:T(8,128)(2,1)S(1)} %add_convert_fusion.3), channel_id=1, source_target_pairs={{0,8},{8,0},{16,24},{24,16},{1,9},{9,1},{17,25},{25,17},{2,10},{10... | collective-permute-start | bytes 98312 | tf_op jit(solution)/shard_map/ppermute | solution.py:212
  44.6 0.5 collective-permute-start.14
  45.1 2.2 %collective-permute-done.9.refs_3_ = bf16[256,256]{1,0:T(8,128)(2,1)S(1)} collective-permute-done((bf16[256,256]{1,0:T(8,128)(2,1)S(1)}, bf16[256,256]{1,0:T(8,128)(2,1)S(1)}, u32[]{:S(2)}, u32[]{:S(2)}) %collective-permute-start.9) | collective-permute-done | bytes 131104 | tf_op jit(solution)/shard_map/ppermute | solution.py:215
  47.3 0.5 collective-permute-start.12
  48.2 0.7 %backward_own.1.refs_1_ = f32[1024,256]{1,0:T(8,128)S(1)} custom-call(bf16[1024,2048]{1,0:T(8,128)(2,1)S(1)} %build.1.refs_0_.st_ref, bf16[256,256]{1,0:T(8,128)(2,1)S(1)} %get-tuple-element.30.refs_1_, bf16[256,256]{1,0:T(8,128)(2,1)S(1)} %collective-permute-done.8.refs_2_, bf16[256,256]{1,0:T(8,128)(2,1)S(1)} %collective-permute-done.9.refs_3_, ...), custom_call_target="tpu_custom_call" | custom-call | flops 536870912 | bytes 1048576 | tf_op jit(solution)/shard_map/backward_own/pallas_call | solution.py:35
  48.9 0.7 %backward_other.1 = (bf16[256,256]{1,0:T(8,128)(2,1)S(1)}, bf16[256,256]{1,0:T(8,128)(2,1)S(1)}, bf16[256,256]{1,0:T(8,128)(2,1)S(1)}, bf16[256,256]{1,0:T(8,128)(2,1)S(1)}) custom-call(bf16[1024,2048]{1,0:T(8,128)(2,1)S(1)} %build.1.refs_0_.st_ref, f32[1024,256]{1,0:T(8,128)S(1)} %backward_own.1.refs_1_, ...), custom_call_target="tpu_custom_call" | custom-call | flops 536870912 | bytes 1048576 | tf_op jit(solution)/shard_map/backward_other/pallas_call | solution.py:35
  49.6 1.6 %collective-permute-start.15 = (bf16[256,256]{1,0:T(8,128)(2,1)S(1)}, bf16[256,256]{1,0:T(8,128)(2,1)S(1)}, u32[]{:S(2)}, u32[]{:S(2)}) collective-permute-start(bf16[256,256]{1,0:T(8,128)(2,1)S(1)} %get-tuple-element.32), channel_id=1, source_target_pairs={{0,8},{8,0},{16,24},{24,16},{1,9},{9,1},{17,25},{25,17},{2,10},{10... | collective-permute-start | bytes 393224 | tf_op jit(solution)/shard_map/ppermute | solution.py:212
  51.2 0.7 %collective-permute-start.16 = (bf16[256,256]{1,0:T(8,128)(2,1)S(1)}, bf16[256,256]{1,0:T(8,128)(2,1)S(1)}, u32[]{:S(2)}, u32[]{:S(2)}) collective-permute-start(bf16[256,256]{1,0:T(8,128)(2,1)S(1)} %get-tuple-element.33), channel_id=1, source_target_pairs={{0,16},{8,24},{16,0},{24,8},{1,17},{9,25},{17,1},{25,9},{2,18},{10... | collective-permute-start | bytes 393224 | tf_op jit(solution)/shard_map/ppermute | solution.py:212
  52.0 1.2 %collective-permute-start.17 = (bf16[256,256]{1,0:T(8,128)(2,1)S(1)}, bf16[256,256]{1,0:T(8,128)(2,1)S(1)}, u32[]{:S(2)}, u32[]{:S(2)}) collective-permute-start(bf16[256,256]{1,0:T(8,128)(2,1)S(1)} %get-tuple-element.34), channel_id=1, source_target_pairs={{0,24},{8,16},{16,8},{24,0},{1,25},{9,17},{17,9},{25,1},{2,26},{10... | collective-permute-start | bytes 393224 | tf_op jit(solution)/shard_map/ppermute | solution.py:212
  53.2 1.4 %collective-permute-start.26 = (bf16[64,256]{1,0:T(8,128)(2,1)S(1)}, bf16[64,256]{1,0:T(8,128)(2,1)S(1)}, u32[]{:S(2)}, u32[]{:S(2)}) collective-permute-start(bf16[64,256]{1,0:T(8,128)(2,1)S(1)} %add_convert_fusion.1.refs_4_), channel_id=1, source_target_pairs={{0,3},{1,2},{2,1},{3,0},{4,7},{5,6},{6,5},{7,4},{8,11},{9,10},{10,... | collective-permute-start | bytes 98312 | tf_op jit(solution)/shard_map/ppermute | solution.py:290
  54.6 1.6 %collective-permute-start.25 = (bf16[64,256]{1,0:T(8,128)(2,1)S(1)}, bf16[64,256]{1,0:T(8,128)(2,1)S(1)}, u32[]{:S(2)}, u32[]{:S(2)}) collective-permute-start(bf16[64,256]{1,0:T(8,128)(2,1)S(1)} %add_convert_fusion.1.refs_4_), channel_id=1, source_target_pairs={{0,2},{1,3},{2,0},{3,1},{4,6},{5,7},{6,4},{7,5},{8,10},{9,11},{10,... | collective-permute-start | bytes 98312 | tf_op jit(solution)/shard_map/ppermute | solution.py:215
  56.6 1.5 %collective-permute-start.24 = (bf16[64,256]{1,0:T(8,128)(2,1)S(1)}, bf16[64,256]{1,0:T(8,128)(2,1)S(1)}, u32[]{:S(2)}, u32[]{:S(2)}) collective-permute-start(bf16[64,256]{1,0:T(8,128)(2,1)S(1)} %add_convert_fusion.1.refs_4_), channel_id=1, source_target_pairs={{0,1},{1,0},{2,3},{3,2},{4,5},{5,4},{6,7},{7,6},{8,9},{9,8},{10,11... | collective-permute-start | bytes 98312 | tf_op jit(solution)/shard_map/ppermute | solution.py:218
  58.1 0.7 %copy.9 = bf16[256,256]{1,0:T(8,128)(2,1)} copy(bf16[256,256]{1,0:T(8,128)(2,1)S(1)} %get-tuple-element.41) | data formatting | bytes 262144
  59.4 0.8 %last.1 = (bf16[256,256]{1,0:T(8,128)(2,1)}, f32[256,256]{1,0:T(8,128)}) custom-call(f32[256,256]{1,0:T(8,128)S(1)} %get-tuple-element.29.grad_agg, bf16[256,256]{1,0:T(8,128)(2,1)S(1)} %get-tuple-element.31.refs_0_, bf16[256,256]{1,0:T(8,128)(2,1)S(1)} %collective-permute-done.15.refs_1_, bf16[256,256]{1,0:T(8,128)(2,1)S(1)} %collective-permute-done.16.refs_2_, ...), custom_call_target="tpu_custom_call" | custom-call | flops 1000000 | bytes 1048576 | tf_op jit(solution)/shard_map/last/pallas_call | solution.py:35
  (50 shorter events, 5.0 us)
Async XLA Ops:
  0.6 8.3 %collective-permute-start.2 = (bf16[256,256]{1,0:T(8,128)(2,1)}, bf16[256,256]{1,0:T(8,128)(2,1)S(1)}, u32[]{:S(2)}, u32[]{:S(2)}) collective-permute-start(bf16[256,256]{1,0:T(8,128)(2,1)} %refs_4_.1), channel_id=1, source_target_pairs={{0,24},{8,16},{16,8},{24,0},{1,25},{9,17},{17,9},{25,1},{2,26},{10... | collective-permute-start | bytes 393224 | tf_op jit(solution)/shard_map/ppermute | solution.py:212
  4.6 6.5 %collective-permute-start.1 = (bf16[256,256]{1,0:T(8,128)(2,1)}, bf16[256,256]{1,0:T(8,128)(2,1)S(1)}, u32[]{:S(2)}, u32[]{:S(2)}) collective-permute-start(bf16[256,256]{1,0:T(8,128)(2,1)} %refs_4_.1), channel_id=1, source_target_pairs={{0,16},{8,24},{16,0},{24,8},{1,17},{9,25},{17,1},{25,9},{2,18},{10... | collective-permute-start | bytes 393224 | tf_op jit(solution)/shard_map/ppermute | solution.py:212
  5.1 6.3 %collective-permute-start = (bf16[256,256]{1,0:T(8,128)(2,1)}, bf16[256,256]{1,0:T(8,128)(2,1)S(1)}, u32[]{:S(2)}, u32[]{:S(2)}) collective-permute-start(bf16[256,256]{1,0:T(8,128)(2,1)} %refs_4_.1), channel_id=1, source_target_pairs={{0,8},{8,0},{16,24},{24,16},{1,9},{9,1},{17,25},{25,17},{2,10},{10... | collective-permute-start | bytes 393224 | tf_op jit(solution)/shard_map/ppermute | solution.py:212
  5.9 1.0 %copy-start.3 = (s32[1,1,64,16,128]{4,3,2,1,0:T(8,128)S(1)}, s32[1,1,64,16,128]{4,3,2,1,0:T(8,128)}, u32[]{:S(2)}) copy-start(s32[1,1,64,16,128]{4,3,2,1,0:T(8,128)} %param.11) | copy-start | bytes 1572868
  6.9 0.7 %copy-start.4 = (s32[1,1,2,64]{3,2,1,0:T(2,128)S(1)}, s32[1,1,2,64]{3,2,1,0:T(2,128)}, u32[]{:S(2)}) copy-start(s32[1,1,2,64]{3,2,1,0:T(2,128)} %param.9) | copy-start | bytes 1540
  7.6 3.8 %copy-start = (bf16[256,256]{1,0:T(8,128)(2,1)S(1)}, bf16[256,256]{1,0:T(8,128)(2,1)}, u32[]{:S(2)}) copy-start(bf16[256,256]{1,0:T(8,128)(2,1)} %refs_4_.1) | copy-start | bytes 393220
  12.3 1.6 %collective-permute-start.3 = (bf16[2,272,256]{2,1,0:T(8,128)(2,1)S(1)}, bf16[2,272,256]{2,1,0:T(8,128)(2,1)S(1)}, u32[]{:S(2)}, u32[]{:S(2)}) collective-permute-start(bf16[2,272,256]{2,1,0:T(8,128)(2,1)S(1)} %forward_near_other.1), channel_id=1, source_target_pairs={{0,1},{1,0},{2,3},{3,2},{4,5},{5,4},{6,7},{7,6},{8,9},{9,8},{10,11... | collective-permute-start | bytes 835592 | tf_op jit(solution)/shard_map/ppermute | solution.py:218
  12.4 3.3 %collective-permute-start.5 = (bf16[2,272,256]{2,1,0:T(8,128)(2,1)S(1)}, bf16[2,272,256]{2,1,0:T(8,128)(2,1)S(1)}, u32[]{:S(2)}, u32[]{:S(2)}) collective-permute-start(bf16[2,272,256]{2,1,0:T(8,128)(2,1)S(1)} %get-tuple-element.25), channel_id=1, source_target_pairs={{0,1},{1,0},{2,3},{3,2},{4,5},{5,4},{6,7},{7,6},{8,9},{9,8},{10,11... | collective-permute-start | bytes 835592 | tf_op jit(solution)/shard_map/ppermute | solution.py:218
  13.4 15.9 %copy-start.1 = (bf16[256,256]{1,0:T(8,128)(2,1)S(1)}, bf16[256,256]{1,0:T(8,128)(2,1)}, u32[]{:S(2)}) copy-start(bf16[256,256]{1,0:T(8,128)(2,1)} %refs_5_.1) | copy-start | bytes 393220
  13.4 15.9 %copy-start.2 = (bf16[256,256]{1,0:T(8,128)(2,1)S(1)}, bf16[256,256]{1,0:T(8,128)(2,1)}, u32[]{:S(2)}) copy-start(bf16[256,256]{1,0:T(8,128)(2,1)} %refs_6_.1) | copy-start | bytes 393220
  14.0 7.9 %collective-permute-start.4 = (bf16[272,256]{1,0:T(8,128)(2,1)S(1)}, bf16[272,256]{1,0:T(8,128)(2,1)S(1)}, u32[]{:S(2)}, u32[]{:S(2)}) collective-permute-start(bf16[272,256]{1,0:T(8,128)(2,1)S(1)} %get-tuple-element.24), channel_id=1, source_target_pairs={{0,2},{1,3},{2,0},{3,1},{4,6},{5,7},{6,4},{7,5},{8,10},{9,11},{10,... | collective-permute-start | bytes 417800 | tf_op jit(solution)/shard_map/ppermute | solution.py:215
  15.7 13.5 %collective-permute-start.6 = (bf16[272,256]{1,0:T(8,128)(2,1)S(1)}, bf16[272,256]{1,0:T(8,128)(2,1)S(1)}, u32[]{:S(2)}, u32[]{:S(2)}) collective-permute-start(bf16[272,256]{1,0:T(8,128)(2,1)S(1)} %get-tuple-element.26), channel_id=1, source_target_pairs={{0,4},{1,5},{2,6},{3,7},{4,0},{5,1},{6,2},{7,3},{8,12},{9,13},{10,... | collective-permute-start | bytes 417800 | tf_op jit(solution)/shard_map/ppermute | solution.py:215
  18.4 10.8 %collective-permute-start.7 = (bf16[272,256]{1,0:T(8,128)(2,1)S(1)}, bf16[272,256]{1,0:T(8,128)(2,1)S(1)}, u32[]{:S(2)}, u32[]{:S(2)}) collective-permute-start(bf16[272,256]{1,0:T(8,128)(2,1)S(1)} %get-tuple-element.27), channel_id=1, source_target_pairs={{0,6},{1,7},{2,4},{3,5},{4,2},{5,3},{6,0},{7,1},{8,14},{9,15},{10,... | collective-permute-start | bytes 417800 | tf_op jit(solution)/shard_map/ppermute | solution.py:215
  29.9 1.3 %collective-permute-start.18 = (bf16[128,256]{1,0:T(8,128)(2,1)S(1)}, bf16[128,256]{1,0:T(8,128)(2,1)S(1)}, u32[]{:S(2)}, u32[]{:S(2)}) collective-permute-start(bf16[128,256]{1,0:T(8,128)(2,1)S(1)} %get-tuple-element.38), channel_id=1, source_target_pairs={{0,1},{1,0},{2,3},{3,2},{4,5},{5,4},{6,7},{7,6},{8,9},{9,8},{10,11... | collective-permute-start | bytes 196616 | tf_op jit(solution)/shard_map/ppermute | solution.py:218
  31.3 6.9 %collective-permute-start.19 = (bf16[64,256]{1,0:T(8,128)(2,1)S(1)}, bf16[64,256]{1,0:T(8,128)(2,1)S(1)}, u32[]{:S(2)}, u32[]{:S(2)}) collective-permute-start(bf16[64,256]{1,0:T(8,128)(2,1)S(1)} %slice.9), channel_id=1, source_target_pairs={{0,2},{1,3},{2,0},{3,1},{4,6},{5,7},{6,4},{7,5},{8,10},{9,11},{10,... | collective-permute-start | bytes 98312 | tf_op jit(solution)/shard_map/ppermute | solution.py:215
  33.8 10.8 %collective-permute-start.10 = (bf16[256,256]{1,0:T(8,128)(2,1)S(1)}, bf16[256,256]{1,0:T(8,128)(2,1)S(1)}, u32[]{:S(2)}, u32[]{:S(2)}) collective-permute-start(bf16[256,256]{1,0:T(8,128)(2,1)S(1)} %get-tuple-element.30.refs_1_), channel_id=1, source_target_pairs={{0,6},{1,7},{2,4},{3,5},{4,2},{5,3},{6,0},{7,1},{8,14},{9,15},{10,... | collective-permute-start | bytes 393224 | tf_op jit(solution)/shard_map/ppermute | solution.py:215
  36.3 10.9 %collective-permute-start.9 = (bf16[256,256]{1,0:T(8,128)(2,1)S(1)}, bf16[256,256]{1,0:T(8,128)(2,1)S(1)}, u32[]{:S(2)}, u32[]{:S(2)}) collective-permute-start(bf16[256,256]{1,0:T(8,128)(2,1)S(1)} %get-tuple-element.30.refs_1_), channel_id=1, source_target_pairs={{0,4},{1,5},{2,6},{3,7},{4,0},{5,1},{6,2},{7,3},{8,12},{9,13},{10,... | collective-permute-start | bytes 393224 | tf_op jit(solution)/shard_map/ppermute | solution.py:215
  36.3 11.0 %collective-permute-start.8 = (bf16[256,256]{1,0:T(8,128)(2,1)S(1)}, bf16[256,256]{1,0:T(8,128)(2,1)S(1)}, u32[]{:S(2)}, u32[]{:S(2)}) collective-permute-start(bf16[256,256]{1,0:T(8,128)(2,1)S(1)} %get-tuple-element.30.refs_1_), channel_id=1, source_target_pairs={{0,2},{1,3},{2,0},{3,1},{4,6},{5,7},{6,4},{7,5},{8,10},{9,11},{10,... | collective-permute-start | bytes 393224 | tf_op jit(solution)/shard_map/ppermute | solution.py:215
  38.2 4.9 %collective-permute-start.22 = (bf16[64,256]{1,0:T(8,128)(2,1)S(1)}, bf16[64,256]{1,0:T(8,128)(2,1)S(1)}, u32[]{:S(2)}, u32[]{:S(2)}) collective-permute-start(bf16[64,256]{1,0:T(8,128)(2,1)S(1)} %add_convert_fusion.3), channel_id=1, source_target_pairs={{0,24},{8,16},{16,8},{24,0},{1,25},{9,17},{17,9},{25,1},{2,26},{10... | collective-permute-start | bytes 98312 | tf_op jit(solution)/shard_map/ppermute | solution.py:212
  40.0 4.7 %collective-permute-start.21 = (bf16[64,256]{1,0:T(8,128)(2,1)S(1)}, bf16[64,256]{1,0:T(8,128)(2,1)S(1)}, u32[]{:S(2)}, u32[]{:S(2)}) collective-permute-start(bf16[64,256]{1,0:T(8,128)(2,1)S(1)} %add_convert_fusion.3), channel_id=1, source_target_pairs={{0,16},{8,24},{16,0},{24,8},{1,17},{9,25},{17,1},{25,9},{2,18},{10... | collective-permute-start | bytes 98312 | tf_op jit(solution)/shard_map/ppermute | solution.py:212
  43.1 4.7 %collective-permute-start.20 = (bf16[64,256]{1,0:T(8,128)(2,1)S(1)}, bf16[64,256]{1,0:T(8,128)(2,1)S(1)}, u32[]{:S(2)}, u32[]{:S(2)}) collective-permute-start(bf16[64,256]{1,0:T(8,128)(2,1)S(1)} %add_convert_fusion.3), channel_id=1, source_target_pairs={{0,8},{8,0},{16,24},{24,16},{1,9},{9,1},{17,25},{25,17},{2,10},{10... | collective-permute-start | bytes 98312 | tf_op jit(solution)/shard_map/ppermute | solution.py:212
  44.6 4.3 %collective-permute-start.11 = (bf16[256,256]{1,0:T(8,128)(2,1)S(1)}, bf16[256,256]{1,0:T(8,128)(2,1)S(1)}, u32[]{:S(2)}, u32[]{:S(2)}) collective-permute-start(bf16[256,256]{1,0:T(8,128)(2,1)S(1)} %get-tuple-element.30.refs_1_), channel_id=1, source_target_pairs={{0,1},{1,0},{2,3},{3,2},{4,5},{5,4},{6,7},{7,6},{8,9},{9,8},{10,11... | collective-permute-start | bytes 393224 | tf_op jit(solution)/shard_map/ppermute | solution.py:218
  44.6 4.3 %collective-permute-start.14 = (bf16[256,256]{1,0:T(8,128)(2,1)S(1)}, bf16[256,256]{1,0:T(8,128)(2,1)S(1)}, u32[]{:S(2)}, u32[]{:S(2)}) collective-permute-start(bf16[256,256]{1,0:T(8,128)(2,1)S(1)} %collective-permute-done.10.refs_4_), channel_id=1, source_target_pairs={{0,1},{1,0},{2,3},{3,2},{4,5},{5,4},{6,7},{7,6},{8,9},{9,8},{10,11... | collective-permute-start | bytes 393224 | tf_op jit(solution)/shard_map/ppermute | solution.py:218
  47.3 1.6 %collective-permute-start.13 = (bf16[256,256]{1,0:T(8,128)(2,1)S(1)}, bf16[256,256]{1,0:T(8,128)(2,1)S(1)}, u32[]{:S(2)}, u32[]{:S(2)}) collective-permute-start(bf16[256,256]{1,0:T(8,128)(2,1)S(1)} %collective-permute-done.9.refs_3_), channel_id=1, source_target_pairs={{0,1},{1,0},{2,3},{3,2},{4,5},{5,4},{6,7},{7,6},{8,9},{9,8},{10,11... | collective-permute-start | bytes 393224 | tf_op jit(solution)/shard_map/ppermute | solution.py:218
  47.3 1.6 %collective-permute-start.12 = (bf16[256,256]{1,0:T(8,128)(2,1)S(1)}, bf16[256,256]{1,0:T(8,128)(2,1)S(1)}, u32[]{:S(2)}, u32[]{:S(2)}) collective-permute-start(bf16[256,256]{1,0:T(8,128)(2,1)S(1)} %collective-permute-done.8.refs_2_), channel_id=1, source_target_pairs={{0,1},{1,0},{2,3},{3,2},{4,5},{5,4},{6,7},{7,6},{8,9},{9,8},{10,11... | collective-permute-start | bytes 393224 | tf_op jit(solution)/shard_map/ppermute | solution.py:218
  47.8 5.4 %collective-permute-start.23 = (bf16[64,256]{1,0:T(8,128)(2,1)S(1)}, bf16[64,256]{1,0:T(8,128)(2,1)S(1)}, u32[]{:S(2)}, u32[]{:S(2)}) collective-permute-start(bf16[64,256]{1,0:T(8,128)(2,1)S(1)} %add_convert_fusion.2), channel_id=1, source_target_pairs={{0,4},{1,5},{2,6},{3,7},{4,0},{5,1},{6,2},{7,3},{8,12},{9,13},{10,... | collective-permute-start | bytes 98312 | tf_op jit(solution)/shard_map/ppermute | solution.py:215
  49.6 9.4 %collective-permute-start.15 = (bf16[256,256]{1,0:T(8,128)(2,1)S(1)}, bf16[256,256]{1,0:T(8,128)(2,1)S(1)}, u32[]{:S(2)}, u32[]{:S(2)}) collective-permute-start(bf16[256,256]{1,0:T(8,128)(2,1)S(1)} %get-tuple-element.32), channel_id=1, source_target_pairs={{0,8},{8,0},{16,24},{24,16},{1,9},{9,1},{17,25},{25,17},{2,10},{10... | collective-permute-start | bytes 393224 | tf_op jit(solution)/shard_map/ppermute | solution.py:212
  51.2 8.2 %collective-permute-start.16 = (bf16[256,256]{1,0:T(8,128)(2,1)S(1)}, bf16[256,256]{1,0:T(8,128)(2,1)S(1)}, u32[]{:S(2)}, u32[]{:S(2)}) collective-permute-start(bf16[256,256]{1,0:T(8,128)(2,1)S(1)} %get-tuple-element.33), channel_id=1, source_target_pairs={{0,16},{8,24},{16,0},{24,8},{1,17},{9,25},{17,1},{25,9},{2,18},{10... | collective-permute-start | bytes 393224 | tf_op jit(solution)/shard_map/ppermute | solution.py:212
  52.0 7.4 %collective-permute-start.17 = (bf16[256,256]{1,0:T(8,128)(2,1)S(1)}, bf16[256,256]{1,0:T(8,128)(2,1)S(1)}, u32[]{:S(2)}, u32[]{:S(2)}) collective-permute-start(bf16[256,256]{1,0:T(8,128)(2,1)S(1)} %get-tuple-element.34), channel_id=1, source_target_pairs={{0,24},{8,16},{16,8},{24,0},{1,25},{9,17},{17,9},{25,1},{2,26},{10... | collective-permute-start | bytes 393224 | tf_op jit(solution)/shard_map/ppermute | solution.py:212
  53.2 3.4 %collective-permute-start.26 = (bf16[64,256]{1,0:T(8,128)(2,1)S(1)}, bf16[64,256]{1,0:T(8,128)(2,1)S(1)}, u32[]{:S(2)}, u32[]{:S(2)}) collective-permute-start(bf16[64,256]{1,0:T(8,128)(2,1)S(1)} %add_convert_fusion.1.refs_4_), channel_id=1, source_target_pairs={{0,3},{1,2},{2,1},{3,0},{4,7},{5,6},{6,5},{7,4},{8,11},{9,10},{10,... | collective-permute-start | bytes 98312 | tf_op jit(solution)/shard_map/ppermute | solution.py:290
  54.6 4.2 %collective-permute-start.25 = (bf16[64,256]{1,0:T(8,128)(2,1)S(1)}, bf16[64,256]{1,0:T(8,128)(2,1)S(1)}, u32[]{:S(2)}, u32[]{:S(2)}) collective-permute-start(bf16[64,256]{1,0:T(8,128)(2,1)S(1)} %add_convert_fusion.1.refs_4_), channel_id=1, source_target_pairs={{0,2},{1,3},{2,0},{3,1},{4,6},{5,7},{6,4},{7,5},{8,10},{9,11},{10,... | collective-permute-start | bytes 98312 | tf_op jit(solution)/shard_map/ppermute | solution.py:215
  56.6 2.4 %collective-permute-start.24 = (bf16[64,256]{1,0:T(8,128)(2,1)S(1)}, bf16[64,256]{1,0:T(8,128)(2,1)S(1)}, u32[]{:S(2)}, u32[]{:S(2)}) collective-permute-start(bf16[64,256]{1,0:T(8,128)(2,1)S(1)} %add_convert_fusion.1.refs_4_), channel_id=1, source_target_pairs={{0,1},{1,0},{2,3},{3,2},{4,5},{5,4},{6,7},{7,6},{8,9},{9,8},{10,11... | collective-permute-start | bytes 98312 | tf_op jit(solution)/shard_map/ppermute | solution.py:218

commit v7 on v6

--- a/solution.py
+++ b/solution.py
@@ -159,29 +159,29 @@
     my_col = lax.axis_index("col")
     core, parity = my_col % 2, (my_col // 2) % 2
     quarter = quarters[0].shape[0]
-    for i, ref in enumerate(quarters):
+    for i, ref in zip((0, 1, 2, 3), quarters):
         at = ((core ^ (i % 2)) * 2 + (parity ^ (i // 2))) * quarter
         weight_ref[pl.ds(pl.multiple_of(at, quarter), quarter), :] = ref[...].astype(f32)
 
 
-def gather_rows(refs, gathered):
+def gather_rows(refs, gathered, order):
     rows, _ = refs[0].shape
-    for i, ref in enumerate(refs):
+    for i, ref in zip(order, refs):
         gathered[i * rows : (i + 1) * rows, :] = ref[...]
 
 
-def backward_first(n_z, *refs):
+def backward_first(n_z, order, *refs):
     st_ref, grads, out, gathered = refs[0], refs[1 : 1 + n_z], refs[-2], refs[-1]
-    gather_rows(grads, gathered)
+    gather_rows(grads, gathered, order)
     rows = grads[0].shape[0]
     for j in range(out.shape[0] // rows):
         lines = slice(j * rows, (j + 1) * rows)
         out[lines, :] = jnp.dot(st_ref[lines, : n_z * rows], gathered[...], preferred_element_type=f32)
 
 
-def backward_rest(n_z, n_row, *refs):
+def backward_rest(n_z, n_row, order, *refs):
     st_ref, product, grads, outs, gathered = refs[0], refs[1], refs[2 : 2 + n_z], refs[2 + n_z : -1], refs[-1]
-    gather_rows(grads, gathered)
+    gather_rows(grads, gathered, order)
     rows = grads[0].shape[0]
     for j, out in enumerate(outs):
         lines = slice(j * rows, (j + 1) * rows)
@@ -265,24 +265,28 @@
     half = tree_sum([keep, over_core(send)]).astype(bf16)
     quarter = width // 4
     part = tree_sum([half[:quarter], over_z(half[quarter:], 1)]).astype(bf16)
-    part = tree_sum([part] + [over_row(part, k) for k in range(1, n_row)]).astype(bf16)
+    part = tree_sum([part] + [over_row(part, k) for k in reversed(range(1, n_row))][::-1]).astype(bf16)
+    row_sum = part
+
+    order_own = [0, 1, 2, 3] + list(range(4, n_z))
+    order_other = [2, 3, 1, 0] + list(range(4, n_z))
+    grads = [scaled, over_z(scaled, 1)] + far
+    (product,) = call(
+        functools.partial(backward_first, n_z, order_own),
+        "backward_own",
+        [((col_len, width), f32)],
+        [st] + [grads[z] for z in order_own],
+        scratch=[pltpu.VMEM((row_len, width), bf16)],
+        flops=flops // 2,
+    )
+    product, part = lax.optimization_barrier((product, row_sum))
     for step in range(1, (n_z - 1).bit_length()):
         part = tree_sum([part, over_z(part, 1 << step)]).astype(bf16)
-
-    grads = [scaled, over_z(scaled, 1)] + far
-    (product,) = call(
-        functools.partial(backward_first, n_z),
-        "backward_own",
-        [((col_len, width), f32)],
-        [st] + grads,
-        scratch=[pltpu.VMEM((row_len, width), bf16)],
-        flops=flops // 2,
-    )
     backs = call(
-        functools.partial(backward_rest, n_z, n_row),
+        functools.partial(backward_rest, n_z, n_row, order_other),
         "backward_other",
         [((rows, width), bf16)] * n_row,
-        [st, product] + [over_core(x) for x in grads],
+        [st, product] + [over_core(grads[z]) for z in order_other],
         scratch=[pltpu.VMEM((row_len, width), bf16)],
         flops=flops // 2,
     )

time: 60.4 us -> 60.4 us (level)
  transfers between devices with their start and end apart: 27 -> 27, of which waited for: 11 -> 12; matrix products, arithmetic and copies ran while one was open for 1% -> 1% of each run, Pallas kernels for 6% -> 7%
where the time goes in v7:
time: 60.4 us; the launch traced here: 60.2 us
  starting transfers between devices  30.2 us (50%)
  waiting for transfers between devices  19.6 us (32%)
  Pallas kernels  6.57 us (11%)
  local copies, waits for them, and re-layouts  2.39 us (4%)
  between operations  1.47 us (2%)
    ppermute x9, starting transfers between devices, over_z(): return lax.ppermute(x, 'col', [(i, i ^ 2 * k) for i in range(n_col)])  13.4 us
    ppermute x9, waiting for transfers between devices, over_z(): return lax.ppermute(x, 'col', [(i, i ^ 2 * k) for i in range(n_col)])  13 us
    ppermute x9, starting transfers between devices, over_row(): return lax.ppermute(x, 'row', [(i, i ^ k) for i in range(n_row)])  12.8 us
    pallas_call x12, Pallas kernels, call(): pl.pallas_call(body, out_shape=shapes, in_specs=smem(n_smem) + [pl.BlockS...  6.57 us
    ppermute x9, waiting for transfers between devices, over_row(): return lax.ppermute(x, 'row', [(i, i ^ k) for i in range(n_row)])  4.31 us
    ppermute x8, starting transfers between devices, over_core(): return lax.ppermute(x, 'col', [(i, i ^ 1) for i in range(n_col)])  2.92 us
    unnamed x11, local copies, waits for them, and re-layouts  2.38 us
    ppermute x8, waiting for transfers between devices, over_core(): return lax.ppermute(x, 'col', [(i, i ^ 1) for i in range(n_col)])  1.55 us
  transfers between devices with their start and end apart: 27, of which 12 were waited for; matrix products, arithmetic and copies ran while one was open for 1% of the time, Pallas kernels for 7%

profile of v7, /device:TPU:0, one launch (start us, length us, event | category | flops | bytes accessed | tf_op | source)
XLA Modules:
  0.0 60.2 jit_solution(18054211431141168838)
XLA Ops:
  0.6 4.0 %collective-permute-start.2 = (bf16[256,256]{1,0:T(8,128)(2,1)}, bf16[256,256]{1,0:T(8,128)(2,1)S(1)}, u32[]{:S(2)}, u32[]{:S(2)}) collective-permute-start(bf16[256,256]{1,0:T(8,128)(2,1)} %refs_4_.1), channel_id=1, source_target_pairs={{0,24},{8,16},{16,8},{24,0},{1,25},{9,17},{17,9},{25,1},{2,26},{10... | collective-permute-start | bytes 393224 | tf_op jit(solution)/shard_map/ppermute | solution.py:212
  4.6 0.5 collective-permute-start.1
  5.9 1.0 %copy-done.3 = s32[1,1,64,16,128]{4,3,2,1,0:T(8,128)S(1)} copy-done((s32[1,1,64,16,128]{4,3,2,1,0:T(8,128)S(1)}, s32[1,1,64,16,128]{4,3,2,1,0:T(8,128)}, u32[]{:S(2)}) %copy-start.3) | copy-done | bytes 524312
  6.9 0.7 %copy-done.4 = s32[1,1,2,64]{3,2,1,0:T(2,128)S(1)} copy-done((s32[1,1,2,64]{3,2,1,0:T(2,128)S(1)}, s32[1,1,2,64]{3,2,1,0:T(2,128)}, u32[]{:S(2)}) %copy-start.4) | copy-done | bytes 536
  7.6 1.7 %build.1.refs_0_.st_ref = bf16[1024,2048]{1,0:T(8,128)(2,1)S(1)} custom-call(s32[2,64]{1,0:T(2,128)S(1)} %bitcast.3, s32[1,1]{1,0:T(1,128)S(6)} %copy.10.count, s32[64,16,128]{2,1,0:T(8,128)S(1)} %bitcast.2), custom_call_target="tpu_custom_call" | custom-call | flops 4000000000 | bytes 1048576 | tf_op jit(solution)/shard_map/build/pallas_call | solution.py:35
  9.3 1.8 %collective-permute-done.1.refs_3_ = bf16[256,256]{1,0:T(8,128)(2,1)S(1)} collective-permute-done((bf16[256,256]{1,0:T(8,128)(2,1)}, bf16[256,256]{1,0:T(8,128)(2,1)S(1)}, u32[]{:S(2)}, u32[]{:S(2)}) %collective-permute-start.1) | collective-permute-done | bytes 131104 | tf_op jit(solution)/shard_map/ppermute | solution.py:212
  14.0 1.6 %collective-permute-start.4 = (bf16[272,256]{1,0:T(8,128)(2,1)S(1)}, bf16[272,256]{1,0:T(8,128)(2,1)S(1)}, u32[]{:S(2)}, u32[]{:S(2)}) collective-permute-start(bf16[272,256]{1,0:T(8,128)(2,1)S(1)} %get-tuple-element.26), channel_id=1, source_target_pairs={{0,2},{1,3},{2,0},{3,1},{4,6},{5,7},{6,4},{7,5},{8,10},{9,11},{10,... | collective-permute-start | bytes 417800 | tf_op jit(solution)/shard_map/ppermute | solution.py:215
  15.7 2.7 %collective-permute-start.6 = (bf16[272,256]{1,0:T(8,128)(2,1)S(1)}, bf16[272,256]{1,0:T(8,128)(2,1)S(1)}, u32[]{:S(2)}, u32[]{:S(2)}) collective-permute-start(bf16[272,256]{1,0:T(8,128)(2,1)S(1)} %get-tuple-element.28), channel_id=1, source_target_pairs={{0,4},{1,5},{2,6},{3,7},{4,0},{5,1},{6,2},{7,3},{8,12},{9,13},{10,... | collective-permute-start | bytes 417800 | tf_op jit(solution)/shard_map/ppermute | solution.py:215
  18.6 3.3 %collective-permute-done.4.refs_1_ = bf16[272,256]{1,0:T(8,128)(2,1)S(1)} collective-permute-done((bf16[272,256]{1,0:T(8,128)(2,1)S(1)}, bf16[272,256]{1,0:T(8,128)(2,1)S(1)}, u32[]{:S(2)}, u32[]{:S(2)}) %collective-permute-start.4) | collective-permute-done | bytes 139296 | tf_op jit(solution)/shard_map/ppermute | solution.py:215
  21.9 7.3 %collective-permute-done.6.refs_2_ = bf16[272,256]{1,0:T(8,128)(2,1)S(1)} collective-permute-done((bf16[272,256]{1,0:T(8,128)(2,1)S(1)}, bf16[272,256]{1,0:T(8,128)(2,1)S(1)}, u32[]{:S(2)}, u32[]{:S(2)}) %collective-permute-start.6) | collective-permute-done | bytes 139296 | tf_op jit(solution)/shard_map/ppermute | solution.py:215
  30.0 1.2 %collective-permute-done.11 = bf16[128,256]{1,0:T(8,128)(2,1)S(1)} collective-permute-done((bf16[128,256]{1,0:T(8,128)(2,1)S(1)}, bf16[128,256]{1,0:T(8,128)(2,1)S(1)}, u32[]{:S(2)}, u32[]{:S(2)}) %collective-permute-start.11) | collective-permute-done | bytes 65568 | tf_op jit(solution)/shard_map/ppermute | solution.py:218
  31.3 2.5 %collective-permute-start.12 = (bf16[64,256]{1,0:T(8,128)(2,1)S(1)}, bf16[64,256]{1,0:T(8,128)(2,1)S(1)}, u32[]{:S(2)}, u32[]{:S(2)}) collective-permute-start(bf16[64,256]{1,0:T(8,128)(2,1)S(1)} %slice.9), channel_id=1, source_target_pairs={{0,2},{1,3},{2,0},{3,1},{4,6},{5,7},{6,4},{7,5},{8,10},{9,11},{10,... | collective-permute-start | bytes 98312 | tf_op jit(solution)/shard_map/ppermute | solution.py:215
  33.8 2.6 %collective-permute-start.10 = (bf16[256,256]{1,0:T(8,128)(2,1)S(1)}, bf16[256,256]{1,0:T(8,128)(2,1)S(1)}, u32[]{:S(2)}, u32[]{:S(2)}) collective-permute-start(bf16[256,256]{1,0:T(8,128)(2,1)S(1)} %get-tuple-element.32.refs_1_), channel_id=1, source_target_pairs={{0,6},{1,7},{2,4},{3,5},{4,2},{5,3},{6,0},{7,1},{8,14},{9,15},{10,... | collective-permute-start | bytes 393224 | tf_op jit(solution)/shard_map/ppermute | solution.py:215
  36.3 1.8 %collective-permute-start.8 = (bf16[256,256]{1,0:T(8,128)(2,1)S(1)}, bf16[256,256]{1,0:T(8,128)(2,1)S(1)}, u32[]{:S(2)}, u32[]{:S(2)}) collective-permute-start(bf16[256,256]{1,0:T(8,128)(2,1)S(1)} %get-tuple-element.32.refs_1_), channel_id=1, source_target_pairs={{0,2},{1,3},{2,0},{3,1},{4,6},{5,7},{6,4},{7,5},{8,10},{9,11},{10,... | collective-permute-start | bytes 393224 | tf_op jit(solution)/shard_map/ppermute | solution.py:215
  38.2 1.8 %collective-permute-start.15 = (bf16[64,256]{1,0:T(8,128)(2,1)S(1)}, bf16[64,256]{1,0:T(8,128)(2,1)S(1)}, u32[]{:S(2)}, u32[]{:S(2)}) collective-permute-start(bf16[64,256]{1,0:T(8,128)(2,1)S(1)} %add_convert_fusion.3), channel_id=1, source_target_pairs={{0,24},{8,16},{16,8},{24,0},{1,25},{9,17},{17,9},{25,1},{2,26},{10... | collective-permute-start | bytes 98312 | tf_op jit(solution)/shard_map/ppermute | solution.py:212
  40.0 1.3 %collective-permute-start.14 = (bf16[64,256]{1,0:T(8,128)(2,1)S(1)}, bf16[64,256]{1,0:T(8,128)(2,1)S(1)}, u32[]{:S(2)}, u32[]{:S(2)}) collective-permute-start(bf16[64,256]{1,0:T(8,128)(2,1)S(1)} %add_convert_fusion.3), channel_id=1, source_target_pairs={{0,16},{8,24},{16,0},{24,8},{1,17},{9,25},{17,1},{25,9},{2,18},{10... | collective-permute-start | bytes 98312 | tf_op jit(solution)/shard_map/ppermute | solution.py:212
  41.3 1.8 %collective-permute-done.15 = bf16[64,256]{1,0:T(8,128)(2,1)S(1)} collective-permute-done((bf16[64,256]{1,0:T(8,128)(2,1)S(1)}, bf16[64,256]{1,0:T(8,128)(2,1)S(1)}, u32[]{:S(2)}, u32[]{:S(2)}) %collective-permute-start.15) | collective-permute-done | bytes 32800 | tf_op jit(solution)/shard_map/ppermute | solution.py:212
  43.1 1.5 %collective-permute-start.13 = (bf16[64,256]{1,0:T(8,128)(2,1)S(1)}, bf16[64,256]{1,0:T(8,128)(2,1)S(1)}, u32[]{:S(2)}, u32[]{:S(2)}) collective-permute-start(bf16[64,256]{1,0:T(8,128)(2,1)S(1)} %add_convert_fusion.3), channel_id=1, source_target_pairs={{0,8},{8,0},{16,24},{24,16},{1,9},{9,1},{17,25},{25,17},{2,10},{10... | collective-permute-start | bytes 98312 | tf_op jit(solution)/shard_map/ppermute | solution.py:212
  44.6 0.5 collective-permute-start.17
  45.1 2.2 %collective-permute-done.9.refs_3_ = bf16[256,256]{1,0:T(8,128)(2,1)S(1)} collective-permute-done((bf16[256,256]{1,0:T(8,128)(2,1)S(1)}, bf16[256,256]{1,0:T(8,128)(2,1)S(1)}, u32[]{:S(2)}, u32[]{:S(2)}) %collective-permute-start.9) | collective-permute-done | bytes 131104 | tf_op jit(solution)/shard_map/ppermute | solution.py:215
  47.3 0.5 collective-permute-start.18
  47.8 0.7 %backward_own.1.refs_1_ = f32[1024,256]{1,0:T(8,128)S(1)} custom-call(bf16[1024,2048]{1,0:T(8,128)(2,1)S(1)} %build.1.refs_0_.st_ref, bf16[256,256]{1,0:T(8,128)(2,1)S(1)} %get-tuple-element.32.refs_1_, bf16[256,256]{1,0:T(8,128)(2,1)S(1)} %collective-permute-done.8.refs_2_, bf16[256,256]{1,0:T(8,128)(2,1)S(1)} %collective-permute-done.9.refs_3_, ...), custom_call_target="tpu_custom_call" | custom-call | flops 536870912 | bytes 1048576 | tf_op jit(solution)/shard_map/backward_own/pallas_call | solution.py:35
  48.9 0.7 %backward_other.1 = (bf16[256,256]{1,0:T(8,128)(2,1)S(1)}, bf16[256,256]{1,0:T(8,128)(2,1)S(1)}, bf16[256,256]{1,0:T(8,128)(2,1)S(1)}, bf16[256,256]{1,0:T(8,128)(2,1)S(1)}) custom-call(bf16[1024,2048]{1,0:T(8,128)(2,1)S(1)} %build.1.refs_0_.st_ref, f32[1024,256]{1,0:T(8,128)S(1)} %backward_own.1.refs_1_, ...), custom_call_target="tpu_custom_call" | custom-call | flops 536870912 | bytes 1048576 | tf_op jit(solution)/shard_map/backward_other/pallas_call | solution.py:35
  49.6 1.6 %collective-permute-start.20 = (bf16[256,256]{1,0:T(8,128)(2,1)S(1)}, bf16[256,256]{1,0:T(8,128)(2,1)S(1)}, u32[]{:S(2)}, u32[]{:S(2)}) collective-permute-start(bf16[256,256]{1,0:T(8,128)(2,1)S(1)} %get-tuple-element.39), channel_id=1, source_target_pairs={{0,8},{8,0},{16,24},{24,16},{1,9},{9,1},{17,25},{25,17},{2,10},{10... | collective-permute-start | bytes 393224 | tf_op jit(solution)/shard_map/ppermute | solution.py:212
  51.2 0.7 %collective-permute-start.21 = (bf16[256,256]{1,0:T(8,128)(2,1)S(1)}, bf16[256,256]{1,0:T(8,128)(2,1)S(1)}, u32[]{:S(2)}, u32[]{:S(2)}) collective-permute-start(bf16[256,256]{1,0:T(8,128)(2,1)S(1)} %get-tuple-element.40), channel_id=1, source_target_pairs={{0,16},{8,24},{16,0},{24,8},{1,17},{9,25},{17,1},{25,9},{2,18},{10... | collective-permute-start | bytes 393224 | tf_op jit(solution)/shard_map/ppermute | solution.py:212
  51.9 1.2 %collective-permute-start.22 = (bf16[256,256]{1,0:T(8,128)(2,1)S(1)}, bf16[256,256]{1,0:T(8,128)(2,1)S(1)}, u32[]{:S(2)}, u32[]{:S(2)}) collective-permute-start(bf16[256,256]{1,0:T(8,128)(2,1)S(1)} %get-tuple-element.41), channel_id=1, source_target_pairs={{0,24},{8,16},{16,8},{24,0},{1,25},{9,17},{17,9},{25,1},{2,26},{10... | collective-permute-start | bytes 393224 | tf_op jit(solution)/shard_map/ppermute | solution.py:212
  53.4 1.2 %collective-permute-start.26 = (bf16[64,256]{1,0:T(8,128)(2,1)S(1)}, bf16[64,256]{1,0:T(8,128)(2,1)S(1)}, u32[]{:S(2)}, u32[]{:S(2)}) collective-permute-start(bf16[64,256]{1,0:T(8,128)(2,1)S(1)} %add_convert_fusion.1.refs_4_), channel_id=1, source_target_pairs={{0,3},{1,2},{2,1},{3,0},{4,7},{5,6},{6,5},{7,4},{8,11},{9,10},{10,... | collective-permute-start | bytes 98312 | tf_op jit(solution)/shard_map/ppermute | solution.py:294
  54.6 1.6 %collective-permute-start.25 = (bf16[64,256]{1,0:T(8,128)(2,1)S(1)}, bf16[64,256]{1,0:T(8,128)(2,1)S(1)}, u32[]{:S(2)}, u32[]{:S(2)}) collective-permute-start(bf16[64,256]{1,0:T(8,128)(2,1)S(1)} %add_convert_fusion.1.refs_4_), channel_id=1, source_target_pairs={{0,2},{1,3},{2,0},{3,1},{4,6},{5,7},{6,4},{7,5},{8,10},{9,11},{10,... | collective-permute-start | bytes 98312 | tf_op jit(solution)/shard_map/ppermute | solution.py:215
  56.2 0.7 %collective-permute-done.26.refs_7_ = bf16[64,256]{1,0:T(8,128)(2,1)S(1)} collective-permute-done((bf16[64,256]{1,0:T(8,128)(2,1)S(1)}, bf16[64,256]{1,0:T(8,128)(2,1)S(1)}, u32[]{:S(2)}, u32[]{:S(2)}) %collective-permute-start.26) | collective-permute-done | bytes 32800 | tf_op jit(solution)/shard_map/ppermute | solution.py:294
  56.9 1.3 %collective-permute-start.24 = (bf16[64,256]{1,0:T(8,128)(2,1)S(1)}, bf16[64,256]{1,0:T(8,128)(2,1)S(1)}, u32[]{:S(2)}, u32[]{:S(2)}) collective-permute-start(bf16[64,256]{1,0:T(8,128)(2,1)S(1)} %add_convert_fusion.1.refs_4_), channel_id=1, source_target_pairs={{0,1},{1,0},{2,3},{3,2},{4,5},{5,4},{6,7},{7,6},{8,9},{9,8},{10,11... | collective-permute-start | bytes 98312 | tf_op jit(solution)/shard_map/ppermute | solution.py:218
  58.1 0.7 %copy.9 = bf16[256,256]{1,0:T(8,128)(2,1)} copy(bf16[256,256]{1,0:T(8,128)(2,1)S(1)} %get-tuple-element.45) | data formatting | bytes 262144
  59.4 0.8 %last.1 = (bf16[256,256]{1,0:T(8,128)(2,1)}, f32[256,256]{1,0:T(8,128)}) custom-call(f32[256,256]{1,0:T(8,128)S(1)} %get-tuple-element.31.grad_agg, bf16[256,256]{1,0:T(8,128)(2,1)S(1)} %get-tuple-element.38.refs_0_, bf16[256,256]{1,0:T(8,128)(2,1)S(1)} %collective-permute-done.20.refs_1_, bf16[256,256]{1,0:T(8,128)(2,1)S(1)} %collective-permute-done.21.refs_2_, ...), custom_call_target="tpu_custom_call" | custom-call | flops 1000000 | bytes 1048576 | tf_op jit(solution)/shard_map/last/pallas_call | solution.py:35
  (50 shorter events, 5.3 us)
Async XLA Ops:
  0.6 8.7 %collective-permute-start.2 = (bf16[256,256]{1,0:T(8,128)(2,1)}, bf16[256,256]{1,0:T(8,128)(2,1)S(1)}, u32[]{:S(2)}, u32[]{:S(2)}) collective-permute-start(bf16[256,256]{1,0:T(8,128)(2,1)} %refs_4_.1), channel_id=1, source_target_pairs={{0,24},{8,16},{16,8},{24,0},{1,25},{9,17},{17,9},{25,1},{2,26},{10... | collective-permute-start | bytes 393224 | tf_op jit(solution)/shard_map/ppermute | solution.py:212
  4.6 6.5 %collective-permute-start.1 = (bf16[256,256]{1,0:T(8,128)(2,1)}, bf16[256,256]{1,0:T(8,128)(2,1)S(1)}, u32[]{:S(2)}, u32[]{:S(2)}) collective-permute-start(bf16[256,256]{1,0:T(8,128)(2,1)} %refs_4_.1), channel_id=1, source_target_pairs={{0,16},{8,24},{16,0},{24,8},{1,17},{9,25},{17,1},{25,9},{2,18},{10... | collective-permute-start | bytes 393224 | tf_op jit(solution)/shard_map/ppermute | solution.py:212
  5.1 6.3 %collective-permute-start = (bf16[256,256]{1,0:T(8,128)(2,1)}, bf16[256,256]{1,0:T(8,128)(2,1)S(1)}, u32[]{:S(2)}, u32[]{:S(2)}) collective-permute-start(bf16[256,256]{1,0:T(8,128)(2,1)} %refs_4_.1), channel_id=1, source_target_pairs={{0,8},{8,0},{16,24},{24,16},{1,9},{9,1},{17,25},{25,17},{2,10},{10... | collective-permute-start | bytes 393224 | tf_op jit(solution)/shard_map/ppermute | solution.py:212
  5.9 1.0 %copy-start.3 = (s32[1,1,64,16,128]{4,3,2,1,0:T(8,128)S(1)}, s32[1,1,64,16,128]{4,3,2,1,0:T(8,128)}, u32[]{:S(2)}) copy-start(s32[1,1,64,16,128]{4,3,2,1,0:T(8,128)} %param.11) | copy-start | bytes 1572868
  6.9 0.7 %copy-start.4 = (s32[1,1,2,64]{3,2,1,0:T(2,128)S(1)}, s32[1,1,2,64]{3,2,1,0:T(2,128)}, u32[]{:S(2)}) copy-start(s32[1,1,2,64]{3,2,1,0:T(2,128)} %param.9) | copy-start | bytes 1540
  7.6 3.8 %copy-start = (bf16[256,256]{1,0:T(8,128)(2,1)S(1)}, bf16[256,256]{1,0:T(8,128)(2,1)}, u32[]{:S(2)}) copy-start(bf16[256,256]{1,0:T(8,128)(2,1)} %refs_4_.1) | copy-start | bytes 393220
  12.3 1.6 %collective-permute-start.3 = (bf16[2,272,256]{2,1,0:T(8,128)(2,1)S(1)}, bf16[2,272,256]{2,1,0:T(8,128)(2,1)S(1)}, u32[]{:S(2)}, u32[]{:S(2)}) collective-permute-start(bf16[2,272,256]{2,1,0:T(8,128)(2,1)S(1)} %forward_near_other.1), channel_id=1, source_target_pairs={{0,1},{1,0},{2,3},{3,2},{4,5},{5,4},{6,7},{7,6},{8,9},{9,8},{10,11... | collective-permute-start | bytes 835592 | tf_op jit(solution)/shard_map/ppermute | solution.py:218
  12.4 3.3 %collective-permute-start.5 = (bf16[2,272,256]{2,1,0:T(8,128)(2,1)S(1)}, bf16[2,272,256]{2,1,0:T(8,128)(2,1)S(1)}, u32[]{:S(2)}, u32[]{:S(2)}) collective-permute-start(bf16[2,272,256]{2,1,0:T(8,128)(2,1)S(1)} %get-tuple-element.27), channel_id=1, source_target_pairs={{0,1},{1,0},{2,3},{3,2},{4,5},{5,4},{6,7},{7,6},{8,9},{9,8},{10,11... | collective-permute-start | bytes 835592 | tf_op jit(solution)/shard_map/ppermute | solution.py:218
  13.4 15.9 %copy-start.1 = (bf16[256,256]{1,0:T(8,128)(2,1)S(1)}, bf16[256,256]{1,0:T(8,128)(2,1)}, u32[]{:S(2)}) copy-start(bf16[256,256]{1,0:T(8,128)(2,1)} %refs_5_.1) | copy-start | bytes 393220
  13.4 15.9 %copy-start.2 = (bf16[256,256]{1,0:T(8,128)(2,1)S(1)}, bf16[256,256]{1,0:T(8,128)(2,1)}, u32[]{:S(2)}) copy-start(bf16[256,256]{1,0:T(8,128)(2,1)} %refs_6_.1) | copy-start | bytes 393220
  14.0 7.9 %collective-permute-start.4 = (bf16[272,256]{1,0:T(8,128)(2,1)S(1)}, bf16[272,256]{1,0:T(8,128)(2,1)S(1)}, u32[]{:S(2)}, u32[]{:S(2)}) collective-permute-start(bf16[272,256]{1,0:T(8,128)(2,1)S(1)} %get-tuple-element.26), channel_id=1, source_target_pairs={{0,2},{1,3},{2,0},{3,1},{4,6},{5,7},{6,4},{7,5},{8,10},{9,11},{10,... | collective-permute-start | bytes 417800 | tf_op jit(solution)/shard_map/ppermute | solution.py:215
  15.7 13.5 %collective-permute-start.6 = (bf16[272,256]{1,0:T(8,128)(2,1)S(1)}, bf16[272,256]{1,0:T(8,128)(2,1)S(1)}, u32[]{:S(2)}, u32[]{:S(2)}) collective-permute-start(bf16[272,256]{1,0:T(8,128)(2,1)S(1)} %get-tuple-element.28), channel_id=1, source_target_pairs={{0,4},{1,5},{2,6},{3,7},{4,0},{5,1},{6,2},{7,3},{8,12},{9,13},{10,... | collective-permute-start | bytes 417800 | tf_op jit(solution)/shard_map/ppermute | solution.py:215
  18.4 10.8 %collective-permute-start.7 = (bf16[272,256]{1,0:T(8,128)(2,1)S(1)}, bf16[272,256]{1,0:T(8,128)(2,1)S(1)}, u32[]{:S(2)}, u32[]{:S(2)}) collective-permute-start(bf16[272,256]{1,0:T(8,128)(2,1)S(1)} %get-tuple-element.29), channel_id=1, source_target_pairs={{0,6},{1,7},{2,4},{3,5},{4,2},{5,3},{6,0},{7,1},{8,14},{9,15},{10,... | collective-permute-start | bytes 417800 | tf_op jit(solution)/shard_map/ppermute | solution.py:215
  29.9 1.3 %collective-permute-start.11 = (bf16[128,256]{1,0:T(8,128)(2,1)S(1)}, bf16[128,256]{1,0:T(8,128)(2,1)S(1)}, u32[]{:S(2)}, u32[]{:S(2)}) collective-permute-start(bf16[128,256]{1,0:T(8,128)(2,1)S(1)} %get-tuple-element.36), channel_id=1, source_target_pairs={{0,1},{1,0},{2,3},{3,2},{4,5},{5,4},{6,7},{7,6},{8,9},{9,8},{10,11... | collective-permute-start | bytes 196616 | tf_op jit(solution)/shard_map/ppermute | solution.py:218
  31.3 6.9 %collective-permute-start.12 = (bf16[64,256]{1,0:T(8,128)(2,1)S(1)}, bf16[64,256]{1,0:T(8,128)(2,1)S(1)}, u32[]{:S(2)}, u32[]{:S(2)}) collective-permute-start(bf16[64,256]{1,0:T(8,128)(2,1)S(1)} %slice.9), channel_id=1, source_target_pairs={{0,2},{1,3},{2,0},{3,1},{4,6},{5,7},{6,4},{7,5},{8,10},{9,11},{10,... | collective-permute-start | bytes 98312 | tf_op jit(solution)/shard_map/ppermute | solution.py:215
  33.8 10.8 %collective-permute-start.10 = (bf16[256,256]{1,0:T(8,128)(2,1)S(1)}, bf16[256,256]{1,0:T(8,128)(2,1)S(1)}, u32[]{:S(2)}, u32[]{:S(2)}) collective-permute-start(bf16[256,256]{1,0:T(8,128)(2,1)S(1)} %get-tuple-element.32.refs_1_), channel_id=1, source_target_pairs={{0,6},{1,7},{2,4},{3,5},{4,2},{5,3},{6,0},{7,1},{8,14},{9,15},{10,... | collective-permute-start | bytes 393224 | tf_op jit(solution)/shard_map/ppermute | solution.py:215
  36.3 10.9 %collective-permute-start.9 = (bf16[256,256]{1,0:T(8,128)(2,1)S(1)}, bf16[256,256]{1,0:T(8,128)(2,1)S(1)}, u32[]{:S(2)}, u32[]{:S(2)}) collective-permute-start(bf16[256,256]{1,0:T(8,128)(2,1)S(1)} %get-tuple-element.32.refs_1_), channel_id=1, source_target_pairs={{0,4},{1,5},{2,6},{3,7},{4,0},{5,1},{6,2},{7,3},{8,12},{9,13},{10,... | collective-permute-start | bytes 393224 | tf_op jit(solution)/shard_map/ppermute | solution.py:215
  36.3 11.0 %collective-permute-start.8 = (bf16[256,256]{1,0:T(8,128)(2,1)S(1)}, bf16[256,256]{1,0:T(8,128)(2,1)S(1)}, u32[]{:S(2)}, u32[]{:S(2)}) collective-permute-start(bf16[256,256]{1,0:T(8,128)(2,1)S(1)} %get-tuple-element.32.refs_1_), channel_id=1, source_target_pairs={{0,2},{1,3},{2,0},{3,1},{4,6},{5,7},{6,4},{7,5},{8,10},{9,11},{10,... | collective-permute-start | bytes 393224 | tf_op jit(solution)/shard_map/ppermute | solution.py:215
  38.2 4.9 %collective-permute-start.15 = (bf16[64,256]{1,0:T(8,128)(2,1)S(1)}, bf16[64,256]{1,0:T(8,128)(2,1)S(1)}, u32[]{:S(2)}, u32[]{:S(2)}) collective-permute-start(bf16[64,256]{1,0:T(8,128)(2,1)S(1)} %add_convert_fusion.3), channel_id=1, source_target_pairs={{0,24},{8,16},{16,8},{24,0},{1,25},{9,17},{17,9},{25,1},{2,26},{10... | collective-permute-start | bytes 98312 | tf_op jit(solution)/shard_map/ppermute | solution.py:212
  40.0 4.7 %collective-permute-start.14 = (bf16[64,256]{1,0:T(8,128)(2,1)S(1)}, bf16[64,256]{1,0:T(8,128)(2,1)S(1)}, u32[]{:S(2)}, u32[]{:S(2)}) collective-permute-start(bf16[64,256]{1,0:T(8,128)(2,1)S(1)} %add_convert_fusion.3), channel_id=1, source_target_pairs={{0,16},{8,24},{16,0},{24,8},{1,17},{9,25},{17,1},{25,9},{2,18},{10... | collective-permute-start | bytes 98312 | tf_op jit(solution)/shard_map/ppermute | solution.py:212
  43.1 4.7 %collective-permute-start.13 = (bf16[64,256]{1,0:T(8,128)(2,1)S(1)}, bf16[64,256]{1,0:T(8,128)(2,1)S(1)}, u32[]{:S(2)}, u32[]{:S(2)}) collective-permute-start(bf16[64,256]{1,0:T(8,128)(2,1)S(1)} %add_convert_fusion.3), channel_id=1, source_target_pairs={{0,8},{8,0},{16,24},{24,16},{1,9},{9,1},{17,25},{25,17},{2,10},{10... | collective-permute-start | bytes 98312 | tf_op jit(solution)/shard_map/ppermute | solution.py:212
  44.6 4.3 %collective-permute-start.19 = (bf16[256,256]{1,0:T(8,128)(2,1)S(1)}, bf16[256,256]{1,0:T(8,128)(2,1)S(1)}, u32[]{:S(2)}, u32[]{:S(2)}) collective-permute-start(bf16[256,256]{1,0:T(8,128)(2,1)S(1)} %get-tuple-element.32.refs_1_), channel_id=1, source_target_pairs={{0,1},{1,0},{2,3},{3,2},{4,5},{5,4},{6,7},{7,6},{8,9},{9,8},{10,11... | collective-permute-start | bytes 393224 | tf_op jit(solution)/shard_map/ppermute | solution.py:218
  44.6 4.3 %collective-permute-start.17 = (bf16[256,256]{1,0:T(8,128)(2,1)S(1)}, bf16[256,256]{1,0:T(8,128)(2,1)S(1)}, u32[]{:S(2)}, u32[]{:S(2)}) collective-permute-start(bf16[256,256]{1,0:T(8,128)(2,1)S(1)} %collective-permute-done.10.refs_4_), channel_id=1, source_target_pairs={{0,1},{1,0},{2,3},{3,2},{4,5},{5,4},{6,7},{7,6},{8,9},{9,8},{10,11... | collective-permute-start | bytes 393224 | tf_op jit(solution)/shard_map/ppermute | solution.py:218
  47.3 1.6 %collective-permute-start.16 = (bf16[256,256]{1,0:T(8,128)(2,1)S(1)}, bf16[256,256]{1,0:T(8,128)(2,1)S(1)}, u32[]{:S(2)}, u32[]{:S(2)}) collective-permute-start(bf16[256,256]{1,0:T(8,128)(2,1)S(1)} %collective-permute-done.9.refs_3_), channel_id=1, source_target_pairs={{0,1},{1,0},{2,3},{3,2},{4,5},{5,4},{6,7},{7,6},{8,9},{9,8},{10,11... | collective-permute-start | bytes 393224 | tf_op jit(solution)/shard_map/ppermute | solution.py:218
  47.3 1.6 %collective-permute-start.18 = (bf16[256,256]{1,0:T(8,128)(2,1)S(1)}, bf16[256,256]{1,0:T(8,128)(2,1)S(1)}, u32[]{:S(2)}, u32[]{:S(2)}) collective-permute-start(bf16[256,256]{1,0:T(8,128)(2,1)S(1)} %collective-permute-done.8.refs_2_), channel_id=1, source_target_pairs={{0,1},{1,0},{2,3},{3,2},{4,5},{5,4},{6,7},{7,6},{8,9},{9,8},{10,11... | collective-permute-start | bytes 393224 | tf_op jit(solution)/shard_map/ppermute | solution.py:218
  48.5 4.9 %collective-permute-start.23 = (bf16[64,256]{1,0:T(8,128)(2,1)S(1)}, bf16[64,256]{1,0:T(8,128)(2,1)S(1)}, u32[]{:S(2)}, u32[]{:S(2)}) collective-permute-start(bf16[64,256]{1,0:T(8,128)(2,1)S(1)} %add_convert_fusion.2), channel_id=1, source_target_pairs={{0,4},{1,5},{2,6},{3,7},{4,0},{5,1},{6,2},{7,3},{8,12},{9,13},{10,... | collective-permute-start | bytes 98312 | tf_op jit(solution)/shard_map/ppermute | solution.py:215
  49.6 9.4 %collective-permute-start.20 = (bf16[256,256]{1,0:T(8,128)(2,1)S(1)}, bf16[256,256]{1,0:T(8,128)(2,1)S(1)}, u32[]{:S(2)}, u32[]{:S(2)}) collective-permute-start(bf16[256,256]{1,0:T(8,128)(2,1)S(1)} %get-tuple-element.39), channel_id=1, source_target_pairs={{0,8},{8,0},{16,24},{24,16},{1,9},{9,1},{17,25},{25,17},{2,10},{10... | collective-permute-start | bytes 393224 | tf_op jit(solution)/shard_map/ppermute | solution.py:212
  51.2 8.2 %collective-permute-start.21 = (bf16[256,256]{1,0:T(8,128)(2,1)S(1)}, bf16[256,256]{1,0:T(8,128)(2,1)S(1)}, u32[]{:S(2)}, u32[]{:S(2)}) collective-permute-start(bf16[256,256]{1,0:T(8,128)(2,1)S(1)} %get-tuple-element.40), channel_id=1, source_target_pairs={{0,16},{8,24},{16,0},{24,8},{1,17},{9,25},{17,1},{25,9},{2,18},{10... | collective-permute-start | bytes 393224 | tf_op jit(solution)/shard_map/ppermute | solution.py:212
  51.9 7.5 %collective-permute-start.22 = (bf16[256,256]{1,0:T(8,128)(2,1)S(1)}, bf16[256,256]{1,0:T(8,128)(2,1)S(1)}, u32[]{:S(2)}, u32[]{:S(2)}) collective-permute-start(bf16[256,256]{1,0:T(8,128)(2,1)S(1)} %get-tuple-element.41), channel_id=1, source_target_pairs={{0,24},{8,16},{16,8},{24,0},{1,25},{9,17},{17,9},{25,1},{2,26},{10... | collective-permute-start | bytes 393224 | tf_op jit(solution)/shard_map/ppermute | solution.py:212
  53.4 3.4 %collective-permute-start.26 = (bf16[64,256]{1,0:T(8,128)(2,1)S(1)}, bf16[64,256]{1,0:T(8,128)(2,1)S(1)}, u32[]{:S(2)}, u32[]{:S(2)}) collective-permute-start(bf16[64,256]{1,0:T(8,128)(2,1)S(1)} %add_convert_fusion.1.refs_4_), channel_id=1, source_target_pairs={{0,3},{1,2},{2,1},{3,0},{4,7},{5,6},{6,5},{7,4},{8,11},{9,10},{10,... | collective-permute-start | bytes 98312 | tf_op jit(solution)/shard_map/ppermute | solution.py:294
  54.6 4.2 %collective-permute-start.25 = (bf16[64,256]{1,0:T(8,128)(2,1)S(1)}, bf16[64,256]{1,0:T(8,128)(2,1)S(1)}, u32[]{:S(2)}, u32[]{:S(2)}) collective-permute-start(bf16[64,256]{1,0:T(8,128)(2,1)S(1)} %add_convert_fusion.1.refs_4_), channel_id=1, source_target_pairs={{0,2},{1,3},{2,0},{3,1},{4,6},{5,7},{6,4},{7,5},{8,10},{9,11},{10,... | collective-permute-start | bytes 98312 | tf_op jit(solution)/shard_map/ppermute | solution.py:215
  56.9 2.1 %collective-permute-start.24 = (bf16[64,256]{1,0:T(8,128)(2,1)S(1)}, bf16[64,256]{1,0:T(8,128)(2,1)S(1)}, u32[]{:S(2)}, u32[]{:S(2)}) collective-permute-start(bf16[64,256]{1,0:T(8,128)(2,1)S(1)} %add_convert_fusion.1.refs_4_), channel_id=1, source_target_pairs={{0,1},{1,0},{2,3},{3,2},{4,5},{5,4},{6,7},{7,6},{8,9},{9,8},{10,11... | collective-permute-start | bytes 98312 | tf_op jit(solution)/shard_map/ppermute | solution.py:218

commit v8 on v7

--- a/solution.py
+++ b/solution.py
@@ -119,7 +119,7 @@
 def dense_kernel(n_z, *refs):
     parts = refs[:n_z]
     feats, cotangent, weight = refs[n_z : n_z + 3]
-    act_ref, scaled_ref, agg_grad_ref, agg_ref, grad_ref = refs[n_z + 3 :]
+    act_ref, scaled_ref, agg_grad_ref, keep_ref, send_ref = refs[n_z + 3 :]
     width = weight.shape[0]
     total = parts[0][...].astype(f32)
     for part in parts[1:]:
@@ -127,24 +127,23 @@
     degree = total[width : width + 1] + total[width + 1 : width + 2]
     scale = lax.rsqrt(degree + 1.0)
     agg_t = (total[:width] * scale + feats[...].astype(f32).T).astype(bf16)
-    agg_ref[...] = agg_t
     w = weight[...]
     preact = jnp.dot(agg_t.T, w, preferred_element_type=f32)
     gate = jax.nn.sigmoid(preact)
     act_ref[...] = (preact * gate).astype(bf16)
     grad_pre = (cotangent[...].astype(f32) * gate * (1.0 + preact * (1.0 - gate))).astype(bf16)
-    grad_ref[...] = grad_pre
     grad_agg = lax.dot_general(grad_pre, w, (((1,), (1,)), ((), ())), preferred_element_type=f32)
     agg_grad_ref[...] = grad_agg
     scale_rows = jnp.broadcast_to(scale, agg_t.shape).T
     scaled_ref[...] = (grad_agg * scale_rows).astype(bf16)
-
-
-def weight_kernel(agg_t, grad_pre, keep_ref, send_ref):
+    weight_quarters(agg_t, grad_pre, keep_ref, send_ref)
+
+
+def weight_quarters(agg_t, grad_pre, keep_ref, send_ref):
     my_col = lax.axis_index("col")
     core, parity = my_col % 2, (my_col // 2) % 2
     quarter = agg_t.shape[0] // 4
-    part = jnp.dot(agg_t[...], grad_pre[...], preferred_element_type=f32).astype(bf16)
+    part = jnp.dot(agg_t, grad_pre, preferred_element_type=f32).astype(bf16)
     cut = [part[i * quarter : (i + 1) * quarter] for i in range(4)]
     for flip, ref in enumerate((keep_ref, send_ref)):
         here = (core ^ flip) == 0
@@ -252,16 +251,15 @@
     near = pair_sum("pair_near", forward("forward_near_own", 0, 2), over_core(sent), 2)
     parts = [near[0], over_z(near[1], 1)] + far
 
-    activated, scaled, grad_agg, agg_t, grad_pre = call(
+    activated, scaled, grad_agg, keep, send = call(
         functools.partial(dense_kernel, n_z),
         "dense",
-        [((rows, width), bf16), ((rows, width), bf16), ((rows, width), f32), ((width, rows), bf16), ((rows, width), bf16)],
+        [((rows, width), bf16), ((rows, width), bf16), ((rows, width), f32)] + [((width // 2, width), bf16)] * 2,
         parts + [features, cotangent, weight],
         flops=4 * rows * width * width,
     )
     far = [over_z(scaled, k) for k in range(2, n_z)]
 
-    keep, send = call(weight_kernel, "weight_part", [((width // 2, width), bf16)] * 2, [agg_t, grad_pre], flops=2e9)
     half = tree_sum([keep, over_core(send)]).astype(bf16)
     quarter = width // 4
     part = tree_sum([half[:quarter], over_z(half[quarter:], 1)]).astype(bf16)

time: 60.4 us -> 60.3 us (level)
    pallas_call x12 -> x11, Pallas kernels: 6.57 us -> 6.43 us  [call(): pl.pallas_call(body, out_shape=shapes, in_specs=smem(n_smem) + [pl.BlockS...]
where the time goes in v8:
time: 60.3 us; the launch traced here: 60.1 us
  starting transfers between devices  30.2 us (50%)
  waiting for transfers between devices  19.6 us (33%)
  Pallas kernels  6.43 us (11%)
  local copies, waits for them, and re-layouts  2.39 us (4%)
  between operations  1.46 us (2%)
    ppermute x9, starting transfers between devices, over_z(): return lax.ppermute(x, 'col', [(i, i ^ 2 * k) for i in range(n_col)])  13.4 us
    ppermute x9, waiting for transfers between devices, over_z(): return lax.ppermute(x, 'col', [(i, i ^ 2 * k) for i in range(n_col)])  13 us
    ppermute x9, starting transfers between devices, over_row(): return lax.ppermute(x, 'row', [(i, i ^ k) for i in range(n_row)])  12.8 us
    pallas_call x11, Pallas kernels, call(): pl.pallas_call(body, out_shape=shapes, in_specs=smem(n_smem) + [pl.BlockS...  6.43 us
    ppermute x9, waiting for transfers between devices, over_row(): return lax.ppermute(x, 'row', [(i, i ^ k) for i in range(n_row)])  4.31 us
    ppermute x8, starting transfers between devices, over_core(): return lax.ppermute(x, 'col', [(i, i ^ 1) for i in range(n_col)])  2.92 us
    unnamed x11, local copies, waits for them, and re-layouts  2.38 us
    ppermute x8, waiting for transfers between devices, over_core(): return lax.ppermute(x, 'col', [(i, i ^ 1) for i in range(n_col)])  1.55 us
  transfers between devices with their start and end apart: 27, of which 12 were waited for; matrix products, arithmetic and copies ran while one was open for 1% of the time, Pallas kernels for 7%

profile of v8, /device:TPU:0, one launch (start us, length us, event | category | flops | bytes accessed | tf_op | source)
XLA Modules:
  0.0 60.1 jit_solution(3508851414253723252)
XLA Ops:
  0.6 4.0 %collective-permute-start.2 = (bf16[256,256]{1,0:T(8,128)(2,1)}, bf16[256,256]{1,0:T(8,128)(2,1)S(1)}, u32[]{:S(2)}, u32[]{:S(2)}) collective-permute-start(bf16[256,256]{1,0:T(8,128)(2,1)} %refs_4_.1), channel_id=1, source_target_pairs={{0,24},{8,16},{16,8},{24,0},{1,25},{9,17},{17,9},{25,1},{2,26},{10... | collective-permute-start | bytes 393224 | tf_op jit(solution)/shard_map/ppermute | solution.py:211
  4.6 0.5 collective-permute-start.1
  5.9 1.0 %copy-done.3 = s32[1,1,64,16,128]{4,3,2,1,0:T(8,128)S(1)} copy-done((s32[1,1,64,16,128]{4,3,2,1,0:T(8,128)S(1)}, s32[1,1,64,16,128]{4,3,2,1,0:T(8,128)}, u32[]{:S(2)}) %copy-start.3) | copy-done | bytes 524312
  6.9 0.7 %copy-done.4 = s32[1,1,2,64]{3,2,1,0:T(2,128)S(1)} copy-done((s32[1,1,2,64]{3,2,1,0:T(2,128)S(1)}, s32[1,1,2,64]{3,2,1,0:T(2,128)}, u32[]{:S(2)}) %copy-start.4) | copy-done | bytes 536
  7.6 1.7 %build.1.refs_0_.st_ref = bf16[1024,2048]{1,0:T(8,128)(2,1)S(1)} custom-call(s32[2,64]{1,0:T(2,128)S(1)} %bitcast.3, s32[1,1]{1,0:T(1,128)S(6)} %copy.10.count, s32[64,16,128]{2,1,0:T(8,128)S(1)} %bitcast.2), custom_call_target="tpu_custom_call" | custom-call | flops 4000000000 | bytes 1048576 | tf_op jit(solution)/shard_map/build/pallas_call | solution.py:35
  9.3 1.8 %collective-permute-done.1.refs_3_ = bf16[256,256]{1,0:T(8,128)(2,1)S(1)} collective-permute-done((bf16[256,256]{1,0:T(8,128)(2,1)}, bf16[256,256]{1,0:T(8,128)(2,1)S(1)}, u32[]{:S(2)}, u32[]{:S(2)}) %collective-permute-start.1) | collective-permute-done | bytes 131104 | tf_op jit(solution)/shard_map/ppermute | solution.py:211
  14.0 1.6 %collective-permute-start.4 = (bf16[272,256]{1,0:T(8,128)(2,1)S(1)}, bf16[272,256]{1,0:T(8,128)(2,1)S(1)}, u32[]{:S(2)}, u32[]{:S(2)}) collective-permute-start(bf16[272,256]{1,0:T(8,128)(2,1)S(1)} %get-tuple-element.24), channel_id=1, source_target_pairs={{0,2},{1,3},{2,0},{3,1},{4,6},{5,7},{6,4},{7,5},{8,10},{9,11},{10,... | collective-permute-start | bytes 417800 | tf_op jit(solution)/shard_map/ppermute | solution.py:214
  15.7 2.7 %collective-permute-start.6 = (bf16[272,256]{1,0:T(8,128)(2,1)S(1)}, bf16[272,256]{1,0:T(8,128)(2,1)S(1)}, u32[]{:S(2)}, u32[]{:S(2)}) collective-permute-start(bf16[272,256]{1,0:T(8,128)(2,1)S(1)} %get-tuple-element.26), channel_id=1, source_target_pairs={{0,4},{1,5},{2,6},{3,7},{4,0},{5,1},{6,2},{7,3},{8,12},{9,13},{10,... | collective-permute-start | bytes 417800 | tf_op jit(solution)/shard_map/ppermute | solution.py:214
  18.6 3.3 %collective-permute-done.4.refs_1_ = bf16[272,256]{1,0:T(8,128)(2,1)S(1)} collective-permute-done((bf16[272,256]{1,0:T(8,128)(2,1)S(1)}, bf16[272,256]{1,0:T(8,128)(2,1)S(1)}, u32[]{:S(2)}, u32[]{:S(2)}) %collective-permute-start.4) | collective-permute-done | bytes 139296 | tf_op jit(solution)/shard_map/ppermute | solution.py:214
  21.9 7.3 %collective-permute-done.6.refs_2_ = bf16[272,256]{1,0:T(8,128)(2,1)S(1)} collective-permute-done((bf16[272,256]{1,0:T(8,128)(2,1)S(1)}, bf16[272,256]{1,0:T(8,128)(2,1)S(1)}, u32[]{:S(2)}, u32[]{:S(2)}) %collective-permute-start.6) | collective-permute-done | bytes 139296 | tf_op jit(solution)/shard_map/ppermute | solution.py:214
  29.2 0.5 dense.1
  29.8 1.2 %collective-permute-done.11 = bf16[128,256]{1,0:T(8,128)(2,1)S(1)} collective-permute-done((bf16[128,256]{1,0:T(8,128)(2,1)S(1)}, bf16[128,256]{1,0:T(8,128)(2,1)S(1)}, u32[]{:S(2)}, u32[]{:S(2)}) %collective-permute-start.11) | collective-permute-done | bytes 65568 | tf_op jit(solution)/shard_map/ppermute | solution.py:217
  31.1 2.5 %collective-permute-start.12 = (bf16[64,256]{1,0:T(8,128)(2,1)S(1)}, bf16[64,256]{1,0:T(8,128)(2,1)S(1)}, u32[]{:S(2)}, u32[]{:S(2)}) collective-permute-start(bf16[64,256]{1,0:T(8,128)(2,1)S(1)} %slice.9), channel_id=1, source_target_pairs={{0,2},{1,3},{2,0},{3,1},{4,6},{5,7},{6,4},{7,5},{8,10},{9,11},{10,... | collective-permute-start | bytes 98312 | tf_op jit(solution)/shard_map/ppermute | solution.py:214
  33.6 2.6 %collective-permute-start.10 = (bf16[256,256]{1,0:T(8,128)(2,1)S(1)}, bf16[256,256]{1,0:T(8,128)(2,1)S(1)}, u32[]{:S(2)}, u32[]{:S(2)}) collective-permute-start(bf16[256,256]{1,0:T(8,128)(2,1)S(1)} %get-tuple-element.30.refs_1_), channel_id=1, source_target_pairs={{0,6},{1,7},{2,4},{3,5},{4,2},{5,3},{6,0},{7,1},{8,14},{9,15},{10,... | collective-permute-start | bytes 393224 | tf_op jit(solution)/shard_map/ppermute | solution.py:214
  36.2 1.8 %collective-permute-start.8 = (bf16[256,256]{1,0:T(8,128)(2,1)S(1)}, bf16[256,256]{1,0:T(8,128)(2,1)S(1)}, u32[]{:S(2)}, u32[]{:S(2)}) collective-permute-start(bf16[256,256]{1,0:T(8,128)(2,1)S(1)} %get-tuple-element.30.refs_1_), channel_id=1, source_target_pairs={{0,2},{1,3},{2,0},{3,1},{4,6},{5,7},{6,4},{7,5},{8,10},{9,11},{10,... | collective-permute-start | bytes 393224 | tf_op jit(solution)/shard_map/ppermute | solution.py:214
  38.1 1.8 %collective-permute-start.15 = (bf16[64,256]{1,0:T(8,128)(2,1)S(1)}, bf16[64,256]{1,0:T(8,128)(2,1)S(1)}, u32[]{:S(2)}, u32[]{:S(2)}) collective-permute-start(bf16[64,256]{1,0:T(8,128)(2,1)S(1)} %add_convert_fusion.3), channel_id=1, source_target_pairs={{0,24},{8,16},{16,8},{24,0},{1,25},{9,17},{17,9},{25,1},{2,26},{10... | collective-permute-start | bytes 98312 | tf_op jit(solution)/shard_map/ppermute | solution.py:211
  39.8 1.3 %collective-permute-start.14 = (bf16[64,256]{1,0:T(8,128)(2,1)S(1)}, bf16[64,256]{1,0:T(8,128)(2,1)S(1)}, u32[]{:S(2)}, u32[]{:S(2)}) collective-permute-start(bf16[64,256]{1,0:T(8,128)(2,1)S(1)} %add_convert_fusion.3), channel_id=1, source_target_pairs={{0,16},{8,24},{16,0},{24,8},{1,17},{9,25},{17,1},{25,9},{2,18},{10... | collective-permute-start | bytes 98312 | tf_op jit(solution)/shard_map/ppermute | solution.py:211
  41.1 1.8 %collective-permute-done.15 = bf16[64,256]{1,0:T(8,128)(2,1)S(1)} collective-permute-done((bf16[64,256]{1,0:T(8,128)(2,1)S(1)}, bf16[64,256]{1,0:T(8,128)(2,1)S(1)}, u32[]{:S(2)}, u32[]{:S(2)}) %collective-permute-start.15) | collective-permute-done | bytes 32800 | tf_op jit(solution)/shard_map/ppermute | solution.py:211
  42.9 1.5 %collective-permute-start.13 = (bf16[64,256]{1,0:T(8,128)(2,1)S(1)}, bf16[64,256]{1,0:T(8,128)(2,1)S(1)}, u32[]{:S(2)}, u32[]{:S(2)}) collective-permute-start(bf16[64,256]{1,0:T(8,128)(2,1)S(1)} %add_convert_fusion.3), channel_id=1, source_target_pairs={{0,8},{8,0},{16,24},{24,16},{1,9},{9,1},{17,25},{25,17},{2,10},{10... | collective-permute-start | bytes 98312 | tf_op jit(solution)/shard_map/ppermute | solution.py:211
  45.0 2.2 %collective-permute-done.9.refs_3_ = bf16[256,256]{1,0:T(8,128)(2,1)S(1)} collective-permute-done((bf16[256,256]{1,0:T(8,128)(2,1)S(1)}, bf16[256,256]{1,0:T(8,128)(2,1)S(1)}, u32[]{:S(2)}, u32[]{:S(2)}) %collective-permute-start.9) | collective-permute-done | bytes 131104 | tf_op jit(solution)/shard_map/ppermute | solution.py:214
  47.2 0.5 collective-permute-start.18
  47.7 0.7 %backward_own.1.refs_1_ = f32[1024,256]{1,0:T(8,128)S(1)} custom-call(bf16[1024,2048]{1,0:T(8,128)(2,1)S(1)} %build.1.refs_0_.st_ref, bf16[256,256]{1,0:T(8,128)(2,1)S(1)} %get-tuple-element.30.refs_1_, bf16[256,256]{1,0:T(8,128)(2,1)S(1)} %collective-permute-done.8.refs_2_, bf16[256,256]{1,0:T(8,128)(2,1)S(1)} %collective-permute-done.9.refs_3_, ...), custom_call_target="tpu_custom_call" | custom-call | flops 536870912 | bytes 1048576 | tf_op jit(solution)/shard_map/backward_own/pallas_call | solution.py:35
  48.8 0.7 %backward_other.1 = (bf16[256,256]{1,0:T(8,128)(2,1)S(1)}, bf16[256,256]{1,0:T(8,128)(2,1)S(1)}, bf16[256,256]{1,0:T(8,128)(2,1)S(1)}, bf16[256,256]{1,0:T(8,128)(2,1)S(1)}) custom-call(bf16[1024,2048]{1,0:T(8,128)(2,1)S(1)} %build.1.refs_0_.st_ref, f32[1024,256]{1,0:T(8,128)S(1)} %backward_own.1.refs_1_, ...), custom_call_target="tpu_custom_call" | custom-call | flops 536870912 | bytes 1048576 | tf_op jit(solution)/shard_map/backward_other/pallas_call | solution.py:35
  49.5 1.6 %collective-permute-start.20 = (bf16[256,256]{1,0:T(8,128)(2,1)S(1)}, bf16[256,256]{1,0:T(8,128)(2,1)S(1)}, u32[]{:S(2)}, u32[]{:S(2)}) collective-permute-start(bf16[256,256]{1,0:T(8,128)(2,1)S(1)} %get-tuple-element.35), channel_id=1, source_target_pairs={{0,8},{8,0},{16,24},{24,16},{1,9},{9,1},{17,25},{25,17},{2,10},{10... | collective-permute-start | bytes 393224 | tf_op jit(solution)/shard_map/ppermute | solution.py:211
  51.1 0.7 %collective-permute-start.21 = (bf16[256,256]{1,0:T(8,128)(2,1)S(1)}, bf16[256,256]{1,0:T(8,128)(2,1)S(1)}, u32[]{:S(2)}, u32[]{:S(2)}) collective-permute-start(bf16[256,256]{1,0:T(8,128)(2,1)S(1)} %get-tuple-element.36), channel_id=1, source_target_pairs={{0,16},{8,24},{16,0},{24,8},{1,17},{9,25},{17,1},{25,9},{2,18},{10... | collective-permute-start | bytes 393224 | tf_op jit(solution)/shard_map/ppermute | solution.py:211
  51.8 1.2 %collective-permute-start.22 = (bf16[256,256]{1,0:T(8,128)(2,1)S(1)}, bf16[256,256]{1,0:T(8,128)(2,1)S(1)}, u32[]{:S(2)}, u32[]{:S(2)}) collective-permute-start(bf16[256,256]{1,0:T(8,128)(2,1)S(1)} %get-tuple-element.37), channel_id=1, source_target_pairs={{0,24},{8,16},{16,8},{24,0},{1,25},{9,17},{17,9},{25,1},{2,26},{10... | collective-permute-start | bytes 393224 | tf_op jit(solution)/shard_map/ppermute | solution.py:211
  53.3 1.2 %collective-permute-start.26 = (bf16[64,256]{1,0:T(8,128)(2,1)S(1)}, bf16[64,256]{1,0:T(8,128)(2,1)S(1)}, u32[]{:S(2)}, u32[]{:S(2)}) collective-permute-start(bf16[64,256]{1,0:T(8,128)(2,1)S(1)} %add_convert_fusion.1.refs_4_), channel_id=1, source_target_pairs={{0,3},{1,2},{2,1},{3,0},{4,7},{5,6},{6,5},{7,4},{8,11},{9,10},{10,... | collective-permute-start | bytes 98312 | tf_op jit(solution)/shard_map/ppermute | solution.py:292
  54.5 1.6 %collective-permute-start.25 = (bf16[64,256]{1,0:T(8,128)(2,1)S(1)}, bf16[64,256]{1,0:T(8,128)(2,1)S(1)}, u32[]{:S(2)}, u32[]{:S(2)}) collective-permute-start(bf16[64,256]{1,0:T(8,128)(2,1)S(1)} %add_convert_fusion.1.refs_4_), channel_id=1, source_target_pairs={{0,2},{1,3},{2,0},{3,1},{4,6},{5,7},{6,4},{7,5},{8,10},{9,11},{10,... | collective-permute-start | bytes 98312 | tf_op jit(solution)/shard_map/ppermute | solution.py:214
  56.0 0.7 %collective-permute-done.26.refs_7_ = bf16[64,256]{1,0:T(8,128)(2,1)S(1)} collective-permute-done((bf16[64,256]{1,0:T(8,128)(2,1)S(1)}, bf16[64,256]{1,0:T(8,128)(2,1)S(1)}, u32[]{:S(2)}, u32[]{:S(2)}) %collective-permute-start.26) | collective-permute-done | bytes 32800 | tf_op jit(solution)/shard_map/ppermute | solution.py:292
  56.7 1.3 %collective-permute-start.24 = (bf16[64,256]{1,0:T(8,128)(2,1)S(1)}, bf16[64,256]{1,0:T(8,128)(2,1)S(1)}, u32[]{:S(2)}, u32[]{:S(2)}) collective-permute-start(bf16[64,256]{1,0:T(8,128)(2,1)S(1)} %add_convert_fusion.1.refs_4_), channel_id=1, source_target_pairs={{0,1},{1,0},{2,3},{3,2},{4,5},{5,4},{6,7},{7,6},{8,9},{9,8},{10,11... | collective-permute-start | bytes 98312 | tf_op jit(solution)/shard_map/ppermute | solution.py:217
  58.0 0.7 %copy.9 = bf16[256,256]{1,0:T(8,128)(2,1)} copy(bf16[256,256]{1,0:T(8,128)(2,1)S(1)} %get-tuple-element.41) | data formatting | bytes 262144
  59.3 0.8 %last.1 = (bf16[256,256]{1,0:T(8,128)(2,1)}, f32[256,256]{1,0:T(8,128)}) custom-call(f32[256,256]{1,0:T(8,128)S(1)} %get-tuple-element.29.grad_agg, bf16[256,256]{1,0:T(8,128)(2,1)S(1)} %get-tuple-element.34.refs_0_, bf16[256,256]{1,0:T(8,128)(2,1)S(1)} %collective-permute-done.20.refs_1_, bf16[256,256]{1,0:T(8,128)(2,1)S(1)} %collective-permute-done.21.refs_2_, ...), custom_call_target="tpu_custom_call" | custom-call | flops 1000000 | bytes 1048576 | tf_op jit(solution)/shard_map/last/pallas_call | solution.py:35
  (49 shorter events, 5.2 us)
Async XLA Ops:
  0.6 8.7 %collective-permute-start.2 = (bf16[256,256]{1,0:T(8,128)(2,1)}, bf16[256,256]{1,0:T(8,128)(2,1)S(1)}, u32[]{:S(2)}, u32[]{:S(2)}) collective-permute-start(bf16[256,256]{1,0:T(8,128)(2,1)} %refs_4_.1), channel_id=1, source_target_pairs={{0,24},{8,16},{16,8},{24,0},{1,25},{9,17},{17,9},{25,1},{2,26},{10... | collective-permute-start | bytes 393224 | tf_op jit(solution)/shard_map/ppermute | solution.py:211
  4.6 6.5 %collective-permute-start.1 = (bf16[256,256]{1,0:T(8,128)(2,1)}, bf16[256,256]{1,0:T(8,128)(2,1)S(1)}, u32[]{:S(2)}, u32[]{:S(2)}) collective-permute-start(bf16[256,256]{1,0:T(8,128)(2,1)} %refs_4_.1), channel_id=1, source_target_pairs={{0,16},{8,24},{16,0},{24,8},{1,17},{9,25},{17,1},{25,9},{2,18},{10... | collective-permute-start | bytes 393224 | tf_op jit(solution)/shard_map/ppermute | solution.py:211
  5.1 6.3 %collective-permute-start = (bf16[256,256]{1,0:T(8,128)(2,1)}, bf16[256,256]{1,0:T(8,128)(2,1)S(1)}, u32[]{:S(2)}, u32[]{:S(2)}) collective-permute-start(bf16[256,256]{1,0:T(8,128)(2,1)} %refs_4_.1), channel_id=1, source_target_pairs={{0,8},{8,0},{16,24},{24,16},{1,9},{9,1},{17,25},{25,17},{2,10},{10... | collective-permute-start | bytes 393224 | tf_op jit(solution)/shard_map/ppermute | solution.py:211
  5.9 1.0 %copy-start.3 = (s32[1,1,64,16,128]{4,3,2,1,0:T(8,128)S(1)}, s32[1,1,64,16,128]{4,3,2,1,0:T(8,128)}, u32[]{:S(2)}) copy-start(s32[1,1,64,16,128]{4,3,2,1,0:T(8,128)} %param.11) | copy-start | bytes 1572868
  6.9 0.7 %copy-start.4 = (s32[1,1,2,64]{3,2,1,0:T(2,128)S(1)}, s32[1,1,2,64]{3,2,1,0:T(2,128)}, u32[]{:S(2)}) copy-start(s32[1,1,2,64]{3,2,1,0:T(2,128)} %param.9) | copy-start | bytes 1540
  7.6 3.8 %copy-start = (bf16[256,256]{1,0:T(8,128)(2,1)S(1)}, bf16[256,256]{1,0:T(8,128)(2,1)}, u32[]{:S(2)}) copy-start(bf16[256,256]{1,0:T(8,128)(2,1)} %refs_4_.1) | copy-start | bytes 393220
  12.3 1.6 %collective-permute-start.3 = (bf16[2,272,256]{2,1,0:T(8,128)(2,1)S(1)}, bf16[2,272,256]{2,1,0:T(8,128)(2,1)S(1)}, u32[]{:S(2)}, u32[]{:S(2)}) collective-permute-start(bf16[2,272,256]{2,1,0:T(8,128)(2,1)S(1)} %forward_near_other.1), channel_id=1, source_target_pairs={{0,1},{1,0},{2,3},{3,2},{4,5},{5,4},{6,7},{7,6},{8,9},{9,8},{10,11... | collective-permute-start | bytes 835592 | tf_op jit(solution)/shard_map/ppermute | solution.py:217
  12.4 3.3 %collective-permute-start.5 = (bf16[2,272,256]{2,1,0:T(8,128)(2,1)S(1)}, bf16[2,272,256]{2,1,0:T(8,128)(2,1)S(1)}, u32[]{:S(2)}, u32[]{:S(2)}) collective-permute-start(bf16[2,272,256]{2,1,0:T(8,128)(2,1)S(1)} %get-tuple-element.25), channel_id=1, source_target_pairs={{0,1},{1,0},{2,3},{3,2},{4,5},{5,4},{6,7},{7,6},{8,9},{9,8},{10,11... | collective-permute-start | bytes 835592 | tf_op jit(solution)/shard_map/ppermute | solution.py:217
  13.4 15.9 %copy-start.1 = (bf16[256,256]{1,0:T(8,128)(2,1)S(1)}, bf16[256,256]{1,0:T(8,128)(2,1)}, u32[]{:S(2)}) copy-start(bf16[256,256]{1,0:T(8,128)(2,1)} %refs_5_.1) | copy-start | bytes 393220
  13.4 15.9 %copy-start.2 = (bf16[256,256]{1,0:T(8,128)(2,1)S(1)}, bf16[256,256]{1,0:T(8,128)(2,1)}, u32[]{:S(2)}) copy-start(bf16[256,256]{1,0:T(8,128)(2,1)} %refs_6_.1) | copy-start | bytes 393220
  14.0 7.9 %collective-permute-start.4 = (bf16[272,256]{1,0:T(8,128)(2,1)S(1)}, bf16[272,256]{1,0:T(8,128)(2,1)S(1)}, u32[]{:S(2)}, u32[]{:S(2)}) collective-permute-start(bf16[272,256]{1,0:T(8,128)(2,1)S(1)} %get-tuple-element.24), channel_id=1, source_target_pairs={{0,2},{1,3},{2,0},{3,1},{4,6},{5,7},{6,4},{7,5},{8,10},{9,11},{10,... | collective-permute-start | bytes 417800 | tf_op jit(solution)/shard_map/ppermute | solution.py:214
  15.7 13.5 %collective-permute-start.6 = (bf16[272,256]{1,0:T(8,128)(2,1)S(1)}, bf16[272,256]{1,0:T(8,128)(2,1)S(1)}, u32[]{:S(2)}, u32[]{:S(2)}) collective-permute-start(bf16[272,256]{1,0:T(8,128)(2,1)S(1)} %get-tuple-element.26), channel_id=1, source_target_pairs={{0,4},{1,5},{2,6},{3,7},{4,0},{5,1},{6,2},{7,3},{8,12},{9,13},{10,... | collective-permute-start | bytes 417800 | tf_op jit(solution)/shard_map/ppermute | solution.py:214
  18.4 10.8 %collective-permute-start.7 = (bf16[272,256]{1,0:T(8,128)(2,1)S(1)}, bf16[272,256]{1,0:T(8,128)(2,1)S(1)}, u32[]{:S(2)}, u32[]{:S(2)}) collective-permute-start(bf16[272,256]{1,0:T(8,128)(2,1)S(1)} %get-tuple-element.27), channel_id=1, source_target_pairs={{0,6},{1,7},{2,4},{3,5},{4,2},{5,3},{6,0},{7,1},{8,14},{9,15},{10,... | collective-permute-start | bytes 417800 | tf_op jit(solution)/shard_map/ppermute | solution.py:214
  29.8 1.3 %collective-permute-start.11 = (bf16[128,256]{1,0:T(8,128)(2,1)S(1)}, bf16[128,256]{1,0:T(8,128)(2,1)S(1)}, u32[]{:S(2)}, u32[]{:S(2)}) collective-permute-start(bf16[128,256]{1,0:T(8,128)(2,1)S(1)} %get-tuple-element.32), channel_id=1, source_target_pairs={{0,1},{1,0},{2,3},{3,2},{4,5},{5,4},{6,7},{7,6},{8,9},{9,8},{10,11... | collective-permute-start | bytes 196616 | tf_op jit(solution)/shard_map/ppermute | solution.py:217
  31.1 6.9 %collective-permute-start.12 = (bf16[64,256]{1,0:T(8,128)(2,1)S(1)}, bf16[64,256]{1,0:T(8,128)(2,1)S(1)}, u32[]{:S(2)}, u32[]{:S(2)}) collective-permute-start(bf16[64,256]{1,0:T(8,128)(2,1)S(1)} %slice.9), channel_id=1, source_target_pairs={{0,2},{1,3},{2,0},{3,1},{4,6},{5,7},{6,4},{7,5},{8,10},{9,11},{10,... | collective-permute-start | bytes 98312 | tf_op jit(solution)/shard_map/ppermute | solution.py:214
  33.6 10.8 %collective-permute-start.10 = (bf16[256,256]{1,0:T(8,128)(2,1)S(1)}, bf16[256,256]{1,0:T(8,128)(2,1)S(1)}, u32[]{:S(2)}, u32[]{:S(2)}) collective-permute-start(bf16[256,256]{1,0:T(8,128)(2,1)S(1)} %get-tuple-element.30.refs_1_), channel_id=1, source_target_pairs={{0,6},{1,7},{2,4},{3,5},{4,2},{5,3},{6,0},{7,1},{8,14},{9,15},{10,... | collective-permute-start | bytes 393224 | tf_op jit(solution)/shard_map/ppermute | solution.py:214
  36.2 10.9 %collective-permute-start.9 = (bf16[256,256]{1,0:T(8,128)(2,1)S(1)}, bf16[256,256]{1,0:T(8,128)(2,1)S(1)}, u32[]{:S(2)}, u32[]{:S(2)}) collective-permute-start(bf16[256,256]{1,0:T(8,128)(2,1)S(1)} %get-tuple-element.30.refs_1_), channel_id=1, source_target_pairs={{0,4},{1,5},{2,6},{3,7},{4,0},{5,1},{6,2},{7,3},{8,12},{9,13},{10,... | collective-permute-start | bytes 393224 | tf_op jit(solution)/shard_map/ppermute | solution.py:214
  36.2 10.9 %collective-permute-start.8 = (bf16[256,256]{1,0:T(8,128)(2,1)S(1)}, bf16[256,256]{1,0:T(8,128)(2,1)S(1)}, u32[]{:S(2)}, u32[]{:S(2)}) collective-permute-start(bf16[256,256]{1,0:T(8,128)(2,1)S(1)} %get-tuple-element.30.refs_1_), channel_id=1, source_target_pairs={{0,2},{1,3},{2,0},{3,1},{4,6},{5,7},{6,4},{7,5},{8,10},{9,11},{10,... | collective-permute-start | bytes 393224 | tf_op jit(solution)/shard_map/ppermute | solution.py:214
  38.1 4.9 %collective-permute-start.15 = (bf16[64,256]{1,0:T(8,128)(2,1)S(1)}, bf16[64,256]{1,0:T(8,128)(2,1)S(1)}, u32[]{:S(2)}, u32[]{:S(2)}) collective-permute-start(bf16[64,256]{1,0:T(8,128)(2,1)S(1)} %add_convert_fusion.3), channel_id=1, source_target_pairs={{0,24},{8,16},{16,8},{24,0},{1,25},{9,17},{17,9},{25,1},{2,26},{10... | collective-permute-start | bytes 98312 | tf_op jit(solution)/shard_map/ppermute | solution.py:211
  39.8 4.7 %collective-permute-start.14 = (bf16[64,256]{1,0:T(8,128)(2,1)S(1)}, bf16[64,256]{1,0:T(8,128)(2,1)S(1)}, u32[]{:S(2)}, u32[]{:S(2)}) collective-permute-start(bf16[64,256]{1,0:T(8,128)(2,1)S(1)} %add_convert_fusion.3), channel_id=1, source_target_pairs={{0,16},{8,24},{16,0},{24,8},{1,17},{9,25},{17,1},{25,9},{2,18},{10... | collective-permute-start | bytes 98312 | tf_op jit(solution)/shard_map/ppermute | solution.py:211
  42.9 4.7 %collective-permute-start.13 = (bf16[64,256]{1,0:T(8,128)(2,1)S(1)}, bf16[64,256]{1,0:T(8,128)(2,1)S(1)}, u32[]{:S(2)}, u32[]{:S(2)}) collective-permute-start(bf16[64,256]{1,0:T(8,128)(2,1)S(1)} %add_convert_fusion.3), channel_id=1, source_target_pairs={{0,8},{8,0},{16,24},{24,16},{1,9},{9,1},{17,25},{25,17},{2,10},{10... | collective-permute-start | bytes 98312 | tf_op jit(solution)/shard_map/ppermute | solution.py:211
  44.5 4.3 %collective-permute-start.19 = (bf16[256,256]{1,0:T(8,128)(2,1)S(1)}, bf16[256,256]{1,0:T(8,128)(2,1)S(1)}, u32[]{:S(2)}, u32[]{:S(2)}) collective-permute-start(bf16[256,256]{1,0:T(8,128)(2,1)S(1)} %get-tuple-element.30.refs_1_), channel_id=1, source_target_pairs={{0,1},{1,0},{2,3},{3,2},{4,5},{5,4},{6,7},{7,6},{8,9},{9,8},{10,11... | collective-permute-start | bytes 393224 | tf_op jit(solution)/shard_map/ppermute | solution.py:217
  44.5 4.3 %collective-permute-start.17 = (bf16[256,256]{1,0:T(8,128)(2,1)S(1)}, bf16[256,256]{1,0:T(8,128)(2,1)S(1)}, u32[]{:S(2)}, u32[]{:S(2)}) collective-permute-start(bf16[256,256]{1,0:T(8,128)(2,1)S(1)} %collective-permute-done.10.refs_4_), channel_id=1, source_target_pairs={{0,1},{1,0},{2,3},{3,2},{4,5},{5,4},{6,7},{7,6},{8,9},{9,8},{10,11... | collective-permute-start | bytes 393224 | tf_op jit(solution)/shard_map/ppermute | solution.py:217
  47.2 1.6 %collective-permute-start.16 = (bf16[256,256]{1,0:T(8,128)(2,1)S(1)}, bf16[256,256]{1,0:T(8,128)(2,1)S(1)}, u32[]{:S(2)}, u32[]{:S(2)}) collective-permute-start(bf16[256,256]{1,0:T(8,128)(2,1)S(1)} %collective-permute-done.9.refs_3_), channel_id=1, source_target_pairs={{0,1},{1,0},{2,3},{3,2},{4,5},{5,4},{6,7},{7,6},{8,9},{9,8},{10,11... | collective-permute-start | bytes 393224 | tf_op jit(solution)/shard_map/ppermute | solution.py:217
  47.2 1.6 %collective-permute-start.18 = (bf16[256,256]{1,0:T(8,128)(2,1)S(1)}, bf16[256,256]{1,0:T(8,128)(2,1)S(1)}, u32[]{:S(2)}, u32[]{:S(2)}) collective-permute-start(bf16[256,256]{1,0:T(8,128)(2,1)S(1)} %collective-permute-done.8.refs_2_), channel_id=1, source_target_pairs={{0,1},{1,0},{2,3},{3,2},{4,5},{5,4},{6,7},{7,6},{8,9},{9,8},{10,11... | collective-permute-start | bytes 393224 | tf_op jit(solution)/shard_map/ppermute | solution.py:217
  48.4 4.9 %collective-permute-start.23 = (bf16[64,256]{1,0:T(8,128)(2,1)S(1)}, bf16[64,256]{1,0:T(8,128)(2,1)S(1)}, u32[]{:S(2)}, u32[]{:S(2)}) collective-permute-start(bf16[64,256]{1,0:T(8,128)(2,1)S(1)} %add_convert_fusion.2), channel_id=1, source_target_pairs={{0,4},{1,5},{2,6},{3,7},{4,0},{5,1},{6,2},{7,3},{8,12},{9,13},{10,... | collective-permute-start | bytes 98312 | tf_op jit(solution)/shard_map/ppermute | solution.py:214
  49.5 9.4 %collective-permute-start.20 = (bf16[256,256]{1,0:T(8,128)(2,1)S(1)}, bf16[256,256]{1,0:T(8,128)(2,1)S(1)}, u32[]{:S(2)}, u32[]{:S(2)}) collective-permute-start(bf16[256,256]{1,0:T(8,128)(2,1)S(1)} %get-tuple-element.35), channel_id=1, source_target_pairs={{0,8},{8,0},{16,24},{24,16},{1,9},{9,1},{17,25},{25,17},{2,10},{10... | collective-permute-start | bytes 393224 | tf_op jit(solution)/shard_map/ppermute | solution.py:211
  51.1 8.2 %collective-permute-start.21 = (bf16[256,256]{1,0:T(8,128)(2,1)S(1)}, bf16[256,256]{1,0:T(8,128)(2,1)S(1)}, u32[]{:S(2)}, u32[]{:S(2)}) collective-permute-start(bf16[256,256]{1,0:T(8,128)(2,1)S(1)} %get-tuple-element.36), channel_id=1, source_target_pairs={{0,16},{8,24},{16,0},{24,8},{1,17},{9,25},{17,1},{25,9},{2,18},{10... | collective-permute-start | bytes 393224 | tf_op jit(solution)/shard_map/ppermute | solution.py:211
  51.8 7.5 %collective-permute-start.22 = (bf16[256,256]{1,0:T(8,128)(2,1)S(1)}, bf16[256,256]{1,0:T(8,128)(2,1)S(1)}, u32[]{:S(2)}, u32[]{:S(2)}) collective-permute-start(bf16[256,256]{1,0:T(8,128)(2,1)S(1)} %get-tuple-element.37), channel_id=1, source_target_pairs={{0,24},{8,16},{16,8},{24,0},{1,25},{9,17},{17,9},{25,1},{2,26},{10... | collective-permute-start | bytes 393224 | tf_op jit(solution)/shard_map/ppermute | solution.py:211
  53.3 3.4 %collective-permute-start.26 = (bf16[64,256]{1,0:T(8,128)(2,1)S(1)}, bf16[64,256]{1,0:T(8,128)(2,1)S(1)}, u32[]{:S(2)}, u32[]{:S(2)}) collective-permute-start(bf16[64,256]{1,0:T(8,128)(2,1)S(1)} %add_convert_fusion.1.refs_4_), channel_id=1, source_target_pairs={{0,3},{1,2},{2,1},{3,0},{4,7},{5,6},{6,5},{7,4},{8,11},{9,10},{10,... | collective-permute-start | bytes 98312 | tf_op jit(solution)/shard_map/ppermute | solution.py:292
  54.5 4.2 %collective-permute-start.25 = (bf16[64,256]{1,0:T(8,128)(2,1)S(1)}, bf16[64,256]{1,0:T(8,128)(2,1)S(1)}, u32[]{:S(2)}, u32[]{:S(2)}) collective-permute-start(bf16[64,256]{1,0:T(8,128)(2,1)S(1)} %add_convert_fusion.1.refs_4_), channel_id=1, source_target_pairs={{0,2},{1,3},{2,0},{3,1},{4,6},{5,7},{6,4},{7,5},{8,10},{9,11},{10,... | collective-permute-start | bytes 98312 | tf_op jit(solution)/shard_map/ppermute | solution.py:214
  56.7 2.1 %collective-permute-start.24 = (bf16[64,256]{1,0:T(8,128)(2,1)S(1)}, bf16[64,256]{1,0:T(8,128)(2,1)S(1)}, u32[]{:S(2)}, u32[]{:S(2)}) collective-permute-start(bf16[64,256]{1,0:T(8,128)(2,1)S(1)} %add_convert_fusion.1.refs_4_), channel_id=1, source_target_pairs={{0,1},{1,0},{2,3},{3,2},{4,5},{5,4},{6,7},{7,6},{8,9},{9,8},{10,11... | collective-permute-start | bytes 98312 | tf_op jit(solution)/shard_map/ppermute | solution.py:217

commit v9 on v7

--- a/solution.py
+++ b/solution.py
@@ -126,7 +126,7 @@
         total = total + part[...].astype(f32)
     degree = total[width : width + 1] + total[width + 1 : width + 2]
     scale = lax.rsqrt(degree + 1.0)
-    agg_t = (total[:width] * scale + feats[...].astype(f32).T).astype(bf16)
+    agg_t = (total[:width] * scale + feats[:width, : cotangent.shape[0]].astype(f32)).astype(bf16)
     agg_ref[...] = agg_t
     w = weight[...]
     preact = jnp.dot(agg_t.T, w, preferred_element_type=f32)
@@ -256,7 +256,7 @@
         functools.partial(dense_kernel, n_z),
         "dense",
         [((rows, width), bf16), ((rows, width), bf16), ((rows, width), f32), ((width, rows), bf16), ((rows, width), bf16)],
-        parts + [features, cotangent, weight],
+        parts + [feats_t, cotangent, weight],
         flops=4 * rows * width * width,
     )
     far = [over_z(scaled, k) for k in range(2, n_z)]

time: 60.4 us -> 60.6 us (level)
  waiting for transfers between devices: 19.6 us -> 20.3 us
  transfers between devices with their start and end apart: 27 -> 27, of which waited for: 12 -> 13; matrix products, arithmetic and copies ran while one was open for 1% -> 1% of each run, Pallas kernels for 7% -> 6%
where the time goes in v9:
time: 60.6 us; the launch traced here: 60.4 us
  starting transfers between devices  30 us (50%)
  waiting for transfers between devices  20.3 us (33%)
  Pallas kernels  6.18 us (10%)
  local copies, waits for them, and re-layouts  2.39 us (4%)
  between operations  1.47 us (2%)
    ppermute x9, starting transfers between devices, over_z(): return lax.ppermute(x, 'col', [(i, i ^ 2 * k) for i in range(n_col)])  13.4 us
    ppermute x9, waiting for transfers between devices, over_z(): return lax.ppermute(x, 'col', [(i, i ^ 2 * k) for i in range(n_col)])  13.2 us
    ppermute x9, starting transfers between devices, over_row(): return lax.ppermute(x, 'row', [(i, i ^ k) for i in range(n_row)])  12.6 us
    pallas_call x12, Pallas kernels, call(): pl.pallas_call(body, out_shape=shapes, in_specs=smem(n_smem) + [pl.BlockS...  6.18 us
    ppermute x9, waiting for transfers between devices, over_row(): return lax.ppermute(x, 'row', [(i, i ^ k) for i in range(n_row)])  4.84 us
    ppermute x8, starting transfers between devices, over_core(): return lax.ppermute(x, 'col', [(i, i ^ 1) for i in range(n_col)])  2.92 us
    unnamed x11, local copies, waits for them, and re-layouts  2.38 us
    ppermute x8, waiting for transfers between devices, over_core(): return lax.ppermute(x, 'col', [(i, i ^ 1) for i in range(n_col)])  1.55 us
  transfers between devices with their start and end apart: 27, of which 13 were waited for; matrix products, arithmetic and copies ran while one was open for 1% of the time, Pallas kernels for 6%

profile of v9, /device:TPU:0, one launch (start us, length us, event | category | flops | bytes accessed | tf_op | source)
XLA Modules:
  0.0 60.4 jit_solution(4847983890820723495)
XLA Ops:
  0.6 3.0 %collective-permute-start.1 = (bf16[256,256]{1,0:T(8,128)(2,1)}, bf16[256,256]{1,0:T(8,128)(2,1)S(1)}, u32[]{:S(2)}, u32[]{:S(2)}) collective-permute-start(bf16[256,256]{1,0:T(8,128)(2,1)} %refs_1_.1), channel_id=1, source_target_pairs={{0,16},{8,24},{16,0},{24,8},{1,17},{9,25},{17,1},{25,9},{2,18},{10... | collective-permute-start | bytes 393224 | tf_op jit(solution)/shard_map/ppermute | solution.py:212
  3.7 1.5 %collective-permute-start = (bf16[256,256]{1,0:T(8,128)(2,1)}, bf16[256,256]{1,0:T(8,128)(2,1)S(1)}, u32[]{:S(2)}, u32[]{:S(2)}) collective-permute-start(bf16[256,256]{1,0:T(8,128)(2,1)} %refs_1_.1), channel_id=1, source_target_pairs={{0,8},{8,0},{16,24},{24,16},{1,9},{9,1},{17,25},{25,17},{2,10},{10... | collective-permute-start | bytes 393224 | tf_op jit(solution)/shard_map/ppermute | solution.py:212
  5.9 1.0 %copy-done.3 = s32[1,1,64,16,128]{4,3,2,1,0:T(8,128)S(1)} copy-done((s32[1,1,64,16,128]{4,3,2,1,0:T(8,128)S(1)}, s32[1,1,64,16,128]{4,3,2,1,0:T(8,128)}, u32[]{:S(2)}) %copy-start.3) | copy-done | bytes 524312
  6.9 0.7 %copy-done.4 = s32[1,1,2,64]{3,2,1,0:T(2,128)S(1)} copy-done((s32[1,1,2,64]{3,2,1,0:T(2,128)S(1)}, s32[1,1,2,64]{3,2,1,0:T(2,128)}, u32[]{:S(2)}) %copy-start.4) | copy-done | bytes 536
  7.6 1.3 %build.1.refs_0_.st_ref = bf16[1024,2048]{1,0:T(8,128)(2,1)S(1)} custom-call(s32[2,64]{1,0:T(2,128)S(1)} %bitcast.3, s32[1,1]{1,0:T(1,128)S(6)} %copy.10.count, s32[64,16,128]{2,1,0:T(8,128)S(1)} %bitcast.2), custom_call_target="tpu_custom_call" | custom-call | flops 4000000000 | bytes 1048576 | tf_op jit(solution)/shard_map/build/pallas_call | solution.py:35
  8.9 1.4 %collective-permute-done.refs_2_ = bf16[256,256]{1,0:T(8,128)(2,1)S(1)} collective-permute-done((bf16[256,256]{1,0:T(8,128)(2,1)}, bf16[256,256]{1,0:T(8,128)(2,1)S(1)}, u32[]{:S(2)}, u32[]{:S(2)}) %collective-permute-start) | collective-permute-done | bytes 131104 | tf_op jit(solution)/shard_map/ppermute | solution.py:212
  10.2 1.2 %collective-permute-done.2.refs_4_ = bf16[256,256]{1,0:T(8,128)(2,1)S(1)} collective-permute-done((bf16[256,256]{1,0:T(8,128)(2,1)}, bf16[256,256]{1,0:T(8,128)(2,1)S(1)}, u32[]{:S(2)}, u32[]{:S(2)}) %collective-permute-start.2) | collective-permute-done | bytes 131104 | tf_op jit(solution)/shard_map/ppermute | solution.py:212
  14.1 1.8 %collective-permute-start.4 = (bf16[272,256]{1,0:T(8,128)(2,1)S(1)}, bf16[272,256]{1,0:T(8,128)(2,1)S(1)}, u32[]{:S(2)}, u32[]{:S(2)}) collective-permute-start(bf16[272,256]{1,0:T(8,128)(2,1)S(1)} %get-tuple-element.26), channel_id=1, source_target_pairs={{0,2},{1,3},{2,0},{3,1},{4,6},{5,7},{6,4},{7,5},{8,10},{9,11},{10,... | collective-permute-start | bytes 417800 | tf_op jit(solution)/shard_map/ppermute | solution.py:215
  16.0 2.7 %collective-permute-start.6 = (bf16[272,256]{1,0:T(8,128)(2,1)S(1)}, bf16[272,256]{1,0:T(8,128)(2,1)S(1)}, u32[]{:S(2)}, u32[]{:S(2)}) collective-permute-start(bf16[272,256]{1,0:T(8,128)(2,1)S(1)} %get-tuple-element.28), channel_id=1, source_target_pairs={{0,4},{1,5},{2,6},{3,7},{4,0},{5,1},{6,2},{7,3},{8,12},{9,13},{10,... | collective-permute-start | bytes 417800 | tf_op jit(solution)/shard_map/ppermute | solution.py:215
  18.7 3.2 %collective-permute-done.4.refs_1_ = bf16[272,256]{1,0:T(8,128)(2,1)S(1)} collective-permute-done((bf16[272,256]{1,0:T(8,128)(2,1)S(1)}, bf16[272,256]{1,0:T(8,128)(2,1)S(1)}, u32[]{:S(2)}, u32[]{:S(2)}) %collective-permute-start.4) | collective-permute-done | bytes 139296 | tf_op jit(solution)/shard_map/ppermute | solution.py:215
  21.9 7.6 %collective-permute-done.6.refs_2_ = bf16[272,256]{1,0:T(8,128)(2,1)S(1)} collective-permute-done((bf16[272,256]{1,0:T(8,128)(2,1)S(1)}, bf16[272,256]{1,0:T(8,128)(2,1)S(1)}, u32[]{:S(2)}, u32[]{:S(2)}) %collective-permute-start.6) | collective-permute-done | bytes 139296 | tf_op jit(solution)/shard_map/ppermute | solution.py:215
  30.2 1.2 %collective-permute-done.11 = bf16[128,256]{1,0:T(8,128)(2,1)S(1)} collective-permute-done((bf16[128,256]{1,0:T(8,128)(2,1)S(1)}, bf16[128,256]{1,0:T(8,128)(2,1)S(1)}, u32[]{:S(2)}, u32[]{:S(2)}) %collective-permute-start.11) | collective-permute-done | bytes 65568 | tf_op jit(solution)/shard_map/ppermute | solution.py:218
  31.5 2.5 %collective-permute-start.12 = (bf16[64,256]{1,0:T(8,128)(2,1)S(1)}, bf16[64,256]{1,0:T(8,128)(2,1)S(1)}, u32[]{:S(2)}, u32[]{:S(2)}) collective-permute-start(bf16[64,256]{1,0:T(8,128)(2,1)S(1)} %slice.9), channel_id=1, source_target_pairs={{0,2},{1,3},{2,0},{3,1},{4,6},{5,7},{6,4},{7,5},{8,10},{9,11},{10,... | collective-permute-start | bytes 98312 | tf_op jit(solution)/shard_map/ppermute | solution.py:215
  34.0 2.6 %collective-permute-start.10 = (bf16[256,256]{1,0:T(8,128)(2,1)S(1)}, bf16[256,256]{1,0:T(8,128)(2,1)S(1)}, u32[]{:S(2)}, u32[]{:S(2)}) collective-permute-start(bf16[256,256]{1,0:T(8,128)(2,1)S(1)} %get-tuple-element.32.refs_1_), channel_id=1, source_target_pairs={{0,6},{1,7},{2,4},{3,5},{4,2},{5,3},{6,0},{7,1},{8,14},{9,15},{10,... | collective-permute-start | bytes 393224 | tf_op jit(solution)/shard_map/ppermute | solution.py:215
  36.6 1.8 %collective-permute-start.8 = (bf16[256,256]{1,0:T(8,128)(2,1)S(1)}, bf16[256,256]{1,0:T(8,128)(2,1)S(1)}, u32[]{:S(2)}, u32[]{:S(2)}) collective-permute-start(bf16[256,256]{1,0:T(8,128)(2,1)S(1)} %get-tuple-element.32.refs_1_), channel_id=1, source_target_pairs={{0,2},{1,3},{2,0},{3,1},{4,6},{5,7},{6,4},{7,5},{8,10},{9,11},{10,... | collective-permute-start | bytes 393224 | tf_op jit(solution)/shard_map/ppermute | solution.py:215
  38.4 2.5 %collective-permute-start.15 = (bf16[64,256]{1,0:T(8,128)(2,1)S(1)}, bf16[64,256]{1,0:T(8,128)(2,1)S(1)}, u32[]{:S(2)}, u32[]{:S(2)}) collective-permute-start(bf16[64,256]{1,0:T(8,128)(2,1)S(1)} %add_convert_fusion.3), channel_id=1, source_target_pairs={{0,24},{8,16},{16,8},{24,0},{1,25},{9,17},{17,9},{25,1},{2,26},{10... | collective-permute-start | bytes 98312 | tf_op jit(solution)/shard_map/ppermute | solution.py:212
  40.9 0.5 collective-permute-start.14
  41.4 1.9 %collective-permute-done.15 = bf16[64,256]{1,0:T(8,128)(2,1)S(1)} collective-permute-done((bf16[64,256]{1,0:T(8,128)(2,1)S(1)}, bf16[64,256]{1,0:T(8,128)(2,1)S(1)}, u32[]{:S(2)}, u32[]{:S(2)}) %collective-permute-start.15) | collective-permute-done | bytes 32800 | tf_op jit(solution)/shard_map/ppermute | solution.py:212
  43.3 1.5 %collective-permute-start.13 = (bf16[64,256]{1,0:T(8,128)(2,1)S(1)}, bf16[64,256]{1,0:T(8,128)(2,1)S(1)}, u32[]{:S(2)}, u32[]{:S(2)}) collective-permute-start(bf16[64,256]{1,0:T(8,128)(2,1)S(1)} %add_convert_fusion.3), channel_id=1, source_target_pairs={{0,8},{8,0},{16,24},{24,16},{1,9},{9,1},{17,25},{25,17},{2,10},{10... | collective-permute-start | bytes 98312 | tf_op jit(solution)/shard_map/ppermute | solution.py:212
  44.8 0.5 collective-permute-start.17
  45.4 2.2 %collective-permute-done.9.refs_3_ = bf16[256,256]{1,0:T(8,128)(2,1)S(1)} collective-permute-done((bf16[256,256]{1,0:T(8,128)(2,1)S(1)}, bf16[256,256]{1,0:T(8,128)(2,1)S(1)}, u32[]{:S(2)}, u32[]{:S(2)}) %collective-permute-start.9) | collective-permute-done | bytes 131104 | tf_op jit(solution)/shard_map/ppermute | solution.py:215
  47.5 0.5 collective-permute-start.18
  48.1 0.7 %backward_own.1.refs_1_ = f32[1024,256]{1,0:T(8,128)S(1)} custom-call(bf16[1024,2048]{1,0:T(8,128)(2,1)S(1)} %build.1.refs_0_.st_ref, bf16[256,256]{1,0:T(8,128)(2,1)S(1)} %get-tuple-element.32.refs_1_, bf16[256,256]{1,0:T(8,128)(2,1)S(1)} %collective-permute-done.8.refs_2_, bf16[256,256]{1,0:T(8,128)(2,1)S(1)} %collective-permute-done.9.refs_3_, ...), custom_call_target="tpu_custom_call" | custom-call | flops 536870912 | bytes 1048576 | tf_op jit(solution)/shard_map/backward_own/pallas_call | solution.py:35
  49.1 0.7 %backward_other.1 = (bf16[256,256]{1,0:T(8,128)(2,1)S(1)}, bf16[256,256]{1,0:T(8,128)(2,1)S(1)}, bf16[256,256]{1,0:T(8,128)(2,1)S(1)}, bf16[256,256]{1,0:T(8,128)(2,1)S(1)}) custom-call(bf16[1024,2048]{1,0:T(8,128)(2,1)S(1)} %build.1.refs_0_.st_ref, f32[1024,256]{1,0:T(8,128)S(1)} %backward_own.1.refs_1_, ...), custom_call_target="tpu_custom_call" | custom-call | flops 536870912 | bytes 1048576 | tf_op jit(solution)/shard_map/backward_other/pallas_call | solution.py:35
  49.9 1.5 %collective-permute-start.20 = (bf16[256,256]{1,0:T(8,128)(2,1)S(1)}, bf16[256,256]{1,0:T(8,128)(2,1)S(1)}, u32[]{:S(2)}, u32[]{:S(2)}) collective-permute-start(bf16[256,256]{1,0:T(8,128)(2,1)S(1)} %get-tuple-element.39), channel_id=1, source_target_pairs={{0,8},{8,0},{16,24},{24,16},{1,9},{9,1},{17,25},{25,17},{2,10},{10... | collective-permute-start | bytes 393224 | tf_op jit(solution)/shard_map/ppermute | solution.py:212
  51.4 1.5 %collective-permute-start.21 = (bf16[256,256]{1,0:T(8,128)(2,1)S(1)}, bf16[256,256]{1,0:T(8,128)(2,1)S(1)}, u32[]{:S(2)}, u32[]{:S(2)}) collective-permute-start(bf16[256,256]{1,0:T(8,128)(2,1)S(1)} %get-tuple-element.40), channel_id=1, source_target_pairs={{0,16},{8,24},{16,0},{24,8},{1,17},{9,25},{17,1},{25,9},{2,18},{10... | collective-permute-start | bytes 393224 | tf_op jit(solution)/shard_map/ppermute | solution.py:212
  53.7 1.2 %collective-permute-start.26 = (bf16[64,256]{1,0:T(8,128)(2,1)S(1)}, bf16[64,256]{1,0:T(8,128)(2,1)S(1)}, u32[]{:S(2)}, u32[]{:S(2)}) collective-permute-start(bf16[64,256]{1,0:T(8,128)(2,1)S(1)} %add_convert_fusion.1.refs_4_), channel_id=1, source_target_pairs={{0,3},{1,2},{2,1},{3,0},{4,7},{5,6},{6,5},{7,4},{8,11},{9,10},{10,... | collective-permute-start | bytes 98312 | tf_op jit(solution)/shard_map/ppermute | solution.py:294
  54.8 1.6 %collective-permute-start.25 = (bf16[64,256]{1,0:T(8,128)(2,1)S(1)}, bf16[64,256]{1,0:T(8,128)(2,1)S(1)}, u32[]{:S(2)}, u32[]{:S(2)}) collective-permute-start(bf16[64,256]{1,0:T(8,128)(2,1)S(1)} %add_convert_fusion.1.refs_4_), channel_id=1, source_target_pairs={{0,2},{1,3},{2,0},{3,1},{4,6},{5,7},{6,4},{7,5},{8,10},{9,11},{10,... | collective-permute-start | bytes 98312 | tf_op jit(solution)/shard_map/ppermute | solution.py:215
  56.4 0.7 %collective-permute-done.26.refs_7_ = bf16[64,256]{1,0:T(8,128)(2,1)S(1)} collective-permute-done((bf16[64,256]{1,0:T(8,128)(2,1)S(1)}, bf16[64,256]{1,0:T(8,128)(2,1)S(1)}, u32[]{:S(2)}, u32[]{:S(2)}) %collective-permute-start.26) | collective-permute-done | bytes 32800 | tf_op jit(solution)/shard_map/ppermute | solution.py:294
  57.1 1.3 %collective-permute-start.24 = (bf16[64,256]{1,0:T(8,128)(2,1)S(1)}, bf16[64,256]{1,0:T(8,128)(2,1)S(1)}, u32[]{:S(2)}, u32[]{:S(2)}) collective-permute-start(bf16[64,256]{1,0:T(8,128)(2,1)S(1)} %add_convert_fusion.1.refs_4_), channel_id=1, source_target_pairs={{0,1},{1,0},{2,3},{3,2},{4,5},{5,4},{6,7},{7,6},{8,9},{9,8},{10,11... | collective-permute-start | bytes 98312 | tf_op jit(solution)/shard_map/ppermute | solution.py:218
  58.4 0.7 %copy.9 = bf16[256,256]{1,0:T(8,128)(2,1)} copy(bf16[256,256]{1,0:T(8,128)(2,1)S(1)} %get-tuple-element.45) | data formatting | bytes 262144
  59.6 0.8 %last.1 = (bf16[256,256]{1,0:T(8,128)(2,1)}, f32[256,256]{1,0:T(8,128)}) custom-call(f32[256,256]{1,0:T(8,128)S(1)} %get-tuple-element.31.grad_agg, bf16[256,256]{1,0:T(8,128)(2,1)S(1)} %get-tuple-element.38.refs_0_, bf16[256,256]{1,0:T(8,128)(2,1)S(1)} %collective-permute-done.20.refs_1_, bf16[256,256]{1,0:T(8,128)(2,1)S(1)} %collective-permute-done.21.refs_2_, ...), custom_call_target="tpu_custom_call" | custom-call | flops 1000000 | bytes 1048576 | tf_op jit(solution)/shard_map/last/pallas_call | solution.py:35
  (50 shorter events, 5.3 us)
Async XLA Ops:
  0.6 8.2 %collective-permute-start.1 = (bf16[256,256]{1,0:T(8,128)(2,1)}, bf16[256,256]{1,0:T(8,128)(2,1)S(1)}, u32[]{:S(2)}, u32[]{:S(2)}) collective-permute-start(bf16[256,256]{1,0:T(8,128)(2,1)} %refs_1_.1), channel_id=1, source_target_pairs={{0,16},{8,24},{16,0},{24,8},{1,17},{9,25},{17,1},{25,9},{2,18},{10... | collective-permute-start | bytes 393224 | tf_op jit(solution)/shard_map/ppermute | solution.py:212
  3.7 6.6 %collective-permute-start = (bf16[256,256]{1,0:T(8,128)(2,1)}, bf16[256,256]{1,0:T(8,128)(2,1)S(1)}, u32[]{:S(2)}, u32[]{:S(2)}) collective-permute-start(bf16[256,256]{1,0:T(8,128)(2,1)} %refs_1_.1), channel_id=1, source_target_pairs={{0,8},{8,0},{16,24},{24,16},{1,9},{9,1},{17,25},{25,17},{2,10},{10... | collective-permute-start | bytes 393224 | tf_op jit(solution)/shard_map/ppermute | solution.py:212
  5.2 6.3 %collective-permute-start.2 = (bf16[256,256]{1,0:T(8,128)(2,1)}, bf16[256,256]{1,0:T(8,128)(2,1)S(1)}, u32[]{:S(2)}, u32[]{:S(2)}) collective-permute-start(bf16[256,256]{1,0:T(8,128)(2,1)} %refs_1_.1), channel_id=1, source_target_pairs={{0,24},{8,16},{16,8},{24,0},{1,25},{9,17},{17,9},{25,1},{2,26},{10... | collective-permute-start | bytes 393224 | tf_op jit(solution)/shard_map/ppermute | solution.py:212
  5.9 1.0 %copy-start.3 = (s32[1,1,64,16,128]{4,3,2,1,0:T(8,128)S(1)}, s32[1,1,64,16,128]{4,3,2,1,0:T(8,128)}, u32[]{:S(2)}) copy-start(s32[1,1,64,16,128]{4,3,2,1,0:T(8,128)} %param.11) | copy-start | bytes 1572868
  6.9 0.7 %copy-start.4 = (s32[1,1,2,64]{3,2,1,0:T(2,128)S(1)}, s32[1,1,2,64]{3,2,1,0:T(2,128)}, u32[]{:S(2)}) copy-start(s32[1,1,2,64]{3,2,1,0:T(2,128)} %param.9) | copy-start | bytes 1540
  7.6 3.9 %copy-start = (bf16[256,256]{1,0:T(8,128)(2,1)S(1)}, bf16[256,256]{1,0:T(8,128)(2,1)}, u32[]{:S(2)}) copy-start(bf16[256,256]{1,0:T(8,128)(2,1)} %refs_1_.1) | copy-start | bytes 393220
  12.4 1.6 %collective-permute-start.3 = (bf16[2,272,256]{2,1,0:T(8,128)(2,1)S(1)}, bf16[2,272,256]{2,1,0:T(8,128)(2,1)S(1)}, u32[]{:S(2)}, u32[]{:S(2)}) collective-permute-start(bf16[2,272,256]{2,1,0:T(8,128)(2,1)S(1)} %forward_near_other.1), channel_id=1, source_target_pairs={{0,1},{1,0},{2,3},{3,2},{4,5},{5,4},{6,7},{7,6},{8,9},{9,8},{10,11... | collective-permute-start | bytes 835592 | tf_op jit(solution)/shard_map/ppermute | solution.py:218
  12.5 3.4 %collective-permute-start.5 = (bf16[2,272,256]{2,1,0:T(8,128)(2,1)S(1)}, bf16[2,272,256]{2,1,0:T(8,128)(2,1)S(1)}, u32[]{:S(2)}, u32[]{:S(2)}) collective-permute-start(bf16[2,272,256]{2,1,0:T(8,128)(2,1)S(1)} %get-tuple-element.27), channel_id=1, source_target_pairs={{0,1},{1,0},{2,3},{3,2},{4,5},{5,4},{6,7},{7,6},{8,9},{9,8},{10,11... | collective-permute-start | bytes 835592 | tf_op jit(solution)/shard_map/ppermute | solution.py:218
  13.4 16.0 %copy-start.1 = (bf16[256,256]{1,0:T(8,128)(2,1)S(1)}, bf16[256,256]{1,0:T(8,128)(2,1)}, u32[]{:S(2)}) copy-start(bf16[256,256]{1,0:T(8,128)(2,1)} %refs_5_.1) | copy-start | bytes 393220
  13.4 16.0 %copy-start.2 = (bf16[256,256]{1,0:T(8,128)(2,1)S(1)}, bf16[256,256]{1,0:T(8,128)(2,1)}, u32[]{:S(2)}) copy-start(bf16[256,256]{1,0:T(8,128)(2,1)} %refs_6_.1) | copy-start | bytes 393220
  14.1 7.8 %collective-permute-start.4 = (bf16[272,256]{1,0:T(8,128)(2,1)S(1)}, bf16[272,256]{1,0:T(8,128)(2,1)S(1)}, u32[]{:S(2)}, u32[]{:S(2)}) collective-permute-start(bf16[272,256]{1,0:T(8,128)(2,1)S(1)} %get-tuple-element.26), channel_id=1, source_target_pairs={{0,2},{1,3},{2,0},{3,1},{4,6},{5,7},{6,4},{7,5},{8,10},{9,11},{10,... | collective-permute-start | bytes 417800 | tf_op jit(solution)/shard_map/ppermute | solution.py:215
  16.0 13.5 %collective-permute-start.6 = (bf16[272,256]{1,0:T(8,128)(2,1)S(1)}, bf16[272,256]{1,0:T(8,128)(2,1)S(1)}, u32[]{:S(2)}, u32[]{:S(2)}) collective-permute-start(bf16[272,256]{1,0:T(8,128)(2,1)S(1)} %get-tuple-element.28), channel_id=1, source_target_pairs={{0,4},{1,5},{2,6},{3,7},{4,0},{5,1},{6,2},{7,3},{8,12},{9,13},{10,... | collective-permute-start | bytes 417800 | tf_op jit(solution)/shard_map/ppermute | solution.py:215
  18.6 10.8 %collective-permute-start.7 = (bf16[272,256]{1,0:T(8,128)(2,1)S(1)}, bf16[272,256]{1,0:T(8,128)(2,1)S(1)}, u32[]{:S(2)}, u32[]{:S(2)}) collective-permute-start(bf16[272,256]{1,0:T(8,128)(2,1)S(1)} %get-tuple-element.29), channel_id=1, source_target_pairs={{0,6},{1,7},{2,4},{3,5},{4,2},{5,3},{6,0},{7,1},{8,14},{9,15},{10,... | collective-permute-start | bytes 417800 | tf_op jit(solution)/shard_map/ppermute | solution.py:215
  30.1 1.3 %collective-permute-start.11 = (bf16[128,256]{1,0:T(8,128)(2,1)S(1)}, bf16[128,256]{1,0:T(8,128)(2,1)S(1)}, u32[]{:S(2)}, u32[]{:S(2)}) collective-permute-start(bf16[128,256]{1,0:T(8,128)(2,1)S(1)} %get-tuple-element.36), channel_id=1, source_target_pairs={{0,1},{1,0},{2,3},{3,2},{4,5},{5,4},{6,7},{7,6},{8,9},{9,8},{10,11... | collective-permute-start | bytes 196616 | tf_op jit(solution)/shard_map/ppermute | solution.py:218
  31.5 6.9 %collective-permute-start.12 = (bf16[64,256]{1,0:T(8,128)(2,1)S(1)}, bf16[64,256]{1,0:T(8,128)(2,1)S(1)}, u32[]{:S(2)}, u32[]{:S(2)}) collective-permute-start(bf16[64,256]{1,0:T(8,128)(2,1)S(1)} %slice.9), channel_id=1, source_target_pairs={{0,2},{1,3},{2,0},{3,1},{4,6},{5,7},{6,4},{7,5},{8,10},{9,11},{10,... | collective-permute-start | bytes 98312 | tf_op jit(solution)/shard_map/ppermute | solution.py:215
  34.0 10.8 %collective-permute-start.10 = (bf16[256,256]{1,0:T(8,128)(2,1)S(1)}, bf16[256,256]{1,0:T(8,128)(2,1)S(1)}, u32[]{:S(2)}, u32[]{:S(2)}) collective-permute-start(bf16[256,256]{1,0:T(8,128)(2,1)S(1)} %get-tuple-element.32.refs_1_), channel_id=1, source_target_pairs={{0,6},{1,7},{2,4},{3,5},{4,2},{5,3},{6,0},{7,1},{8,14},{9,15},{10,... | collective-permute-start | bytes 393224 | tf_op jit(solution)/shard_map/ppermute | solution.py:215
  36.6 10.9 %collective-permute-start.9 = (bf16[256,256]{1,0:T(8,128)(2,1)S(1)}, bf16[256,256]{1,0:T(8,128)(2,1)S(1)}, u32[]{:S(2)}, u32[]{:S(2)}) collective-permute-start(bf16[256,256]{1,0:T(8,128)(2,1)S(1)} %get-tuple-element.32.refs_1_), channel_id=1, source_target_pairs={{0,4},{1,5},{2,6},{3,7},{4,0},{5,1},{6,2},{7,3},{8,12},{9,13},{10,... | collective-permute-start | bytes 393224 | tf_op jit(solution)/shard_map/ppermute | solution.py:215
  36.6 10.9 %collective-permute-start.8 = (bf16[256,256]{1,0:T(8,128)(2,1)S(1)}, bf16[256,256]{1,0:T(8,128)(2,1)S(1)}, u32[]{:S(2)}, u32[]{:S(2)}) collective-permute-start(bf16[256,256]{1,0:T(8,128)(2,1)S(1)} %get-tuple-element.32.refs_1_), channel_id=1, source_target_pairs={{0,2},{1,3},{2,0},{3,1},{4,6},{5,7},{6,4},{7,5},{8,10},{9,11},{10,... | collective-permute-start | bytes 393224 | tf_op jit(solution)/shard_map/ppermute | solution.py:215
  38.4 4.9 %collective-permute-start.15 = (bf16[64,256]{1,0:T(8,128)(2,1)S(1)}, bf16[64,256]{1,0:T(8,128)(2,1)S(1)}, u32[]{:S(2)}, u32[]{:S(2)}) collective-permute-start(bf16[64,256]{1,0:T(8,128)(2,1)S(1)} %add_convert_fusion.3), channel_id=1, source_target_pairs={{0,24},{8,16},{16,8},{24,0},{1,25},{9,17},{17,9},{25,1},{2,26},{10... | collective-permute-start | bytes 98312 | tf_op jit(solution)/shard_map/ppermute | solution.py:212
  40.9 3.9 %collective-permute-start.14 = (bf16[64,256]{1,0:T(8,128)(2,1)S(1)}, bf16[64,256]{1,0:T(8,128)(2,1)S(1)}, u32[]{:S(2)}, u32[]{:S(2)}) collective-permute-start(bf16[64,256]{1,0:T(8,128)(2,1)S(1)} %add_convert_fusion.3), channel_id=1, source_target_pairs={{0,16},{8,24},{16,0},{24,8},{1,17},{9,25},{17,1},{25,9},{2,18},{10... | collective-permute-start | bytes 98312 | tf_op jit(solution)/shard_map/ppermute | solution.py:212
  43.3 4.7 %collective-permute-start.13 = (bf16[64,256]{1,0:T(8,128)(2,1)S(1)}, bf16[64,256]{1,0:T(8,128)(2,1)S(1)}, u32[]{:S(2)}, u32[]{:S(2)}) collective-permute-start(bf16[64,256]{1,0:T(8,128)(2,1)S(1)} %add_convert_fusion.3), channel_id=1, source_target_pairs={{0,8},{8,0},{16,24},{24,16},{1,9},{9,1},{17,25},{25,17},{2,10},{10... | collective-permute-start | bytes 98312 | tf_op jit(solution)/shard_map/ppermute | solution.py:212
  44.8 4.3 %collective-permute-start.19 = (bf16[256,256]{1,0:T(8,128)(2,1)S(1)}, bf16[256,256]{1,0:T(8,128)(2,1)S(1)}, u32[]{:S(2)}, u32[]{:S(2)}) collective-permute-start(bf16[256,256]{1,0:T(8,128)(2,1)S(1)} %get-tuple-element.32.refs_1_), channel_id=1, source_target_pairs={{0,1},{1,0},{2,3},{3,2},{4,5},{5,4},{6,7},{7,6},{8,9},{9,8},{10,11... | collective-permute-start | bytes 393224 | tf_op jit(solution)/shard_map/ppermute | solution.py:218
  44.8 4.3 %collective-permute-start.17 = (bf16[256,256]{1,0:T(8,128)(2,1)S(1)}, bf16[256,256]{1,0:T(8,128)(2,1)S(1)}, u32[]{:S(2)}, u32[]{:S(2)}) collective-permute-start(bf16[256,256]{1,0:T(8,128)(2,1)S(1)} %collective-permute-done.10.refs_4_), channel_id=1, source_target_pairs={{0,1},{1,0},{2,3},{3,2},{4,5},{5,4},{6,7},{7,6},{8,9},{9,8},{10,11... | collective-permute-start | bytes 393224 | tf_op jit(solution)/shard_map/ppermute | solution.py:218
  47.5 1.6 %collective-permute-start.16 = (bf16[256,256]{1,0:T(8,128)(2,1)S(1)}, bf16[256,256]{1,0:T(8,128)(2,1)S(1)}, u32[]{:S(2)}, u32[]{:S(2)}) collective-permute-start(bf16[256,256]{1,0:T(8,128)(2,1)S(1)} %collective-permute-done.9.refs_3_), channel_id=1, source_target_pairs={{0,1},{1,0},{2,3},{3,2},{4,5},{5,4},{6,7},{7,6},{8,9},{9,8},{10,11... | collective-permute-start | bytes 393224 | tf_op jit(solution)/shard_map/ppermute | solution.py:218
  47.5 1.6 %collective-permute-start.18 = (bf16[256,256]{1,0:T(8,128)(2,1)S(1)}, bf16[256,256]{1,0:T(8,128)(2,1)S(1)}, u32[]{:S(2)}, u32[]{:S(2)}) collective-permute-start(bf16[256,256]{1,0:T(8,128)(2,1)S(1)} %collective-permute-done.8.refs_2_), channel_id=1, source_target_pairs={{0,1},{1,0},{2,3},{3,2},{4,5},{5,4},{6,7},{7,6},{8,9},{9,8},{10,11... | collective-permute-start | bytes 393224 | tf_op jit(solution)/shard_map/ppermute | solution.py:218
  48.8 4.9 %collective-permute-start.23 = (bf16[64,256]{1,0:T(8,128)(2,1)S(1)}, bf16[64,256]{1,0:T(8,128)(2,1)S(1)}, u32[]{:S(2)}, u32[]{:S(2)}) collective-permute-start(bf16[64,256]{1,0:T(8,128)(2,1)S(1)} %add_convert_fusion.2), channel_id=1, source_target_pairs={{0,4},{1,5},{2,6},{3,7},{4,0},{5,1},{6,2},{7,3},{8,12},{9,13},{10,... | collective-permute-start | bytes 98312 | tf_op jit(solution)/shard_map/ppermute | solution.py:215
  49.9 9.4 %collective-permute-start.20 = (bf16[256,256]{1,0:T(8,128)(2,1)S(1)}, bf16[256,256]{1,0:T(8,128)(2,1)S(1)}, u32[]{:S(2)}, u32[]{:S(2)}) collective-permute-start(bf16[256,256]{1,0:T(8,128)(2,1)S(1)} %get-tuple-element.39), channel_id=1, source_target_pairs={{0,8},{8,0},{16,24},{24,16},{1,9},{9,1},{17,25},{25,17},{2,10},{10... | collective-permute-start | bytes 393224 | tf_op jit(solution)/shard_map/ppermute | solution.py:212
  51.4 8.2 %collective-permute-start.21 = (bf16[256,256]{1,0:T(8,128)(2,1)S(1)}, bf16[256,256]{1,0:T(8,128)(2,1)S(1)}, u32[]{:S(2)}, u32[]{:S(2)}) collective-permute-start(bf16[256,256]{1,0:T(8,128)(2,1)S(1)} %get-tuple-element.40), channel_id=1, source_target_pairs={{0,16},{8,24},{16,0},{24,8},{1,17},{9,25},{17,1},{25,9},{2,18},{10... | collective-permute-start | bytes 393224 | tf_op jit(solution)/shard_map/ppermute | solution.py:212
  52.9 6.6 %collective-permute-start.22 = (bf16[256,256]{1,0:T(8,128)(2,1)S(1)}, bf16[256,256]{1,0:T(8,128)(2,1)S(1)}, u32[]{:S(2)}, u32[]{:S(2)}) collective-permute-start(bf16[256,256]{1,0:T(8,128)(2,1)S(1)} %get-tuple-element.41), channel_id=1, source_target_pairs={{0,24},{8,16},{16,8},{24,0},{1,25},{9,17},{17,9},{25,1},{2,26},{10... | collective-permute-start | bytes 393224 | tf_op jit(solution)/shard_map/ppermute | solution.py:212
  53.7 3.4 %collective-permute-start.26 = (bf16[64,256]{1,0:T(8,128)(2,1)S(1)}, bf16[64,256]{1,0:T(8,128)(2,1)S(1)}, u32[]{:S(2)}, u32[]{:S(2)}) collective-permute-start(bf16[64,256]{1,0:T(8,128)(2,1)S(1)} %add_convert_fusion.1.refs_4_), channel_id=1, source_target_pairs={{0,3},{1,2},{2,1},{3,0},{4,7},{5,6},{6,5},{7,4},{8,11},{9,10},{10,... | collective-permute-start | bytes 98312 | tf_op jit(solution)/shard_map/ppermute | solution.py:294
  54.8 4.2 %collective-permute-start.25 = (bf16[64,256]{1,0:T(8,128)(2,1)S(1)}, bf16[64,256]{1,0:T(8,128)(2,1)S(1)}, u32[]{:S(2)}, u32[]{:S(2)}) collective-permute-start(bf16[64,256]{1,0:T(8,128)(2,1)S(1)} %add_convert_fusion.1.refs_4_), channel_id=1, source_target_pairs={{0,2},{1,3},{2,0},{3,1},{4,6},{5,7},{6,4},{7,5},{8,10},{9,11},{10,... | collective-permute-start | bytes 98312 | tf_op jit(solution)/shard_map/ppermute | solution.py:215
  57.1 2.1 %collective-permute-start.24 = (bf16[64,256]{1,0:T(8,128)(2,1)S(1)}, bf16[64,256]{1,0:T(8,128)(2,1)S(1)}, u32[]{:S(2)}, u32[]{:S(2)}) collective-permute-start(bf16[64,256]{1,0:T(8,128)(2,1)S(1)} %add_convert_fusion.1.refs_4_), channel_id=1, source_target_pairs={{0,1},{1,0},{2,3},{3,2},{4,5},{5,4},{6,7},{7,6},{8,9},{9,8},{10,11... | collective-permute-start | bytes 98312 | tf_op jit(solution)/shard_map/ppermute | solution.py:218

commit v10 on v7

--- a/solution.py
+++ b/solution.py
@@ -250,7 +250,7 @@
     far = [over_z(x, k) for k, x in enumerate(far, 2)]
     sent = forward("forward_near_other", n_z, 2)
     near = pair_sum("pair_near", forward("forward_near_own", 0, 2), over_core(sent), 2)
-    parts = [near[0], over_z(near[1], 1)] + far
+    parts = far + [over_z(near[1], 1), near[0]]
 
     activated, scaled, grad_agg, agg_t, grad_pre = call(
         functools.partial(dense_kernel, n_z),

time: 60.4 us -> 60.4 us (level)
  transfers between devices with their start and end apart: 27 -> 27, of which waited for: 12 -> 12; matrix products, arithmetic and copies ran while one was open for 1% -> 1% of each run, Pallas kernels for 7% -> 6%
where the time goes in v10:
time: 60.4 us; the launch traced here: 60.2 us
  starting transfers between devices  30.2 us (50%)
  waiting for transfers between devices  19.9 us (33%)
  Pallas kernels  6.25 us (10%)
  local copies, waits for them, and re-layouts  2.39 us (4%)
  between operations  1.47 us (2%)
    ppermute x9, starting transfers between devices, over_z(): return lax.ppermute(x, 'col', [(i, i ^ 2 * k) for i in range(n_col)])  13.4 us
    ppermute x9, waiting for transfers between devices, over_z(): return lax.ppermute(x, 'col', [(i, i ^ 2 * k) for i in range(n_col)])  13 us
    ppermute x9, starting transfers between devices, over_row(): return lax.ppermute(x, 'row', [(i, i ^ k) for i in range(n_row)])  12.8 us
    pallas_call x12, Pallas kernels, call(): pl.pallas_call(body, out_shape=shapes, in_specs=smem(n_smem) + [pl.BlockS...  6.25 us
    ppermute x9, waiting for transfers between devices, over_row(): return lax.ppermute(x, 'row', [(i, i ^ k) for i in range(n_row)])  4.63 us
    ppermute x8, starting transfers between devices, over_core(): return lax.ppermute(x, 'col', [(i, i ^ 1) for i in range(n_col)])  2.92 us
    unnamed x11, local copies, waits for them, and re-layouts  2.38 us
    ppermute x8, waiting for transfers between devices, over_core(): return lax.ppermute(x, 'col', [(i, i ^ 1) for i in range(n_col)])  1.55 us
  transfers between devices with their start and end apart: 27, of which 12 were waited for; matrix products, arithmetic and copies ran while one was open for 1% of the time, Pallas kernels for 6%

profile of v10, /device:TPU:0, one launch (start us, length us, event | category | flops | bytes accessed | tf_op | source)
XLA Modules:
  0.0 60.2 jit_solution(15315334231359735162)
XLA Ops:
  0.6 4.0 %collective-permute-start.2 = (bf16[256,256]{1,0:T(8,128)(2,1)}, bf16[256,256]{1,0:T(8,128)(2,1)S(1)}, u32[]{:S(2)}, u32[]{:S(2)}) collective-permute-start(bf16[256,256]{1,0:T(8,128)(2,1)} %refs_4_.1), channel_id=1, source_target_pairs={{0,24},{8,16},{16,8},{24,0},{1,25},{9,17},{17,9},{25,1},{2,26},{10... | collective-permute-start | bytes 393224 | tf_op jit(solution)/shard_map/ppermute | solution.py:212
  4.6 0.5 collective-permute-start.1
  5.9 1.0 %copy-done.3 = s32[1,1,64,16,128]{4,3,2,1,0:T(8,128)S(1)} copy-done((s32[1,1,64,16,128]{4,3,2,1,0:T(8,128)S(1)}, s32[1,1,64,16,128]{4,3,2,1,0:T(8,128)}, u32[]{:S(2)}) %copy-start.3) | copy-done | bytes 524312
  6.9 0.7 %copy-done.4 = s32[1,1,2,64]{3,2,1,0:T(2,128)S(1)} copy-done((s32[1,1,2,64]{3,2,1,0:T(2,128)S(1)}, s32[1,1,2,64]{3,2,1,0:T(2,128)}, u32[]{:S(2)}) %copy-start.4) | copy-done | bytes 536
  7.6 1.3 %build.1.refs_0_.st_ref = bf16[1024,2048]{1,0:T(8,128)(2,1)S(1)} custom-call(s32[2,64]{1,0:T(2,128)S(1)} %bitcast.3, s32[1,1]{1,0:T(1,128)S(6)} %copy.10.count, s32[64,16,128]{2,1,0:T(8,128)S(1)} %bitcast.2), custom_call_target="tpu_custom_call" | custom-call | flops 4000000000 | bytes 1048576 | tf_op jit(solution)/shard_map/build/pallas_call | solution.py:35
  9.0 2.1 %collective-permute-done.1.refs_3_ = bf16[256,256]{1,0:T(8,128)(2,1)S(1)} collective-permute-done((bf16[256,256]{1,0:T(8,128)(2,1)}, bf16[256,256]{1,0:T(8,128)(2,1)S(1)}, u32[]{:S(2)}, u32[]{:S(2)}) %collective-permute-start.1) | collective-permute-done | bytes 131104 | tf_op jit(solution)/shard_map/ppermute | solution.py:212
  14.0 1.6 %collective-permute-start.7 = (bf16[272,256]{1,0:T(8,128)(2,1)S(1)}, bf16[272,256]{1,0:T(8,128)(2,1)S(1)}, u32[]{:S(2)}, u32[]{:S(2)}) collective-permute-start(bf16[272,256]{1,0:T(8,128)(2,1)S(1)} %get-tuple-element.28), channel_id=1, source_target_pairs={{0,2},{1,3},{2,0},{3,1},{4,6},{5,7},{6,4},{7,5},{8,10},{9,11},{10,... | collective-permute-start | bytes 417800 | tf_op jit(solution)/shard_map/ppermute | solution.py:215
  15.7 2.7 %collective-permute-start.4 = (bf16[272,256]{1,0:T(8,128)(2,1)S(1)}, bf16[272,256]{1,0:T(8,128)(2,1)S(1)}, u32[]{:S(2)}, u32[]{:S(2)}) collective-permute-start(bf16[272,256]{1,0:T(8,128)(2,1)S(1)} %get-tuple-element.26), channel_id=1, source_target_pairs={{0,4},{1,5},{2,6},{3,7},{4,0},{5,1},{6,2},{7,3},{8,12},{9,13},{10,... | collective-permute-start | bytes 417800 | tf_op jit(solution)/shard_map/ppermute | solution.py:215
  18.6 3.3 %collective-permute-done.7.refs_2_ = bf16[272,256]{1,0:T(8,128)(2,1)S(1)} collective-permute-done((bf16[272,256]{1,0:T(8,128)(2,1)S(1)}, bf16[272,256]{1,0:T(8,128)(2,1)S(1)}, u32[]{:S(2)}, u32[]{:S(2)}) %collective-permute-start.7) | collective-permute-done | bytes 139296 | tf_op jit(solution)/shard_map/ppermute | solution.py:215
  21.9 7.3 %collective-permute-done.4.refs_0_ = bf16[272,256]{1,0:T(8,128)(2,1)S(1)} collective-permute-done((bf16[272,256]{1,0:T(8,128)(2,1)S(1)}, bf16[272,256]{1,0:T(8,128)(2,1)S(1)}, u32[]{:S(2)}, u32[]{:S(2)}) %collective-permute-start.4) | collective-permute-done | bytes 139296 | tf_op jit(solution)/shard_map/ppermute | solution.py:215
  30.0 1.2 %collective-permute-done.11 = bf16[128,256]{1,0:T(8,128)(2,1)S(1)} collective-permute-done((bf16[128,256]{1,0:T(8,128)(2,1)S(1)}, bf16[128,256]{1,0:T(8,128)(2,1)S(1)}, u32[]{:S(2)}, u32[]{:S(2)}) %collective-permute-start.11) | collective-permute-done | bytes 65568 | tf_op jit(solution)/shard_map/ppermute | solution.py:218
  31.3 2.5 %collective-permute-start.12 = (bf16[64,256]{1,0:T(8,128)(2,1)S(1)}, bf16[64,256]{1,0:T(8,128)(2,1)S(1)}, u32[]{:S(2)}, u32[]{:S(2)}) collective-permute-start(bf16[64,256]{1,0:T(8,128)(2,1)S(1)} %slice.9), channel_id=1, source_target_pairs={{0,2},{1,3},{2,0},{3,1},{4,6},{5,7},{6,4},{7,5},{8,10},{9,11},{10,... | collective-permute-start | bytes 98312 | tf_op jit(solution)/shard_map/ppermute | solution.py:215
  33.8 2.6 %collective-permute-start.10 = (bf16[256,256]{1,0:T(8,128)(2,1)S(1)}, bf16[256,256]{1,0:T(8,128)(2,1)S(1)}, u32[]{:S(2)}, u32[]{:S(2)}) collective-permute-start(bf16[256,256]{1,0:T(8,128)(2,1)S(1)} %get-tuple-element.32.refs_1_), channel_id=1, source_target_pairs={{0,6},{1,7},{2,4},{3,5},{4,2},{5,3},{6,0},{7,1},{8,14},{9,15},{10,... | collective-permute-start | bytes 393224 | tf_op jit(solution)/shard_map/ppermute | solution.py:215
  36.4 1.8 %collective-permute-start.8 = (bf16[256,256]{1,0:T(8,128)(2,1)S(1)}, bf16[256,256]{1,0:T(8,128)(2,1)S(1)}, u32[]{:S(2)}, u32[]{:S(2)}) collective-permute-start(bf16[256,256]{1,0:T(8,128)(2,1)S(1)} %get-tuple-element.32.refs_1_), channel_id=1, source_target_pairs={{0,2},{1,3},{2,0},{3,1},{4,6},{5,7},{6,4},{7,5},{8,10},{9,11},{10,... | collective-permute-start | bytes 393224 | tf_op jit(solution)/shard_map/ppermute | solution.py:215
  38.2 1.9 %collective-permute-start.15 = (bf16[64,256]{1,0:T(8,128)(2,1)S(1)}, bf16[64,256]{1,0:T(8,128)(2,1)S(1)}, u32[]{:S(2)}, u32[]{:S(2)}) collective-permute-start(bf16[64,256]{1,0:T(8,128)(2,1)S(1)} %add_convert_fusion.3), channel_id=1, source_target_pairs={{0,24},{8,16},{16,8},{24,0},{1,25},{9,17},{17,9},{25,1},{2,26},{10... | collective-permute-start | bytes 98312 | tf_op jit(solution)/shard_map/ppermute | solution.py:212
  40.2 1.1 %collective-permute-start.14 = (bf16[64,256]{1,0:T(8,128)(2,1)S(1)}, bf16[64,256]{1,0:T(8,128)(2,1)S(1)}, u32[]{:S(2)}, u32[]{:S(2)}) collective-permute-start(bf16[64,256]{1,0:T(8,128)(2,1)S(1)} %add_convert_fusion.3), channel_id=1, source_target_pairs={{0,16},{8,24},{16,0},{24,8},{1,17},{9,25},{17,1},{25,9},{2,18},{10... | collective-permute-start | bytes 98312 | tf_op jit(solution)/shard_map/ppermute | solution.py:212
  41.3 1.8 %collective-permute-done.15 = bf16[64,256]{1,0:T(8,128)(2,1)S(1)} collective-permute-done((bf16[64,256]{1,0:T(8,128)(2,1)S(1)}, bf16[64,256]{1,0:T(8,128)(2,1)S(1)}, u32[]{:S(2)}, u32[]{:S(2)}) %collective-permute-start.15) | collective-permute-done | bytes 32800 | tf_op jit(solution)/shard_map/ppermute | solution.py:212
  43.1 1.5 %collective-permute-start.13 = (bf16[64,256]{1,0:T(8,128)(2,1)S(1)}, bf16[64,256]{1,0:T(8,128)(2,1)S(1)}, u32[]{:S(2)}, u32[]{:S(2)}) collective-permute-start(bf16[64,256]{1,0:T(8,128)(2,1)S(1)} %add_convert_fusion.3), channel_id=1, source_target_pairs={{0,8},{8,0},{16,24},{24,16},{1,9},{9,1},{17,25},{25,17},{2,10},{10... | collective-permute-start | bytes 98312 | tf_op jit(solution)/shard_map/ppermute | solution.py:212
  44.6 0.5 collective-permute-start.17
  45.1 2.2 %collective-permute-done.9.refs_3_ = bf16[256,256]{1,0:T(8,128)(2,1)S(1)} collective-permute-done((bf16[256,256]{1,0:T(8,128)(2,1)S(1)}, bf16[256,256]{1,0:T(8,128)(2,1)S(1)}, u32[]{:S(2)}, u32[]{:S(2)}) %collective-permute-start.9) | collective-permute-done | bytes 131104 | tf_op jit(solution)/shard_map/ppermute | solution.py:215
  47.3 0.5 collective-permute-start.18
  47.8 0.7 %backward_own.1.refs_1_ = f32[1024,256]{1,0:T(8,128)S(1)} custom-call(bf16[1024,2048]{1,0:T(8,128)(2,1)S(1)} %build.1.refs_0_.st_ref, bf16[256,256]{1,0:T(8,128)(2,1)S(1)} %get-tuple-element.32.refs_1_, bf16[256,256]{1,0:T(8,128)(2,1)S(1)} %collective-permute-done.8.refs_2_, bf16[256,256]{1,0:T(8,128)(2,1)S(1)} %collective-permute-done.9.refs_3_, ...), custom_call_target="tpu_custom_call" | custom-call | flops 536870912 | bytes 1048576 | tf_op jit(solution)/shard_map/backward_own/pallas_call | solution.py:35
  48.9 0.7 %backward_other.1 = (bf16[256,256]{1,0:T(8,128)(2,1)S(1)}, bf16[256,256]{1,0:T(8,128)(2,1)S(1)}, bf16[256,256]{1,0:T(8,128)(2,1)S(1)}, bf16[256,256]{1,0:T(8,128)(2,1)S(1)}) custom-call(bf16[1024,2048]{1,0:T(8,128)(2,1)S(1)} %build.1.refs_0_.st_ref, f32[1024,256]{1,0:T(8,128)S(1)} %backward_own.1.refs_1_, ...), custom_call_target="tpu_custom_call" | custom-call | flops 536870912 | bytes 1048576 | tf_op jit(solution)/shard_map/backward_other/pallas_call | solution.py:35
  49.6 1.6 %collective-permute-start.20 = (bf16[256,256]{1,0:T(8,128)(2,1)S(1)}, bf16[256,256]{1,0:T(8,128)(2,1)S(1)}, u32[]{:S(2)}, u32[]{:S(2)}) collective-permute-start(bf16[256,256]{1,0:T(8,128)(2,1)S(1)} %get-tuple-element.39), channel_id=1, source_target_pairs={{0,8},{8,0},{16,24},{24,16},{1,9},{9,1},{17,25},{25,17},{2,10},{10... | collective-permute-start | bytes 393224 | tf_op jit(solution)/shard_map/ppermute | solution.py:212
  51.2 1.0 %collective-permute-start.21 = (bf16[256,256]{1,0:T(8,128)(2,1)S(1)}, bf16[256,256]{1,0:T(8,128)(2,1)S(1)}, u32[]{:S(2)}, u32[]{:S(2)}) collective-permute-start(bf16[256,256]{1,0:T(8,128)(2,1)S(1)} %get-tuple-element.40), channel_id=1, source_target_pairs={{0,16},{8,24},{16,0},{24,8},{1,17},{9,25},{17,1},{25,9},{2,18},{10... | collective-permute-start | bytes 393224 | tf_op jit(solution)/shard_map/ppermute | solution.py:212
  52.2 1.0 %collective-permute-start.22 = (bf16[256,256]{1,0:T(8,128)(2,1)S(1)}, bf16[256,256]{1,0:T(8,128)(2,1)S(1)}, u32[]{:S(2)}, u32[]{:S(2)}) collective-permute-start(bf16[256,256]{1,0:T(8,128)(2,1)S(1)} %get-tuple-element.41), channel_id=1, source_target_pairs={{0,24},{8,16},{16,8},{24,0},{1,25},{9,17},{17,9},{25,1},{2,26},{10... | collective-permute-start | bytes 393224 | tf_op jit(solution)/shard_map/ppermute | solution.py:212
  53.5 1.2 %collective-permute-start.26 = (bf16[64,256]{1,0:T(8,128)(2,1)S(1)}, bf16[64,256]{1,0:T(8,128)(2,1)S(1)}, u32[]{:S(2)}, u32[]{:S(2)}) collective-permute-start(bf16[64,256]{1,0:T(8,128)(2,1)S(1)} %add_convert_fusion.1.refs_4_), channel_id=1, source_target_pairs={{0,3},{1,2},{2,1},{3,0},{4,7},{5,6},{6,5},{7,4},{8,11},{9,10},{10,... | collective-permute-start | bytes 98312 | tf_op jit(solution)/shard_map/ppermute | solution.py:294
  54.6 1.6 %collective-permute-start.25 = (bf16[64,256]{1,0:T(8,128)(2,1)S(1)}, bf16[64,256]{1,0:T(8,128)(2,1)S(1)}, u32[]{:S(2)}, u32[]{:S(2)}) collective-permute-start(bf16[64,256]{1,0:T(8,128)(2,1)S(1)} %add_convert_fusion.1.refs_4_), channel_id=1, source_target_pairs={{0,2},{1,3},{2,0},{3,1},{4,6},{5,7},{6,4},{7,5},{8,10},{9,11},{10,... | collective-permute-start | bytes 98312 | tf_op jit(solution)/shard_map/ppermute | solution.py:215
  56.2 0.7 %collective-permute-done.26.refs_7_ = bf16[64,256]{1,0:T(8,128)(2,1)S(1)} collective-permute-done((bf16[64,256]{1,0:T(8,128)(2,1)S(1)}, bf16[64,256]{1,0:T(8,128)(2,1)S(1)}, u32[]{:S(2)}, u32[]{:S(2)}) %collective-permute-start.26) | collective-permute-done | bytes 32800 | tf_op jit(solution)/shard_map/ppermute | solution.py:294
  56.9 1.3 %collective-permute-start.24 = (bf16[64,256]{1,0:T(8,128)(2,1)S(1)}, bf16[64,256]{1,0:T(8,128)(2,1)S(1)}, u32[]{:S(2)}, u32[]{:S(2)}) collective-permute-start(bf16[64,256]{1,0:T(8,128)(2,1)S(1)} %add_convert_fusion.1.refs_4_), channel_id=1, source_target_pairs={{0,1},{1,0},{2,3},{3,2},{4,5},{5,4},{6,7},{7,6},{8,9},{9,8},{10,11... | collective-permute-start | bytes 98312 | tf_op jit(solution)/shard_map/ppermute | solution.py:218
  58.1 0.7 %copy.9 = bf16[256,256]{1,0:T(8,128)(2,1)} copy(bf16[256,256]{1,0:T(8,128)(2,1)S(1)} %get-tuple-element.45) | data formatting | bytes 262144
  59.4 0.8 %last.1 = (bf16[256,256]{1,0:T(8,128)(2,1)}, f32[256,256]{1,0:T(8,128)}) custom-call(f32[256,256]{1,0:T(8,128)S(1)} %get-tuple-element.31.grad_agg, bf16[256,256]{1,0:T(8,128)(2,1)S(1)} %get-tuple-element.38.refs_0_, bf16[256,256]{1,0:T(8,128)(2,1)S(1)} %collective-permute-done.20.refs_1_, bf16[256,256]{1,0:T(8,128)(2,1)S(1)} %collective-permute-done.21.refs_2_, ...), custom_call_target="tpu_custom_call" | custom-call | flops 1000000 | bytes 1048576 | tf_op jit(solution)/shard_map/last/pallas_call | solution.py:35
  (50 shorter events, 5.3 us)
Async XLA Ops:
  0.6 8.3 %collective-permute-start.2 = (bf16[256,256]{1,0:T(8,128)(2,1)}, bf16[256,256]{1,0:T(8,128)(2,1)S(1)}, u32[]{:S(2)}, u32[]{:S(2)}) collective-permute-start(bf16[256,256]{1,0:T(8,128)(2,1)} %refs_4_.1), channel_id=1, source_target_pairs={{0,24},{8,16},{16,8},{24,0},{1,25},{9,17},{17,9},{25,1},{2,26},{10... | collective-permute-start | bytes 393224 | tf_op jit(solution)/shard_map/ppermute | solution.py:212
  4.6 6.5 %collective-permute-start.1 = (bf16[256,256]{1,0:T(8,128)(2,1)}, bf16[256,256]{1,0:T(8,128)(2,1)S(1)}, u32[]{:S(2)}, u32[]{:S(2)}) collective-permute-start(bf16[256,256]{1,0:T(8,128)(2,1)} %refs_4_.1), channel_id=1, source_target_pairs={{0,16},{8,24},{16,0},{24,8},{1,17},{9,25},{17,1},{25,9},{2,18},{10... | collective-permute-start | bytes 393224 | tf_op jit(solution)/shard_map/ppermute | solution.py:212
  5.1 6.3 %collective-permute-start = (bf16[256,256]{1,0:T(8,128)(2,1)}, bf16[256,256]{1,0:T(8,128)(2,1)S(1)}, u32[]{:S(2)}, u32[]{:S(2)}) collective-permute-start(bf16[256,256]{1,0:T(8,128)(2,1)} %refs_4_.1), channel_id=1, source_target_pairs={{0,8},{8,0},{16,24},{24,16},{1,9},{9,1},{17,25},{25,17},{2,10},{10... | collective-permute-start | bytes 393224 | tf_op jit(solution)/shard_map/ppermute | solution.py:212
  5.9 1.0 %copy-start.3 = (s32[1,1,64,16,128]{4,3,2,1,0:T(8,128)S(1)}, s32[1,1,64,16,128]{4,3,2,1,0:T(8,128)}, u32[]{:S(2)}) copy-start(s32[1,1,64,16,128]{4,3,2,1,0:T(8,128)} %param.11) | copy-start | bytes 1572868
  6.9 0.7 %copy-start.4 = (s32[1,1,2,64]{3,2,1,0:T(2,128)S(1)}, s32[1,1,2,64]{3,2,1,0:T(2,128)}, u32[]{:S(2)}) copy-start(s32[1,1,2,64]{3,2,1,0:T(2,128)} %param.9) | copy-start | bytes 1540
  7.6 3.8 %copy-start = (bf16[256,256]{1,0:T(8,128)(2,1)S(1)}, bf16[256,256]{1,0:T(8,128)(2,1)}, u32[]{:S(2)}) copy-start(bf16[256,256]{1,0:T(8,128)(2,1)} %refs_4_.1) | copy-start | bytes 393220
  12.3 1.6 %collective-permute-start.6 = (bf16[2,272,256]{2,1,0:T(8,128)(2,1)S(1)}, bf16[2,272,256]{2,1,0:T(8,128)(2,1)S(1)}, u32[]{:S(2)}, u32[]{:S(2)}) collective-permute-start(bf16[2,272,256]{2,1,0:T(8,128)(2,1)S(1)} %forward_near_other.1), channel_id=1, source_target_pairs={{0,1},{1,0},{2,3},{3,2},{4,5},{5,4},{6,7},{7,6},{8,9},{9,8},{10,11... | collective-permute-start | bytes 835592 | tf_op jit(solution)/shard_map/ppermute | solution.py:218
  12.4 3.3 %collective-permute-start.3 = (bf16[2,272,256]{2,1,0:T(8,128)(2,1)S(1)}, bf16[2,272,256]{2,1,0:T(8,128)(2,1)S(1)}, u32[]{:S(2)}, u32[]{:S(2)}) collective-permute-start(bf16[2,272,256]{2,1,0:T(8,128)(2,1)S(1)} %get-tuple-element.25), channel_id=1, source_target_pairs={{0,1},{1,0},{2,3},{3,2},{4,5},{5,4},{6,7},{7,6},{8,9},{9,8},{10,11... | collective-permute-start | bytes 835592 | tf_op jit(solution)/shard_map/ppermute | solution.py:218
  13.4 15.9 %copy-start.1 = (bf16[256,256]{1,0:T(8,128)(2,1)S(1)}, bf16[256,256]{1,0:T(8,128)(2,1)}, u32[]{:S(2)}) copy-start(bf16[256,256]{1,0:T(8,128)(2,1)} %refs_5_.1) | copy-start | bytes 393220
  13.4 15.9 %copy-start.2 = (bf16[256,256]{1,0:T(8,128)(2,1)S(1)}, bf16[256,256]{1,0:T(8,128)(2,1)}, u32[]{:S(2)}) copy-start(bf16[256,256]{1,0:T(8,128)(2,1)} %refs_6_.1) | copy-start | bytes 393220
  14.0 7.9 %collective-permute-start.7 = (bf16[272,256]{1,0:T(8,128)(2,1)S(1)}, bf16[272,256]{1,0:T(8,128)(2,1)S(1)}, u32[]{:S(2)}, u32[]{:S(2)}) collective-permute-start(bf16[272,256]{1,0:T(8,128)(2,1)S(1)} %get-tuple-element.28), channel_id=1, source_target_pairs={{0,2},{1,3},{2,0},{3,1},{4,6},{5,7},{6,4},{7,5},{8,10},{9,11},{10,... | collective-permute-start | bytes 417800 | tf_op jit(solution)/shard_map/ppermute | solution.py:215
  15.7 13.5 %collective-permute-start.4 = (bf16[272,256]{1,0:T(8,128)(2,1)S(1)}, bf16[272,256]{1,0:T(8,128)(2,1)S(1)}, u32[]{:S(2)}, u32[]{:S(2)}) collective-permute-start(bf16[272,256]{1,0:T(8,128)(2,1)S(1)} %get-tuple-element.26), channel_id=1, source_target_pairs={{0,4},{1,5},{2,6},{3,7},{4,0},{5,1},{6,2},{7,3},{8,12},{9,13},{10,... | collective-permute-start | bytes 417800 | tf_op jit(solution)/shard_map/ppermute | solution.py:215
  18.4 10.8 %collective-permute-start.5 = (bf16[272,256]{1,0:T(8,128)(2,1)S(1)}, bf16[272,256]{1,0:T(8,128)(2,1)S(1)}, u32[]{:S(2)}, u32[]{:S(2)}) collective-permute-start(bf16[272,256]{1,0:T(8,128)(2,1)S(1)} %get-tuple-element.27), channel_id=1, source_target_pairs={{0,6},{1,7},{2,4},{3,5},{4,2},{5,3},{6,0},{7,1},{8,14},{9,15},{10,... | collective-permute-start | bytes 417800 | tf_op jit(solution)/shard_map/ppermute | solution.py:215
  29.9 1.3 %collective-permute-start.11 = (bf16[128,256]{1,0:T(8,128)(2,1)S(1)}, bf16[128,256]{1,0:T(8,128)(2,1)S(1)}, u32[]{:S(2)}, u32[]{:S(2)}) collective-permute-start(bf16[128,256]{1,0:T(8,128)(2,1)S(1)} %get-tuple-element.36), channel_id=1, source_target_pairs={{0,1},{1,0},{2,3},{3,2},{4,5},{5,4},{6,7},{7,6},{8,9},{9,8},{10,11... | collective-permute-start | bytes 196616 | tf_op jit(solution)/shard_map/ppermute | solution.py:218
  31.3 6.9 %collective-permute-start.12 = (bf16[64,256]{1,0:T(8,128)(2,1)S(1)}, bf16[64,256]{1,0:T(8,128)(2,1)S(1)}, u32[]{:S(2)}, u32[]{:S(2)}) collective-permute-start(bf16[64,256]{1,0:T(8,128)(2,1)S(1)} %slice.9), channel_id=1, source_target_pairs={{0,2},{1,3},{2,0},{3,1},{4,6},{5,7},{6,4},{7,5},{8,10},{9,11},{10,... | collective-permute-start | bytes 98312 | tf_op jit(solution)/shard_map/ppermute | solution.py:215
  33.8 10.8 %collective-permute-start.10 = (bf16[256,256]{1,0:T(8,128)(2,1)S(1)}, bf16[256,256]{1,0:T(8,128)(2,1)S(1)}, u32[]{:S(2)}, u32[]{:S(2)}) collective-permute-start(bf16[256,256]{1,0:T(8,128)(2,1)S(1)} %get-tuple-element.32.refs_1_), channel_id=1, source_target_pairs={{0,6},{1,7},{2,4},{3,5},{4,2},{5,3},{6,0},{7,1},{8,14},{9,15},{10,... | collective-permute-start | bytes 393224 | tf_op jit(solution)/shard_map/ppermute | solution.py:215
  36.4 10.9 %collective-permute-start.9 = (bf16[256,256]{1,0:T(8,128)(2,1)S(1)}, bf16[256,256]{1,0:T(8,128)(2,1)S(1)}, u32[]{:S(2)}, u32[]{:S(2)}) collective-permute-start(bf16[256,256]{1,0:T(8,128)(2,1)S(1)} %get-tuple-element.32.refs_1_), channel_id=1, source_target_pairs={{0,4},{1,5},{2,6},{3,7},{4,0},{5,1},{6,2},{7,3},{8,12},{9,13},{10,... | collective-permute-start | bytes 393224 | tf_op jit(solution)/shard_map/ppermute | solution.py:215
  36.4 10.9 %collective-permute-start.8 = (bf16[256,256]{1,0:T(8,128)(2,1)S(1)}, bf16[256,256]{1,0:T(8,128)(2,1)S(1)}, u32[]{:S(2)}, u32[]{:S(2)}) collective-permute-start(bf16[256,256]{1,0:T(8,128)(2,1)S(1)} %get-tuple-element.32.refs_1_), channel_id=1, source_target_pairs={{0,2},{1,3},{2,0},{3,1},{4,6},{5,7},{6,4},{7,5},{8,10},{9,11},{10,... | collective-permute-start | bytes 393224 | tf_op jit(solution)/shard_map/ppermute | solution.py:215
  38.2 4.9 %collective-permute-start.15 = (bf16[64,256]{1,0:T(8,128)(2,1)S(1)}, bf16[64,256]{1,0:T(8,128)(2,1)S(1)}, u32[]{:S(2)}, u32[]{:S(2)}) collective-permute-start(bf16[64,256]{1,0:T(8,128)(2,1)S(1)} %add_convert_fusion.3), channel_id=1, source_target_pairs={{0,24},{8,16},{16,8},{24,0},{1,25},{9,17},{17,9},{25,1},{2,26},{10... | collective-permute-start | bytes 98312 | tf_op jit(solution)/shard_map/ppermute | solution.py:212
  40.2 4.5 %collective-permute-start.14 = (bf16[64,256]{1,0:T(8,128)(2,1)S(1)}, bf16[64,256]{1,0:T(8,128)(2,1)S(1)}, u32[]{:S(2)}, u32[]{:S(2)}) collective-permute-start(bf16[64,256]{1,0:T(8,128)(2,1)S(1)} %add_convert_fusion.3), channel_id=1, source_target_pairs={{0,16},{8,24},{16,0},{24,8},{1,17},{9,25},{17,1},{25,9},{2,18},{10... | collective-permute-start | bytes 98312 | tf_op jit(solution)/shard_map/ppermute | solution.py:212
  43.1 4.7 %collective-permute-start.13 = (bf16[64,256]{1,0:T(8,128)(2,1)S(1)}, bf16[64,256]{1,0:T(8,128)(2,1)S(1)}, u32[]{:S(2)}, u32[]{:S(2)}) collective-permute-start(bf16[64,256]{1,0:T(8,128)(2,1)S(1)} %add_convert_fusion.3), channel_id=1, source_target_pairs={{0,8},{8,0},{16,24},{24,16},{1,9},{9,1},{17,25},{25,17},{2,10},{10... | collective-permute-start | bytes 98312 | tf_op jit(solution)/shard_map/ppermute | solution.py:212
  44.6 4.3 %collective-permute-start.19 = (bf16[256,256]{1,0:T(8,128)(2,1)S(1)}, bf16[256,256]{1,0:T(8,128)(2,1)S(1)}, u32[]{:S(2)}, u32[]{:S(2)}) collective-permute-start(bf16[256,256]{1,0:T(8,128)(2,1)S(1)} %get-tuple-element.32.refs_1_), channel_id=1, source_target_pairs={{0,1},{1,0},{2,3},{3,2},{4,5},{5,4},{6,7},{7,6},{8,9},{9,8},{10,11... | collective-permute-start | bytes 393224 | tf_op jit(solution)/shard_map/ppermute | solution.py:218
  44.6 4.3 %collective-permute-start.17 = (bf16[256,256]{1,0:T(8,128)(2,1)S(1)}, bf16[256,256]{1,0:T(8,128)(2,1)S(1)}, u32[]{:S(2)}, u32[]{:S(2)}) collective-permute-start(bf16[256,256]{1,0:T(8,128)(2,1)S(1)} %collective-permute-done.10.refs_4_), channel_id=1, source_target_pairs={{0,1},{1,0},{2,3},{3,2},{4,5},{5,4},{6,7},{7,6},{8,9},{9,8},{10,11... | collective-permute-start | bytes 393224 | tf_op jit(solution)/shard_map/ppermute | solution.py:218
  47.3 1.6 %collective-permute-start.16 = (bf16[256,256]{1,0:T(8,128)(2,1)S(1)}, bf16[256,256]{1,0:T(8,128)(2,1)S(1)}, u32[]{:S(2)}, u32[]{:S(2)}) collective-permute-start(bf16[256,256]{1,0:T(8,128)(2,1)S(1)} %collective-permute-done.9.refs_3_), channel_id=1, source_target_pairs={{0,1},{1,0},{2,3},{3,2},{4,5},{5,4},{6,7},{7,6},{8,9},{9,8},{10,11... | collective-permute-start | bytes 393224 | tf_op jit(solution)/shard_map/ppermute | solution.py:218
  47.3 1.6 %collective-permute-start.18 = (bf16[256,256]{1,0:T(8,128)(2,1)S(1)}, bf16[256,256]{1,0:T(8,128)(2,1)S(1)}, u32[]{:S(2)}, u32[]{:S(2)}) collective-permute-start(bf16[256,256]{1,0:T(8,128)(2,1)S(1)} %collective-permute-done.8.refs_2_), channel_id=1, source_target_pairs={{0,1},{1,0},{2,3},{3,2},{4,5},{5,4},{6,7},{7,6},{8,9},{9,8},{10,11... | collective-permute-start | bytes 393224 | tf_op jit(solution)/shard_map/ppermute | solution.py:218
  48.5 4.9 %collective-permute-start.23 = (bf16[64,256]{1,0:T(8,128)(2,1)S(1)}, bf16[64,256]{1,0:T(8,128)(2,1)S(1)}, u32[]{:S(2)}, u32[]{:S(2)}) collective-permute-start(bf16[64,256]{1,0:T(8,128)(2,1)S(1)} %add_convert_fusion.2), channel_id=1, source_target_pairs={{0,4},{1,5},{2,6},{3,7},{4,0},{5,1},{6,2},{7,3},{8,12},{9,13},{10,... | collective-permute-start | bytes 98312 | tf_op jit(solution)/shard_map/ppermute | solution.py:215
  49.6 9.4 %collective-permute-start.20 = (bf16[256,256]{1,0:T(8,128)(2,1)S(1)}, bf16[256,256]{1,0:T(8,128)(2,1)S(1)}, u32[]{:S(2)}, u32[]{:S(2)}) collective-permute-start(bf16[256,256]{1,0:T(8,128)(2,1)S(1)} %get-tuple-element.39), channel_id=1, source_target_pairs={{0,8},{8,0},{16,24},{24,16},{1,9},{9,1},{17,25},{25,17},{2,10},{10... | collective-permute-start | bytes 393224 | tf_op jit(solution)/shard_map/ppermute | solution.py:212
  51.2 8.2 %collective-permute-start.21 = (bf16[256,256]{1,0:T(8,128)(2,1)S(1)}, bf16[256,256]{1,0:T(8,128)(2,1)S(1)}, u32[]{:S(2)}, u32[]{:S(2)}) collective-permute-start(bf16[256,256]{1,0:T(8,128)(2,1)S(1)} %get-tuple-element.40), channel_id=1, source_target_pairs={{0,16},{8,24},{16,0},{24,8},{1,17},{9,25},{17,1},{25,9},{2,18},{10... | collective-permute-start | bytes 393224 | tf_op jit(solution)/shard_map/ppermute | solution.py:212
  52.2 7.2 %collective-permute-start.22 = (bf16[256,256]{1,0:T(8,128)(2,1)S(1)}, bf16[256,256]{1,0:T(8,128)(2,1)S(1)}, u32[]{:S(2)}, u32[]{:S(2)}) collective-permute-start(bf16[256,256]{1,0:T(8,128)(2,1)S(1)} %get-tuple-element.41), channel_id=1, source_target_pairs={{0,24},{8,16},{16,8},{24,0},{1,25},{9,17},{17,9},{25,1},{2,26},{10... | collective-permute-start | bytes 393224 | tf_op jit(solution)/shard_map/ppermute | solution.py:212
  53.5 3.4 %collective-permute-start.26 = (bf16[64,256]{1,0:T(8,128)(2,1)S(1)}, bf16[64,256]{1,0:T(8,128)(2,1)S(1)}, u32[]{:S(2)}, u32[]{:S(2)}) collective-permute-start(bf16[64,256]{1,0:T(8,128)(2,1)S(1)} %add_convert_fusion.1.refs_4_), channel_id=1, source_target_pairs={{0,3},{1,2},{2,1},{3,0},{4,7},{5,6},{6,5},{7,4},{8,11},{9,10},{10,... | collective-permute-start | bytes 98312 | tf_op jit(solution)/shard_map/ppermute | solution.py:294
  54.6 4.2 %collective-permute-start.25 = (bf16[64,256]{1,0:T(8,128)(2,1)S(1)}, bf16[64,256]{1,0:T(8,128)(2,1)S(1)}, u32[]{:S(2)}, u32[]{:S(2)}) collective-permute-start(bf16[64,256]{1,0:T(8,128)(2,1)S(1)} %add_convert_fusion.1.refs_4_), channel_id=1, source_target_pairs={{0,2},{1,3},{2,0},{3,1},{4,6},{5,7},{6,4},{7,5},{8,10},{9,11},{10,... | collective-permute-start | bytes 98312 | tf_op jit(solution)/shard_map/ppermute | solution.py:215
  56.9 2.1 %collective-permute-start.24 = (bf16[64,256]{1,0:T(8,128)(2,1)S(1)}, bf16[64,256]{1,0:T(8,128)(2,1)S(1)}, u32[]{:S(2)}, u32[]{:S(2)}) collective-permute-start(bf16[64,256]{1,0:T(8,128)(2,1)S(1)} %add_convert_fusion.1.refs_4_), channel_id=1, source_target_pairs={{0,1},{1,0},{2,3},{3,2},{4,5},{5,4},{6,7},{7,6},{8,9},{9,8},{10,11... | collective-permute-start | bytes 98312 | tf_op jit(solution)/shard_map/ppermute | solution.py:218
